TPU v7x, 32 devices: a whole 2x2x4 slice. The times are simulated.
32 devices in a mesh: tm: 4 (over z), lat: 2 (over x), lon: 4 (over y, core).
Axes of the slice: x: 2, y: 2, z: 4, core: 2. Of those that a mesh axis runs over, the one named last changes fastest.
Arguments:
- tokens: bfloat16 [16, 8, 32, 768], P('tm', 'lat', 'lon'), may hold values from -40 to 40
- key_count: int32 [4, 2, 8], P('tm', 'lat', 'lon'), may hold values from 1 to 64
- norm_gain: float32 [768], replicated, may hold values from 0.1 to 1.9
- qkv_weight: bfloat16 [3, 768, 384], replicated, may hold values from -0.21875 to 0.21875
- out_weight: bfloat16 [384, 768], replicated, may hold values from -0.3125 to 0.3125
- logit_scale: float32 [6], replicated, may hold values from 1 to 3
- grad_out: bfloat16 [16, 8, 32, 768], P('tm', 'lat', 'lon'), may hold values from -12 to 12
Outputs:
- grad_tokens: bfloat16 [16, 8, 32, 768], P('tm', 'lat', 'lon')
All inputs are finite; a program needn't handle non-finite values.
Results may differ from a plain program's by a relative error of at most 0.012.
The roundings to bfloat16 on the way count: a program that leaves them out, or rounds other values in their place, can miss the bound.
Values may be sent and summed in bfloat16 or wider, within the bound.
No kernel may reach another device: no remote copies, remote signals or barrier semaphores. Data moves between devices by JAX's collectives and lax.ppermute only.
A program may use at most 128 MiB of HBM per device.

v0:
```python
import functools
import math

import jax
import jax.numpy as jnp
from jax import lax
from jax.experimental import pallas as pl
from jax.experimental.pallas import tpu as pltpu
from jax.sharding import PartitionSpec as P

HEADS = 6
HEAD_DIM = 64
BLOCK = 4
CELLS = BLOCK * BLOCK * BLOCK
HALF = HEADS // 2
HALF_WIDTH = HALF * HEAD_DIM
PAIR_WIDTH = 2 * HALF_WIDTH
TILE = 2 * HEAD_DIM
TILES = PAIR_WIDTH // TILE
DEAD_TOKEN = 1024.0
DEAD_KEY = 64.0
DROPPED = -1e30

EPS = 1e-06
F32 = jnp.float32
BF16 = jnp.bfloat16


def pair_swap(array, axis, phase, periodic):
    count = lax.axis_size(axis)
    pairs = []
    for device in range(count):
        partner = device + 1 if device % 2 == phase else device - 1
        if periodic:
            partner = partner % count
        if 0 <= partner < count:
            pairs.append((device, partner))
    return lax.ppermute(array, axis, pairs)


def shift_by(array, axis, step):
    count = lax.axis_size(axis)
    pairs = [(i, i + step) for i in range(count) if 0 <= i + step < count]
    return lax.ppermute(array, axis, pairs)


def dot(a, b):
    return lax.dot_general(a, b, (((1,), (0,)), ((), ())), preferred_element_type=F32)


def dot_last(a, b):
    return lax.dot_general(a, b, (((1,), (1,)), ((), ())), preferred_element_type=F32)


def dot_first(a, b):
    return lax.dot_general(a, b, (((0,), (0,)), ((), ())), preferred_element_type=F32)


def head_means(values):
    rows = lax.broadcasted_iota(jnp.int32, (TILE, TILE), 0) // HEAD_DIM
    cols = lax.broadcasted_iota(jnp.int32, (TILE, TILE), 1) // HEAD_DIM
    ones = (rows == cols).astype(F32).astype(BF16)
    high = values.astype(BF16)
    low = (values - high.astype(F32)).astype(BF16)
    pieces = []
    for start in range(0, values.shape[1], TILE):
        cut = slice(start, start + TILE)
        pieces.append(dot(high[:, cut], ones) + dot(low[:, cut], ones))
    return jnp.concatenate(pieces, 1) * (1.0 / HEAD_DIM)


def block_order(lat_rows, lon_cols, count, parity):
    blocks = lon_cols // BLOCK
    row = lax.broadcasted_iota(jnp.int32, (count, count), 0)
    source = lax.broadcasted_iota(jnp.int32, (count, count), 1)
    slot = row // CELLS
    place = row % CELLS
    frame = place // (BLOCK * BLOCK)
    lat = (place // BLOCK) % BLOCK
    col = place % BLOCK
    block = jnp.where(parity == 1, blocks - 1 - slot, slot)
    wanted = (frame * lat_rows + lat) * lon_cols + block * BLOCK + col
    return (source == wanted).astype(F32).astype(BF16)


def norm_kernel(count_ref, tokens_ref, gain_ref, normed_ref, first_ref, last_ref):
    frames, lat_rows, lon_cols, width = tokens_ref.shape
    cells = frames * lat_rows * lon_cols
    blocks = lon_cols // BLOCK
    parity = lax.rem(lax.axis_index("lon"), 2)
    x = tokens_ref[...].astype(F32).reshape(cells, width)
    inverse = lax.rsqrt(jnp.mean(x * x, -1, keepdims=True) + EPS)
    normed = (x * inverse * gain_ref[...]).astype(BF16)
    normed = dot(block_order(lat_rows, lon_cols, cells, parity), normed)
    normed_ref[...] = normed.astype(BF16)
    place = lax.broadcasted_iota(jnp.int32, (CELLS, 1), 0)
    for slot, out in ((0, first_ref), (blocks - 1, last_ref)):
        block = jnp.where(parity == 1, blocks - 1 - slot, slot)
        live = place < count_ref[0, 0, block]
        rows = normed[slot * CELLS : (slot + 1) * CELLS]
        out[...] = jnp.where(live, rows, DEAD_TOKEN).astype(BF16)


def halves(first, second):
    low = jnp.concatenate([first[:, :HALF_WIDTH], second[:, :HALF_WIDTH]], 1)
    high = jnp.concatenate([first[:, HALF_WIDTH:], second[:, HALF_WIDTH:]], 1)
    return low, high


def project_kernel(
    count_ref, normed_ref, grad_ref, qkv_ref, out_weight_ref,
    kv_own_ref, kv_other_ref, qg_own_ref, qg_other_ref, raw_ref,
):
    frames, lat_rows, lon_cols, width = grad_ref.shape
    cells = frames * lat_rows * lon_cols
    blocks = lon_cols // BLOCK
    parity = lax.rem(lax.axis_index("lon"), 2)
    upper = lax.rem(lax.axis_index("lat"), 2) == 1
    normed = normed_ref[...]
    query = dot(normed, qkv_ref[0])
    key = dot(normed, qkv_ref[1])
    value = dot(normed, qkv_ref[2])
    raw_ref[:, : HEADS * HEAD_DIM] = query
    raw_ref[:, HEADS * HEAD_DIM :] = key
    grad = dot_last(
        grad_ref[...].astype(F32).reshape(cells, width).astype(BF16), out_weight_ref[...]
    ).astype(BF16)
    grad = dot(block_order(lat_rows, lon_cols, cells, parity), grad)
    query = query * lax.rsqrt(head_means(query * query) + EPS)
    key = key * lax.rsqrt(head_means(key * key) + EPS)
    place = lax.broadcasted_iota(jnp.int32, (CELLS, 1), 0)
    live = []
    for slot in range(blocks):
        block = jnp.where(parity == 1, blocks - 1 - slot, slot)
        live.append(place < count_ref[0, 0, block])
    key = jnp.where(jnp.concatenate(live, 0), key, DEAD_KEY)
    low, high = halves(key, value)
    shape = (blocks, CELLS, PAIR_WIDTH)
    kv_own_ref[1 : blocks + 1] = jnp.where(upper, high, low).astype(BF16).reshape(shape)
    kv_other_ref[1 : blocks + 1] = jnp.where(upper, low, high).astype(BF16).reshape(shape)
    low, high = halves(query, grad)
    qg_own_ref[...] = jnp.where(upper, high, low).astype(BF16).reshape(shape)
    qg_other_ref[...] = jnp.where(upper, low, high).astype(BF16).reshape(shape)


def halo_kernel(first_ref, last_ref, qkv_ref, own_in, other_in, kv_own_ref, kv_other_ref):
    slots = own_in.shape[0]
    upper = lax.rem(lax.axis_index("lat"), 2) == 1
    normed = jnp.concatenate([first_ref[...], last_ref[...]], 0)
    key = dot(normed, qkv_ref[1])
    value = dot(normed, qkv_ref[2])
    key = key * lax.rsqrt(head_means(key * key) + EPS)
    dead = normed[:, 0:1].astype(F32) > 0.5 * DEAD_TOKEN
    key = jnp.where(dead, DEAD_KEY, key)
    low, high = halves(key, value)
    own = jnp.where(upper, high, low).astype(BF16)
    other = jnp.where(upper, low, high).astype(BF16)
    for made, source, out in ((own, own_in, kv_own_ref), (other, other_in, kv_other_ref)):
        out[0] = made[:CELLS]
        out[1 : slots - 1] = source[1 : slots - 1]
        out[slots - 1] = made[CELLS:]


def attend_kernel(rows, scale_ref, qg_own_ref, qg_other_ref, *refs):
    kv_refs, refs = refs[: 3 * rows], refs[3 * rows :]
    (own_ref, near_ref, far_ref, dq_own_ref, dq_other_ref,
     mid, left, right, backward, weights, e_buf, p_buf, d_buf, dkv_mid, dkv_left, dkv_right) = refs
    groups = 3 * rows
    tm = lax.axis_index("tm")
    tm_odd = lax.rem(tm, 2) == 1
    frames = lax.axis_size("tm")
    lat = lax.axis_index("lat")
    upper = lax.rem(lat, 2)
    pair = lat // 2
    near_at = jnp.where(tm_odd, tm - 1, tm + 1)
    far_at = jnp.where(tm_odd, tm + 1, tm - 1)
    near_in = ((near_at >= 0) & (near_at < frames)).astype(F32)
    far_in = ((far_at >= 0) & (far_at < frames)).astype(F32)
    queries = 4 * CELLS
    side = 2 * CELLS

    q_rows = jnp.concatenate(
        [qg_own_ref[0], qg_other_ref[0], qg_own_ref[1], qg_other_ref[1]], 0
    ).astype(F32)
    q_cols = q_rows.T
    lane_half = lax.broadcasted_iota(jnp.int32, (queries, TILE), 1) // HEAD_DIM
    row_half = lax.broadcasted_iota(jnp.int32, (TILE, queries), 0) // HEAD_DIM
    for j in range(2 * HALF):
        tile = slice((j // 2) * TILE, (j // 2 + 1) * TILE)
        backward[j] = jnp.where(lane_half == j % 2, q_rows[:, tile], 0.0).astype(BF16)
        weights[j] = jnp.where(row_half == j % 2, q_cols[tile], 0.0).astype(BF16)
    for group, ref in enumerate(kv_refs):
        left[group * CELLS : (group + 1) * CELLS] = ref[0]
        mid[group * side : group * side + CELLS] = ref[1]
        mid[group * side + CELLS : (group + 1) * side] = ref[2]
        right[group * CELLS : (group + 1) * CELLS] = ref[3]

    lane_row = (lax.broadcasted_iota(jnp.int32, (1, queries), 1) // CELLS) % 2

    def group_bias(group):
        frame, row = group // rows, lax.rem(group, rows)
        there = jnp.where(frame == 0, 1.0, jnp.where(frame == 1, near_in, far_in))
        if rows == 2:
            return jnp.full((1, queries), (1.0 - there) * DROPPED)
        pairs = lax.axis_size("lat") // 2
        before = (row == 2).astype(F32) * (pair > 0).astype(F32)
        after = (row == 3).astype(F32) * (pair < pairs - 1).astype(F32)
        inside = (row < 2).astype(F32)
        even = (lane_row == upper).astype(F32)
        return (1.0 - there * (inside + before * even + after * (1.0 - even))) * DROPPED

    scales = [scale_ref[upper * HALF + h] * (1.0 / math.sqrt(HEAD_DIM)) for h in range(HALF)]
    to_exp2 = [s * math.log2(math.e) for s in scales]

    def first_pass(chunk, carry, scores_of, bias_of, count):
        out = []
        start = pl.multiple_of(chunk * count, count)
        bias = bias_of()
        for h in range(HALF):
            total, inner = carry[2 * h], carry[2 * h + 1]
            scores = scores_of(h)
            grad_prob = scores_of(HALF + h)
            masked = jnp.exp2(scores * to_exp2[h] + bias)
            e_buf[h, pl.ds(start, count)] = masked
            p_buf[h, pl.ds(start, count)] = grad_prob
            out.append(total + jnp.sum(masked.reshape(count // 8, 8, queries), 0))
            out.append(inner + jnp.sum((masked * grad_prob).reshape(count // 8, 8, queries), 0))
        return tuple(out)

    def row_bias(keys):
        return jnp.where(keys[:, 0:1].astype(F32) < 0.5 * DEAD_KEY, 0.0, DROPPED)

    def mid_chunk(group, carry):
        keys = mid[pl.ds(pl.multiple_of(group * side, side), side)]

        def scores_of(j):
            tile = slice((j // 2) * TILE, (j // 2 + 1) * TILE)
            return dot(keys[:, tile], weights[j])

        return first_pass(
            group, carry, scores_of, lambda: row_bias(keys) + group_bias(group), side
        )

    def edge_chunk(group, carry):
        at = pl.ds(pl.multiple_of(group * CELLS, CELLS), CELLS)
        keys_left, keys_right = left[at], right[at]

        def scores_of(j):
            tile = slice((j // 2) * TILE, (j // 2 + 1) * TILE)
            return jnp.concatenate(
                [
                    dot(keys_left[:, tile], weights[j, :, :side]),
                    dot(keys_right[:, tile], weights[j, :, side:]),
                ],
                1,
            )

        def bias_of():
            both = jnp.concatenate(
                [
                    jnp.broadcast_to(row_bias(keys_left), (CELLS, side)),
                    jnp.broadcast_to(row_bias(keys_right), (CELLS, side)),
                ],
                1,
            )
            return both + group_bias(group)

        return first_pass(group + 2 * groups, carry, scores_of, bias_of, CELLS)

    carry = tuple(jnp.zeros((8, queries), F32) for _ in range(2 * HALF))
    carry = lax.fori_loop(0, groups, mid_chunk, carry)
    carry = lax.fori_loop(0, groups, edge_chunk, carry)
    inverse, delta = [], []
    for h in range(HALF):
        total = jnp.sum(carry[2 * h], 0, keepdims=True)
        inverse.append(1.0 / total)
        delta.append(jnp.sum(carry[2 * h + 1], 0, keepdims=True) * inverse[h])

    def parts(start, count):
        at = pl.ds(start, count)
        grads, probs = [], []
        for h in range(HALF):
            prob = e_buf[h, at] * inverse[h]
            probs.append(prob.astype(BF16))
            grads.append((prob * (p_buf[h, at] - delta[h]) * scales[h]).astype(BF16))
            d_buf[h, at] = grads[h]
        return grads + probs

    def mid_back(group, carry):
        start = pl.multiple_of(group * side, side)
        pieces = parts(start, side)
        for tile in range(TILES):
            both = jnp.concatenate([pieces[2 * tile], pieces[2 * tile + 1]], 1)
            dkv_mid[pl.ds(start, side), tile * TILE : (tile + 1) * TILE] = dot(
                both, backward[2 * tile : 2 * tile + 2].reshape(2 * queries, TILE)
            )
        return carry

    def edge_back(group, carry):
        start = pl.multiple_of(group * CELLS, CELLS)
        pieces = parts(start + groups * side, CELLS)
        for tile in range(TILES):
            cut = slice(tile * TILE, (tile + 1) * TILE)
            for out, lanes in ((dkv_left, slice(0, side)), (dkv_right, slice(side, queries))):
                both = jnp.concatenate(
                    [pieces[2 * tile][:, lanes], pieces[2 * tile + 1][:, lanes]], 1
                )
                out[pl.ds(start, CELLS), cut] = dot(
                    both, backward[2 * tile : 2 * tile + 2, lanes].reshape(2 * side, TILE)
                )
        return carry

    lax.fori_loop(0, groups, mid_back, 0)
    lax.fori_loop(0, groups, edge_back, 0)

    mid_total = groups * side
    columns = []
    for h in range(HALF):
        tile = slice((h // 2) * TILE, (h // 2 + 1) * TILE)
        own = slice((h % 2) * HEAD_DIM, (h % 2 + 1) * HEAD_DIM)
        from_mid = dot_first(mid[:, tile], d_buf[h, :mid_total])[own]
        from_left = dot_first(left[:, tile], d_buf[h, mid_total:, :side])[own]
        from_right = dot_first(right[:, tile], d_buf[h, mid_total:, side:])[own]
        columns.append(from_mid + jnp.concatenate([from_left, from_right], 1))
    dq = jnp.concatenate(columns, 0).T
    dq_own_ref[...] = jnp.concatenate([dq[:CELLS], dq[2 * CELLS : 3 * CELLS]], 1)
    dq_other_ref[...] = jnp.concatenate([dq[CELLS : 2 * CELLS], dq[3 * CELLS :]], 1)

    for group in range(groups):
        out = (own_ref, near_ref, far_ref)[group // rows]
        row = group % rows
        out[row, 0] = dkv_left[group * CELLS : (group + 1) * CELLS].astype(out.dtype)
        out[row, 1] = dkv_mid[group * side : group * side + CELLS].astype(out.dtype)
        out[row, 2] = dkv_mid[group * side + CELLS : (group + 1) * side].astype(out.dtype)
        out[row, 3] = dkv_right[group * CELLS : (group + 1) * CELLS].astype(out.dtype)


def frame_sum_kernel(own_ref, near_ref, far_ref, inner_ref, first_ref, last_ref):
    total = own_ref[...] + near_ref[...].astype(F32) + far_ref[...].astype(F32)
    slots = own_ref.shape[1]
    first_ref[...] = total[:, 0].astype(BF16)
    last_ref[...] = total[:, slots - 1].astype(BF16)
    inner_ref[...] = total[:, 1 : slots - 1]


def column_sum_kernel(inner_ref, first_ref, last_ref, dq_other_ref, own_ref, other_ref):
    first = inner_ref[:, 0] + first_ref[...].astype(F32)
    last = inner_ref[:, 1] + last_ref[...].astype(F32)
    own_ref[0] = first[0]
    own_ref[1] = last[0]
    other_ref[0] = first[1].astype(BF16)
    other_ref[1] = last[1].astype(BF16)
    other_ref[2] = dq_other_ref[...].astype(BF16)


def finish_kernel(
    dkv_ref, dq_ref, other_ref, raw_ref, tokens_ref, gain_ref, qkv_ref, out_ref
):
    frames, lat_rows, lon_cols, width = tokens_ref.shape
    cells = frames * lat_rows * lon_cols
    parity = lax.rem(lax.axis_index("lon"), 2)
    upper = lax.rem(lax.axis_index("lat"), 2) == 1

    def joined(mine, theirs):
        return jnp.where(
            upper, jnp.concatenate([theirs, mine], 1), jnp.concatenate([mine, theirs], 1)
        )

    def by_slot(packed):
        return jnp.concatenate([packed[:, :HALF_WIDTH], packed[:, HALF_WIDTH:]], 0)

    dkv_mine = dkv_ref[...].reshape(cells, PAIR_WIDTH)
    dkv_theirs = other_ref[:2].astype(F32).reshape(cells, PAIR_WIDTH)
    grads = [
        joined(by_slot(dq_ref[...]), by_slot(other_ref[2].astype(F32))),
        joined(dkv_mine[:, :HALF_WIDTH], dkv_theirs[:, :HALF_WIDTH]),
        joined(dkv_mine[:, HALF_WIDTH:], dkv_theirs[:, HALF_WIDTH:]),
    ]
    head_width = HEADS * HEAD_DIM
    grad_normed = dot_last(grads[2].astype(BF16), qkv_ref[2])
    for c in range(2):
        raw = raw_ref[:, c * head_width : (c + 1) * head_width]
        inverse = lax.rsqrt(head_means(raw * raw) + EPS)
        inner = head_means(raw * grads[c])
        grad_raw = inverse * grads[c] - inverse * inverse * inverse * raw * inner
        grad_normed = grad_normed + dot_last(grad_raw.astype(BF16), qkv_ref[c])
    order = block_order(lat_rows, lon_cols, cells, parity)
    x = tokens_ref[...].astype(F32).reshape(cells, width)
    x = dot(order, x.astype(BF16))
    inverse = lax.rsqrt(jnp.mean(x * x, -1, keepdims=True) + EPS)
    grad = gain_ref[...] * grad_normed
    inner = jnp.mean(x * grad, -1, keepdims=True)
    grad = (inverse * grad - inverse * inverse * inverse * x * inner).astype(BF16)
    grad = dot_first(order, grad)
    out_ref[...] = grad.reshape(tokens_ref.shape).astype(BF16)


SMEM = pl.BlockSpec(memory_space=pltpu.SMEM)
VMEM = pl.BlockSpec(memory_space=pltpu.VMEM)


def kernel_call(body, name, outs, args, smem=0, scratch=(), limit_mib=16, flops=0, moved=0):
    return pl.pallas_call(
        body,
        name=name,
        out_shape=[jax.ShapeDtypeStruct(shape, dtype) for shape, dtype in outs],
        in_specs=[SMEM] * smem + [VMEM] * (len(args) - smem),
        out_specs=[VMEM] * len(outs),
        scratch_shapes=list(scratch),
        compiler_params=pltpu.CompilerParams(vmem_limit_bytes=limit_mib * 1024 * 1024),
        cost_estimate=pl.CostEstimate(flops=flops, bytes_accessed=moved, transcendentals=0),
    )(*args)


def per_device(tokens, key_count, norm_gain, qkv_weight, out_weight, logit_scale, grad_out):
    frames, lat_rows, lon_cols, width = tokens.shape
    assert frames == BLOCK and lat_rows == BLOCK and lon_cols == 2 * BLOCK
    assert lax.axis_size("lat") % 2 == 0 and lax.axis_size("lon") % 2 == 0
    cells = frames * lat_rows * lon_cols
    blocks = lon_cols // BLOCK
    head_width = HEADS * HEAD_DIM
    gain = norm_gain.reshape(1, width)
    kv_shape = ((blocks + 2, CELLS, PAIR_WIDTH), BF16)
    qg_shape = ((blocks, CELLS, PAIR_WIDTH), BF16)

    normed, first, last = kernel_call(
        norm_kernel, "norm",
        [((cells, width), BF16), ((CELLS, width), BF16), ((CELLS, width), BF16)],
        [key_count, tokens, gain], smem=1,
    )
    near_first = pair_swap(first, "lon", 1, True)
    near_last = pair_swap(last, "lon", 0, True)
    kv_own, kv_other, qg_own, qg_other, raw = kernel_call(
        project_kernel, "project",
        [kv_shape, kv_shape, qg_shape, qg_shape, ((cells, 2 * head_width), F32)],
        [key_count, normed, grad_out, qkv_weight, out_weight], smem=1,
        flops=8 * cells * width * head_width, moved=5_000_000,
    )
    kv_own, kv_other = kernel_call(
        halo_kernel, "halo", [kv_shape, kv_shape],
        [near_first, near_last, qkv_weight, kv_own, kv_other],
    )
    kv_rows = [kv_own, pair_swap(kv_other, "lat", 0, False)]
    qg_other = pair_swap(qg_other, "lat", 0, False)
    upper = lax.rem(lax.axis_index("lat"), 2) == 1
    wide = lax.axis_size("lat") > 2
    if wide:
        even = jnp.where(upper, kv_rows[1], kv_rows[0])
        odd = jnp.where(upper, kv_rows[0], kv_rows[1])
        kv_rows += [shift_by(odd, "lat", 2), shift_by(even, "lat", -2)]
    rows = len(kv_rows)
    kv_all = list(kv_rows)
    for phase in range(2):
        kv_all += [pair_swap(kv, "tm", phase, False) for kv in kv_rows]

    groups = 3 * rows
    queries = 4 * CELLS
    part_shape = (rows, blocks + 2, CELLS, PAIR_WIDTH)
    packed = (CELLS, 2 * HALF_WIDTH)
    own, near, far, dq_own, dq_other = kernel_call(
        functools.partial(attend_kernel, rows), "attend",
        [(part_shape, F32), (part_shape, BF16), (part_shape, BF16), (packed, F32), (packed, F32)],
        [logit_scale, qg_own, qg_other, *kv_all], smem=1,
        scratch=[
            pltpu.VMEM((groups * 2 * CELLS, PAIR_WIDTH), BF16),
            pltpu.VMEM((groups * CELLS, PAIR_WIDTH), BF16),
            pltpu.VMEM((groups * CELLS, PAIR_WIDTH), BF16),
            pltpu.VMEM((2 * HALF, queries, TILE), BF16),
            pltpu.VMEM((2 * HALF, TILE, queries), BF16),
            pltpu.VMEM((HALF, groups * 3 * CELLS, queries), F32),
            pltpu.VMEM((HALF, groups * 3 * CELLS, queries), F32),
            pltpu.VMEM((HALF, groups * 3 * CELLS, queries), BF16),
            pltpu.VMEM((groups * 2 * CELLS, PAIR_WIDTH), F32),
            pltpu.VMEM((groups * CELLS, PAIR_WIDTH), F32),
            pltpu.VMEM((groups * CELLS, PAIR_WIDTH), F32),
        ],
        limit_mib=24 * rows // 2,
        flops=24 * groups * 3 * CELLS * queries * HALF * HEAD_DIM, moved=5_000_000,
    )
    if wide:
        summed = []
        for part in (own, near, far):
            to_below = shift_by(part[2].astype(BF16), "lat", -2)
            to_above = shift_by(part[3].astype(BF16), "lat", 2)
            to_odd, to_even = to_below.astype(F32), to_above.astype(F32)
            add_own = jnp.where(upper, to_odd, to_even)
            add_other = jnp.where(upper, to_even, to_odd)
            both = part[:2].astype(F32) + jnp.stack([add_own, add_other], 0)
            summed.append(both.astype(part.dtype))
        own, near, far = summed
    near = pair_swap(near, "tm", 0, False)
    far = pair_swap(far, "tm", 1, False)
    edge = ((2, CELLS, PAIR_WIDTH), BF16)
    inner, first, last = kernel_call(
        frame_sum_kernel, "frame_sum",
        [((2, blocks, CELLS, PAIR_WIDTH), F32), edge, edge], [own, near, far],
    )
    first = pair_swap(first, "lon", 1, True)
    last = pair_swap(last, "lon", 0, True)
    dkv_own, other = kernel_call(
        column_sum_kernel, "column_sum",
        [((blocks, CELLS, PAIR_WIDTH), F32), ((blocks + 1, CELLS, PAIR_WIDTH), BF16)],
        [inner, first, last, dq_other],
    )
    other = pair_swap(other, "lat", 0, False)
    (grad_tokens,) = kernel_call(
        finish_kernel, "finish", [(tokens.shape, BF16)],
        [dkv_own, dq_own, other, raw, tokens, gain, qkv_weight],
        flops=6 * cells * width * head_width, moved=4_000_000,
    )
    return grad_tokens


def solution(mesh):
    in_specs = (
        P("tm", "lat", "lon", None),
        P("tm", "lat", "lon"),
        P(),
        P(),
        P(),
        P(),
        P("tm", "lat", "lon", None),
    )
    out_specs = P("tm", "lat", "lon", None)
    return jax.shard_map(
        per_device, mesh=mesh, in_specs=in_specs, out_specs=out_specs, check_vma=False
    )
```

profile of v0, /device:TPU:12, one launch (start us, length us, event | category | flops | bytes accessed | tf_op | source)
XLA Modules:
  0.0 57.7 jit_solution(2774166935040148649)
XLA Ops:
  0.0 0.7 %reshape.3.gain_ref = f32[1,768]{1,0:T(1,128)S(1)} reshape(f32[768]{0:T(1024)} %param.9) | data formatting | bytes 6144 | tf_op jit(solution)/shard_map/reshape | solution.py:422
  0.7 0.0 copy-start.2
  0.7 0.9 %copy-done.2 = bf16[4,4,8,768]{3,2,1,0:T(8,128)(2,1)S(1)} copy-done((bf16[4,4,8,768]{3,2,1,0:T(8,128)(2,1)S(1)}, bf16[4,4,8,768]{3,2,1,0:T(8,128)(2,1)}, u32[]{:S(2)}) %copy-start.2) | copy-done | bytes 196632
  1.6 0.0 copy-start.6
  1.6 0.7 %copy-done.6 = s32[1,1,2]{2,1,0:T(1,128)S(1)} copy-done((s32[1,1,2]{2,1,0:T(1,128)S(1)}, s32[1,1,2]{2,1,0:T(1,128)}, u32[]{:S(2)}) %copy-start.6) | copy-done | bytes 32
  2.3 0.9 %norm.1 = (bf16[128,768]{1,0:T(8,128)(2,1)S(1)}, bf16[64,768]{1,0:T(8,128)(2,1)S(1)}, bf16[64,768]{1,0:T(8,128)(2,1)S(1)}) custom-call(s32[1,1,2]{2,1,0:T(1,128)S(1)} %copy-done.6, bf16[4,4,8,768]{3,2,1,0:T(8,128)(2,1)S(1)} %copy-done.2, f32[1,768]{1,0:T(1,128)S(1)} %reshape.3.gain_ref), custom_call_target="tpu_custom_call" | custom-call | tf_op jit(solution)/shard_map/norm/pallas_call | solution.py:403
  3.1 0.1 collective-permute-start.1
  3.2 0.6 %collective-permute-start.2 = (bf16[64,768]{1,0:T(8,128)(2,1)S(1)}, bf16[64,768]{1,0:T(8,128)(2,1)S(1)}, u32[]{:S(2)}, u32[]{:S(2)}) collective-permute-start(bf16[64,768]{1,0:T(8,128)(2,1)S(1)} %get-tuple-element.29), channel_id=1, source_target_pairs={{0,1},{1,0},{2,3},{3,2},{4,5},{5,4},{6,7},{7,6},{8,9},{9,8},{10,11... | collective-permute-start | bytes 294920 | tf_op jit(solution)/shard_map/ppermute | solution.py:38
  3.8 0.0 copy-start
  3.8 1.5 %copy-done = bf16[3,768,384]{2,1,0:T(8,128)(2,1)S(1)} copy-done((bf16[3,768,384]{2,1,0:T(8,128)(2,1)S(1)}, bf16[3,768,384]{2,1,0:T(8,128)(2,1)}, u32[]{:S(2)}) %copy-start) | copy-done | bytes 1769496
  5.3 0.0 copy-start.4
  5.3 1.1 %copy-done.4 = bf16[384,768]{1,0:T(8,128)(2,1)S(1)} copy-done((bf16[384,768]{1,0:T(8,128)(2,1)S(1)}, bf16[384,768]{1,0:T(8,128)(2,1)}, u32[]{:S(2)}) %copy-start.4) | copy-done | bytes 589848
  6.4 0.0 copy-start.5
  6.4 0.9 %copy-done.5 = bf16[4,4,8,768]{3,2,1,0:T(8,128)(2,1)S(1)} copy-done((bf16[4,4,8,768]{3,2,1,0:T(8,128)(2,1)S(1)}, bf16[4,4,8,768]{3,2,1,0:T(8,128)(2,1)}, u32[]{:S(2)}) %copy-start.5) | copy-done | bytes 196632
  7.3 0.0 copy-start.1
  7.3 1.6 %project.1 = (bf16[4,64,384]{2,1,0:T(8,128)(2,1)S(1)}, bf16[4,64,384]{2,1,0:T(8,128)(2,1)S(1)}, bf16[2,64,384]{2,1,0:T(8,128)(2,1)S(1)}, bf16[2,64,384]{2,1,0:T(8,128)(2,1)S(1)}, f32[128,768]{1,0:T(8,128)S(1)}) custom-call(s32[1,1,2]{2,1,0:T(1,128)S(1)} %copy-done.6, bf16[128,768]{1,0:T(8,128)(2,1)S(1)} %get-tuple-element.25.normed_ref, ...), custom_call_target="tpu_custom_call" | custom-call | flops 301989888 | bytes 5000000 | tf_op jit(solution)/shard_map/project/pallas_call | solution.py:403
  8.9 0.0 copy-start.7
  8.9 0.0 collective-permute-done.1.first_ref
  8.9 0.0 collective-permute-done.2.last_ref
  8.9 0.0 copy-done.1
  8.9 0.5 halo.1
  9.5 1.6 %collective-permute-start.3 = (bf16[4,64,384]{2,1,0:T(8,128)(2,1)S(1)}, bf16[4,64,384]{2,1,0:T(8,128)(2,1)S(1)}, u32[]{:S(2)}, u32[]{:S(2)}) collective-permute-start(bf16[4,64,384]{2,1,0:T(8,128)(2,1)S(1)} %get-tuple-element.33), channel_id=1, source_target_pairs={{0,4},{4,0},{1,5},{5,1},{2,6},{6,2},{3,7},{7,3},{8,12},{12,8},{9,1... | collective-permute-start | bytes 589832 | tf_op jit(solution)/shard_map/ppermute | solution.py:38
  11.0 3.5 %collective-permute-start.6 = (bf16[4,64,384]{2,1,0:T(8,128)(2,1)S(1)}, bf16[4,64,384]{2,1,0:T(8,128)(2,1)S(1)}, u32[]{:S(2)}, u32[]{:S(2)}) collective-permute-start(bf16[4,64,384]{2,1,0:T(8,128)(2,1)S(1)} %get-tuple-element.32.refs_0_), channel_id=1, source_target_pairs={{8,16},{16,8},{9,17},{17,9},{10,18},{18,10},{11,19},{19,11},{12,20... | collective-permute-start | bytes 589832 | tf_op jit(solution)/shard_map/ppermute | solution.py:38
  14.5 0.1 collective-permute-start.4
  14.6 1.8 %collective-permute-done.3.refs_1_ = bf16[4,64,384]{2,1,0:T(8,128)(2,1)S(1)} collective-permute-done((bf16[4,64,384]{2,1,0:T(8,128)(2,1)S(1)}, bf16[4,64,384]{2,1,0:T(8,128)(2,1)S(1)}, u32[]{:S(2)}, u32[]{:S(2)}) %collective-permute-start.3) | collective-permute-done | bytes 196640 | tf_op jit(solution)/shard_map/ppermute | solution.py:38
  16.4 3.5 %collective-permute-start.7 = (bf16[4,64,384]{2,1,0:T(8,128)(2,1)S(1)}, bf16[4,64,384]{2,1,0:T(8,128)(2,1)S(1)}, u32[]{:S(2)}, u32[]{:S(2)}) collective-permute-start(bf16[4,64,384]{2,1,0:T(8,128)(2,1)S(1)} %collective-permute-done.3.refs_1_), channel_id=1, source_target_pairs={{8,16},{16,8},{9,17},{17,9},{10,18},{18,10},{11,19},{19,11},{12,20... | collective-permute-start | bytes 589832 | tf_op jit(solution)/shard_map/ppermute | solution.py:38
  19.8 0.1 collective-permute-start.5
  19.9 1.6 %collective-permute-start = (bf16[2,64,384]{2,1,0:T(8,128)(2,1)S(1)}, bf16[2,64,384]{2,1,0:T(8,128)(2,1)S(1)}, u32[]{:S(2)}, u32[]{:S(2)}) collective-permute-start(bf16[2,64,384]{2,1,0:T(8,128)(2,1)S(1)} %get-tuple-element.27), channel_id=1, source_target_pairs={{0,4},{4,0},{1,5},{5,1},{2,6},{6,2},{3,7},{7,3},{8,12},{12,8},{9,1... | collective-permute-start | bytes 294920 | tf_op jit(solution)/shard_map/ppermute | solution.py:38
  21.5 3.1 %collective-permute-done.qg_other_ref = bf16[2,64,384]{2,1,0:T(8,128)(2,1)S(1)} collective-permute-done((bf16[2,64,384]{2,1,0:T(8,128)(2,1)S(1)}, bf16[2,64,384]{2,1,0:T(8,128)(2,1)S(1)}, u32[]{:S(2)}, u32[]{:S(2)}) %collective-permute-start) | collective-permute-done | bytes 98336 | tf_op jit(solution)/shard_map/ppermute | solution.py:38
  24.6 0.0 collective-permute-done.6.refs_4_
  24.6 0.0 collective-permute-done.4.refs_2_
  24.6 0.0 collective-permute-done.7.refs_5_
  24.6 1.0 %collective-permute-done.5.refs_3_ = bf16[4,64,384]{2,1,0:T(8,128)(2,1)S(1)} collective-permute-done((bf16[4,64,384]{2,1,0:T(8,128)(2,1)S(1)}, bf16[4,64,384]{2,1,0:T(8,128)(2,1)S(1)}, u32[]{:S(2)}, u32[]{:S(2)}) %collective-permute-start.5) | collective-permute-done | bytes 196640 | tf_op jit(solution)/shard_map/ppermute | solution.py:38
  25.6 0.0 copy-done.7
  25.6 7.3 %attend.1 = (f32[2,4,64,384]{3,2,1,0:T(8,128)S(1)}, bf16[2,4,64,384]{3,2,1,0:T(8,128)(2,1)S(1)}, bf16[2,4,64,384]{3,2,1,0:T(8,128)(2,1)S(1)}, f32[64,384]{1,0:T(8,128)S(1)}, f32[64,384]{1,0:T(8,128)S(1)}) custom-call(f32[6]{0:T(128)S(1)} %copy-done.7, bf16[2,64,384]{2,1,0:T(8,128)(2,1)S(1)} %get-tuple-element.26.qg_own_ref, ...), custom_call_target="tpu_custom_call" | custom-call | flops 1358954496 | bytes 5000000 | tf_op jit(solution)/shard_map/attend/pallas_call | solution.py:403
  32.9 0.0 copy-start.3
  32.9 1.1 %collective-permute-start.8 = (bf16[2,4,64,384]{3,2,1,0:T(8,128)(2,1)S(1)}, bf16[2,4,64,384]{3,2,1,0:T(8,128)(2,1)S(1)}, u32[]{:S(2)}, u32[]{:S(2)}) collective-permute-start(bf16[2,4,64,384]{3,2,1,0:T(8,128)(2,1)S(1)} %get-tuple-element.35), channel_id=1, source_target_pairs={{0,8},{8,0},{16,24},{24,16},{1,9},{9,1},{17,25},{25,17},{2,10},{10... | collective-permute-start | bytes 1179656 | tf_op jit(solution)/shard_map/ppermute | solution.py:38
  34.0 2.3 %collective-permute-start.9 = (bf16[2,4,64,384]{3,2,1,0:T(8,128)(2,1)S(1)}, bf16[2,4,64,384]{3,2,1,0:T(8,128)(2,1)S(1)}, u32[]{:S(2)}, u32[]{:S(2)}) collective-permute-start(bf16[2,4,64,384]{3,2,1,0:T(8,128)(2,1)S(1)} %get-tuple-element.36), channel_id=1, source_target_pairs={{8,16},{16,8},{9,17},{17,9},{10,18},{18,10},{11,19},{19,11},{12,20... | collective-permute-start | bytes 1179656 | tf_op jit(solution)/shard_map/ppermute | solution.py:38
  36.4 5.7 %collective-permute-done.8.near_ref = bf16[2,4,64,384]{3,2,1,0:T(8,128)(2,1)S(1)} collective-permute-done((bf16[2,4,64,384]{3,2,1,0:T(8,128)(2,1)S(1)}, bf16[2,4,64,384]{3,2,1,0:T(8,128)(2,1)S(1)}, u32[]{:S(2)}, u32[]{:S(2)}) %collective-permute-start.8) | collective-permute-done | bytes 393248 | tf_op jit(solution)/shard_map/ppermute | solution.py:38
  42.1 2.3 %collective-permute-done.9.far_ref = bf16[2,4,64,384]{3,2,1,0:T(8,128)(2,1)S(1)} collective-permute-done((bf16[2,4,64,384]{3,2,1,0:T(8,128)(2,1)S(1)}, bf16[2,4,64,384]{3,2,1,0:T(8,128)(2,1)S(1)}, u32[]{:S(2)}, u32[]{:S(2)}) %collective-permute-start.9) | collective-permute-done | bytes 393248 | tf_op jit(solution)/shard_map/ppermute | solution.py:38
  44.4 0.1 frame_sum.1
  44.5 0.1 collective-permute-start.10
  44.6 1.6 %collective-permute-start.11 = (bf16[2,64,384]{2,1,0:T(8,128)(2,1)S(1)}, bf16[2,64,384]{2,1,0:T(8,128)(2,1)S(1)}, u32[]{:S(2)}, u32[]{:S(2)}) collective-permute-start(bf16[2,64,384]{2,1,0:T(8,128)(2,1)S(1)} %get-tuple-element.39), channel_id=1, source_target_pairs={{0,1},{1,0},{2,3},{3,2},{4,5},{5,4},{6,7},{7,6},{8,9},{9,8},{10,11... | collective-permute-start | bytes 294920 | tf_op jit(solution)/shard_map/ppermute | solution.py:38
  46.2 3.4 %collective-permute-done.10.first_ref = bf16[2,64,384]{2,1,0:T(8,128)(2,1)S(1)} collective-permute-done((bf16[2,64,384]{2,1,0:T(8,128)(2,1)S(1)}, bf16[2,64,384]{2,1,0:T(8,128)(2,1)S(1)}, u32[]{:S(2)}, u32[]{:S(2)}) %collective-permute-start.10) | collective-permute-done | bytes 98336 | tf_op jit(solution)/shard_map/ppermute | solution.py:38
  49.6 0.0 collective-permute-done.11.last_ref
  49.7 1.5 %collective-permute-start.12 = (bf16[3,64,384]{2,1,0:T(8,128)(2,1)S(1)}, bf16[3,64,384]{2,1,0:T(8,128)(2,1)S(1)}, u32[]{:S(2)}, u32[]{:S(2)}) collective-permute-start(bf16[3,64,384]{2,1,0:T(8,128)(2,1)S(1)} %get-tuple-element.43), channel_id=1, source_target_pairs={{0,4},{4,0},{1,5},{5,1},{2,6},{6,2},{3,7},{7,3},{8,12},{12,8},{9,1... | collective-permute-start | bytes 442376 | tf_op jit(solution)/shard_map/ppermute | solution.py:38
  51.2 4.4 %collective-permute-done.12.other_ref = bf16[3,64,384]{2,1,0:T(8,128)(2,1)S(1)} collective-permute-done((bf16[3,64,384]{2,1,0:T(8,128)(2,1)S(1)}, bf16[3,64,384]{2,1,0:T(8,128)(2,1)S(1)}, u32[]{:S(2)}, u32[]{:S(2)}) %collective-permute-start.12) | collective-permute-done | bytes 147488 | tf_op jit(solution)/shard_map/ppermute | solution.py:38
  55.6 0.0 copy-done.3
  55.6 2.1 %finish.1 = bf16[4,4,8,768]{3,2,1,0:T(8,128)(2,1)} custom-call(f32[2,64,384]{2,1,0:T(8,128)S(1)} %get-tuple-element.41.dkv_ref, f32[64,384]{1,0:T(8,128)S(1)} %get-tuple-element.42.dq_ref, bf16[3,64,384]{2,1,0:T(8,128)(2,1)S(1)} %collective-permute-done.12.other_ref, f32[128,768]{1,0:T(8,128)S(1)} %get-tuple-element.44.raw_ref, ...), custom_call_target="tpu_custom_call" | custom-call | flops 226492416 | bytes 4000000 | tf_op jit(solution)/shard_map/finish/pallas_call | solution.py:403
  (1 shorter events, 0.0 us)
Async XLA Ops:
  0.7 0.9 %copy-start.2 = (bf16[4,4,8,768]{3,2,1,0:T(8,128)(2,1)S(1)}, bf16[4,4,8,768]{3,2,1,0:T(8,128)(2,1)}, u32[]{:S(2)}) copy-start(bf16[4,4,8,768]{3,2,1,0:T(8,128)(2,1)} %tokens_ref.3) | copy-start | bytes 589828
  1.6 0.7 %copy-start.6 = (s32[1,1,2]{2,1,0:T(1,128)S(1)}, s32[1,1,2]{2,1,0:T(1,128)}, u32[]{:S(2)}) copy-start(s32[1,1,2]{2,1,0:T(1,128)} %count_ref.3) | copy-start | bytes 28
  3.1 5.8 %collective-permute-start.1 = (bf16[64,768]{1,0:T(8,128)(2,1)S(1)}, bf16[64,768]{1,0:T(8,128)(2,1)S(1)}, u32[]{:S(2)}, u32[]{:S(2)}) collective-permute-start(bf16[64,768]{1,0:T(8,128)(2,1)S(1)} %get-tuple-element.28), channel_id=1, source_target_pairs={{0,3},{1,2},{2,1},{3,0},{4,7},{5,6},{6,5},{7,4},{8,11},{9,10},{10,... | collective-permute-start | bytes 294920 | tf_op jit(solution)/shard_map/ppermute | solution.py:38
  3.2 5.7 %collective-permute-start.2 = (bf16[64,768]{1,0:T(8,128)(2,1)S(1)}, bf16[64,768]{1,0:T(8,128)(2,1)S(1)}, u32[]{:S(2)}, u32[]{:S(2)}) collective-permute-start(bf16[64,768]{1,0:T(8,128)(2,1)S(1)} %get-tuple-element.29), channel_id=1, source_target_pairs={{0,1},{1,0},{2,3},{3,2},{4,5},{5,4},{6,7},{7,6},{8,9},{9,8},{10,11... | collective-permute-start | bytes 294920 | tf_op jit(solution)/shard_map/ppermute | solution.py:38
  3.8 1.5 %copy-start = (bf16[3,768,384]{2,1,0:T(8,128)(2,1)S(1)}, bf16[3,768,384]{2,1,0:T(8,128)(2,1)}, u32[]{:S(2)}) copy-start(bf16[3,768,384]{2,1,0:T(8,128)(2,1)} %qkv_ref.5) | copy-start | bytes 5308420
  5.3 1.1 %copy-start.4 = (bf16[384,768]{1,0:T(8,128)(2,1)S(1)}, bf16[384,768]{1,0:T(8,128)(2,1)}, u32[]{:S(2)}) copy-start(bf16[384,768]{1,0:T(8,128)(2,1)} %out_weight_ref.1) | copy-start | bytes 1769476
  6.4 0.9 %copy-start.5 = (bf16[4,4,8,768]{3,2,1,0:T(8,128)(2,1)S(1)}, bf16[4,4,8,768]{3,2,1,0:T(8,128)(2,1)}, u32[]{:S(2)}) copy-start(bf16[4,4,8,768]{3,2,1,0:T(8,128)(2,1)} %grad_ref.1) | copy-start | bytes 589828
  7.3 1.6 %copy-start.1 = (bf16[3,768,384]{2,1,0:T(8,128)(2,1)S(1)}, bf16[3,768,384]{2,1,0:T(8,128)(2,1)}, u32[]{:S(2)}) copy-start(bf16[3,768,384]{2,1,0:T(8,128)(2,1)} %qkv_ref.5) | copy-start | bytes 5308420
  8.9 16.7 %copy-start.7 = (f32[6]{0:T(128)S(1)}, f32[6]{0:T(128)}, u32[]{:S(2)}) copy-start(f32[6]{0:T(128)} %scale_ref.1) | copy-start | bytes 76
  9.5 6.9 %collective-permute-start.3 = (bf16[4,64,384]{2,1,0:T(8,128)(2,1)S(1)}, bf16[4,64,384]{2,1,0:T(8,128)(2,1)S(1)}, u32[]{:S(2)}, u32[]{:S(2)}) collective-permute-start(bf16[4,64,384]{2,1,0:T(8,128)(2,1)S(1)} %get-tuple-element.33), channel_id=1, source_target_pairs={{0,4},{4,0},{1,5},{5,1},{2,6},{6,2},{3,7},{7,3},{8,12},{12,8},{9,1... | collective-permute-start | bytes 589832 | tf_op jit(solution)/shard_map/ppermute | solution.py:38
  11.0 13.6 %collective-permute-start.6 = (bf16[4,64,384]{2,1,0:T(8,128)(2,1)S(1)}, bf16[4,64,384]{2,1,0:T(8,128)(2,1)S(1)}, u32[]{:S(2)}, u32[]{:S(2)}) collective-permute-start(bf16[4,64,384]{2,1,0:T(8,128)(2,1)S(1)} %get-tuple-element.32.refs_0_), channel_id=1, source_target_pairs={{8,16},{16,8},{9,17},{17,9},{10,18},{18,10},{11,19},{19,11},{12,20... | collective-permute-start | bytes 589832 | tf_op jit(solution)/shard_map/ppermute | solution.py:38
  14.5 10.1 %collective-permute-start.4 = (bf16[4,64,384]{2,1,0:T(8,128)(2,1)S(1)}, bf16[4,64,384]{2,1,0:T(8,128)(2,1)S(1)}, u32[]{:S(2)}, u32[]{:S(2)}) collective-permute-start(bf16[4,64,384]{2,1,0:T(8,128)(2,1)S(1)} %get-tuple-element.32.refs_0_), channel_id=1, source_target_pairs={{0,8},{8,0},{16,24},{24,16},{1,9},{9,1},{17,25},{25,17},{2,10},{10... | collective-permute-start | bytes 589832 | tf_op jit(solution)/shard_map/ppermute | solution.py:38
  16.4 8.3 %collective-permute-start.7 = (bf16[4,64,384]{2,1,0:T(8,128)(2,1)S(1)}, bf16[4,64,384]{2,1,0:T(8,128)(2,1)S(1)}, u32[]{:S(2)}, u32[]{:S(2)}) collective-permute-start(bf16[4,64,384]{2,1,0:T(8,128)(2,1)S(1)} %collective-permute-done.3.refs_1_), channel_id=1, source_target_pairs={{8,16},{16,8},{9,17},{17,9},{10,18},{18,10},{11,19},{19,11},{12,20... | collective-permute-start | bytes 589832 | tf_op jit(solution)/shard_map/ppermute | solution.py:38
  19.8 5.7 %collective-permute-start.5 = (bf16[4,64,384]{2,1,0:T(8,128)(2,1)S(1)}, bf16[4,64,384]{2,1,0:T(8,128)(2,1)S(1)}, u32[]{:S(2)}, u32[]{:S(2)}) collective-permute-start(bf16[4,64,384]{2,1,0:T(8,128)(2,1)S(1)} %collective-permute-done.3.refs_1_), channel_id=1, source_target_pairs={{0,8},{8,0},{16,24},{24,16},{1,9},{9,1},{17,25},{25,17},{2,10},{10... | collective-permute-start | bytes 589832 | tf_op jit(solution)/shard_map/ppermute | solution.py:38
  19.9 4.7 %collective-permute-start = (bf16[2,64,384]{2,1,0:T(8,128)(2,1)S(1)}, bf16[2,64,384]{2,1,0:T(8,128)(2,1)S(1)}, u32[]{:S(2)}, u32[]{:S(2)}) collective-permute-start(bf16[2,64,384]{2,1,0:T(8,128)(2,1)S(1)} %get-tuple-element.27), channel_id=1, source_target_pairs={{0,4},{4,0},{1,5},{5,1},{2,6},{6,2},{3,7},{7,3},{8,12},{12,8},{9,1... | collective-permute-start | bytes 294920 | tf_op jit(solution)/shard_map/ppermute | solution.py:38
  32.9 22.7 %copy-start.3 = (bf16[4,4,8,768]{3,2,1,0:T(8,128)(2,1)S(1)}, bf16[4,4,8,768]{3,2,1,0:T(8,128)(2,1)}, u32[]{:S(2)}) copy-start(bf16[4,4,8,768]{3,2,1,0:T(8,128)(2,1)} %tokens_ref.3) | copy-start | bytes 589828
  32.9 9.1 %collective-permute-start.8 = (bf16[2,4,64,384]{3,2,1,0:T(8,128)(2,1)S(1)}, bf16[2,4,64,384]{3,2,1,0:T(8,128)(2,1)S(1)}, u32[]{:S(2)}, u32[]{:S(2)}) collective-permute-start(bf16[2,4,64,384]{3,2,1,0:T(8,128)(2,1)S(1)} %get-tuple-element.35), channel_id=1, source_target_pairs={{0,8},{8,0},{16,24},{24,16},{1,9},{9,1},{17,25},{25,17},{2,10},{10... | collective-permute-start | bytes 1179656 | tf_op jit(solution)/shard_map/ppermute | solution.py:38
  34.0 10.4 %collective-permute-start.9 = (bf16[2,4,64,384]{3,2,1,0:T(8,128)(2,1)S(1)}, bf16[2,4,64,384]{3,2,1,0:T(8,128)(2,1)S(1)}, u32[]{:S(2)}, u32[]{:S(2)}) collective-permute-start(bf16[2,4,64,384]{3,2,1,0:T(8,128)(2,1)S(1)} %get-tuple-element.36), channel_id=1, source_target_pairs={{8,16},{16,8},{9,17},{17,9},{10,18},{18,10},{11,19},{19,11},{12,20... | collective-permute-start | bytes 1179656 | tf_op jit(solution)/shard_map/ppermute | solution.py:38
  44.5 5.1 %collective-permute-start.10 = (bf16[2,64,384]{2,1,0:T(8,128)(2,1)S(1)}, bf16[2,64,384]{2,1,0:T(8,128)(2,1)S(1)}, u32[]{:S(2)}, u32[]{:S(2)}) collective-permute-start(bf16[2,64,384]{2,1,0:T(8,128)(2,1)S(1)} %get-tuple-element.38), channel_id=1, source_target_pairs={{0,3},{1,2},{2,1},{3,0},{4,7},{5,6},{6,5},{7,4},{8,11},{9,10},{10,... | collective-permute-start | bytes 294920 | tf_op jit(solution)/shard_map/ppermute | solution.py:38
  44.6 5.0 %collective-permute-start.11 = (bf16[2,64,384]{2,1,0:T(8,128)(2,1)S(1)}, bf16[2,64,384]{2,1,0:T(8,128)(2,1)S(1)}, u32[]{:S(2)}, u32[]{:S(2)}) collective-permute-start(bf16[2,64,384]{2,1,0:T(8,128)(2,1)S(1)} %get-tuple-element.39), channel_id=1, source_target_pairs={{0,1},{1,0},{2,3},{3,2},{4,5},{5,4},{6,7},{7,6},{8,9},{9,8},{10,11... | collective-permute-start | bytes 294920 | tf_op jit(solution)/shard_map/ppermute | solution.py:38
  49.7 5.9 %collective-permute-start.12 = (bf16[3,64,384]{2,1,0:T(8,128)(2,1)S(1)}, bf16[3,64,384]{2,1,0:T(8,128)(2,1)S(1)}, u32[]{:S(2)}, u32[]{:S(2)}) collective-permute-start(bf16[3,64,384]{2,1,0:T(8,128)(2,1)S(1)} %get-tuple-element.43), channel_id=1, source_target_pairs={{0,4},{4,0},{1,5},{5,1},{2,6},{6,2},{3,7},{7,3},{8,12},{12,8},{9,1... | collective-permute-start | bytes 442376 | tf_op jit(solution)/shard_map/ppermute | solution.py:38
where the time goes:
time: 58 us; the launch traced here: 57.7 us
  waiting for transfers between devices  21.7 us (37%)
  starting transfers between devices  17.5 us (30%)
  Pallas kernels  12.6 us (22%)
  local copies, waits for them, and re-layouts  5.75 us (10%)
    ppermute x13, waiting for transfers between devices, pair_swap(): return lax.ppermute(array, axis, pairs)  21.7 us
    ppermute x13, starting transfers between devices, pair_swap(): return lax.ppermute(array, axis, pairs)  17.5 us
    pallas_call x7, Pallas kernels, kernel_call(): pl.pallas_call(body, name=name, out_shape=[jax.ShapeDtypeStruct(shape, dt...  12.6 us
    unnamed x16, local copies, waits for them, and re-layouts  5.06 us
  transfers between devices with their start and end apart: 13, of which 7 were waited for; matrix products, arithmetic and copies ran while one was open for 0% of the time, Pallas kernels for 3%

commit v1 on v0

v1 whole, which is shorter than its diff:
```python
import functools
import math

import jax
import jax.numpy as jnp
from jax import lax
from jax.experimental import pallas as pl
from jax.experimental.pallas import tpu as pltpu
from jax.sharding import PartitionSpec as P

HEADS = 6
HEAD_DIM = 64
BLOCK = 4
CELLS = BLOCK * BLOCK * BLOCK
HALF = HEADS // 2
HALF_WIDTH = HALF * HEAD_DIM
PAIR_WIDTH = 2 * HALF_WIDTH
TILE = 2 * HEAD_DIM
TILES = PAIR_WIDTH // TILE
DEAD_KEY = 64.0
DROPPED = -1e30
FLOPS_PER_US = 1e9

EPS = 1e-06
F32 = jnp.float32
BF16 = jnp.bfloat16


def partner_of(device, count, phase):
    return device + 1 if device % 2 == phase else device - 1


def pair_swap(array, axis, phase):
    count = lax.axis_size(axis)
    pairs = [(device, partner_of(device, count, phase) % count) for device in range(count)]
    return lax.ppermute(array, axis, pairs)


def frame_swap(array, phase):
    frames, lons = lax.axis_size("tm"), lax.axis_size("lon")
    pairs = []
    for frame in range(frames):
        for lon in range(lons):
            to = (partner_of(frame, frames, phase), lon)
            if not 0 <= to[0] < frames:
                to = (frame, partner_of(lon, lons, 0))
            pairs.append((frame * lons + lon, to[0] * lons + to[1]))
    return lax.ppermute(array, ("tm", "lon"), pairs)


def corner_swap(array):
    lats, lons = lax.axis_size("lat"), lax.axis_size("lon")
    pairs = []
    for lat in range(lats):
        for lon in range(lons):
            to = partner_of(lat, lats, 0) * lons + partner_of(lon, lons, 1) % lons
            pairs.append((lat * lons + lon, to))
    return lax.ppermute(array, ("lat", "lon"), pairs)


def shift_by(array, axis, step):
    count = lax.axis_size(axis)
    pairs = [(i, i + step) for i in range(count) if 0 <= i + step < count]
    return lax.ppermute(array, axis, pairs)


def dot(a, b):
    return lax.dot_general(a, b, (((1,), (0,)), ((), ())), preferred_element_type=F32)


def dot_last(a, b):
    return lax.dot_general(a, b, (((1,), (1,)), ((), ())), preferred_element_type=F32)


def dot_first(a, b):
    return lax.dot_general(a, b, (((0,), (0,)), ((), ())), preferred_element_type=F32)


def head_means(values):
    rows = lax.broadcasted_iota(jnp.int32, (TILE, TILE), 0) // HEAD_DIM
    cols = lax.broadcasted_iota(jnp.int32, (TILE, TILE), 1) // HEAD_DIM
    ones = (rows == cols).astype(F32).astype(BF16)
    high = values.astype(BF16)
    low = (values - high.astype(F32)).astype(BF16)
    pieces = []
    for start in range(0, values.shape[1], TILE):
        cut = slice(start, start + TILE)
        pieces.append(dot(high[:, cut], ones) + dot(low[:, cut], ones))
    return jnp.concatenate(pieces, 1) * (1.0 / HEAD_DIM)


def block_order(lat_rows, lon_cols, count, parity):
    blocks = lon_cols // BLOCK
    row = lax.broadcasted_iota(jnp.int32, (count, count), 0)
    source = lax.broadcasted_iota(jnp.int32, (count, count), 1)
    slot = row // CELLS
    place = row % CELLS
    frame = place // (BLOCK * BLOCK)
    lat = (place // BLOCK) % BLOCK
    col = place % BLOCK
    block = jnp.where(parity == 1, blocks - 1 - slot, slot)
    wanted = (frame * lat_rows + lat) * lon_cols + block * BLOCK + col
    return (source == wanted).astype(F32).astype(BF16)


def halves(first, second):
    low = jnp.concatenate([first[:, :HALF_WIDTH], second[:, :HALF_WIDTH]], 1)
    high = jnp.concatenate([first[:, HALF_WIDTH:], second[:, HALF_WIDTH:]], 1)
    return low, high


def normalised(x, gain_ref):
    inverse = lax.rsqrt(jnp.mean(x * x, -1, keepdims=True) + EPS)
    return (x * inverse * gain_ref[...].reshape(1, x.shape[1])).astype(BF16)


def order_kernel(lat_rows, lon_cols, order_ref):
    parity = lax.rem(lax.axis_index("lon"), 2)
    order_ref[...] = block_order(lat_rows, lon_cols, order_ref.shape[0], parity)


def project_kernel(
    count_ref, order_ref, tokens_ref, gain_ref, grad_ref, qkv_ref, out_weight_ref,
    kv_own_ref, qg_own_ref, kv_other_ref, qg_other_ref, raw_ref, inverse_ref, x_ref,
):
    frames, lat_rows, lon_cols, width = grad_ref.shape
    cells = frames * lat_rows * lon_cols
    blocks = lon_cols // BLOCK
    parity = lax.rem(lax.axis_index("lon"), 2)
    upper = lax.rem(lax.axis_index("lat"), 2) == 1
    order = order_ref[...]
    x = tokens_ref[...].astype(F32).reshape(cells, width)
    x = dot(order, x.astype(BF16))
    x_ref[...] = x.astype(BF16)
    normed = normalised(x, gain_ref)
    query, key, value = (dot(normed, qkv_ref[c]) for c in range(3))
    head_width = HEADS * HEAD_DIM
    raw_ref[:, :head_width] = query
    raw_ref[:, head_width:] = key
    grad = dot_last(
        grad_ref[...].astype(F32).reshape(cells, width).astype(BF16), out_weight_ref[...]
    ).astype(BF16)
    grad = dot(order, grad)
    query_inverse = lax.rsqrt(head_means(query * query) + EPS)
    key_inverse = lax.rsqrt(head_means(key * key) + EPS)
    inverse_ref[:, :head_width] = query_inverse
    inverse_ref[:, head_width:] = key_inverse
    query = query * query_inverse
    key = key * key_inverse
    place = lax.broadcasted_iota(jnp.int32, (CELLS, 1), 0)
    live = []
    for slot in range(blocks):
        block = jnp.where(parity == 1, blocks - 1 - slot, slot)
        live.append(place < count_ref[0, 0, block])
    key = jnp.where(jnp.concatenate(live, 0), key, DEAD_KEY)
    shape = (blocks, CELLS, PAIR_WIDTH)
    low, high = halves(key, value)
    kv_own_ref[...] = jnp.where(upper, high, low).astype(BF16).reshape(shape)
    kv_other_ref[...] = jnp.where(upper, low, high).astype(BF16).reshape(shape)
    low, high = halves(query, grad)
    qg_own_ref[...] = jnp.where(upper, high, low).astype(BF16).reshape(shape)
    qg_other_ref[...] = jnp.where(upper, low, high).astype(BF16).reshape(shape)


def halo_kernel(blocks, count_ref, first_ref, gain_ref, qkv_ref, other_ref, half_ref):
    upper = lax.rem(lax.axis_index("lat"), 2) == 1
    x = first_ref[...].astype(F32)
    normed = normalised(x, gain_ref)
    key = dot(normed, qkv_ref[1])
    value = dot(normed, qkv_ref[2])
    key = key * lax.rsqrt(head_means(key * key) + EPS)
    odd = lax.rem(lax.axis_index("lon"), 2) == 1
    live = count_ref[0, 0, jnp.where(odd, 0, blocks - 1)]
    place = lax.broadcasted_iota(jnp.int32, (CELLS, 1), 0)
    key = jnp.where(place < live, key, DEAD_KEY)
    low, high = halves(key, value)
    half_ref[...] = jnp.where(upper, high, low).astype(BF16)
    other_ref[...] = jnp.where(upper, low, high).astype(BF16)


def join_kernel(half_ref, own_in, kv_own_ref):
    kv_own_ref[0] = half_ref[...]
    kv_own_ref[1:] = own_in[...]


def lane_tile(j):
    return slice((j // 2) * TILE, (j // 2 + 1) * TILE)


class Place:
    def __init__(self, rows):
        self.rows = rows
        tm, frames = lax.axis_index("tm"), lax.axis_size("tm")
        odd = lax.rem(tm, 2) == 1
        near, far = jnp.where(odd, tm - 1, tm + 1), jnp.where(odd, tm + 1, tm - 1)
        self.there = [None] + [((at >= 0) & (at < frames)) for at in (near, far)]
        self.upper = lax.rem(lax.axis_index("lat"), 2)

    def bias(self, frame, row, lanes):
        there = self.there[frame]
        total = 0.0 if there is None else jnp.where(there, 0.0, DROPPED)
        if row < 2:
            return total
        pair, pairs = lax.axis_index("lat") // 2, lax.axis_size("lat") // 2
        if row == 2:
            inside, wanted = pair > 0, self.upper
        else:
            inside, wanted = pair < pairs - 1, 1 - self.upper
        lane_row = (lax.broadcasted_iota(jnp.int32, (1, lanes), 1) // CELLS) % 2
        seen = (lane_row == wanted) & inside
        return total + jnp.where(seen, 0.0, DROPPED)


def head_scales(scale_ref):
    upper = lax.rem(lax.axis_index("lat"), 2)
    return [scale_ref[upper * HALF + h] * (1.0 / math.sqrt(HEAD_DIM)) for h in range(HALF)]


def key_bias(keys):
    return jnp.where(keys[:, 0:1].astype(F32) < 0.5 * DEAD_KEY, 0.0, DROPPED)


def score(keys, bias, weights_ref, lanes, scales, sums):
    count = keys.shape[0]
    exps, probs = [], []
    for h in range(HALF):
        scores = dot(keys[:, lane_tile(h)], weights_ref[h, :, lanes])
        grad_prob = dot(keys[:, lane_tile(HALF + h)], weights_ref[HALF + h, :, lanes])
        masked = jnp.exp2(scores * (scales[h] * math.log2(math.e)) + bias)
        shape = (count // 8, 8, masked.shape[1])
        sums[h] = sums[h] + jnp.sum(masked.reshape(shape), 0)
        sums[HALF + h] = sums[HALF + h] + jnp.sum((masked * grad_prob).reshape(shape), 0)
        exps.append(masked)
        probs.append(grad_prob)
    return exps, probs


ALL = slice(0, 4 * CELLS)
FIRST = slice(0, 2 * CELLS)
LAST = slice(2 * CELLS, 4 * CELLS)


def score_groups(place, frames, kv_refs, weights_ref, scales, sums, e_mid, p_mid, e_left, p_left):
    rows = place.rows
    side = [jnp.zeros((8, 2 * CELLS), F32) for _ in range(2 * HALF)]
    for index, ref in enumerate(kv_refs):
        frame, row = frames[index // rows], index % rows
        keys = ref[1:3].reshape(2 * CELLS, PAIR_WIDTH)
        bias = key_bias(keys) + place.bias(frame, row, 4 * CELLS)
        exps, probs = score(keys, bias, weights_ref, ALL, scales, sums)
        for h in range(HALF):
            e_mid[h, index * 2 * CELLS : (index + 1) * 2 * CELLS] = exps[h]
            p_mid[h, index * 2 * CELLS : (index + 1) * 2 * CELLS] = probs[h]
    for index in range(0, len(kv_refs), 2):
        frame, row = frames[index // rows], index % rows
        pair = [kv_refs[index][0], kv_refs[index + 1][0]]
        bias = jnp.concatenate(
            [
                jnp.broadcast_to(
                    key_bias(keys) + place.bias(frame, row + i, 2 * CELLS), (CELLS, 2 * CELLS)
                )
                for i, keys in enumerate(pair)
            ],
            0,
        )
        keys = jnp.concatenate(pair, 0)
        exps, probs = score(keys, bias, weights_ref, FIRST, scales, side)
        for h in range(HALF):
            e_left[h, index * CELLS : (index + 2) * CELLS] = exps[h]
            p_left[h, index * CELLS : (index + 2) * CELLS] = probs[h]
    return [jnp.concatenate([a[:, FIRST] + b, a[:, LAST]], 1) for a, b in zip(sums, side)]


def own_score_kernel(rows, scale_ref, qg_own_ref, qg_other_ref, *refs):
    kv_refs, refs = refs[:rows], refs[rows:]
    weights, backward, sums_ref, e_mid, p_mid, e_left, p_left = refs
    queries = 4 * CELLS
    q_rows = jnp.concatenate(
        [qg_own_ref[0], qg_other_ref[0], qg_own_ref[1], qg_other_ref[1]], 0
    ).astype(F32)
    q_cols = q_rows.T
    lane_half = lax.broadcasted_iota(jnp.int32, (queries, TILE), 1) // HEAD_DIM
    row_half = lax.broadcasted_iota(jnp.int32, (TILE, queries), 0) // HEAD_DIM
    for j in range(2 * HALF):
        backward[j] = jnp.where(lane_half == j % 2, q_rows[:, lane_tile(j)], 0.0).astype(BF16)
        weights[j] = jnp.where(row_half == j % 2, q_cols[lane_tile(j)], 0.0).astype(BF16)
    sums = [jnp.zeros((8, queries), F32) for _ in range(2 * HALF)]
    sums = score_groups(
        Place(rows), (0,), kv_refs, weights, head_scales(scale_ref), sums,
        e_mid, p_mid, e_left, p_left,
    )
    for j in range(2 * HALF):
        sums_ref[j] = sums[j]


def away_score_kernel(rows, scale_ref, weights, sums_in, *refs):
    kv_refs, refs = refs[: 2 * rows], refs[2 * rows :]
    sums_ref, e_mid, p_mid, e_left, p_left = refs
    sums = [sums_in[j] for j in range(2 * HALF)]
    sums = score_groups(
        Place(rows), (1, 2), kv_refs, weights, head_scales(scale_ref), sums,
        e_mid, p_mid, e_left, p_left,
    )
    for j in range(2 * HALF):
        sums_ref[j] = sums[j]


def grad_parts(exps, probs, inverse, delta, scales):
    grads, halves_of = [], []
    for h in range(HALF):
        prob = exps[h] * inverse[h]
        halves_of.append(prob.astype(BF16))
        grads.append((prob * (probs[h] - delta[h]) * scales[h]).astype(BF16))
    return grads + halves_of


def key_grads(pieces, backward, lanes):
    outs = []
    for tile in range(TILES):
        both = jnp.concatenate([pieces[2 * tile], pieces[2 * tile + 1]], 1)
        rows = jnp.concatenate(
            [backward[2 * tile, lanes], backward[2 * tile + 1, lanes]], 0
        )
        outs.append(dot(both, rows))
    return jnp.concatenate(outs, 1)


def query_grads(keys, grads, h):
    own = slice((h % 2) * HEAD_DIM, (h % 2 + 1) * HEAD_DIM)
    return dot_first(keys[:, lane_tile(h)], grads)[own]


def sibling_kernel(
    rows, scale_ref, weights, backward, sums_in, keys_ref, part_ref, stats_ref, dq_ref
):
    place, scales = Place(rows), head_scales(scale_ref)
    side = [jnp.zeros((8, 2 * CELLS), F32) for _ in range(2 * HALF)]
    made = []
    for index in range(0, 3 * rows, 2):
        frame, row = index // rows, index % rows
        bias = jnp.concatenate(
            [
                jnp.broadcast_to(
                    key_bias(keys_ref[index + i]) + place.bias(frame, row + i, 2 * CELLS),
                    (CELLS, 2 * CELLS),
                )
                for i in range(2)
            ],
            0,
        )
        keys = keys_ref[index : index + 2].reshape(2 * CELLS, PAIR_WIDTH)
        made.append(score(keys, bias, weights, LAST, scales, side))
    inverse, delta = [], []
    for h in range(HALF):
        total, inner = (
            jnp.concatenate([sums_in[j, :, FIRST], sums_in[j, :, LAST] + side[j]], 1)
            for j in (h, HALF + h)
        )
        inverse.append(1.0 / jnp.sum(total, 0, keepdims=True))
        delta.append(jnp.sum(inner, 0, keepdims=True) * inverse[h])
        stats_ref[h : h + 1] = inverse[h]
        stats_ref[HALF + h : HALF + h + 1] = delta[h]
    inverse = [a[:, LAST] for a in inverse]
    delta = [a[:, LAST] for a in delta]
    grads = []
    for index in range(0, 3 * rows, 2):
        pieces = grad_parts(*made[index // 2], inverse, delta, scales)
        grads.append(pieces[:HALF])
        made_part = key_grads(pieces, backward, LAST)
        part_ref[index : index + 2] = made_part.reshape(2, CELLS, PAIR_WIDTH).astype(BF16)
    keys = keys_ref[...].reshape(3 * rows * CELLS, PAIR_WIDTH)
    for h in range(HALF):
        dq_ref[h * HEAD_DIM : (h + 1) * HEAD_DIM] = query_grads(
            keys, jnp.concatenate([g[h] for g in grads], 0), h
        )


def back_groups(scales, stats_ref, backward, e_mid, p_mid, e_left, p_left, d_mid, d_left, put):
    inverse = [stats_ref[h : h + 1] for h in range(HALF)]
    delta = [stats_ref[HALF + h : HALF + h + 1] for h in range(HALF)]
    count = e_left.shape[1] // CELLS
    for index in range(count):
        at = slice(index * 2 * CELLS, (index + 1) * 2 * CELLS)
        exps, probs = [e_mid[h, at] for h in range(HALF)], [p_mid[h, at] for h in range(HALF)]
        pieces = grad_parts(exps, probs, inverse, delta, scales)
        for h in range(HALF):
            d_mid[h, at] = pieces[h]
        part = key_grads(pieces, backward, ALL)
        put(index, 1, part[:CELLS])
        put(index, 2, part[CELLS:])
    inverse = [a[:, FIRST] for a in inverse]
    delta = [a[:, FIRST] for a in delta]
    for index in range(0, count, 2):
        at = slice(index * CELLS, (index + 2) * CELLS)
        exps, probs = [e_left[h, at] for h in range(HALF)], [p_left[h, at] for h in range(HALF)]
        pieces = grad_parts(exps, probs, inverse, delta, scales)
        for h in range(HALF):
            d_left[h, at] = pieces[h]
        part = key_grads(pieces, backward, FIRST)
        put(index, 0, part[:CELLS])
        put(index + 1, 0, part[CELLS:])


def away_back_kernel(
    rows, scale_ref, stats_ref, backward, e_mid, p_mid, e_left, p_left,
    near_ref, far_ref, d_mid, d_left,
):
    def put(index, slot, part):
        (near_ref, far_ref)[index // rows][index % rows, slot] = part

    back_groups(
        head_scales(scale_ref), stats_ref, backward, e_mid, p_mid, e_left, p_left,
        d_mid, d_left, put,
    )


def sibling_sum_kernel(rows, near_in, far_in, sibling_ref, near_ref, far_ref):
    for frame, part, out in ((1, near_in, near_ref), (2, far_in, far_ref)):
        out[:, :2] = part[:, :2].astype(BF16)
        added = sibling_ref[frame * rows : (frame + 1) * rows].astype(F32)
        out[:, 2] = (part[:, 2] + added).astype(BF16)


def own_back_kernel(
    rows, scale_ref, stats_ref, backward, e_mid, p_mid, e_left, p_left,
    away_mid, away_left, dq_sibling, sibling_ref, *refs,
):
    kv_refs, refs = refs[: 3 * rows], refs[3 * rows :]
    own_ref, dq_own_ref, dq_other_ref, d_mid, d_left = refs

    def put(index, slot, part):
        if slot == 2:
            part = part + sibling_ref[index].astype(F32)
        own_ref[index, slot] = part

    back_groups(
        head_scales(scale_ref), stats_ref, backward, e_mid, p_mid, e_left, p_left,
        d_mid, d_left, put,
    )
    mid = jnp.concatenate([ref[1:3].reshape(2 * CELLS, PAIR_WIDTH) for ref in kv_refs], 0)
    left = jnp.concatenate([ref[0] for ref in kv_refs], 0)
    columns = []
    for h in range(HALF):
        made = query_grads(mid, jnp.concatenate([d_mid[h], away_mid[h]], 0), h)
        first = query_grads(left, jnp.concatenate([d_left[h], away_left[h]], 0), h)
        last = dq_sibling[h * HEAD_DIM : (h + 1) * HEAD_DIM]
        columns.append(made + jnp.concatenate([first, last], 1))
    dq = jnp.concatenate(columns, 0).T
    dq_own_ref[...] = jnp.concatenate([dq[:CELLS], dq[2 * CELLS : 3 * CELLS]], 1)
    dq_other_ref[...] = jnp.concatenate([dq[CELLS : 2 * CELLS], dq[3 * CELLS :]], 1)


def frame_sum_kernel(
    own_ref, near_ref, far_ref, dq_other_ref, inner_ref, to_lat_ref, edge_ref, corner_ref
):
    def total(row, slots):
        away = near_ref[row, slots].astype(F32) + far_ref[row, slots].astype(F32)
        return own_ref[row, slots] + away

    inner_ref[...] = total(0, slice(1, 3))
    to_lat_ref[:2] = total(1, slice(1, 3)).astype(BF16)
    to_lat_ref[2] = dq_other_ref[...].astype(BF16)
    edge_ref[...] = total(0, 0).astype(BF16)
    corner_ref[...] = total(1, 0).astype(BF16)


def finish_kernel(
    inner_ref, dq_ref, other_ref, edge_ref, corner_ref,
    raw_ref, inverse_ref, x_ref, order_ref, gain_ref, qkv_ref, out_ref,
):
    frames, lat_rows, lon_cols, width = out_ref.shape
    cells = frames * lat_rows * lon_cols
    parity = lax.rem(lax.axis_index("lon"), 2)
    upper = lax.rem(lax.axis_index("lat"), 2) == 1

    def joined(mine, theirs):
        return jnp.where(
            upper, jnp.concatenate([theirs, mine], 1), jnp.concatenate([mine, theirs], 1)
        )

    def by_slot(packed):
        return jnp.concatenate([packed[:, :HALF_WIDTH], packed[:, HALF_WIDTH:]], 0)

    def with_edge(inner, edge):
        return jnp.concatenate([inner[0] + edge.astype(F32), inner[1]], 0)

    dkv_mine = with_edge(inner_ref[...], edge_ref[...])
    dkv_theirs = with_edge(other_ref[:2].astype(F32), corner_ref[...])
    grads = [
        joined(by_slot(dq_ref[...]), by_slot(other_ref[2].astype(F32))),
        joined(dkv_mine[:, :HALF_WIDTH], dkv_theirs[:, :HALF_WIDTH]),
        joined(dkv_mine[:, HALF_WIDTH:], dkv_theirs[:, HALF_WIDTH:]),
    ]
    head_width = HEADS * HEAD_DIM
    grad_normed = dot_last(grads[2].astype(BF16), qkv_ref[2])
    for c in range(2):
        raw = raw_ref[:, c * head_width : (c + 1) * head_width]
        inverse = inverse_ref[:, c * head_width : (c + 1) * head_width]
        inner = head_means(raw * grads[c])
        grad_raw = inverse * grads[c] - inverse * inverse * inverse * raw * inner
        grad_normed = grad_normed + dot_last(grad_raw.astype(BF16), qkv_ref[c])
    order = order_ref[...]
    x = x_ref[...].astype(F32)
    inverse = lax.rsqrt(jnp.mean(x * x, -1, keepdims=True) + EPS)
    grad = gain_ref[...].reshape(1, width) * grad_normed
    inner = jnp.mean(x * grad, -1, keepdims=True)
    grad = (inverse * grad - inverse * inverse * inverse * x * inner).astype(BF16)
    grad = dot_first(order, grad)
    out_ref[...] = grad.reshape(out_ref.shape).astype(BF16)


SMEM = pl.BlockSpec(memory_space=pltpu.SMEM)
VMEM = pl.BlockSpec(memory_space=pltpu.VMEM)


def kernel_call(
    body, name, outs, args, smem=0, scratch=(), limit_mib=16, micros=1.0
):
    return pl.pallas_call(
        body,
        name=name,
        out_shape=[jax.ShapeDtypeStruct(shape, dtype) for shape, dtype in outs],
        in_specs=[SMEM] * smem + [VMEM] * (len(args) - smem),
        out_specs=[VMEM] * len(outs),
        scratch_shapes=list(scratch),
        compiler_params=pltpu.CompilerParams(vmem_limit_bytes=limit_mib * 1024 * 1024),
        cost_estimate=pl.CostEstimate(
            flops=int(micros * FLOPS_PER_US), bytes_accessed=0, transcendentals=0
        ),
    )(*args)


def per_device(tokens, key_count, norm_gain, qkv_weight, out_weight, logit_scale, grad_out):
    frames, lat_rows, lon_cols, width = tokens.shape
    assert frames == BLOCK and lat_rows == BLOCK and lon_cols == 2 * BLOCK
    assert lax.axis_size("lat") % 2 == 0 and lax.axis_size("lon") % 2 == 0
    cells = frames * lat_rows * lon_cols
    blocks = lon_cols // BLOCK
    head_width = HEADS * HEAD_DIM
    qg_shape = ((blocks, CELLS, PAIR_WIDTH), BF16)
    edge_shape = ((CELLS, PAIR_WIDTH), BF16)
    kv_shape = ((blocks + 1, CELLS, PAIR_WIDTH), BF16)

    start = jnp.where(lax.rem(lax.axis_index("lon"), 2) == 1, lon_cols - BLOCK, 0)
    first = lax.dynamic_slice_in_dim(tokens, start, BLOCK, 2).reshape(CELLS, width)
    first, count = pair_swap(first, "lon", 1), pair_swap(key_count, "lon", 1)
    (order,) = kernel_call(
        functools.partial(order_kernel, lat_rows, lon_cols), "order",
        [((cells, cells), BF16)], [], micros=10.0,
    )
    kv_own, qg_own, kv_other, qg_other, raw, inverse, x = kernel_call(
        project_kernel, "project",
        [qg_shape, qg_shape, qg_shape, qg_shape,
         ((cells, 2 * head_width), F32), ((cells, 2 * head_width), F32), ((cells, width), BF16)],
        [key_count, order, tokens, norm_gain, grad_out, qkv_weight, out_weight],
        smem=1, micros=3.0,
    )
    kv_other, qg_other = pair_swap(kv_other, "lat", 0), pair_swap(qg_other, "lat", 0)
    other_half, half = kernel_call(
        functools.partial(halo_kernel, blocks), "halo", [edge_shape, edge_shape],
        [count, first, norm_gain, qkv_weight], smem=1,
    )
    other_half = pair_swap(other_half, "lat", 0)
    (kv_own,) = kernel_call(join_kernel, "join", [kv_shape], [half, kv_own])
    kv_rows = [kv_own, jnp.concatenate([other_half[None], kv_other], 0)]
    upper = lax.rem(lax.axis_index("lat"), 2) == 1
    wide = lax.axis_size("lat") > 2
    if wide:
        even = jnp.where(upper, kv_rows[1], kv_rows[0])
        odd = jnp.where(upper, kv_rows[0], kv_rows[1])
        kv_rows += [shift_by(odd, "lat", 2), shift_by(even, "lat", -2)]
    rows = len(kv_rows)
    kv_away = []
    for phase in range(2):
        kv_away += [frame_swap(kv, phase) for kv in kv_rows]

    queries = 4 * CELLS
    tables = [((2 * HALF, TILE, queries), BF16), ((2 * HALF, queries, TILE), BF16)]
    sums_shape = ((2 * HALF, 8, queries), F32)

    def kept(groups):
        mid = ((HALF, groups * 2 * CELLS, queries), F32)
        left = ((HALF, groups * CELLS, 2 * CELLS), F32)
        return [mid, mid, left, left]

    def grads_kept(groups):
        return [
            ((HALF, groups * 2 * CELLS, queries), BF16),
            ((HALF, groups * CELLS, 2 * CELLS), BF16),
        ]

    weights, backward, sums, *own_kept = kernel_call(
        functools.partial(own_score_kernel, rows), "own_score",
        tables + [sums_shape] + kept(rows),
        [logit_scale, qg_own, qg_other, *kv_rows], smem=1, micros=1.5,
    )
    siblings = pair_swap(jnp.stack([kv[2] for kv in kv_rows + kv_away], 0), "lon", 0)
    sums, *away_kept = kernel_call(
        functools.partial(away_score_kernel, rows), "away_score",
        [sums_shape] + kept(2 * rows), [logit_scale, weights, sums, *kv_away], smem=1,
        micros=20.0,
    )
    sibling_part, stats, dq_sibling = kernel_call(
        functools.partial(sibling_kernel, rows), "sibling",
        [
            ((3 * rows, CELLS, PAIR_WIDTH), BF16), ((2 * HALF, queries), F32),
            ((HALF_WIDTH, 2 * CELLS), F32),
        ],
        [logit_scale, weights, backward, sums, siblings], smem=1,
    )
    sibling_part = pair_swap(sibling_part, "lon", 0)
    part = (rows, blocks + 1, CELLS, PAIR_WIDTH)
    near, far, *away_grads = kernel_call(
        functools.partial(away_back_kernel, rows), "away_back",
        [(part, F32), (part, F32)] + grads_kept(2 * rows),
        [logit_scale, stats, backward, *away_kept], smem=1, micros=1.5,
    )
    near, far = kernel_call(
        functools.partial(sibling_sum_kernel, rows), "sibling_sum",
        [(part, BF16), (part, BF16)], [near, far, sibling_part],
    )
    near, far = frame_swap(near, 0), frame_swap(far, 1)
    own, dq_own, dq_other = kernel_call(
        functools.partial(own_back_kernel, rows), "own_back",
        [(part, F32), ((CELLS, 2 * HALF_WIDTH), F32), ((CELLS, 2 * HALF_WIDTH), F32)],
        [logit_scale, stats, backward, *own_kept, *away_grads, dq_sibling, sibling_part,
         *kv_rows, *kv_away],
        smem=1, micros=1.5,
        scratch=[pltpu.VMEM(shape, dtype) for shape, dtype in grads_kept(rows)],
    )
    if wide:
        summed = []
        for array in (own, near, far):
            to_odd = shift_by(array[2].astype(BF16), "lat", -2).astype(F32)
            to_even = shift_by(array[3].astype(BF16), "lat", 2).astype(F32)
            added = jnp.stack(
                [jnp.where(upper, to_odd, to_even), jnp.where(upper, to_even, to_odd)], 0
            )
            summed.append((array[:2].astype(F32) + added).astype(array.dtype))
        own, near, far = summed
    inner, to_lat, edge, corner = kernel_call(
        frame_sum_kernel, "frame_sum",
        [((blocks, CELLS, PAIR_WIDTH), F32), ((blocks + 1, CELLS, PAIR_WIDTH), BF16),
         edge_shape, edge_shape],
        [own, near, far, dq_other],
    )
    edge = pair_swap(edge, "lon", 1)
    corner = corner_swap(corner)
    other = pair_swap(to_lat, "lat", 0)
    (grad_tokens,) = kernel_call(
        finish_kernel, "finish", [(tokens.shape, BF16)],
        [inner, dq_own, other, edge, corner, raw, inverse, x, order, norm_gain, qkv_weight],
        micros=2.0,
    )
    return grad_tokens


def solution(mesh):
    in_specs = (
        P("tm", "lat", "lon", None),
        P("tm", "lat", "lon"),
        P(),
        P(),
        P(),
        P(),
        P("tm", "lat", "lon", None),
    )
    out_specs = P("tm", "lat", "lon", None)
    return jax.shard_map(
        per_device, mesh=mesh, in_specs=in_specs, out_specs=out_specs, check_vma=False
    )
```

time: 58 us -> 46.9 us (0.81)
  the two profiles are of different devices: /device:TPU:12 before, /device:TPU:1 now
where the time goes in v1:
time: 46.9 us; the launch traced here: 46.7 us
  waiting for transfers between devices  16.9 us (36%)
  starting transfers between devices  15.1 us (32%)
  Pallas kernels  11.8 us (25%)
  local copies, waits for them, and re-layouts  2.64 us (6%)
    pallas_call x12, Pallas kernels, kernel_call(): pl.pallas_call(body, name=name, out_shape=[jax.ShapeDtypeStruct(shape, dt...  11.8 us
    ppermute x6, waiting for transfers between devices, frame_swap(): return lax.ppermute(array, ('tm', 'lon'), pairs)  10.6 us
    ppermute x9, starting transfers between devices, pair_swap(): return lax.ppermute(array, axis, pairs)  9.69 us
    ppermute x6, starting transfers between devices, frame_swap(): return lax.ppermute(array, ('tm', 'lon'), pairs)  5.37 us
    ppermute x9, waiting for transfers between devices, pair_swap(): return lax.ppermute(array, axis, pairs)  4.11 us
    ppermute x1, waiting for transfers between devices, corner_swap(): return lax.ppermute(array, ('lat', 'lon'), pairs)  2.26 us
    unnamed x19, local copies, waits for them, and re-layouts  1.62 us
    dynamic_slice x1, local copies, waits for them, and re-layouts, per_device(): lax.dynamic_slice_in_dim(tokens, start, BLOCK, 2).reshape(CELLS, width)  0.98 us
  transfers between devices with their start and end apart: 16, of which 6 were waited for; matrix products, arithmetic and copies ran while one was open for 2% of the time, Pallas kernels for 18%

profile of v1, /device:TPU:1, one launch (start us, length us, event | category | flops | bytes accessed | tf_op | source)
XLA Modules:
  0.0 46.7 jit_solution(3416969058902144060)
XLA Ops:
  0.0 2.6 %collective-permute-start.1 = (s32[1,1,2]{2,1,0:T(1,128)}, s32[1,1,2]{2,1,0:T(1,128)S(1)}, u32[]{:S(2)}, u32[]{:S(2)}) collective-permute-start(s32[1,1,2]{2,1,0:T(1,128)} %count_ref.1), channel_id=1, source_target_pairs={{0,3},{1,2},{2,1},{3,0},{4,7},{5,6},{6,5},{7,4},{8,11},{9,10},{10,... | collective-permute-start | bytes 32 | tf_op jit(solution)/shard_map/ppermute | solution.py:36
  2.6 1.0 %constant_dynamic-slice_fusion = bf16[4,4,4,768]{3,2,1,0:T(4,128)(2,1)S(1)} fusion(bf16[4,4,8,768]{3,2,1,0:T(8,128)(2,1)} %tokens_ref.1, s32[]{:T(128)S(6)} %select_n.5), kind=kLoop, calls=%fused_computation.7 | loop fusion | bytes 196612 | tf_op jit(solution)/shard_map/dynamic_slice | solution.py:545
  3.6 0.0 copy-start
  3.7 0.0 copy-start.1
  3.7 0.0 copy-start.2
  3.7 0.0 copy-start.3
  3.7 0.0 copy-start.4
  3.7 0.0 copy-start.5
  3.7 0.1 collective-permute-start.2
  3.8 0.1 order.1.order_ref
  3.9 0.7 %copy-done = bf16[4,4,8,768]{3,2,1,0:T(8,128)(2,1)S(1)} copy-done((bf16[4,4,8,768]{3,2,1,0:T(8,128)(2,1)S(1)}, bf16[4,4,8,768]{3,2,1,0:T(8,128)(2,1)}, u32[]{:S(2)}) %copy-start) | copy-done | bytes 196632
  4.6 0.7 %copy-done.1 = bf16[3,768,384]{2,1,0:T(8,128)(2,1)S(1)} copy-done((bf16[3,768,384]{2,1,0:T(8,128)(2,1)S(1)}, bf16[3,768,384]{2,1,0:T(8,128)(2,1)}, u32[]{:S(2)}) %copy-start.1) | copy-done | bytes 1769496
  5.2 0.1 copy-done.2
  5.4 0.0 copy-done.3
  5.4 0.0 copy-done.4
  5.4 0.0 copy-done.5
  5.4 1.9 %project.1 = (bf16[2,64,384]{2,1,0:T(8,128)(2,1)S(1)}, bf16[2,64,384]{2,1,0:T(8,128)(2,1)S(1)}, bf16[2,64,384]{2,1,0:T(8,128)(2,1)S(1)}, bf16[2,64,384]{2,1,0:T(...) custom-call(s32[1,1,2]{2,1,0:T(1,128)S(1)} %copy-done.5, ...), custom_call_target="tpu_custom_call" | custom-call | flops 3000000000 | tf_op jit(solution)/shard_map/project/pallas_call | solution.py:519
  7.3 1.3 %collective-permute-start = (bf16[2,64,384]{2,1,0:T(8,128)(2,1)S(1)}, bf16[2,64,384]{2,1,0:T(8,128)(2,1)S(1)}, u32[]{:S(2)}, u32[]{:S(2)}) collective-permute-start(bf16[2,64,384]{2,1,0:T(8,128)(2,1)S(1)} %get-tuple-element.43), channel_id=1, source_target_pairs={{0,4},{4,0},{1,5},{5,1},{2,6},{6,2},{3,7},{7,3},{8,12},{12,8},{9,1... | collective-permute-start | bytes 294920 | tf_op jit(solution)/shard_map/ppermute | solution.py:36
  8.5 0.3 collective-permute-start.4
  8.8 0.0 collective-permute-done.1.count_ref
  8.8 0.0 collective-permute-done.2.first_ref
  8.8 1.1 %halo.1 = (bf16[64,384]{1,0:T(8,128)(2,1)S(1)}, bf16[64,384]{1,0:T(8,128)(2,1)S(1)}) custom-call(s32[1,1,2]{2,1,0:T(1,128)S(1)} %collective-permute-done.1.count_ref, bf16[64,768]{1,0:T(8,128)(2,1)S(1)} %collective-permute-done.2.first_ref, f32[768]{0:T(1024)S(1)} %copy-done.4, bf16[3,768,384]{2,1,0:T(8,128)(2,1)S(1)} %copy-done.1), custom_call_target="tpu_custom_call" | custom-call | flops 1000000000 | tf_op jit(solution)/shard_map/halo/pallas_call | solution.py:519
  9.9 0.0 copy-start.6
  10.0 0.5 %collective-permute-start.7 = (bf16[3,64,384]{2,1,0:T(8,128)(2,1)S(1)}, bf16[3,64,384]{2,1,0:T(8,128)(2,1)S(1)}, u32[]{:S(2)}, u32[]{:S(2)}) collective-permute-start(bf16[3,64,384]{2,1,0:T(8,128)(2,1)S(1)} %join.1.refs_0_), channel_id=1, source_target_pairs={{0,1},{1,0},{2,3},{3,2},{8,16},{9,17},{10,18},{11,19},{16,8},{17,9... | collective-permute-start | bytes 442376 | tf_op jit(solution)/shard_map/ppermute | solution.py:48
  10.5 2.2 %collective-permute-start.5 = (bf16[3,64,384]{2,1,0:T(8,128)(2,1)S(1)}, bf16[3,64,384]{2,1,0:T(8,128)(2,1)S(1)}, u32[]{:S(2)}, u32[]{:S(2)}) collective-permute-start(bf16[3,64,384]{2,1,0:T(8,128)(2,1)S(1)} %join.1.refs_0_), channel_id=1, source_target_pairs={{0,8},{1,9},{2,10},{3,11},{8,0},{9,1},{10,2},{11,3},{16,24},{17,25... | collective-permute-start | bytes 442376 | tf_op jit(solution)/shard_map/ppermute | solution.py:48
  12.6 1.2 %collective-permute-start.3 = (bf16[64,384]{1,0:T(8,128)(2,1)S(1)}, bf16[64,384]{1,0:T(8,128)(2,1)S(1)}, u32[]{:S(2)}, u32[]{:S(2)}) collective-permute-start(bf16[64,384]{1,0:T(8,128)(2,1)S(1)} %get-tuple-element.46), channel_id=1, source_target_pairs={{0,4},{4,0},{1,5},{5,1},{2,6},{6,2},{3,7},{7,3},{8,12},{12,8},{9,1... | collective-permute-start | bytes 147464 | tf_op jit(solution)/shard_map/ppermute | solution.py:36
  13.8 0.1 collective-permute-done.4
  14.0 1.9 %collective-permute-done.3 = bf16[64,384]{1,0:T(8,128)(2,1)S(1)} collective-permute-done((bf16[64,384]{1,0:T(8,128)(2,1)S(1)}, bf16[64,384]{1,0:T(8,128)(2,1)S(1)}, u32[]{:S(2)}, u32[]{:S(2)}) %collective-permute-start.3) | collective-permute-done | bytes 49184 | tf_op jit(solution)/shard_map/ppermute | solution.py:36
  15.9 1.9 %collective-permute-start.8 = (bf16[3,64,384]{2,1,0:T(8,128)(2,1)S(1)}, bf16[3,64,384]{2,1,0:T(8,128)(2,1)S(1)}, u32[]{:S(2)}, u32[]{:S(2)}) collective-permute-start(bf16[3,64,384]{2,1,0:T(8,128)(2,1)S(1)} %pad_maximum_fusion.refs_1_), channel_id=1, source_target_pairs={{0,1},{1,0},{2,3},{3,2},{8,16},{9,17},{10,18},{11,19},{16,8},{17,9... | collective-permute-start | bytes 442376 | tf_op jit(solution)/shard_map/ppermute | solution.py:48
  17.8 0.0 collective-permute-start.6
  17.8 0.0 collective-permute-done.qg_other_ref
  17.8 0.0 copy-done.6
  17.8 1.1 %own_score.1 = (bf16[6,128,256]{2,1,0:T(8,128)(2,1)S(1)}, bf16[6,256,128]{2,1,0:T(8,128)(2,1)S(1)}, f32[6,8,256]{2,1,0:T(8,128)S(1)}, f32[3,256,256]{2,1,0:T(8,1...) custom-call(f32[6]{0:T(128)S(1)} %copy-done.6, ...), custom_call_target="tpu_custom_call" | custom-call | flops 1500000000 | tf_op jit(solution)/shard_map/own_score/pallas_call | solution.py:519
  18.9 0.0 collective-permute-done.5.refs_0_.refs_2_
  18.9 4.3 %collective-permute-done.6.refs_1_.refs_3_ = bf16[3,64,384]{2,1,0:T(8,128)(2,1)S(1)} collective-permute-done((bf16[3,64,384]{2,1,0:T(8,128)(2,1)S(1)}, bf16[3,64,384]{2,1,0:T(8,128)(2,1)S(1)}, u32[]{:S(2)}, u32[]{:S(2)}) %collective-permute-start.6) | collective-permute-done | bytes 147488 | tf_op jit(solution)/shard_map/ppermute | solution.py:48
  23.2 0.0 collective-permute-done.7.refs_2_.refs_4_
  23.3 0.0 collective-permute-done.8.refs_3_.refs_5_
  23.3 0.9 %collective-permute-start.9 = (bf16[6,64,384]{2,1,0:T(8,128)(2,1)S(1)}, bf16[6,64,384]{2,1,0:T(8,128)(2,1)S(1)}, u32[]{:S(2)}, u32[]{:S(2)}) collective-permute-start(bf16[6,64,384]{2,1,0:T(8,128)(2,1)S(1)} %slice_dynamic-update-slice_fusion), channel_id=1, source_target_pairs={{0,1},{1,0},{2,3},{3,2},{4,5},{5,4},{6,7},{7,6},{8,9},{9,8},{10,11... | collective-permute-start | bytes 884744 | tf_op jit(solution)/shard_map/ppermute | solution.py:36
  24.2 1.2 %away_score.1 = (f32[6,8,256]{2,1,0:T(8,128)S(1)}, f32[3,512,256]{2,1,0:T(8,128)S(1)}, f32[3,512,256]{2,1,0:T(8,128)S(1)}, f32[3,256,128]{2,1,0:T(8,128)S(1)}, f32[3,256,128]{2,1,0:T(8,128)S(1)}) custom-call(f32[6]{0:T(128)S(1)} %copy-done.6, bf16[6,128,256]{2,1,0:T(8,128)(2,1)S(1)} %get-tuple-element.48.weights, ...), custom_call_target="tpu_custom_call" | custom-call | flops 20000000000 | tf_op jit(solution)/shard_map/away_score/pallas_call | solution.py:519
  25.4 0.0 collective-permute-done.9.keys_ref
  25.4 1.3 %sibling.1 = (bf16[6,64,384]{2,1,0:T(8,128)(2,1)S(1)}, f32[6,256]{1,0:T(8,128)S(1)}, f32[192,128]{1,0:T(8,128)S(1)}) custom-call(f32[6]{0:T(128)S(1)} %copy-done.6, bf16[6,128,256]{2,1,0:T(8,128)(2,1)S(1)} %get-tuple-element.48.weights, bf16[6,256,128]{2,1,0:T(8,128)(2,1)S(1)} %get-tuple-element.49.backward, f32[6,8,256]{2,1,0:T(8,128)S(1)} %get-tuple-element.51.sums_in, ...), custom_call_target="tpu_custom_call" | custom-call | flops 1000000000 | tf_op jit(solution)/shard_map/sibling/pallas_call | solution.py:519
  26.8 0.4 collective-permute-start.10
  27.2 1.4 %away_back.1 = (f32[2,3,64,384]{3,2,1,0:T(8,128)S(1)}, f32[2,3,64,384]{3,2,1,0:T(8,128)S(1)}, bf16[3,512,256]{2,1,0:T(8,128)(2,1)S(1)}, bf16[3,256,128]{2,1,0:T(8,128)(2,1)S(1)}) custom-call(f32[6]{0:T(128)S(1)} %copy-done.6, f32[6,256]{1,0:T(8,128)S(1)} %get-tuple-element.52.stats_ref, bf16[6,256,128]{2,1,0:T(8,128)(2,1)S(1)} %get-tuple-element.49.backward, ...), custom_call_target="tpu_custom_call" | custom-call | flops 1500000000 | tf_op jit(solution)/shard_map/away_back/pallas_call | solution.py:519
  28.6 0.0 collective-permute-done.10.sibling_ref
  28.6 0.1 sibling_sum.1
  28.7 0.4 collective-permute-start.11
  29.1 0.4 collective-permute-start.12
  29.5 1.5 %own_back.1 = (f32[2,3,64,384]{3,2,1,0:T(8,128)S(1)}, f32[64,384]{1,0:T(8,128)S(1)}, f32[64,384]{1,0:T(8,128)S(1)}) custom-call(f32[6]{0:T(128)S(1)} %copy-done.6, f32[6,256]{1,0:T(8,128)S(1)} %get-tuple-element.52.stats_ref, bf16[6,256,128]{2,1,0:T(8,128)(2,1)S(1)} %get-tuple-element.49.backward, f32[3,256,256]{2,1,0:T(8,128)S(1)} %get-tuple-element.53.e_mid, ...), custom_call_target="tpu_custom_call" | custom-call | flops 1500000000 | tf_op jit(solution)/shard_map/own_back/pallas_call | solution.py:519
  31.0 6.2 %collective-permute-done.11.near_ref = bf16[2,3,64,384]{3,2,1,0:T(8,128)(2,1)S(1)} collective-permute-done((bf16[2,3,64,384]{3,2,1,0:T(8,128)(2,1)S(1)}, bf16[2,3,64,384]{3,2,1,0:T(8,128)(2,1)S(1)}, u32[]{:S(2)}, u32[]{:S(2)}) %collective-permute-start.11) | collective-permute-done | bytes 294944 | tf_op jit(solution)/shard_map/ppermute | solution.py:48
  37.2 0.0 collective-permute-done.12.far_ref
  37.2 0.1 frame_sum.1
  37.4 1.3 %collective-permute-start.13 = (bf16[3,64,384]{2,1,0:T(8,128)(2,1)S(1)}, bf16[3,64,384]{2,1,0:T(8,128)(2,1)S(1)}, u32[]{:S(2)}, u32[]{:S(2)}) collective-permute-start(bf16[3,64,384]{2,1,0:T(8,128)(2,1)S(1)} %get-tuple-element.73), channel_id=1, source_target_pairs={{0,4},{4,0},{1,5},{5,1},{2,6},{6,2},{3,7},{7,3},{8,12},{12,8},{9,1... | collective-permute-start | bytes 442376 | tf_op jit(solution)/shard_map/ppermute | solution.py:36
  38.6 1.7 %collective-permute-start.14 = (bf16[64,384]{1,0:T(8,128)(2,1)S(1)}, bf16[64,384]{1,0:T(8,128)(2,1)S(1)}, u32[]{:S(2)}, u32[]{:S(2)}) collective-permute-start(bf16[64,384]{1,0:T(8,128)(2,1)S(1)} %get-tuple-element.74), channel_id=1, source_target_pairs={{0,3},{1,2},{2,1},{3,0},{4,7},{5,6},{6,5},{7,4},{8,11},{9,10},{10,... | collective-permute-start | bytes 147464 | tf_op jit(solution)/shard_map/ppermute | solution.py:36
  40.3 0.1 collective-permute-start.15
  40.4 2.1 %collective-permute-done.14.edge_ref = bf16[64,384]{1,0:T(8,128)(2,1)S(1)} collective-permute-done((bf16[64,384]{1,0:T(8,128)(2,1)S(1)}, bf16[64,384]{1,0:T(8,128)(2,1)S(1)}, u32[]{:S(2)}, u32[]{:S(2)}) %collective-permute-start.14) | collective-permute-done | bytes 49184 | tf_op jit(solution)/shard_map/ppermute | solution.py:36
  42.4 2.3 %collective-permute-done.15.corner_ref = bf16[64,384]{1,0:T(8,128)(2,1)S(1)} collective-permute-done((bf16[64,384]{1,0:T(8,128)(2,1)S(1)}, bf16[64,384]{1,0:T(8,128)(2,1)S(1)}, u32[]{:S(2)}, u32[]{:S(2)}) %collective-permute-start.15) | collective-permute-done | bytes 49184 | tf_op jit(solution)/shard_map/ppermute | solution.py:58
  44.7 0.0 collective-permute-done.13.other_ref
  44.7 2.0 %finish.1 = bf16[4,4,8,768]{3,2,1,0:T(8,128)(2,1)} custom-call(f32[2,64,384]{2,1,0:T(8,128)S(1)} %get-tuple-element.71.inner_ref, f32[64,384]{1,0:T(8,128)S(1)} %get-tuple-element.72.dq_ref, bf16[3,64,384]{2,1,0:T(8,128)(2,1)S(1)} %collective-permute-done.13.other_ref, bf16[64,384]{1,0:T(8,128)(2,1)S(1)} %collective-permute-done.14.edge_ref, ...), custom_call_target="tpu_custom_call" | custom-call | flops 2000000000 | tf_op jit(solution)/shard_map/finish/pallas_call | solution.py:519
  (9 shorter events, 0.1 us)
Async XLA Ops:
  0.0 8.8 %collective-permute-start.1 = (s32[1,1,2]{2,1,0:T(1,128)}, s32[1,1,2]{2,1,0:T(1,128)S(1)}, u32[]{:S(2)}, u32[]{:S(2)}) collective-permute-start(s32[1,1,2]{2,1,0:T(1,128)} %count_ref.1), channel_id=1, source_target_pairs={{0,3},{1,2},{2,1},{3,0},{4,7},{5,6},{6,5},{7,4},{8,11},{9,10},{10,... | collective-permute-start | bytes 32 | tf_op jit(solution)/shard_map/ppermute | solution.py:36
  3.6 0.9 %copy-start = (bf16[4,4,8,768]{3,2,1,0:T(8,128)(2,1)S(1)}, bf16[4,4,8,768]{3,2,1,0:T(8,128)(2,1)}, u32[]{:S(2)}) copy-start(bf16[4,4,8,768]{3,2,1,0:T(8,128)(2,1)} %tokens_ref.1) | copy-start | bytes 589828
  3.7 1.6 %copy-start.1 = (bf16[3,768,384]{2,1,0:T(8,128)(2,1)S(1)}, bf16[3,768,384]{2,1,0:T(8,128)(2,1)}, u32[]{:S(2)}) copy-start(bf16[3,768,384]{2,1,0:T(8,128)(2,1)} %qkv_ref.5) | copy-start | bytes 5308420
  3.7 1.7 %copy-start.2 = (bf16[384,768]{1,0:T(8,128)(2,1)S(1)}, bf16[384,768]{1,0:T(8,128)(2,1)}, u32[]{:S(2)}) copy-start(bf16[384,768]{1,0:T(8,128)(2,1)} %out_weight_ref.1) | copy-start | bytes 1769476
  3.7 1.7 %copy-start.3 = (bf16[4,4,8,768]{3,2,1,0:T(8,128)(2,1)S(1)}, bf16[4,4,8,768]{3,2,1,0:T(8,128)(2,1)}, u32[]{:S(2)}) copy-start(bf16[4,4,8,768]{3,2,1,0:T(8,128)(2,1)} %grad_ref.1) | copy-start | bytes 589828
  3.7 1.7 %copy-start.4 = (f32[768]{0:T(1024)S(1)}, f32[768]{0:T(1024)}, u32[]{:S(2)}) copy-start(f32[768]{0:T(1024)} %gain_ref.5) | copy-start | bytes 9220
  3.7 1.7 %copy-start.5 = (s32[1,1,2]{2,1,0:T(1,128)S(1)}, s32[1,1,2]{2,1,0:T(1,128)}, u32[]{:S(2)}) copy-start(s32[1,1,2]{2,1,0:T(1,128)} %count_ref.1) | copy-start | bytes 28
  3.7 5.1 %collective-permute-start.2 = (bf16[64,768]{1,0:T(8,128)(2,1)S(1)}, bf16[64,768]{1,0:T(8,128)(2,1)S(1)}, u32[]{:S(2)}, u32[]{:S(2)}) collective-permute-start(bf16[64,768]{1,0:T(8,128)(2,1)S(1)} %reshape.3), channel_id=1, source_target_pairs={{0,3},{1,2},{2,1},{3,0},{4,7},{5,6},{6,5},{7,4},{8,11},{9,10},{10,... | collective-permute-start | bytes 294920 | tf_op jit(solution)/shard_map/ppermute | solution.py:36
  7.3 10.5 %collective-permute-start = (bf16[2,64,384]{2,1,0:T(8,128)(2,1)S(1)}, bf16[2,64,384]{2,1,0:T(8,128)(2,1)S(1)}, u32[]{:S(2)}, u32[]{:S(2)}) collective-permute-start(bf16[2,64,384]{2,1,0:T(8,128)(2,1)S(1)} %get-tuple-element.43), channel_id=1, source_target_pairs={{0,4},{4,0},{1,5},{5,1},{2,6},{6,2},{3,7},{7,3},{8,12},{12,8},{9,1... | collective-permute-start | bytes 294920 | tf_op jit(solution)/shard_map/ppermute | solution.py:36
  8.5 5.4 %collective-permute-start.4 = (bf16[2,64,384]{2,1,0:T(8,128)(2,1)S(1)}, bf16[2,64,384]{2,1,0:T(8,128)(2,1)S(1)}, u32[]{:S(2)}, u32[]{:S(2)}) collective-permute-start(bf16[2,64,384]{2,1,0:T(8,128)(2,1)S(1)} %get-tuple-element.47), channel_id=1, source_target_pairs={{0,4},{4,0},{1,5},{5,1},{2,6},{6,2},{3,7},{7,3},{8,12},{12,8},{9,1... | collective-permute-start | bytes 294920 | tf_op jit(solution)/shard_map/ppermute | solution.py:36
  9.9 7.9 %copy-start.6 = (f32[6]{0:T(128)S(1)}, f32[6]{0:T(128)}, u32[]{:S(2)}) copy-start(f32[6]{0:T(128)} %scale_ref.9) | copy-start | bytes 76
  10.0 13.3 %collective-permute-start.7 = (bf16[3,64,384]{2,1,0:T(8,128)(2,1)S(1)}, bf16[3,64,384]{2,1,0:T(8,128)(2,1)S(1)}, u32[]{:S(2)}, u32[]{:S(2)}) collective-permute-start(bf16[3,64,384]{2,1,0:T(8,128)(2,1)S(1)} %join.1.refs_0_), channel_id=1, source_target_pairs={{0,1},{1,0},{2,3},{3,2},{8,16},{9,17},{10,18},{11,19},{16,8},{17,9... | collective-permute-start | bytes 442376 | tf_op jit(solution)/shard_map/ppermute | solution.py:48
  10.5 8.4 %collective-permute-start.5 = (bf16[3,64,384]{2,1,0:T(8,128)(2,1)S(1)}, bf16[3,64,384]{2,1,0:T(8,128)(2,1)S(1)}, u32[]{:S(2)}, u32[]{:S(2)}) collective-permute-start(bf16[3,64,384]{2,1,0:T(8,128)(2,1)S(1)} %join.1.refs_0_), channel_id=1, source_target_pairs={{0,8},{1,9},{2,10},{3,11},{8,0},{9,1},{10,2},{11,3},{16,24},{17,25... | collective-permute-start | bytes 442376 | tf_op jit(solution)/shard_map/ppermute | solution.py:48
  12.6 3.2 %collective-permute-start.3 = (bf16[64,384]{1,0:T(8,128)(2,1)S(1)}, bf16[64,384]{1,0:T(8,128)(2,1)S(1)}, u32[]{:S(2)}, u32[]{:S(2)}) collective-permute-start(bf16[64,384]{1,0:T(8,128)(2,1)S(1)} %get-tuple-element.46), channel_id=1, source_target_pairs={{0,4},{4,0},{1,5},{5,1},{2,6},{6,2},{3,7},{7,3},{8,12},{12,8},{9,1... | collective-permute-start | bytes 147464 | tf_op jit(solution)/shard_map/ppermute | solution.py:36
  15.9 7.4 %collective-permute-start.8 = (bf16[3,64,384]{2,1,0:T(8,128)(2,1)S(1)}, bf16[3,64,384]{2,1,0:T(8,128)(2,1)S(1)}, u32[]{:S(2)}, u32[]{:S(2)}) collective-permute-start(bf16[3,64,384]{2,1,0:T(8,128)(2,1)S(1)} %pad_maximum_fusion.refs_1_), channel_id=1, source_target_pairs={{0,1},{1,0},{2,3},{3,2},{8,16},{9,17},{10,18},{11,19},{16,8},{17,9... | collective-permute-start | bytes 442376 | tf_op jit(solution)/shard_map/ppermute | solution.py:48
  17.8 5.4 %collective-permute-start.6 = (bf16[3,64,384]{2,1,0:T(8,128)(2,1)S(1)}, bf16[3,64,384]{2,1,0:T(8,128)(2,1)S(1)}, u32[]{:S(2)}, u32[]{:S(2)}) collective-permute-start(bf16[3,64,384]{2,1,0:T(8,128)(2,1)S(1)} %pad_maximum_fusion.refs_1_), channel_id=1, source_target_pairs={{0,8},{1,9},{2,10},{3,11},{8,0},{9,1},{10,2},{11,3},{16,24},{17,25... | collective-permute-start | bytes 442376 | tf_op jit(solution)/shard_map/ppermute | solution.py:48
  23.3 2.1 %collective-permute-start.9 = (bf16[6,64,384]{2,1,0:T(8,128)(2,1)S(1)}, bf16[6,64,384]{2,1,0:T(8,128)(2,1)S(1)}, u32[]{:S(2)}, u32[]{:S(2)}) collective-permute-start(bf16[6,64,384]{2,1,0:T(8,128)(2,1)S(1)} %slice_dynamic-update-slice_fusion), channel_id=1, source_target_pairs={{0,1},{1,0},{2,3},{3,2},{4,5},{5,4},{6,7},{7,6},{8,9},{9,8},{10,11... | collective-permute-start | bytes 884744 | tf_op jit(solution)/shard_map/ppermute | solution.py:36
  26.8 1.8 %collective-permute-start.10 = (bf16[6,64,384]{2,1,0:T(8,128)(2,1)S(1)}, bf16[6,64,384]{2,1,0:T(8,128)(2,1)S(1)}, u32[]{:S(2)}, u32[]{:S(2)}) collective-permute-start(bf16[6,64,384]{2,1,0:T(8,128)(2,1)S(1)} %get-tuple-element.64), channel_id=1, source_target_pairs={{0,1},{1,0},{2,3},{3,2},{4,5},{5,4},{6,7},{7,6},{8,9},{9,8},{10,11... | collective-permute-start | bytes 884744 | tf_op jit(solution)/shard_map/ppermute | solution.py:36
  28.7 8.5 %collective-permute-start.11 = (bf16[2,3,64,384]{3,2,1,0:T(8,128)(2,1)S(1)}, bf16[2,3,64,384]{3,2,1,0:T(8,128)(2,1)S(1)}, u32[]{:S(2)}, u32[]{:S(2)}) collective-permute-start(bf16[2,3,64,384]{3,2,1,0:T(8,128)(2,1)S(1)} %get-tuple-element.68), channel_id=1, source_target_pairs={{0,8},{1,9},{2,10},{3,11},{8,0},{9,1},{10,2},{11,3},{16,24},{17,25... | collective-permute-start | bytes 884744 | tf_op jit(solution)/shard_map/ppermute | solution.py:48
  29.1 8.2 %collective-permute-start.12 = (bf16[2,3,64,384]{3,2,1,0:T(8,128)(2,1)S(1)}, bf16[2,3,64,384]{3,2,1,0:T(8,128)(2,1)S(1)}, u32[]{:S(2)}, u32[]{:S(2)}) collective-permute-start(bf16[2,3,64,384]{3,2,1,0:T(8,128)(2,1)S(1)} %get-tuple-element.69), channel_id=1, source_target_pairs={{0,1},{1,0},{2,3},{3,2},{8,16},{9,17},{10,18},{11,19},{16,8},{17,9... | collective-permute-start | bytes 884744 | tf_op jit(solution)/shard_map/ppermute | solution.py:48
  37.4 7.3 %collective-permute-start.13 = (bf16[3,64,384]{2,1,0:T(8,128)(2,1)S(1)}, bf16[3,64,384]{2,1,0:T(8,128)(2,1)S(1)}, u32[]{:S(2)}, u32[]{:S(2)}) collective-permute-start(bf16[3,64,384]{2,1,0:T(8,128)(2,1)S(1)} %get-tuple-element.73), channel_id=1, source_target_pairs={{0,4},{4,0},{1,5},{5,1},{2,6},{6,2},{3,7},{7,3},{8,12},{12,8},{9,1... | collective-permute-start | bytes 442376 | tf_op jit(solution)/shard_map/ppermute | solution.py:36
  38.6 3.8 %collective-permute-start.14 = (bf16[64,384]{1,0:T(8,128)(2,1)S(1)}, bf16[64,384]{1,0:T(8,128)(2,1)S(1)}, u32[]{:S(2)}, u32[]{:S(2)}) collective-permute-start(bf16[64,384]{1,0:T(8,128)(2,1)S(1)} %get-tuple-element.74), channel_id=1, source_target_pairs={{0,3},{1,2},{2,1},{3,0},{4,7},{5,6},{6,5},{7,4},{8,11},{9,10},{10,... | collective-permute-start | bytes 147464 | tf_op jit(solution)/shard_map/ppermute | solution.py:36
  40.3 4.4 %collective-permute-start.15 = (bf16[64,384]{1,0:T(8,128)(2,1)S(1)}, bf16[64,384]{1,0:T(8,128)(2,1)S(1)}, u32[]{:S(2)}, u32[]{:S(2)}) collective-permute-start(bf16[64,384]{1,0:T(8,128)(2,1)S(1)} %get-tuple-element.75), channel_id=1, source_target_pairs={{0,7},{1,6},{2,5},{3,4},{4,3},{5,2},{6,1},{7,0},{8,15},{9,14},{10,... | collective-permute-start | bytes 147464 | tf_op jit(solution)/shard_map/ppermute | solution.py:58

commit v2 on v1

v2 whole, which is shorter than its diff:
```python
import functools
import math

import jax
import jax.numpy as jnp
from jax import lax
from jax.experimental import pallas as pl
from jax.experimental.pallas import tpu as pltpu
from jax.sharding import PartitionSpec as P

HEADS = 6
HEAD_DIM = 64
BLOCK = 4
CELLS = BLOCK * BLOCK * BLOCK
HALF = HEADS // 2
HALF_WIDTH = HALF * HEAD_DIM
PAIR_WIDTH = 2 * HALF_WIDTH
TILE = 2 * HEAD_DIM
TILES = PAIR_WIDTH // TILE
DEAD_KEY = 64.0
DROPPED = -1e30
FLOPS_PER_US = 1e9

EPS = 1e-06
F32 = jnp.float32
BF16 = jnp.bfloat16


def partner_of(device, count, phase):
    return device + 1 if device % 2 == phase else device - 1


def pair_swap(array, axis, phase):
    count = lax.axis_size(axis)
    pairs = [(device, partner_of(device, count, phase) % count) for device in range(count)]
    return lax.ppermute(array, axis, pairs)


def frame_swap(array, phase):
    frames, lons = lax.axis_size("tm"), lax.axis_size("lon")
    pairs = []
    for frame in range(frames):
        for lon in range(lons):
            to = (partner_of(frame, frames, phase), lon)
            if not 0 <= to[0] < frames:
                to = (frame, partner_of(lon, lons, 0))
            pairs.append((frame * lons + lon, to[0] * lons + to[1]))
    return lax.ppermute(array, ("tm", "lon"), pairs)


def corner_swap(array):
    lats, lons = lax.axis_size("lat"), lax.axis_size("lon")
    pairs = []
    for lat in range(lats):
        for lon in range(lons):
            to = partner_of(lat, lats, 0) * lons + partner_of(lon, lons, 1) % lons
            pairs.append((lat * lons + lon, to))
    return lax.ppermute(array, ("lat", "lon"), pairs)


def shift_by(array, axis, step):
    count = lax.axis_size(axis)
    pairs = [(i, i + step) for i in range(count) if 0 <= i + step < count]
    return lax.ppermute(array, axis, pairs)


def dot(a, b):
    return lax.dot_general(a, b, (((1,), (0,)), ((), ())), preferred_element_type=F32)


def dot_last(a, b):
    return lax.dot_general(a, b, (((1,), (1,)), ((), ())), preferred_element_type=F32)


def dot_first(a, b):
    return lax.dot_general(a, b, (((0,), (0,)), ((), ())), preferred_element_type=F32)


def head_means(values):
    rows = lax.broadcasted_iota(jnp.int32, (TILE, TILE), 0) // HEAD_DIM
    cols = lax.broadcasted_iota(jnp.int32, (TILE, TILE), 1) // HEAD_DIM
    ones = (rows == cols).astype(F32).astype(BF16)
    high = values.astype(BF16)
    low = (values - high.astype(F32)).astype(BF16)
    pieces = []
    for start in range(0, values.shape[1], TILE):
        cut = slice(start, start + TILE)
        pieces.append(dot(high[:, cut], ones) + dot(low[:, cut], ones))
    return jnp.concatenate(pieces, 1) * (1.0 / HEAD_DIM)


def block_order(lat_rows, lon_cols, count, parity):
    blocks = lon_cols // BLOCK
    row = lax.broadcasted_iota(jnp.int32, (count, count), 0)
    source = lax.broadcasted_iota(jnp.int32, (count, count), 1)
    slot = row // CELLS
    place = row % CELLS
    frame = place // (BLOCK * BLOCK)
    lat = (place // BLOCK) % BLOCK
    col = place % BLOCK
    block = jnp.where(parity == 1, blocks - 1 - slot, slot)
    wanted = (frame * lat_rows + lat) * lon_cols + block * BLOCK + col
    return (source == wanted).astype(F32).astype(BF16)


def halves(first, second):
    low = jnp.concatenate([first[:, :HALF_WIDTH], second[:, :HALF_WIDTH]], 1)
    high = jnp.concatenate([first[:, HALF_WIDTH:], second[:, HALF_WIDTH:]], 1)
    return low, high


def normalised(x, gain_ref):
    inverse = lax.rsqrt(jnp.mean(x * x, -1, keepdims=True) + EPS)
    return (x * inverse * gain_ref[...].reshape(1, x.shape[1])).astype(BF16)


def order_kernel(tokens_ref, order_ref, x_ref):
    frames, lat_rows, lon_cols, width = tokens_ref.shape
    cells = frames * lat_rows * lon_cols
    order = block_order(lat_rows, lon_cols, cells, lax.rem(lax.axis_index("lon"), 2))
    order_ref[...] = order
    x = dot(order, tokens_ref[...].astype(F32).reshape(cells, width).astype(BF16)).astype(BF16)
    x_ref[...] = x


def project_kernel(
    count_ref, scale_in, order_ref, x_ref, gain_ref, grad_ref, qkv_ref, out_weight_ref,
    kv_own_ref, qg_own_ref, kv_other_ref, qg_other_ref, edge_ref, corner_ref,
    raw_ref, inverse_ref, scale_ref,
):
    frames, lat_rows, lon_cols, width = grad_ref.shape
    cells = frames * lat_rows * lon_cols
    blocks = lon_cols // BLOCK
    parity = lax.rem(lax.axis_index("lon"), 2)
    upper = lax.rem(lax.axis_index("lat"), 2) == 1
    all_scales = scale_in[...].reshape(1, HEADS) * (1.0 / math.sqrt(HEAD_DIM))
    for h in range(HALF):
        mine = jnp.where(
            upper, all_scales[:, HALF + h : HALF + h + 1], all_scales[:, h : h + 1]
        )
        scale_ref[h : h + 1] = jnp.broadcast_to(mine, (1, 4 * CELLS))
    counts = count_ref[0]
    order = order_ref[...]
    normed = normalised(x_ref[...].astype(F32), gain_ref)
    query, key, value = (dot(normed, qkv_ref[c]) for c in range(3))
    head_width = HEADS * HEAD_DIM
    raw_ref[:, :head_width] = query
    raw_ref[:, head_width:] = key
    grad = dot_last(
        grad_ref[...].astype(F32).reshape(cells, width).astype(BF16), out_weight_ref[...]
    ).astype(BF16)
    grad = dot(order, grad)
    query_inverse = lax.rsqrt(head_means(query * query) + EPS)
    key_inverse = lax.rsqrt(head_means(key * key) + EPS)
    inverse_ref[:, :head_width] = query_inverse
    inverse_ref[:, head_width:] = key_inverse
    query = query * query_inverse
    key = key * key_inverse
    place = lax.broadcasted_iota(jnp.int32, (CELLS, 1), 0)
    live = []
    for slot in range(blocks):
        flip = blocks - 1 - slot
        live.append(
            place
            < jnp.where(parity == 1, counts[:, flip : flip + 1], counts[:, slot : slot + 1])
        )
    key = jnp.where(jnp.concatenate(live, 0), key, DEAD_KEY)
    shape = (blocks, CELLS, PAIR_WIDTH)
    low, high = halves(key, value)
    kv_own_ref[...] = jnp.where(upper, high, low).astype(BF16).reshape(shape)
    kv_other_ref[...] = jnp.where(upper, low, high).astype(BF16).reshape(shape)
    edge_ref[...] = kv_own_ref[0]
    corner_ref[...] = kv_other_ref[0]
    low, high = halves(query, grad)
    qg_own_ref[...] = jnp.where(upper, high, low).astype(BF16).reshape(shape)
    qg_other_ref[...] = jnp.where(upper, low, high).astype(BF16).reshape(shape)


def lane_tile(j):
    return slice((j // 2) * TILE, (j // 2 + 1) * TILE)


class Place:
    def __init__(self, rows):
        self.rows = rows
        tm, frames = lax.axis_index("tm"), lax.axis_size("tm")
        odd = lax.rem(tm, 2) == 1
        near, far = jnp.where(odd, tm - 1, tm + 1), jnp.where(odd, tm + 1, tm - 1)
        self.there = [None] + [((at >= 0) & (at < frames)) for at in (near, far)]
        self.upper = lax.rem(lax.axis_index("lat"), 2)

    def bias(self, frame, row, lanes):
        there = self.there[frame]
        total = 0.0 if there is None else jnp.where(there, 0.0, DROPPED)
        if row < 2:
            return total
        pair, pairs = lax.axis_index("lat") // 2, lax.axis_size("lat") // 2
        if row == 2:
            inside, wanted = pair > 0, self.upper
        else:
            inside, wanted = pair < pairs - 1, 1 - self.upper
        lane_row = (lax.broadcasted_iota(jnp.int32, (1, lanes), 1) // CELLS) % 2
        seen = (lane_row == wanted) & inside
        return total + jnp.where(seen, 0.0, DROPPED)


def head_scales(scale_ref, lanes):
    return [scale_ref[h : h + 1, lanes] for h in range(HALF)]


def key_bias(keys):
    return jnp.where(keys[:, 0:1].astype(F32) < 0.5 * DEAD_KEY, 0.0, DROPPED)


def score(keys, bias, weights_ref, lanes, scale_ref, sums):
    to_exp2 = [s * math.log2(math.e) for s in head_scales(scale_ref, lanes)]
    count = keys.shape[0]
    exps, probs = [], []
    for h in range(HALF):
        scores = dot(keys[:, lane_tile(h)], weights_ref[h, :, lanes])
        grad_prob = dot(keys[:, lane_tile(HALF + h)], weights_ref[HALF + h, :, lanes])
        masked = jnp.exp2(scores * to_exp2[h] + bias)
        if sums is not None:
            shape = (count // 8, 8, masked.shape[1])
            sums[h] = sums[h] + jnp.sum(masked.reshape(shape), 0)
            inner = (masked * grad_prob).reshape(shape)
            sums[HALF + h] = sums[HALF + h] + jnp.sum(inner, 0)
        exps.append(masked)
        probs.append(grad_prob)
    return exps, probs


ALL = slice(0, 4 * CELLS)
FIRST = slice(0, 2 * CELLS)
LAST = slice(2 * CELLS, 4 * CELLS)


def score_groups(place, frames, kv_refs, weights_ref, scale_ref, sums, e_mid, p_mid, e_left, p_left):
    rows = place.rows
    side = [jnp.zeros((8, 2 * CELLS), F32) for _ in range(2 * HALF)]
    for index, ref in enumerate(kv_refs):
        frame, row = frames[index // rows], index % rows
        keys = ref[1:3].reshape(2 * CELLS, PAIR_WIDTH)
        bias = key_bias(keys) + place.bias(frame, row, 4 * CELLS)
        exps, probs = score(keys, bias, weights_ref, ALL, scale_ref, sums)
        for h in range(HALF):
            e_mid[h, index * 2 * CELLS : (index + 1) * 2 * CELLS] = exps[h]
            p_mid[h, index * 2 * CELLS : (index + 1) * 2 * CELLS] = probs[h]
    for index in range(0, len(kv_refs), 2):
        frame, row = frames[index // rows], index % rows
        pair = [kv_refs[index][0], kv_refs[index + 1][0]]
        bias = jnp.concatenate(
            [
                jnp.broadcast_to(
                    key_bias(keys) + place.bias(frame, row + i, 2 * CELLS), (CELLS, 2 * CELLS)
                )
                for i, keys in enumerate(pair)
            ],
            0,
        )
        keys = jnp.concatenate(pair, 0)
        exps, probs = score(keys, bias, weights_ref, FIRST, scale_ref, side)
        for h in range(HALF):
            e_left[h, index * CELLS : (index + 2) * CELLS] = exps[h]
            p_left[h, index * CELLS : (index + 2) * CELLS] = probs[h]
    return [jnp.concatenate([a[:, FIRST] + b, a[:, LAST]], 1) for a, b in zip(sums, side)]


def query_tables(qg_ref, weights, backward):
    rows = jnp.concatenate([qg_ref[0], qg_ref[2], qg_ref[1], qg_ref[3]], 0).astype(F32)
    cols = rows.T
    count = rows.shape[0]
    lane_half = lax.broadcasted_iota(jnp.int32, (count, TILE), 1) // HEAD_DIM
    row_half = lax.broadcasted_iota(jnp.int32, (TILE, count), 0) // HEAD_DIM
    for j in range(2 * HALF):
        backward[j] = jnp.where(lane_half == j % 2, rows[:, lane_tile(j)], 0.0).astype(BF16)
        weights[j] = jnp.where(row_half == j % 2, cols[lane_tile(j)], 0.0).astype(BF16)


def own_score_kernel(rows, scale_ref, qg_ref, *refs):
    kv_refs, refs = refs[:rows], refs[rows:]
    weights, backward, sums_ref, e_mid, p_mid, e_left, p_left = refs
    queries = 4 * CELLS
    query_tables(qg_ref, weights, backward)
    sums = [jnp.zeros((8, queries), F32) for _ in range(2 * HALF)]
    sums = score_groups(
        Place(rows), (0,), kv_refs, weights, scale_ref, sums,
        e_mid, p_mid, e_left, p_left,
    )
    for j in range(2 * HALF):
        sums_ref[j] = sums[j]


def away_score_kernel(rows, scale_ref, weights, sums_in, *refs):
    kv_refs, refs = refs[: 2 * rows], refs[2 * rows :]
    sums_ref, e_mid, p_mid, e_left, p_left = refs
    sums = [sums_in[j] for j in range(2 * HALF)]
    sums = score_groups(
        Place(rows), (1, 2), kv_refs, weights, scale_ref, sums,
        e_mid, p_mid, e_left, p_left,
    )
    for j in range(2 * HALF):
        sums_ref[j] = sums[j]


def grad_parts(exps, probs, inverse, delta, scales):
    grads, halves_of = [], []
    for h in range(HALF):
        prob = exps[h] * inverse[h]
        halves_of.append(prob.astype(BF16))
        grads.append((prob * (probs[h] - delta[h]) * scales[h]).astype(BF16))
    return grads + halves_of


def key_grads(pieces, backward, lanes):
    outs = []
    for tile in range(TILES):
        both = jnp.concatenate([pieces[2 * tile], pieces[2 * tile + 1]], 1)
        rows = jnp.concatenate(
            [backward[2 * tile, lanes], backward[2 * tile + 1, lanes]], 0
        )
        outs.append(dot(both, rows))
    return jnp.concatenate(outs, 1)


def query_grads(keys, grads, h):
    own = slice((h % 2) * HEAD_DIM, (h % 2 + 1) * HEAD_DIM)
    return dot_first(keys[:, lane_tile(h)], grads)[own]


def side_bias(place, frame, row, keys):
    return jnp.concatenate(
        [
            jnp.broadcast_to(
                key_bias(keys[i]) + place.bias(frame, row + i, 2 * CELLS), (CELLS, 2 * CELLS)
            )
            for i in range(2)
        ],
        0,
    )


def sibling_kernel(
    rows, scale_ref, weights, backward, sums_in, keys_ref, part_ref, stats_ref, dq_ref
):
    place = Place(rows)
    side = [jnp.zeros((8, 2 * CELLS), F32) for _ in range(2 * HALF)]
    made = []
    for index in range(0, 3 * rows, 2):
        bias = side_bias(
            place, index // rows, index % rows, [keys_ref[index], keys_ref[index + 1]]
        )
        keys = keys_ref[index : index + 2].reshape(2 * CELLS, PAIR_WIDTH)
        made.append(score(keys, bias, weights, LAST, scale_ref, side))
    inverse, delta = [], []
    for h in range(HALF):
        total, inner = (
            jnp.concatenate([sums_in[j, :, FIRST], sums_in[j, :, LAST] + side[j]], 1)
            for j in (h, HALF + h)
        )
        inverse.append(1.0 / jnp.sum(total, 0, keepdims=True))
        delta.append(jnp.sum(inner, 0, keepdims=True) * inverse[h])
        stats_ref[h : h + 1] = inverse[h]
        stats_ref[HALF + h : HALF + h + 1] = delta[h]
    inverse = [a[:, LAST] for a in inverse]
    delta = [a[:, LAST] for a in delta]
    scales = head_scales(scale_ref, LAST)
    grads = []
    for index in range(0, 3 * rows, 2):
        pieces = grad_parts(*made[index // 2], inverse, delta, scales)
        grads.append(pieces[:HALF])
        if index < rows:
            part = key_grads(pieces, backward, LAST)
            part_ref[index : index + 2] = part.reshape(2, CELLS, PAIR_WIDTH)
    keys = keys_ref[...].reshape(3 * rows * CELLS, PAIR_WIDTH)
    for h in range(HALF):
        dq_ref[h * HEAD_DIM : (h + 1) * HEAD_DIM] = query_grads(
            keys, jnp.concatenate([g[h] for g in grads], 0), h
        )


def cross_score_kernel(rows, scale_ref, *refs):
    qg_refs, refs = refs[:2], refs[2:]
    kv_refs, sibling_ref, refs = refs[:rows], refs[rows], refs[rows + 1 :]
    backward, e_mid, p_mid, e_side, p_side, weights = refs
    place = Place(rows)
    for side in range(2):
        query_tables(qg_refs[side], weights.at[side], backward.at[side])
    for row in range(rows):
        keys = kv_refs[row][1:3].reshape(2 * CELLS, PAIR_WIDTH)
        bias = key_bias(keys) + place.bias(0, row, 4 * CELLS)
        at = slice(row * 2 * CELLS, (row + 1) * 2 * CELLS)
        for side in range(2):
            exps, probs = score(keys, bias, weights.at[side], ALL, scale_ref, None)
            for h in range(HALF):
                e_mid[side, h, at] = exps[h]
                p_mid[side, h, at] = probs[h]
    for row in range(0, rows, 2):
        at = slice(row * CELLS, (row + 2) * CELLS)
        for edge, lanes in ((0, FIRST), (1, LAST)):
            if edge == 0:
                pair = [kv_refs[row][0], kv_refs[row + 1][0]]
            else:
                pair = [sibling_ref[row], sibling_ref[row + 1]]
            bias = side_bias(place, 0, row, pair)
            keys = jnp.concatenate(pair, 0)
            for side in range(2):
                exps, probs = score(keys, bias, weights.at[side], lanes, scale_ref, None)
                for h in range(HALF):
                    e_side[side, edge, h, at] = exps[h]
                    p_side[side, edge, h, at] = probs[h]


def cross_stats(rows, stats_refs, lanes):
    place = Place(rows)
    both = []
    for side, ref in enumerate(stats_refs):
        there = jnp.where(place.there[1 + side], 1.0, 0.0)
        inverse = [ref[h : h + 1, lanes] * there for h in range(HALF)]
        both.append((inverse, [ref[HALF + h : HALF + h + 1, lanes] for h in range(HALF)]))
    return both


def cross_sibling_kernel(
    rows, scale_ref, near_stats, far_stats, backward, e_side, p_side, part_in, part_ref
):
    scales = head_scales(scale_ref, LAST)
    stats = cross_stats(rows, (near_stats, far_stats), LAST)
    for row in range(0, rows, 2):
        at = slice(row * CELLS, (row + 2) * CELLS)
        total = part_in[row : row + 2].reshape(2 * CELLS, PAIR_WIDTH)
        for side in range(2):
            pieces = grad_parts(
                [e_side[side, 1, h, at] for h in range(HALF)],
                [p_side[side, 1, h, at] for h in range(HALF)],
                *stats[side], scales,
            )
            total = total + key_grads(pieces, backward.at[side], LAST)
        part_ref[row : row + 2] = total.reshape(2, CELLS, PAIR_WIDTH).astype(BF16)


def cross_back_kernel(
    rows, scale_ref, near_stats, far_stats, backward, e_mid, p_mid, e_side, p_side,
    own_ref, total_ref,
):
    scales = head_scales(scale_ref, ALL)
    stats = cross_stats(rows, (near_stats, far_stats), ALL)
    for row in range(rows):
        at = slice(row * 2 * CELLS, (row + 1) * 2 * CELLS)
        total = own_ref[row, 1:3].reshape(2 * CELLS, PAIR_WIDTH)
        for side in range(2):
            pieces = grad_parts(
                [e_mid[side, h, at] for h in range(HALF)],
                [p_mid[side, h, at] for h in range(HALF)],
                *stats[side], scales,
            )
            total = total + key_grads(pieces, backward.at[side], ALL)
        total_ref[row, 1:3] = total.reshape(2, CELLS, PAIR_WIDTH)
    scales = head_scales(scale_ref, FIRST)
    stats = cross_stats(rows, (near_stats, far_stats), FIRST)
    for row in range(0, rows, 2):
        at = slice(row * CELLS, (row + 2) * CELLS)
        total = own_ref[row : row + 2, 0].reshape(2 * CELLS, PAIR_WIDTH)
        for side in range(2):
            pieces = grad_parts(
                [e_side[side, 0, h, at] for h in range(HALF)],
                [p_side[side, 0, h, at] for h in range(HALF)],
                *stats[side], scales,
            )
            total = total + key_grads(pieces, backward.at[side], FIRST)
        total_ref[row : row + 2, 0] = total.reshape(2, CELLS, PAIR_WIDTH)


def own_back_kernel(
    rows, scale_ref, stats_ref, backward, e_mid, p_mid, e_left, p_left,
    away_e_mid, away_p_mid, away_e_left, away_p_left, dq_sibling, *refs,
):
    kv_refs, refs = refs[: 3 * rows], refs[3 * rows :]
    own_ref, dq_own_ref, dq_other_ref, d_mid, d_left = refs
    scales = head_scales(scale_ref, ALL)
    inverse = [stats_ref[h : h + 1] for h in range(HALF)]
    delta = [stats_ref[HALF + h : HALF + h + 1] for h in range(HALF)]
    for index in range(3 * rows):
        at = slice(index * 2 * CELLS, (index + 1) * 2 * CELLS)
        if index < rows:
            exps, probs, start = e_mid, p_mid, index * 2 * CELLS
        else:
            exps, probs, start = away_e_mid, away_p_mid, (index - rows) * 2 * CELLS
        cut = slice(start, start + 2 * CELLS)
        pieces = grad_parts(
            [exps[h, cut] for h in range(HALF)], [probs[h, cut] for h in range(HALF)],
            inverse, delta, scales,
        )
        for h in range(HALF):
            d_mid[h, at] = pieces[h]
        if index < rows:
            part = key_grads(pieces, backward, ALL)
            own_ref[index, 1:3] = part.reshape(2, CELLS, PAIR_WIDTH)
    scales = head_scales(scale_ref, FIRST)
    inverse = [a[:, FIRST] for a in inverse]
    delta = [a[:, FIRST] for a in delta]
    for index in range(0, 3 * rows, 2):
        at = slice(index * CELLS, (index + 2) * CELLS)
        if index < rows:
            exps, probs, start = e_left, p_left, index * CELLS
        else:
            exps, probs, start = away_e_left, away_p_left, (index - rows) * CELLS
        cut = slice(start, start + 2 * CELLS)
        pieces = grad_parts(
            [exps[h, cut] for h in range(HALF)], [probs[h, cut] for h in range(HALF)],
            inverse, delta, scales,
        )
        for h in range(HALF):
            d_left[h, at] = pieces[h]
        if index < rows:
            part = key_grads(pieces, backward, FIRST)
            own_ref[index : index + 2, 0] = part.reshape(2, CELLS, PAIR_WIDTH)
    mid = jnp.concatenate([ref[1:3].reshape(2 * CELLS, PAIR_WIDTH) for ref in kv_refs], 0)
    left = jnp.concatenate([ref[0] for ref in kv_refs], 0)
    columns = []
    for h in range(HALF):
        made = query_grads(mid, d_mid[h], h)
        first = query_grads(left, d_left[h], h)
        last = dq_sibling[h * HEAD_DIM : (h + 1) * HEAD_DIM]
        columns.append(made + jnp.concatenate([first, last], 1))
    dq = jnp.concatenate(columns, 0).T
    dq_own_ref[...] = jnp.concatenate([dq[:CELLS], dq[2 * CELLS : 3 * CELLS]], 1)
    dq_other_ref[...] = jnp.concatenate([dq[CELLS : 2 * CELLS], dq[3 * CELLS :]], 1).astype(BF16)


def column_out_kernel(total_ref, sibling_ref, dq_other_ref, inner_ref, to_lat_ref, edge_ref, corner_ref):
    inner_ref[0] = total_ref[0, 1]
    inner_ref[1] = total_ref[0, 2] + sibling_ref[0].astype(F32)
    to_lat_ref[0] = total_ref[1, 1].astype(BF16)
    to_lat_ref[2] = dq_other_ref[...]
    to_lat_ref[1] = (total_ref[1, 2] + sibling_ref[1].astype(F32)).astype(BF16)
    edge_ref[...] = total_ref[0, 0].astype(BF16)
    corner_ref[...] = total_ref[1, 0].astype(BF16)


def finish_kernel(
    inner_ref, dq_ref, other_ref, edge_ref, corner_ref,
    raw_ref, inverse_ref, x_ref, order_ref, gain_ref, qkv_ref, out_ref,
):
    frames, lat_rows, lon_cols, width = out_ref.shape
    cells = frames * lat_rows * lon_cols
    parity = lax.rem(lax.axis_index("lon"), 2)
    upper = lax.rem(lax.axis_index("lat"), 2) == 1

    def joined(mine, theirs):
        return jnp.where(
            upper, jnp.concatenate([theirs, mine], 1), jnp.concatenate([mine, theirs], 1)
        )

    def by_slot(packed):
        return jnp.concatenate([packed[:, :HALF_WIDTH], packed[:, HALF_WIDTH:]], 0)

    def with_edge(inner, edge):
        return jnp.concatenate([inner[0] + edge.astype(F32), inner[1]], 0)

    dkv_mine = with_edge(inner_ref[...], edge_ref[...])
    dkv_theirs = with_edge(other_ref[:2].astype(F32), corner_ref[...])
    grads = [
        joined(by_slot(dq_ref[...]), by_slot(other_ref[2].astype(F32))),
        joined(dkv_mine[:, :HALF_WIDTH], dkv_theirs[:, :HALF_WIDTH]),
        joined(dkv_mine[:, HALF_WIDTH:], dkv_theirs[:, HALF_WIDTH:]),
    ]
    head_width = HEADS * HEAD_DIM
    grad_normed = dot_last(grads[2].astype(BF16), qkv_ref[2])
    for c in range(2):
        raw = raw_ref[:, c * head_width : (c + 1) * head_width]
        inverse = inverse_ref[:, c * head_width : (c + 1) * head_width]
        inner = head_means(raw * grads[c])
        grad_raw = inverse * grads[c] - inverse * inverse * inverse * raw * inner
        grad_normed = grad_normed + dot_last(grad_raw.astype(BF16), qkv_ref[c])
    order = order_ref[...]
    x = x_ref[...].astype(F32)
    inverse = lax.rsqrt(jnp.mean(x * x, -1, keepdims=True) + EPS)
    grad = gain_ref[...].reshape(1, width) * grad_normed
    inner = jnp.mean(x * grad, -1, keepdims=True)
    grad = (inverse * grad - inverse * inverse * inverse * x * inner).astype(BF16)
    grad = dot_first(order, grad)
    out_ref[...] = grad.reshape(out_ref.shape).astype(BF16)


VMEM = pl.BlockSpec(memory_space=pltpu.VMEM)


def kernel_call(
    body, name, outs, args, scratch=(), limit_mib=16, micros=1.0
):
    return pl.pallas_call(
        body,
        name=name,
        out_shape=[jax.ShapeDtypeStruct(shape, dtype) for shape, dtype in outs],
        in_specs=[VMEM] * len(args),
        out_specs=[VMEM] * len(outs),
        scratch_shapes=list(scratch),
        compiler_params=pltpu.CompilerParams(vmem_limit_bytes=limit_mib * 1024 * 1024),
        cost_estimate=pl.CostEstimate(
            flops=int(micros * FLOPS_PER_US), bytes_accessed=0, transcendentals=0
        ),
    )(*args)


def per_device(tokens, key_count, norm_gain, qkv_weight, out_weight, logit_scale, grad_out):
    frames, lat_rows, lon_cols, width = tokens.shape
    assert frames == BLOCK and lat_rows == BLOCK and lon_cols == 2 * BLOCK
    assert lax.axis_size("lat") % 2 == 0 and lax.axis_size("lon") % 2 == 0
    cells = frames * lat_rows * lon_cols
    blocks = lon_cols // BLOCK
    head_width = HEADS * HEAD_DIM
    qg_shape = ((blocks, CELLS, PAIR_WIDTH), BF16)
    edge_shape = ((CELLS, PAIR_WIDTH), BF16)

    order, x = kernel_call(
        order_kernel, "order", [((cells, cells), BF16), ((cells, width), BF16)], [tokens],
        micros=10.0,
    )
    kv_own, qg_own, kv_other, qg_other, edge, corner, raw, inverse, scales = kernel_call(
        project_kernel, "project",
        [qg_shape, qg_shape, qg_shape, qg_shape, edge_shape, edge_shape, ((cells, 2 * head_width), F32), ((cells, 2 * head_width), F32),
         ((HALF, 4 * CELLS), F32)],
        [key_count, logit_scale, order, x, norm_gain, grad_out, qkv_weight, out_weight],
        micros=40.0,
    )
    edge = pair_swap(edge, "lon", 1)
    corner = corner_swap(corner)
    kv_other = pair_swap(kv_other, "lat", 0)
    kv_rows = [
        jnp.concatenate([edge[None], kv_own], 0),
        jnp.concatenate([corner[None], kv_other], 0),
    ]
    qg_other, kv_other = lax.optimization_barrier((qg_other, kv_other))
    qg_other = pair_swap(qg_other, "lat", 0)
    upper = lax.rem(lax.axis_index("lat"), 2) == 1
    wide = lax.axis_size("lat") > 2
    if wide:
        even = jnp.where(upper, kv_rows[1], kv_rows[0])
        odd = jnp.where(upper, kv_rows[0], kv_rows[1])
        kv_rows += [shift_by(odd, "lat", 2), shift_by(even, "lat", -2)]
    rows = len(kv_rows)
    kv_away = [frame_swap(kv, phase) for phase in range(2) for kv in kv_rows]
    qg_both = jnp.concatenate([qg_own, qg_other], 0)
    qg_away = [frame_swap(qg_both, phase) for phase in range(2)]

    queries = 4 * CELLS
    tables = [((2 * HALF, TILE, queries), BF16), ((2 * HALF, queries, TILE), BF16)]
    sums_shape = ((2 * HALF, 8, queries), F32)

    def kept(groups):
        mid = ((HALF, groups * 2 * CELLS, queries), F32)
        left = ((HALF, groups * CELLS, 2 * CELLS), F32)
        return [mid, mid, left, left]

    weights, backward, sums, *own_kept = kernel_call(
        functools.partial(own_score_kernel, rows), "own_score",
        tables + [sums_shape] + kept(rows),
        [scales, qg_both, *kv_rows], micros=1.5,
    )
    siblings = jnp.stack([kv[2] for kv in kv_rows + kv_away], 0)
    siblings = pair_swap(siblings, "lon", 0)
    sums, *away_kept = kernel_call(
        functools.partial(away_score_kernel, rows), "away_score",
        [sums_shape] + kept(2 * rows), [scales, weights, sums, *kv_away],
        micros=20.0,
    )
    half_part = (rows, CELLS, PAIR_WIDTH)
    sibling_part, stats, dq_sibling = kernel_call(
        functools.partial(sibling_kernel, rows), "sibling",
        [(half_part, F32), ((2 * HALF, queries), F32), ((HALF_WIDTH, 2 * CELLS), F32)],
        [scales, weights, backward, sums, siblings], micros=1.5,
    )
    near_stats, far_stats = frame_swap(stats, 0), frame_swap(stats, 1)
    cross_mid = ((2, HALF, rows * 2 * CELLS, queries), F32)
    cross_side = ((2, 2, HALF, rows * CELLS, 2 * CELLS), F32)
    cross_backward, e_mid, p_mid, e_side, p_side = kernel_call(
        functools.partial(cross_score_kernel, rows), "cross_score",
        [((2,) + tables[1][0], BF16), cross_mid, cross_mid, cross_side, cross_side],
        [scales, *qg_away, *kv_rows, siblings], micros=2.0,
        scratch=[pltpu.VMEM((2,) + tables[0][0], BF16)],
    )
    part = (rows, blocks + 1, CELLS, PAIR_WIDTH)
    packed = (CELLS, 2 * HALF_WIDTH)
    own_part, dq_own, dq_other = kernel_call(
        functools.partial(own_back_kernel, rows), "own_back",
        [(part, F32), (packed, F32), (packed, BF16)],
        [scales, stats, backward, *own_kept, *away_kept, dq_sibling, *kv_rows, *kv_away],
        micros=2.0,
        scratch=[
            pltpu.VMEM((HALF, 3 * rows * 2 * CELLS, queries), BF16),
            pltpu.VMEM((HALF, 3 * rows * CELLS, 2 * CELLS), BF16),
        ],
    )
    (sibling_part,) = kernel_call(
        functools.partial(cross_sibling_kernel, rows), "cross_sibling", [(half_part, BF16)],
        [scales, near_stats, far_stats, cross_backward, e_side, p_side, sibling_part],
        micros=0.5,
    )
    sibling_part = pair_swap(sibling_part, "lon", 0)
    (total,) = kernel_call(
        functools.partial(cross_back_kernel, rows), "cross_back", [(part, F32)],
        [scales, near_stats, far_stats, cross_backward, e_mid, p_mid, e_side, p_side,
         own_part],
        micros=1.5,
    )
    if wide:
        total = total.at[:, blocks].add(sibling_part.astype(F32))
        sibling_part = jnp.zeros_like(sibling_part)
        to_odd = shift_by(total[2].astype(BF16), "lat", -2).astype(F32)
        to_even = shift_by(total[3].astype(BF16), "lat", 2).astype(F32)
        total = total[:2] + jnp.stack(
            [jnp.where(upper, to_odd, to_even), jnp.where(upper, to_even, to_odd)], 0
        )
    inner, to_lat, edge, corner = kernel_call(
        column_out_kernel, "column_out",
        [((blocks, CELLS, PAIR_WIDTH), F32), ((blocks + 1, CELLS, PAIR_WIDTH), BF16),
         edge_shape, edge_shape],
        [total, sibling_part, dq_other],
    )
    edge = pair_swap(edge, "lon", 1)
    corner = corner_swap(corner)
    other = pair_swap(to_lat, "lat", 0)
    (grad_tokens,) = kernel_call(
        finish_kernel, "finish", [(tokens.shape, BF16)],
        [inner, dq_own, other, edge, corner, raw, inverse, x, order, norm_gain, qkv_weight],
        micros=2.0,
    )
    return grad_tokens


def solution(mesh):
    in_specs = (
        P("tm", "lat", "lon", None),
        P("tm", "lat", "lon"),
        P(),
        P(),
        P(),
        P(),
        P("tm", "lat", "lon", None),
    )
    out_specs = P("tm", "lat", "lon", None)
    return jax.shard_map(
        per_device, mesh=mesh, in_specs=in_specs, out_specs=out_specs, check_vma=False
    )
```

time: 46.9 us -> 40.8 us (0.87)
  waiting for transfers between devices: 16.9 us -> 9.78 us
  starting transfers between devices: 15.1 us -> 20.2 us
  Pallas kernels: 11.8 us -> 8.48 us
  local copies, waits for them, and re-layouts: 2.64 us -> 2.05 us
    ppermute x6 -> x8, waiting for transfers between devices: 10.6 us -> 1.54 us  [frame_swap(): return lax.ppermute(array, ('tm', 'lon'), pairs)]
    ppermute x6 -> x8, starting transfers between devices: 5.37 us -> 9.2 us  [frame_swap(): return lax.ppermute(array, ('tm', 'lon'), pairs)]
    pallas_call x12 -> x11, Pallas kernels: 11.8 us -> 8.48 us  [kernel_call(): pl.pallas_call(body, name=name, out_shape=[jax.ShapeDtypeStruct(shape, dt...]
    ppermute x9 -> x7, waiting for transfers between devices: 4.11 us -> 5.95 us  [pair_swap(): return lax.ppermute(array, axis, pairs)]
    ppermute x1 -> x2, starting transfers between devices: 0.07 us -> 1.31 us  [corner_swap(): return lax.ppermute(array, ('lat', 'lon'), pairs)]
    dynamic_slice x1 -> x0, local copies, waits for them, and re-layouts: 0.98 us -> none  [per_device(): lax.dynamic_slice_in_dim(tokens, start, BLOCK, 2).reshape(CELLS, width)]
    unnamed x19 -> x20, local copies, waits for them, and re-layouts: 1.62 us -> 2.02 us
    ppermute x1 -> x2, waiting for transfers between devices: 2.26 us -> 2.29 us  [corner_swap(): return lax.ppermute(array, ('lat', 'lon'), pairs)]
  transfers between devices with their start and end apart: 16 -> 17, of which waited for: 6 -> 7; matrix products, arithmetic and copies ran while one was open for 2% -> 0% of each run, Pallas kernels for 18% -> 12%
where the time goes in v2:
time: 40.8 us; the launch traced here: 40.7 us
  starting transfers between devices  20.2 us (50%)
  waiting for transfers between devices  9.78 us (24%)
  Pallas kernels  8.48 us (21%)
  local copies, waits for them, and re-layouts  2.05 us (5%)
    ppermute x7, starting transfers between devices, pair_swap(): return lax.ppermute(array, axis, pairs)  9.66 us
    ppermute x8, starting transfers between devices, frame_swap(): return lax.ppermute(array, ('tm', 'lon'), pairs)  9.2 us
    pallas_call x11, Pallas kernels, kernel_call(): pl.pallas_call(body, name=name, out_shape=[jax.ShapeDtypeStruct(shape, dt...  8.48 us
    ppermute x7, waiting for transfers between devices, pair_swap(): return lax.ppermute(array, axis, pairs)  5.95 us
    ppermute x2, waiting for transfers between devices, corner_swap(): return lax.ppermute(array, ('lat', 'lon'), pairs)  2.29 us
    unnamed x20, local copies, waits for them, and re-layouts  2.02 us
    ppermute x8, waiting for transfers between devices, frame_swap(): return lax.ppermute(array, ('tm', 'lon'), pairs)  1.54 us
    ppermute x2, starting transfers between devices, corner_swap(): return lax.ppermute(array, ('lat', 'lon'), pairs)  1.31 us
  transfers between devices with their start and end apart: 17, of which 7 were waited for; matrix products, arithmetic and copies ran while one was open for 0% of the time, Pallas kernels for 12%

profile of v2, /device:TPU:1, one launch (start us, length us, event | category | flops | bytes accessed | tf_op | source)
XLA Modules:
  0.0 40.7 jit_solution(7549414517931395871)
XLA Ops:
  0.0 0.0 copy-start
  0.0 0.0 copy-start.1
  0.0 0.0 copy-start.2
  0.0 1.1 %copy-done.2 = bf16[4,4,8,768]{3,2,1,0:T(8,128)(2,1)S(1)} copy-done((bf16[4,4,8,768]{3,2,1,0:T(8,128)(2,1)S(1)}, bf16[4,4,8,768]{3,2,1,0:T(8,128)(2,1)}, u32[]{:S(2)}) %copy-start.2) | copy-done | bytes 196632
  1.1 0.0 copy-start.3
  1.1 0.0 copy-start.4
  1.1 0.0 copy-start.5
  1.1 0.0 copy-start.6
  1.1 0.2 order.1
  1.3 0.3 copy-done
  1.6 0.1 copy-done.1
  1.7 0.5 %copy-done.3 = bf16[4,4,8,768]{3,2,1,0:T(8,128)(2,1)S(1)} copy-done((bf16[4,4,8,768]{3,2,1,0:T(8,128)(2,1)S(1)}, bf16[4,4,8,768]{3,2,1,0:T(8,128)(2,1)}, u32[]{:S(2)}) %copy-start.3) | copy-done | bytes 196632
  2.2 0.0 copy-done.4
  2.2 0.0 copy-done.5
  2.2 0.0 copy-done.6
  2.2 1.2 %project.1 = (bf16[2,64,384]{2,1,0:T(8,128)(2,1)S(1)}, bf16[2,64,384]{2,1,0:T(8,128)(2,1)S(1)}, bf16[2,64,384]{2,1,0:T(8,128)(2,1)S(1)}, bf16[2,64,384]{2,1,0:T(...) custom-call(s32[1,1,2]{2,1,0:T(1,128)S(1)} %copy-done.5, ...), custom_call_target="tpu_custom_call" | custom-call | flops 40000000000 | tf_op jit(solution)/shard_map/project/pallas_call | solution.py:592
  3.4 2.7 %collective-permute-start.2 = (bf16[64,384]{1,0:T(8,128)(2,1)S(1)}, bf16[64,384]{1,0:T(8,128)(2,1)S(1)}, u32[]{:S(2)}, u32[]{:S(2)}) collective-permute-start(bf16[64,384]{1,0:T(8,128)(2,1)S(1)} %get-tuple-element.51), channel_id=1, source_target_pairs={{0,3},{1,2},{2,1},{3,0},{4,7},{5,6},{6,5},{7,4},{8,11},{9,10},{10,... | collective-permute-start | bytes 147464 | tf_op jit(solution)/shard_map/ppermute | solution.py:36
  6.1 1.0 %collective-permute-start.3 = (bf16[64,384]{1,0:T(8,128)(2,1)S(1)}, bf16[64,384]{1,0:T(8,128)(2,1)S(1)}, u32[]{:S(2)}, u32[]{:S(2)}) collective-permute-start(bf16[64,384]{1,0:T(8,128)(2,1)S(1)} %get-tuple-element.53), channel_id=1, source_target_pairs={{0,7},{1,6},{2,5},{3,4},{4,3},{5,2},{6,1},{7,0},{8,15},{9,14},{10,... | collective-permute-start | bytes 147464 | tf_op jit(solution)/shard_map/ppermute | solution.py:58
  7.1 0.3 collective-permute-start
  7.3 0.5 %collective-permute-done.2 = bf16[64,384]{1,0:T(8,128)(2,1)S(1)} collective-permute-done((bf16[64,384]{1,0:T(8,128)(2,1)S(1)}, bf16[64,384]{1,0:T(8,128)(2,1)S(1)}, u32[]{:S(2)}, u32[]{:S(2)}) %collective-permute-start.2) | collective-permute-done | bytes 49184 | tf_op jit(solution)/shard_map/ppermute | solution.py:36
  7.9 0.4 collective-permute-start.6
  8.2 2.9 %collective-permute-start.4 = (bf16[3,64,384]{2,1,0:T(8,128)(2,1)S(1)}, bf16[3,64,384]{2,1,0:T(8,128)(2,1)S(1)}, u32[]{:S(2)}, u32[]{:S(2)}) collective-permute-start(bf16[3,64,384]{2,1,0:T(8,128)(2,1)S(1)} %pad_maximum_fusion.refs_0_.refs_2_), channel_id=1, source_target_pairs={{0,8},{1,9},{2,10},{3,11},{8,0},{9,1},{10,2},{11,3},{16,24},{17,25... | collective-permute-start | bytes 442376 | tf_op jit(solution)/shard_map/ppermute | solution.py:48
  11.2 0.0 collective-permute-done.3
  11.2 0.0 collective-permute-done
  11.2 1.1 %collective-permute-start.7 = (bf16[3,64,384]{2,1,0:T(8,128)(2,1)S(1)}, bf16[3,64,384]{2,1,0:T(8,128)(2,1)S(1)}, u32[]{:S(2)}, u32[]{:S(2)}) collective-permute-start(bf16[3,64,384]{2,1,0:T(8,128)(2,1)S(1)} %pad_maximum_fusion.1.refs_1_.refs_3_), channel_id=1, source_target_pairs={{0,1},{1,0},{2,3},{3,2},{8,16},{9,17},{10,18},{11,19},{16,8},{17,9... | collective-permute-start | bytes 442376 | tf_op jit(solution)/shard_map/ppermute | solution.py:48
  12.4 1.3 %collective-permute-start.5 = (bf16[3,64,384]{2,1,0:T(8,128)(2,1)S(1)}, bf16[3,64,384]{2,1,0:T(8,128)(2,1)S(1)}, u32[]{:S(2)}, u32[]{:S(2)}) collective-permute-start(bf16[3,64,384]{2,1,0:T(8,128)(2,1)S(1)} %pad_maximum_fusion.1.refs_1_.refs_3_), channel_id=1, source_target_pairs={{0,8},{1,9},{2,10},{3,11},{8,0},{9,1},{10,2},{11,3},{16,24},{17,25... | collective-permute-start | bytes 442376 | tf_op jit(solution)/shard_map/ppermute | solution.py:48
  13.6 1.3 %collective-permute-start.1 = (bf16[2,64,384]{2,1,0:T(8,128)(2,1)S(1)}, bf16[2,64,384]{2,1,0:T(8,128)(2,1)S(1)}, u32[]{:S(2)}, u32[]{:S(2)}) collective-permute-start(bf16[2,64,384]{2,1,0:T(8,128)(2,1)S(1)} %get-tuple-element.50), channel_id=1, source_target_pairs={{0,4},{4,0},{1,5},{5,1},{2,6},{6,2},{3,7},{7,3},{8,12},{12,8},{9,1... | collective-permute-start | bytes 294920 | tf_op jit(solution)/shard_map/ppermute | solution.py:36
  14.9 2.5 %collective-permute-done.1 = bf16[2,64,384]{2,1,0:T(8,128)(2,1)S(1)} collective-permute-done((bf16[2,64,384]{2,1,0:T(8,128)(2,1)S(1)}, bf16[2,64,384]{2,1,0:T(8,128)(2,1)S(1)}, u32[]{:S(2)}, u32[]{:S(2)}) %collective-permute-start.1) | collective-permute-done | bytes 98336 | tf_op jit(solution)/shard_map/ppermute | solution.py:36
  17.4 2.8 %collective-permute-start.12 = (bf16[4,64,384]{2,1,0:T(8,128)(2,1)S(1)}, bf16[4,64,384]{2,1,0:T(8,128)(2,1)S(1)}, u32[]{:S(2)}, u32[]{:S(2)}) collective-permute-start(bf16[4,64,384]{2,1,0:T(8,128)(2,1)S(1)} %constant_dynamic-update-slice_fusion.qg_ref), channel_id=1, source_target_pairs={{0,1},{1,0},{2,3},{3,2},{8,16},{9,17},{10,18},{11,19},{16,8},{17,9... | collective-permute-start | bytes 589832 | tf_op jit(solution)/shard_map/ppermute | solution.py:48
  20.3 0.0 collective-permute-done.4.refs_0_.refs_2_
  20.3 0.2 collective-permute-start.11
  20.4 0.5 %own_score.1 = (bf16[6,128,256]{2,1,0:T(8,128)(2,1)S(1)}, bf16[6,256,128]{2,1,0:T(8,128)(2,1)S(1)}, f32[6,8,256]{2,1,0:T(8,128)S(1)}, f32[3,256,256]{2,1,0:T(8,1...) custom-call(f32[3,256]{1,0:T(4,128)S(1)} %get-tuple-element.46.scale_ref, ...), custom_call_target="tpu_custom_call" | custom-call | flops 1500000000 | tf_op jit(solution)/shard_map/own_score/pallas_call | solution.py:592
  21.0 0.0 collective-permute-done.5.refs_1_.refs_3_
  21.0 0.0 collective-permute-done.6.refs_2_.refs_4_
  21.0 0.0 collective-permute-done.7.refs_3_.refs_5_
  21.1 1.8 %collective-permute-start.8 = (bf16[6,64,384]{2,1,0:T(8,128)(2,1)S(1)}, bf16[6,64,384]{2,1,0:T(8,128)(2,1)S(1)}, u32[]{:S(2)}, u32[]{:S(2)}) collective-permute-start(bf16[6,64,384]{2,1,0:T(8,128)(2,1)S(1)} %slice_dynamic-update-slice_fusion), channel_id=1, source_target_pairs={{0,1},{1,0},{2,3},{3,2},{4,5},{5,4},{6,7},{7,6},{8,9},{9,8},{10,11... | collective-permute-start | bytes 884744 | tf_op jit(solution)/shard_map/ppermute | solution.py:36
  22.9 0.7 %away_score.1 = (f32[6,8,256]{2,1,0:T(8,128)S(1)}, f32[3,512,256]{2,1,0:T(8,128)S(1)}, f32[3,512,256]{2,1,0:T(8,128)S(1)}, f32[3,256,128]{2,1,0:T(8,128)S(1)}, f32[3,256,128]{2,1,0:T(8,128)S(1)}) custom-call(f32[3,256]{1,0:T(4,128)S(1)} %get-tuple-element.46.scale_ref, bf16[6,128,256]{2,1,0:T(8,128)(2,1)S(1)} %get-tuple-element.54.weights, ...), custom_call_target="tpu_custom_call" | custom-call | flops 20000000000 | tf_op jit(solution)/shard_map/away_score/pallas_call | solution.py:592
  23.5 0.5 %collective-permute-done.8.keys_ref.refs_4_ = bf16[6,64,384]{2,1,0:T(8,128)(2,1)S(1)} collective-permute-done((bf16[6,64,384]{2,1,0:T(8,128)(2,1)S(1)}, bf16[6,64,384]{2,1,0:T(8,128)(2,1)S(1)}, u32[]{:S(2)}, u32[]{:S(2)}) %collective-permute-start.8) | collective-permute-done | bytes 294944 | tf_op jit(solution)/shard_map/ppermute | solution.py:36
  24.1 0.7 %sibling.1 = (f32[2,64,384]{2,1,0:T(8,128)S(1)}, f32[6,256]{1,0:T(8,128)S(1)}, f32[192,128]{1,0:T(8,128)S(1)}) custom-call(f32[3,256]{1,0:T(4,128)S(1)} %get-tuple-element.46.scale_ref, bf16[6,128,256]{2,1,0:T(8,128)(2,1)S(1)} %get-tuple-element.54.weights, bf16[6,256,128]{2,1,0:T(8,128)(2,1)S(1)} %get-tuple-element.55.backward, ...), custom_call_target="tpu_custom_call" | custom-call | flops 1500000000 | tf_op jit(solution)/shard_map/sibling/pallas_call | solution.py:592
  24.8 0.4 %collective-permute-start.10 = (f32[6,256]{1,0:T(8,128)S(1)}, f32[6,256]{1,0:T(8,128)S(1)}, u32[]{:S(2)}, u32[]{:S(2)}) collective-permute-start(f32[6,256]{1,0:T(8,128)S(1)} %get-tuple-element.58.stats_ref), channel_id=1, source_target_pairs={{0,1},{1,0},{2,3},{3,2},{8,16},{9,17},{10,18},{11,19},{16,8},{17,9... | collective-permute-start | bytes 18440 | tf_op jit(solution)/shard_map/ppermute | solution.py:48
  25.2 0.0 collective-permute-start.9
  25.2 0.0 collective-permute-done.12.refs_1_
  25.2 1.5 %collective-permute-done.11.refs_0_ = bf16[4,64,384]{2,1,0:T(8,128)(2,1)S(1)} collective-permute-done((bf16[4,64,384]{2,1,0:T(8,128)(2,1)S(1)}, bf16[4,64,384]{2,1,0:T(8,128)(2,1)S(1)}, u32[]{:S(2)}, u32[]{:S(2)}) %collective-permute-start.11) | collective-permute-done | bytes 196640 | tf_op jit(solution)/shard_map/ppermute | solution.py:48
  26.7 0.9 %cross_score.1 = (bf16[2,6,256,128]{3,2,1,0:T(8,128)(2,1)S(1)}, f32[2,3,256,256]{3,2,1,0:T(8,128)S(1)}, f32[2,3,256,256]{3,2,1,0:T(8,128)S(1)}, f32[2,2,3,128,12...) custom-call(f32[3,256]{1,0:T(4,128)S(1)} %get-tuple-element.46.scale_ref, ...), custom_call_target="tpu_custom_call" | custom-call | flops 2000000000 | tf_op jit(solution)/shard_map/cross_score/pallas_call | solution.py:592
  27.6 1.2 %own_back.1 = (f32[2,3,64,384]{3,2,1,0:T(8,128)S(1)}, f32[64,384]{1,0:T(8,128)S(1)}, bf16[64,384]{1,0:T(8,128)(2,1)S(1)}) custom-call(f32[3,256]{1,0:T(4,128)S(1)} %get-tuple-element.46.scale_ref, f32[6,256]{1,0:T(8,128)S(1)} %get-tuple-element.58.stats_ref, bf16[6,256,128]{2,1,0:T(8,128)(2,1)S(1)} %get-tuple-element.55.backward, ...), custom_call_target="tpu_custom_call" | custom-call | flops 2000000000 | tf_op jit(solution)/shard_map/own_back/pallas_call | solution.py:592
  28.8 0.0 collective-permute-done.10.far_stats
  28.8 0.0 collective-permute-done.9.near_stats
  28.8 0.3 cross_sibling.1
  29.1 0.9 %collective-permute-start.13 = (bf16[2,64,384]{2,1,0:T(8,128)(2,1)S(1)}, bf16[2,64,384]{2,1,0:T(8,128)(2,1)S(1)}, u32[]{:S(2)}, u32[]{:S(2)}) collective-permute-start(bf16[2,64,384]{2,1,0:T(8,128)(2,1)S(1)} %cross_sibling.1), channel_id=1, source_target_pairs={{0,1},{1,0},{2,3},{3,2},{4,5},{5,4},{6,7},{7,6},{8,9},{9,8},{10,11... | collective-permute-start | bytes 294920 | tf_op jit(solution)/shard_map/ppermute | solution.py:36
  30.0 0.8 %cross_back.1.total_ref = f32[2,3,64,384]{3,2,1,0:T(8,128)S(1)} custom-call(f32[3,256]{1,0:T(4,128)S(1)} %get-tuple-element.46.scale_ref, f32[6,256]{1,0:T(8,128)S(1)} %collective-permute-done.9.near_stats, f32[6,256]{1,0:T(8,128)S(1)} %collective-permute-done.10.far_stats, bf16[2,6,256,128]{3,2,1,0:T(8,128)(2,1)S(1)} %get-tuple-element.59.backward, ...), custom_call_target="tpu_custom_call" | custom-call | flops 1500000000 | tf_op jit(solution)/shard_map/cross_back/pallas_call | solution.py:592
  30.8 0.1 collective-permute-done.13.sibling_ref
  31.0 1.1 %collective-permute-start.14 = (bf16[3,64,384]{2,1,0:T(8,128)(2,1)S(1)}, bf16[3,64,384]{2,1,0:T(8,128)(2,1)S(1)}, u32[]{:S(2)}, u32[]{:S(2)}) collective-permute-start(bf16[3,64,384]{2,1,0:T(8,128)(2,1)S(1)} %get-tuple-element.78), channel_id=1, source_target_pairs={{0,4},{4,0},{1,5},{5,1},{2,6},{6,2},{3,7},{7,3},{8,12},{12,8},{9,1... | collective-permute-start | bytes 442376 | tf_op jit(solution)/shard_map/ppermute | solution.py:36
  32.1 1.6 %collective-permute-start.15 = (bf16[64,384]{1,0:T(8,128)(2,1)S(1)}, bf16[64,384]{1,0:T(8,128)(2,1)S(1)}, u32[]{:S(2)}, u32[]{:S(2)}) collective-permute-start(bf16[64,384]{1,0:T(8,128)(2,1)S(1)} %get-tuple-element.79), channel_id=1, source_target_pairs={{0,3},{1,2},{2,1},{3,0},{4,7},{5,6},{6,5},{7,4},{8,11},{9,10},{10,... | collective-permute-start | bytes 147464 | tf_op jit(solution)/shard_map/ppermute | solution.py:36
  33.7 0.3 collective-permute-start.16
  34.0 2.4 %collective-permute-done.15.edge_ref = bf16[64,384]{1,0:T(8,128)(2,1)S(1)} collective-permute-done((bf16[64,384]{1,0:T(8,128)(2,1)S(1)}, bf16[64,384]{1,0:T(8,128)(2,1)S(1)}, u32[]{:S(2)}, u32[]{:S(2)}) %collective-permute-start.15) | collective-permute-done | bytes 49184 | tf_op jit(solution)/shard_map/ppermute | solution.py:36
  36.4 2.3 %collective-permute-done.16.corner_ref = bf16[64,384]{1,0:T(8,128)(2,1)S(1)} collective-permute-done((bf16[64,384]{1,0:T(8,128)(2,1)S(1)}, bf16[64,384]{1,0:T(8,128)(2,1)S(1)}, u32[]{:S(2)}, u32[]{:S(2)}) %collective-permute-start.16) | collective-permute-done | bytes 49184 | tf_op jit(solution)/shard_map/ppermute | solution.py:58
  38.7 0.0 collective-permute-done.14.other_ref
  38.7 2.0 %finish.1 = bf16[4,4,8,768]{3,2,1,0:T(8,128)(2,1)} custom-call(f32[2,64,384]{2,1,0:T(8,128)S(1)} %get-tuple-element.76.inner_ref, f32[64,384]{1,0:T(8,128)S(1)} %get-tuple-element.77.dq_ref, bf16[3,64,384]{2,1,0:T(8,128)(2,1)S(1)} %collective-permute-done.14.other_ref, bf16[64,384]{1,0:T(8,128)(2,1)S(1)} %collective-permute-done.15.edge_ref, ...), custom_call_target="tpu_custom_call" | custom-call | flops 2000000000 | tf_op jit(solution)/shard_map/finish/pallas_call | solution.py:592
  (11 shorter events, 0.2 us)
Async XLA Ops:
  0.0 1.6 %copy-start = (bf16[3,768,384]{2,1,0:T(8,128)(2,1)S(1)}, bf16[3,768,384]{2,1,0:T(8,128)(2,1)}, u32[]{:S(2)}) copy-start(bf16[3,768,384]{2,1,0:T(8,128)(2,1)} %qkv_ref.3) | copy-start | bytes 5308420
  0.0 1.7 %copy-start.1 = (bf16[384,768]{1,0:T(8,128)(2,1)S(1)}, bf16[384,768]{1,0:T(8,128)(2,1)}, u32[]{:S(2)}) copy-start(bf16[384,768]{1,0:T(8,128)(2,1)} %out_weight_ref.1) | copy-start | bytes 1769476
  0.0 1.1 %copy-start.2 = (bf16[4,4,8,768]{3,2,1,0:T(8,128)(2,1)S(1)}, bf16[4,4,8,768]{3,2,1,0:T(8,128)(2,1)}, u32[]{:S(2)}) copy-start(bf16[4,4,8,768]{3,2,1,0:T(8,128)(2,1)} %tokens_ref.1) | copy-start | bytes 589828
  1.1 1.1 %copy-start.3 = (bf16[4,4,8,768]{3,2,1,0:T(8,128)(2,1)S(1)}, bf16[4,4,8,768]{3,2,1,0:T(8,128)(2,1)}, u32[]{:S(2)}) copy-start(bf16[4,4,8,768]{3,2,1,0:T(8,128)(2,1)} %grad_ref.1) | copy-start | bytes 589828
  1.1 1.1 %copy-start.4 = (f32[768]{0:T(1024)S(1)}, f32[768]{0:T(1024)}, u32[]{:S(2)}) copy-start(f32[768]{0:T(1024)} %gain_ref.3) | copy-start | bytes 9220
  1.1 1.1 %copy-start.5 = (s32[1,1,2]{2,1,0:T(1,128)S(1)}, s32[1,1,2]{2,1,0:T(1,128)}, u32[]{:S(2)}) copy-start(s32[1,1,2]{2,1,0:T(1,128)} %count_ref.1) | copy-start | bytes 28
  1.1 1.1 %copy-start.6 = (f32[6]{0:T(128)S(1)}, f32[6]{0:T(128)}, u32[]{:S(2)}) copy-start(f32[6]{0:T(128)} %scale_in.1) | copy-start | bytes 76
  3.4 4.5 %collective-permute-start.2 = (bf16[64,384]{1,0:T(8,128)(2,1)S(1)}, bf16[64,384]{1,0:T(8,128)(2,1)S(1)}, u32[]{:S(2)}, u32[]{:S(2)}) collective-permute-start(bf16[64,384]{1,0:T(8,128)(2,1)S(1)} %get-tuple-element.51), channel_id=1, source_target_pairs={{0,3},{1,2},{2,1},{3,0},{4,7},{5,6},{6,5},{7,4},{8,11},{9,10},{10,... | collective-permute-start | bytes 147464 | tf_op jit(solution)/shard_map/ppermute | solution.py:36
  6.1 5.1 %collective-permute-start.3 = (bf16[64,384]{1,0:T(8,128)(2,1)S(1)}, bf16[64,384]{1,0:T(8,128)(2,1)S(1)}, u32[]{:S(2)}, u32[]{:S(2)}) collective-permute-start(bf16[64,384]{1,0:T(8,128)(2,1)S(1)} %get-tuple-element.53), channel_id=1, source_target_pairs={{0,7},{1,6},{2,5},{3,4},{4,3},{5,2},{6,1},{7,0},{8,15},{9,14},{10,... | collective-permute-start | bytes 147464 | tf_op jit(solution)/shard_map/ppermute | solution.py:58
  7.1 4.1 %collective-permute-start = (bf16[2,64,384]{2,1,0:T(8,128)(2,1)S(1)}, bf16[2,64,384]{2,1,0:T(8,128)(2,1)S(1)}, u32[]{:S(2)}, u32[]{:S(2)}) collective-permute-start(bf16[2,64,384]{2,1,0:T(8,128)(2,1)S(1)} %get-tuple-element.49), channel_id=1, source_target_pairs={{0,4},{4,0},{1,5},{5,1},{2,6},{6,2},{3,7},{7,3},{8,12},{12,8},{9,1... | collective-permute-start | bytes 294920 | tf_op jit(solution)/shard_map/ppermute | solution.py:36
  7.9 13.1 %collective-permute-start.6 = (bf16[3,64,384]{2,1,0:T(8,128)(2,1)S(1)}, bf16[3,64,384]{2,1,0:T(8,128)(2,1)S(1)}, u32[]{:S(2)}, u32[]{:S(2)}) collective-permute-start(bf16[3,64,384]{2,1,0:T(8,128)(2,1)S(1)} %pad_maximum_fusion.refs_0_.refs_2_), channel_id=1, source_target_pairs={{0,1},{1,0},{2,3},{3,2},{8,16},{9,17},{10,18},{11,19},{16,8},{17,9... | collective-permute-start | bytes 442376 | tf_op jit(solution)/shard_map/ppermute | solution.py:48
  8.2 12.0 %collective-permute-start.4 = (bf16[3,64,384]{2,1,0:T(8,128)(2,1)S(1)}, bf16[3,64,384]{2,1,0:T(8,128)(2,1)S(1)}, u32[]{:S(2)}, u32[]{:S(2)}) collective-permute-start(bf16[3,64,384]{2,1,0:T(8,128)(2,1)S(1)} %pad_maximum_fusion.refs_0_.refs_2_), channel_id=1, source_target_pairs={{0,8},{1,9},{2,10},{3,11},{8,0},{9,1},{10,2},{11,3},{16,24},{17,25... | collective-permute-start | bytes 442376 | tf_op jit(solution)/shard_map/ppermute | solution.py:48
  11.2 9.8 %collective-permute-start.7 = (bf16[3,64,384]{2,1,0:T(8,128)(2,1)S(1)}, bf16[3,64,384]{2,1,0:T(8,128)(2,1)S(1)}, u32[]{:S(2)}, u32[]{:S(2)}) collective-permute-start(bf16[3,64,384]{2,1,0:T(8,128)(2,1)S(1)} %pad_maximum_fusion.1.refs_1_.refs_3_), channel_id=1, source_target_pairs={{0,1},{1,0},{2,3},{3,2},{8,16},{9,17},{10,18},{11,19},{16,8},{17,9... | collective-permute-start | bytes 442376 | tf_op jit(solution)/shard_map/ppermute | solution.py:48
  12.4 8.6 %collective-permute-start.5 = (bf16[3,64,384]{2,1,0:T(8,128)(2,1)S(1)}, bf16[3,64,384]{2,1,0:T(8,128)(2,1)S(1)}, u32[]{:S(2)}, u32[]{:S(2)}) collective-permute-start(bf16[3,64,384]{2,1,0:T(8,128)(2,1)S(1)} %pad_maximum_fusion.1.refs_1_.refs_3_), channel_id=1, source_target_pairs={{0,8},{1,9},{2,10},{3,11},{8,0},{9,1},{10,2},{11,3},{16,24},{17,25... | collective-permute-start | bytes 442376 | tf_op jit(solution)/shard_map/ppermute | solution.py:48
  13.6 3.8 %collective-permute-start.1 = (bf16[2,64,384]{2,1,0:T(8,128)(2,1)S(1)}, bf16[2,64,384]{2,1,0:T(8,128)(2,1)S(1)}, u32[]{:S(2)}, u32[]{:S(2)}) collective-permute-start(bf16[2,64,384]{2,1,0:T(8,128)(2,1)S(1)} %get-tuple-element.50), channel_id=1, source_target_pairs={{0,4},{4,0},{1,5},{5,1},{2,6},{6,2},{3,7},{7,3},{8,12},{12,8},{9,1... | collective-permute-start | bytes 294920 | tf_op jit(solution)/shard_map/ppermute | solution.py:36
  17.4 7.8 %collective-permute-start.12 = (bf16[4,64,384]{2,1,0:T(8,128)(2,1)S(1)}, bf16[4,64,384]{2,1,0:T(8,128)(2,1)S(1)}, u32[]{:S(2)}, u32[]{:S(2)}) collective-permute-start(bf16[4,64,384]{2,1,0:T(8,128)(2,1)S(1)} %constant_dynamic-update-slice_fusion.qg_ref), channel_id=1, source_target_pairs={{0,1},{1,0},{2,3},{3,2},{8,16},{9,17},{10,18},{11,19},{16,8},{17,9... | collective-permute-start | bytes 589832 | tf_op jit(solution)/shard_map/ppermute | solution.py:48
  20.3 6.5 %collective-permute-start.11 = (bf16[4,64,384]{2,1,0:T(8,128)(2,1)S(1)}, bf16[4,64,384]{2,1,0:T(8,128)(2,1)S(1)}, u32[]{:S(2)}, u32[]{:S(2)}) collective-permute-start(bf16[4,64,384]{2,1,0:T(8,128)(2,1)S(1)} %constant_dynamic-update-slice_fusion.qg_ref), channel_id=1, source_target_pairs={{0,8},{1,9},{2,10},{3,11},{8,0},{9,1},{10,2},{11,3},{16,24},{17,25... | collective-permute-start | bytes 589832 | tf_op jit(solution)/shard_map/ppermute | solution.py:48
  21.1 3.0 %collective-permute-start.8 = (bf16[6,64,384]{2,1,0:T(8,128)(2,1)S(1)}, bf16[6,64,384]{2,1,0:T(8,128)(2,1)S(1)}, u32[]{:S(2)}, u32[]{:S(2)}) collective-permute-start(bf16[6,64,384]{2,1,0:T(8,128)(2,1)S(1)} %slice_dynamic-update-slice_fusion), channel_id=1, source_target_pairs={{0,1},{1,0},{2,3},{3,2},{4,5},{5,4},{6,7},{7,6},{8,9},{9,8},{10,11... | collective-permute-start | bytes 884744 | tf_op jit(solution)/shard_map/ppermute | solution.py:36
  24.8 4.0 %collective-permute-start.10 = (f32[6,256]{1,0:T(8,128)S(1)}, f32[6,256]{1,0:T(8,128)S(1)}, u32[]{:S(2)}, u32[]{:S(2)}) collective-permute-start(f32[6,256]{1,0:T(8,128)S(1)} %get-tuple-element.58.stats_ref), channel_id=1, source_target_pairs={{0,1},{1,0},{2,3},{3,2},{8,16},{9,17},{10,18},{11,19},{16,8},{17,9... | collective-permute-start | bytes 18440 | tf_op jit(solution)/shard_map/ppermute | solution.py:48
  25.2 3.6 %collective-permute-start.9 = (f32[6,256]{1,0:T(8,128)S(1)}, f32[6,256]{1,0:T(8,128)S(1)}, u32[]{:S(2)}, u32[]{:S(2)}) collective-permute-start(f32[6,256]{1,0:T(8,128)S(1)} %get-tuple-element.58.stats_ref), channel_id=1, source_target_pairs={{0,8},{1,9},{2,10},{3,11},{8,0},{9,1},{10,2},{11,3},{16,24},{17,25... | collective-permute-start | bytes 18440 | tf_op jit(solution)/shard_map/ppermute | solution.py:48
  29.1 1.9 %collective-permute-start.13 = (bf16[2,64,384]{2,1,0:T(8,128)(2,1)S(1)}, bf16[2,64,384]{2,1,0:T(8,128)(2,1)S(1)}, u32[]{:S(2)}, u32[]{:S(2)}) collective-permute-start(bf16[2,64,384]{2,1,0:T(8,128)(2,1)S(1)} %cross_sibling.1), channel_id=1, source_target_pairs={{0,1},{1,0},{2,3},{3,2},{4,5},{5,4},{6,7},{7,6},{8,9},{9,8},{10,11... | collective-permute-start | bytes 294920 | tf_op jit(solution)/shard_map/ppermute | solution.py:36
  31.0 7.7 %collective-permute-start.14 = (bf16[3,64,384]{2,1,0:T(8,128)(2,1)S(1)}, bf16[3,64,384]{2,1,0:T(8,128)(2,1)S(1)}, u32[]{:S(2)}, u32[]{:S(2)}) collective-permute-start(bf16[3,64,384]{2,1,0:T(8,128)(2,1)S(1)} %get-tuple-element.78), channel_id=1, source_target_pairs={{0,4},{4,0},{1,5},{5,1},{2,6},{6,2},{3,7},{7,3},{8,12},{12,8},{9,1... | collective-permute-start | bytes 442376 | tf_op jit(solution)/shard_map/ppermute | solution.py:36
  32.1 4.3 %collective-permute-start.15 = (bf16[64,384]{1,0:T(8,128)(2,1)S(1)}, bf16[64,384]{1,0:T(8,128)(2,1)S(1)}, u32[]{:S(2)}, u32[]{:S(2)}) collective-permute-start(bf16[64,384]{1,0:T(8,128)(2,1)S(1)} %get-tuple-element.79), channel_id=1, source_target_pairs={{0,3},{1,2},{2,1},{3,0},{4,7},{5,6},{6,5},{7,4},{8,11},{9,10},{10,... | collective-permute-start | bytes 147464 | tf_op jit(solution)/shard_map/ppermute | solution.py:36
  33.7 4.9 %collective-permute-start.16 = (bf16[64,384]{1,0:T(8,128)(2,1)S(1)}, bf16[64,384]{1,0:T(8,128)(2,1)S(1)}, u32[]{:S(2)}, u32[]{:S(2)}) collective-permute-start(bf16[64,384]{1,0:T(8,128)(2,1)S(1)} %get-tuple-element.80), channel_id=1, source_target_pairs={{0,7},{1,6},{2,5},{3,4},{4,3},{5,2},{6,1},{7,0},{8,15},{9,14},{10,... | collective-permute-start | bytes 147464 | tf_op jit(solution)/shard_map/ppermute | solution.py:58

commit v3 on v2

--- a/solution.py
+++ b/solution.py
@@ -123,40 +123,22 @@
     x_ref[...] = x
 
 
-def project_kernel(
-    count_ref, scale_in, order_ref, x_ref, gain_ref, grad_ref, qkv_ref, out_weight_ref,
-    kv_own_ref, qg_own_ref, kv_other_ref, qg_other_ref, edge_ref, corner_ref,
-    raw_ref, inverse_ref, scale_ref,
+def key_value_kernel(
+    count_ref, x_ref, gain_ref, qkv_ref,
+    kv_own_ref, kv_other_ref, edge_ref, corner_ref, normed_ref, raw_ref, inverse_ref,
 ):
-    frames, lat_rows, lon_cols, width = grad_ref.shape
-    cells = frames * lat_rows * lon_cols
-    blocks = lon_cols // BLOCK
+    cells = x_ref.shape[0]
+    blocks = cells // CELLS
     parity = lax.rem(lax.axis_index("lon"), 2)
     upper = lax.rem(lax.axis_index("lat"), 2) == 1
-    all_scales = scale_in[...].reshape(1, HEADS) * (1.0 / math.sqrt(HEAD_DIM))
-    for h in range(HALF):
-        mine = jnp.where(
-            upper, all_scales[:, HALF + h : HALF + h + 1], all_scales[:, h : h + 1]
-        )
-        scale_ref[h : h + 1] = jnp.broadcast_to(mine, (1, 4 * CELLS))
+    normed = normalised(x_ref[...].astype(F32), gain_ref)
+    normed_ref[...] = normed
+    key, value = dot(normed, qkv_ref[1]), dot(normed, qkv_ref[2])
+    raw_ref[...] = key
+    inverse = lax.rsqrt(head_means(key * key) + EPS)
+    inverse_ref[...] = inverse
+    place = lax.broadcasted_iota(jnp.int32, (CELLS, 1), 0)
     counts = count_ref[0]
-    order = order_ref[...]
-    normed = normalised(x_ref[...].astype(F32), gain_ref)
-    query, key, value = (dot(normed, qkv_ref[c]) for c in range(3))
-    head_width = HEADS * HEAD_DIM
-    raw_ref[:, :head_width] = query
-    raw_ref[:, head_width:] = key
-    grad = dot_last(
-        grad_ref[...].astype(F32).reshape(cells, width).astype(BF16), out_weight_ref[...]
-    ).astype(BF16)
-    grad = dot(order, grad)
-    query_inverse = lax.rsqrt(head_means(query * query) + EPS)
-    key_inverse = lax.rsqrt(head_means(key * key) + EPS)
-    inverse_ref[:, :head_width] = query_inverse
-    inverse_ref[:, head_width:] = key_inverse
-    query = query * query_inverse
-    key = key * key_inverse
-    place = lax.broadcasted_iota(jnp.int32, (CELLS, 1), 0)
     live = []
     for slot in range(blocks):
         flip = blocks - 1 - slot
@@ -164,16 +146,42 @@
             place
             < jnp.where(parity == 1, counts[:, flip : flip + 1], counts[:, slot : slot + 1])
         )
-    key = jnp.where(jnp.concatenate(live, 0), key, DEAD_KEY)
+    key = jnp.where(jnp.concatenate(live, 0), key * inverse, DEAD_KEY)
     shape = (blocks, CELLS, PAIR_WIDTH)
     low, high = halves(key, value)
     kv_own_ref[...] = jnp.where(upper, high, low).astype(BF16).reshape(shape)
     kv_other_ref[...] = jnp.where(upper, low, high).astype(BF16).reshape(shape)
     edge_ref[...] = kv_own_ref[0]
     corner_ref[...] = kv_other_ref[0]
-    low, high = halves(query, grad)
+
+
+def query_grad_kernel(
+    scale_in, order_ref, normed_ref, grad_ref, qkv_ref, out_weight_ref,
+    qg_own_ref, qg_other_ref, raw_ref, inverse_ref, scale_ref,
+):
+    cells, width = normed_ref.shape
+    upper = lax.rem(lax.axis_index("lat"), 2) == 1
+    all_scales = scale_in[...].reshape(1, HEADS) * (1.0 / math.sqrt(HEAD_DIM))
+    for h in range(HALF):
+        mine = jnp.where(
+            upper, all_scales[:, HALF + h : HALF + h + 1], all_scales[:, h : h + 1]
+        )
+        scale_ref[h : h + 1] = jnp.broadcast_to(mine, (1, 4 * CELLS))
+    query = dot(normed_ref[...], qkv_ref[0])
+    raw_ref[...] = query
+    inverse = lax.rsqrt(head_means(query * query) + EPS)
+    inverse_ref[...] = inverse
+    grad = dot_last(
+        grad_ref[...].astype(F32).reshape(cells, width).astype(BF16), out_weight_ref[...]
+    ).astype(BF16)
+    low, high = halves(query * inverse, dot(order_ref[...], grad))
+    shape = (cells // CELLS, CELLS, PAIR_WIDTH)
     qg_own_ref[...] = jnp.where(upper, high, low).astype(BF16).reshape(shape)
     qg_other_ref[...] = jnp.where(upper, low, high).astype(BF16).reshape(shape)
+
+
+def join_kernel(kv_in, kv_ref):
+    kv_ref[...] = kv_in[...]
 
 
 def lane_tile(j):
@@ -540,7 +548,7 @@
 
 def finish_kernel(
     inner_ref, dq_ref, other_ref, edge_ref, corner_ref,
-    raw_ref, inverse_ref, x_ref, order_ref, gain_ref, qkv_ref, out_ref,
+    query_raw, query_inverse, key_raw, key_inverse, x_ref, order_ref, gain_ref, qkv_ref, out_ref,
 ):
     frames, lat_rows, lon_cols, width = out_ref.shape
     cells = frames * lat_rows * lon_cols
@@ -565,11 +573,9 @@
         joined(dkv_mine[:, :HALF_WIDTH], dkv_theirs[:, :HALF_WIDTH]),
         joined(dkv_mine[:, HALF_WIDTH:], dkv_theirs[:, HALF_WIDTH:]),
     ]
-    head_width = HEADS * HEAD_DIM
     grad_normed = dot_last(grads[2].astype(BF16), qkv_ref[2])
-    for c in range(2):
-        raw = raw_ref[:, c * head_width : (c + 1) * head_width]
-        inverse = inverse_ref[:, c * head_width : (c + 1) * head_width]
+    for c, (raw, inverse) in enumerate(((query_raw, query_inverse), (key_raw, key_inverse))):
+        raw, inverse = raw[...], inverse[...]
         inner = head_means(raw * grads[c])
         grad_raw = inverse * grads[c] - inverse * inverse * inverse * raw * inner
         grad_normed = grad_normed + dot_last(grad_raw.astype(BF16), qkv_ref[c])
@@ -617,22 +623,26 @@
         order_kernel, "order", [((cells, cells), BF16), ((cells, width), BF16)], [tokens],
         micros=10.0,
     )
-    kv_own, qg_own, kv_other, qg_other, edge, corner, raw, inverse, scales = kernel_call(
-        project_kernel, "project",
-        [qg_shape, qg_shape, qg_shape, qg_shape, edge_shape, edge_shape, ((cells, 2 * head_width), F32), ((cells, 2 * head_width), F32),
-         ((HALF, 4 * CELLS), F32)],
-        [key_count, logit_scale, order, x, norm_gain, grad_out, qkv_weight, out_weight],
-        micros=40.0,
+    projected = ((cells, head_width), F32)
+    kv_own, kv_other, edge, corner, normed, key_raw, key_inverse = kernel_call(
+        key_value_kernel, "key_value",
+        [qg_shape, qg_shape, edge_shape, edge_shape, ((cells, width), BF16), projected, projected],
+        [key_count, x, norm_gain, qkv_weight], micros=2.0,
     )
     edge = pair_swap(edge, "lon", 1)
     corner = corner_swap(corner)
     kv_other = pair_swap(kv_other, "lat", 0)
+    qg_own, qg_other, query_raw, query_inverse, scales = kernel_call(
+        query_grad_kernel, "query_grad",
+        [qg_shape, qg_shape, projected, projected, ((HALF, 4 * CELLS), F32)],
+        [logit_scale, order, normed, grad_out, qkv_weight, out_weight], micros=5.0,
+    )
+    qg_other = pair_swap(qg_other, "lat", 0)
+    (kv_other,) = kernel_call(join_kernel, "join", [qg_shape], [kv_other], micros=3.0)
     kv_rows = [
         jnp.concatenate([edge[None], kv_own], 0),
         jnp.concatenate([corner[None], kv_other], 0),
     ]
-    qg_other, kv_other = lax.optimization_barrier((qg_other, kv_other))
-    qg_other = pair_swap(qg_other, "lat", 0)
     upper = lax.rem(lax.axis_index("lat"), 2) == 1
     wide = lax.axis_size("lat") > 2
     if wide:
@@ -723,7 +733,8 @@
     other = pair_swap(to_lat, "lat", 0)
     (grad_tokens,) = kernel_call(
         finish_kernel, "finish", [(tokens.shape, BF16)],
-        [inner, dq_own, other, edge, corner, raw, inverse, x, order, norm_gain, qkv_weight],
+        [inner, dq_own, other, edge, corner, query_raw, query_inverse, key_raw, key_inverse,
+         x, order, norm_gain, qkv_weight],
         micros=2.0,
     )
     return grad_tokens

time: 40.8 us -> 38.7 us (0.949)
  waiting for transfers between devices: 9.78 us -> 6.12 us
  starting transfers between devices: 20.2 us -> 21.6 us
    ppermute x7, waiting for transfers between devices: 5.95 us -> 2.51 us  [pair_swap(): return lax.ppermute(array, axis, pairs)]
    ppermute x8, starting transfers between devices: 9.2 us -> 10.7 us  [frame_swap(): return lax.ppermute(array, ('tm', 'lon'), pairs)]
    ppermute x8, waiting for transfers between devices: 1.54 us -> 0.83 us  [frame_swap(): return lax.ppermute(array, ('tm', 'lon'), pairs)]
    ppermute x7, starting transfers between devices: 9.66 us -> 9.13 us  [pair_swap(): return lax.ppermute(array, axis, pairs)]
    ppermute x2, waiting for transfers between devices: 2.29 us -> 2.78 us  [corner_swap(): return lax.ppermute(array, ('lat', 'lon'), pairs)]
    ppermute x2, starting transfers between devices: 1.31 us -> 1.74 us  [corner_swap(): return lax.ppermute(array, ('lat', 'lon'), pairs)]
    pallas_call x11 -> x13, Pallas kernels: 8.48 us -> 8.78 us  [kernel_call(): pl.pallas_call(body, name=name, out_shape=[jax.ShapeDtypeStruct(shape, dt...]
  transfers between devices with their start and end apart: 17 -> 17, of which waited for: 7 -> 5; matrix products, arithmetic and copies ran while one was open for 0% -> 0% of each run, Pallas kernels for 12% -> 15%
where the time goes in v3:
time: 38.7 us; the launch traced here: 38.5 us
  starting transfers between devices  21.6 us (56%)
  Pallas kernels  8.78 us (23%)
  waiting for transfers between devices  6.12 us (16%)
  local copies, waits for them, and re-layouts  1.76 us (5%)
    ppermute x8, starting transfers between devices, frame_swap(): return lax.ppermute(array, ('tm', 'lon'), pairs)  10.7 us
    ppermute x7, starting transfers between devices, pair_swap(): return lax.ppermute(array, axis, pairs)  9.13 us
    pallas_call x13, Pallas kernels, kernel_call(): pl.pallas_call(body, name=name, out_shape=[jax.ShapeDtypeStruct(shape, dt...  8.78 us
    ppermute x2, waiting for transfers between devices, corner_swap(): return lax.ppermute(array, ('lat', 'lon'), pairs)  2.78 us
    ppermute x7, waiting for transfers between devices, pair_swap(): return lax.ppermute(array, axis, pairs)  2.51 us
    ppermute x2, starting transfers between devices, corner_swap(): return lax.ppermute(array, ('lat', 'lon'), pairs)  1.74 us
    unnamed x20, local copies, waits for them, and re-layouts  1.73 us
    ppermute x8, waiting for transfers between devices, frame_swap(): return lax.ppermute(array, ('tm', 'lon'), pairs)  0.83 us
  transfers between devices with their start and end apart: 17, of which 5 were waited for; matrix products, arithmetic and copies ran while one was open for 0% of the time, Pallas kernels for 15%

profile of v3, /device:TPU:1, one launch (start us, length us, event | category | flops | bytes accessed | tf_op | source)
XLA Modules:
  0.0 38.5 jit_solution(8244521714610145458)
XLA Ops:
  0.0 0.0 copy-start
  0.0 0.0 copy-start.2
  0.0 1.1 %copy-done.2 = bf16[4,4,8,768]{3,2,1,0:T(8,128)(2,1)S(1)} copy-done((bf16[4,4,8,768]{3,2,1,0:T(8,128)(2,1)S(1)}, bf16[4,4,8,768]{3,2,1,0:T(8,128)(2,1)}, u32[]{:S(2)}) %copy-start.2) | copy-done | bytes 196632
  1.1 0.0 copy-start.4
  1.1 0.0 copy-start.5
  1.1 0.2 order.1
  1.3 0.3 copy-done
  1.6 0.3 copy-done.4
  1.9 0.0 copy-done.5
  1.9 0.0 copy-start.1
  1.9 0.0 copy-start.3
  1.9 0.0 copy-start.6
  1.9 0.6 %key_value.1 = (bf16[2,64,384]{2,1,0:T(8,128)(2,1)S(1)}, bf16[2,64,384]{2,1,0:T(8,128)(2,1)S(1)}, bf16[64,384]{1,0:T(8,128)(2,1)S(1)}, bf16[64,384]{1,0:T(8,128)...) custom-call(s32[1,1,2]{2,1,0:T(1,128)S(1)} %copy-done.5, ...), custom_call_target="tpu_custom_call" | custom-call | flops 2000000000 | tf_op jit(solution)/shard_map/key_value/pallas_call | solution.py:598
  2.5 2.7 %collective-permute-start.1 = (bf16[64,384]{1,0:T(8,128)(2,1)S(1)}, bf16[64,384]{1,0:T(8,128)(2,1)S(1)}, u32[]{:S(2)}, u32[]{:S(2)}) collective-permute-start(bf16[64,384]{1,0:T(8,128)(2,1)S(1)} %get-tuple-element.52), channel_id=1, source_target_pairs={{0,3},{1,2},{2,1},{3,0},{4,7},{5,6},{6,5},{7,4},{8,11},{9,10},{10,... | collective-permute-start | bytes 147464 | tf_op jit(solution)/shard_map/ppermute | solution.py:36
  5.2 1.0 %collective-permute-start.2 = (bf16[64,384]{1,0:T(8,128)(2,1)S(1)}, bf16[64,384]{1,0:T(8,128)(2,1)S(1)}, u32[]{:S(2)}, u32[]{:S(2)}) collective-permute-start(bf16[64,384]{1,0:T(8,128)(2,1)S(1)} %get-tuple-element.54), channel_id=1, source_target_pairs={{0,7},{1,6},{2,5},{3,4},{4,3},{5,2},{6,1},{7,0},{8,15},{9,14},{10,... | collective-permute-start | bytes 147464 | tf_op jit(solution)/shard_map/ppermute | solution.py:58
  6.2 0.3 collective-permute-start.3
  6.5 0.0 copy-done.1
  6.5 0.0 copy-done.3
  6.5 0.0 copy-done.6
  6.5 0.8 %query_grad.1 = (bf16[2,64,384]{2,1,0:T(8,128)(2,1)S(1)}, bf16[2,64,384]{2,1,0:T(8,128)(2,1)S(1)}, f32[128,384]{1,0:T(8,128)S(1)}, f32[128,384]{1,0:T(8,128)S(1)}, f32[3,256]{1,0:T(4,128)S(1)}) custom-call(f32[6]{0:T(128)S(1)} %copy-done.6, bf16[128,128]{1,0:T(8,128)(2,1)S(1)} %get-tuple-element.46.order_ref, ...), custom_call_target="tpu_custom_call" | custom-call | flops 5000000000 | tf_op jit(solution)/shard_map/query_grad/pallas_call | solution.py:598
  7.3 1.3 %collective-permute-start = (bf16[2,64,384]{2,1,0:T(8,128)(2,1)S(1)}, bf16[2,64,384]{2,1,0:T(8,128)(2,1)S(1)}, u32[]{:S(2)}, u32[]{:S(2)}) collective-permute-start(bf16[2,64,384]{2,1,0:T(8,128)(2,1)S(1)} %get-tuple-element.51), channel_id=1, source_target_pairs={{0,4},{4,0},{1,5},{5,1},{2,6},{6,2},{3,7},{7,3},{8,12},{12,8},{9,1... | collective-permute-start | bytes 294920 | tf_op jit(solution)/shard_map/ppermute | solution.py:36
  8.6 0.0 collective-permute-done.1
  8.7 1.2 %collective-permute-start.6 = (bf16[3,64,384]{2,1,0:T(8,128)(2,1)S(1)}, bf16[3,64,384]{2,1,0:T(8,128)(2,1)S(1)}, u32[]{:S(2)}, u32[]{:S(2)}) collective-permute-start(bf16[3,64,384]{2,1,0:T(8,128)(2,1)S(1)} %pad_maximum_fusion.refs_0_.refs_2_), channel_id=1, source_target_pairs={{0,1},{1,0},{2,3},{3,2},{8,16},{9,17},{10,18},{11,19},{16,8},{17,9... | collective-permute-start | bytes 442376 | tf_op jit(solution)/shard_map/ppermute | solution.py:48
  9.8 1.5 %collective-permute-start.4 = (bf16[3,64,384]{2,1,0:T(8,128)(2,1)S(1)}, bf16[3,64,384]{2,1,0:T(8,128)(2,1)S(1)}, u32[]{:S(2)}, u32[]{:S(2)}) collective-permute-start(bf16[3,64,384]{2,1,0:T(8,128)(2,1)S(1)} %pad_maximum_fusion.refs_0_.refs_2_), channel_id=1, source_target_pairs={{0,8},{1,9},{2,10},{3,11},{8,0},{9,1},{10,2},{11,3},{16,24},{17,25... | collective-permute-start | bytes 442376 | tf_op jit(solution)/shard_map/ppermute | solution.py:48
  11.3 0.0 collective-permute-done.3.kv_in
  11.3 0.0 collective-permute-done.2
  11.4 1.7 %collective-permute-start.7 = (bf16[3,64,384]{2,1,0:T(8,128)(2,1)S(1)}, bf16[3,64,384]{2,1,0:T(8,128)(2,1)S(1)}, u32[]{:S(2)}, u32[]{:S(2)}) collective-permute-start(bf16[3,64,384]{2,1,0:T(8,128)(2,1)S(1)} %pad_maximum_fusion.1.refs_1_.refs_3_), channel_id=1, source_target_pairs={{0,1},{1,0},{2,3},{3,2},{8,16},{9,17},{10,18},{11,19},{16,8},{17,9... | collective-permute-start | bytes 442376 | tf_op jit(solution)/shard_map/ppermute | solution.py:48
  13.1 0.8 %collective-permute-start.5 = (bf16[3,64,384]{2,1,0:T(8,128)(2,1)S(1)}, bf16[3,64,384]{2,1,0:T(8,128)(2,1)S(1)}, u32[]{:S(2)}, u32[]{:S(2)}) collective-permute-start(bf16[3,64,384]{2,1,0:T(8,128)(2,1)S(1)} %pad_maximum_fusion.1.refs_1_.refs_3_), channel_id=1, source_target_pairs={{0,8},{1,9},{2,10},{3,11},{8,0},{9,1},{10,2},{11,3},{16,24},{17,25... | collective-permute-start | bytes 442376 | tf_op jit(solution)/shard_map/ppermute | solution.py:48
  13.9 0.0 collective-permute-done
  13.9 1.9 %collective-permute-start.12 = (bf16[4,64,384]{2,1,0:T(8,128)(2,1)S(1)}, bf16[4,64,384]{2,1,0:T(8,128)(2,1)S(1)}, u32[]{:S(2)}, u32[]{:S(2)}) collective-permute-start(bf16[4,64,384]{2,1,0:T(8,128)(2,1)S(1)} %constant_dynamic-update-slice_fusion.qg_ref), channel_id=1, source_target_pairs={{0,1},{1,0},{2,3},{3,2},{8,16},{9,17},{10,18},{11,19},{16,8},{17,9... | collective-permute-start | bytes 589832 | tf_op jit(solution)/shard_map/ppermute | solution.py:48
  15.8 0.5 %own_score.1 = (bf16[6,128,256]{2,1,0:T(8,128)(2,1)S(1)}, bf16[6,256,128]{2,1,0:T(8,128)(2,1)S(1)}, f32[6,8,256]{2,1,0:T(8,128)S(1)}, f32[3,256,256]{2,1,0:T(8,1...) custom-call(f32[3,256]{1,0:T(4,128)S(1)} %get-tuple-element.49.scale_ref, ...), custom_call_target="tpu_custom_call" | custom-call | flops 1500000000 | tf_op jit(solution)/shard_map/own_score/pallas_call | solution.py:598
  16.3 0.0 collective-permute-done.4.refs_0_.refs_2_
  16.3 0.8 %collective-permute-start.11 = (bf16[4,64,384]{2,1,0:T(8,128)(2,1)S(1)}, bf16[4,64,384]{2,1,0:T(8,128)(2,1)S(1)}, u32[]{:S(2)}, u32[]{:S(2)}) collective-permute-start(bf16[4,64,384]{2,1,0:T(8,128)(2,1)S(1)} %constant_dynamic-update-slice_fusion.qg_ref), channel_id=1, source_target_pairs={{0,8},{1,9},{2,10},{3,11},{8,0},{9,1},{10,2},{11,3},{16,24},{17,25... | collective-permute-start | bytes 589832 | tf_op jit(solution)/shard_map/ppermute | solution.py:48
  17.2 0.8 %collective-permute-done.5.refs_1_.refs_3_ = bf16[3,64,384]{2,1,0:T(8,128)(2,1)S(1)} collective-permute-done((bf16[3,64,384]{2,1,0:T(8,128)(2,1)S(1)}, bf16[3,64,384]{2,1,0:T(8,128)(2,1)S(1)}, u32[]{:S(2)}, u32[]{:S(2)}) %collective-permute-start.5) | collective-permute-done | bytes 147488 | tf_op jit(solution)/shard_map/ppermute | solution.py:48
  18.0 0.0 collective-permute-done.6.refs_2_.refs_4_
  18.0 0.0 collective-permute-done.7.refs_3_.refs_5_
  18.0 1.6 %collective-permute-start.8 = (bf16[6,64,384]{2,1,0:T(8,128)(2,1)S(1)}, bf16[6,64,384]{2,1,0:T(8,128)(2,1)S(1)}, u32[]{:S(2)}, u32[]{:S(2)}) collective-permute-start(bf16[6,64,384]{2,1,0:T(8,128)(2,1)S(1)} %slice_dynamic-update-slice_fusion), channel_id=1, source_target_pairs={{0,1},{1,0},{2,3},{3,2},{4,5},{5,4},{6,7},{7,6},{8,9},{9,8},{10,11... | collective-permute-start | bytes 884744 | tf_op jit(solution)/shard_map/ppermute | solution.py:36
  19.6 0.7 %away_score.1 = (f32[6,8,256]{2,1,0:T(8,128)S(1)}, f32[3,512,256]{2,1,0:T(8,128)S(1)}, f32[3,512,256]{2,1,0:T(8,128)S(1)}, f32[3,256,128]{2,1,0:T(8,128)S(1)}, f32[3,256,128]{2,1,0:T(8,128)S(1)}) custom-call(f32[3,256]{1,0:T(4,128)S(1)} %get-tuple-element.49.scale_ref, bf16[6,128,256]{2,1,0:T(8,128)(2,1)S(1)} %get-tuple-element.56.weights, ...), custom_call_target="tpu_custom_call" | custom-call | flops 20000000000 | tf_op jit(solution)/shard_map/away_score/pallas_call | solution.py:598
  20.3 0.5 %collective-permute-done.8.keys_ref.refs_4_ = bf16[6,64,384]{2,1,0:T(8,128)(2,1)S(1)} collective-permute-done((bf16[6,64,384]{2,1,0:T(8,128)(2,1)S(1)}, bf16[6,64,384]{2,1,0:T(8,128)(2,1)S(1)}, u32[]{:S(2)}, u32[]{:S(2)}) %collective-permute-start.8) | collective-permute-done | bytes 294944 | tf_op jit(solution)/shard_map/ppermute | solution.py:36
  20.8 0.7 %sibling.1 = (f32[2,64,384]{2,1,0:T(8,128)S(1)}, f32[6,256]{1,0:T(8,128)S(1)}, f32[192,128]{1,0:T(8,128)S(1)}) custom-call(f32[3,256]{1,0:T(4,128)S(1)} %get-tuple-element.49.scale_ref, bf16[6,128,256]{2,1,0:T(8,128)(2,1)S(1)} %get-tuple-element.56.weights, bf16[6,256,128]{2,1,0:T(8,128)(2,1)S(1)} %get-tuple-element.57.backward, ...), custom_call_target="tpu_custom_call" | custom-call | flops 1500000000 | tf_op jit(solution)/shard_map/sibling/pallas_call | solution.py:598
  21.5 0.4 %collective-permute-start.10 = (f32[6,256]{1,0:T(8,128)S(1)}, f32[6,256]{1,0:T(8,128)S(1)}, u32[]{:S(2)}, u32[]{:S(2)}) collective-permute-start(f32[6,256]{1,0:T(8,128)S(1)} %get-tuple-element.60.stats_ref), channel_id=1, source_target_pairs={{0,1},{1,0},{2,3},{3,2},{8,16},{9,17},{10,18},{11,19},{16,8},{17,9... | collective-permute-start | bytes 18440 | tf_op jit(solution)/shard_map/ppermute | solution.py:48
  22.0 2.4 %collective-permute-start.9 = (f32[6,256]{1,0:T(8,128)S(1)}, f32[6,256]{1,0:T(8,128)S(1)}, u32[]{:S(2)}, u32[]{:S(2)}) collective-permute-start(f32[6,256]{1,0:T(8,128)S(1)} %get-tuple-element.60.stats_ref), channel_id=1, source_target_pairs={{0,8},{1,9},{2,10},{3,11},{8,0},{9,1},{10,2},{11,3},{16,24},{17,25... | collective-permute-start | bytes 18440 | tf_op jit(solution)/shard_map/ppermute | solution.py:48
  24.4 0.0 collective-permute-done.12.refs_1_
  24.4 0.0 collective-permute-done.11.refs_0_
  24.4 0.9 %cross_score.1 = (bf16[2,6,256,128]{3,2,1,0:T(8,128)(2,1)S(1)}, f32[2,3,256,256]{3,2,1,0:T(8,128)S(1)}, f32[2,3,256,256]{3,2,1,0:T(8,128)S(1)}, f32[2,2,3,128,12...) custom-call(f32[3,256]{1,0:T(4,128)S(1)} %get-tuple-element.49.scale_ref, ...), custom_call_target="tpu_custom_call" | custom-call | flops 2000000000 | tf_op jit(solution)/shard_map/cross_score/pallas_call | solution.py:598
  25.3 1.2 %own_back.1 = (f32[2,3,64,384]{3,2,1,0:T(8,128)S(1)}, f32[64,384]{1,0:T(8,128)S(1)}, bf16[64,384]{1,0:T(8,128)(2,1)S(1)}) custom-call(f32[3,256]{1,0:T(4,128)S(1)} %get-tuple-element.49.scale_ref, f32[6,256]{1,0:T(8,128)S(1)} %get-tuple-element.60.stats_ref, bf16[6,256,128]{2,1,0:T(8,128)(2,1)S(1)} %get-tuple-element.57.backward, ...), custom_call_target="tpu_custom_call" | custom-call | flops 2000000000 | tf_op jit(solution)/shard_map/own_back/pallas_call | solution.py:598
  26.5 0.0 collective-permute-done.10.far_stats
  26.5 0.0 collective-permute-done.9.near_stats
  26.5 0.3 cross_sibling.1
  26.8 1.0 %collective-permute-start.13 = (bf16[2,64,384]{2,1,0:T(8,128)(2,1)S(1)}, bf16[2,64,384]{2,1,0:T(8,128)(2,1)S(1)}, u32[]{:S(2)}, u32[]{:S(2)}) collective-permute-start(bf16[2,64,384]{2,1,0:T(8,128)(2,1)S(1)} %cross_sibling.1), channel_id=1, source_target_pairs={{0,1},{1,0},{2,3},{3,2},{4,5},{5,4},{6,7},{7,6},{8,9},{9,8},{10,11... | collective-permute-start | bytes 294920 | tf_op jit(solution)/shard_map/ppermute | solution.py:36
  27.8 0.8 %cross_back.1.total_ref = f32[2,3,64,384]{3,2,1,0:T(8,128)S(1)} custom-call(f32[3,256]{1,0:T(4,128)S(1)} %get-tuple-element.49.scale_ref, f32[6,256]{1,0:T(8,128)S(1)} %collective-permute-done.9.near_stats, f32[6,256]{1,0:T(8,128)S(1)} %collective-permute-done.10.far_stats, bf16[2,6,256,128]{3,2,1,0:T(8,128)(2,1)S(1)} %get-tuple-element.61.backward, ...), custom_call_target="tpu_custom_call" | custom-call | flops 1500000000 | tf_op jit(solution)/shard_map/cross_back/pallas_call | solution.py:598
  28.6 0.1 collective-permute-done.13.sibling_ref
  28.8 0.6 %collective-permute-start.14 = (bf16[3,64,384]{2,1,0:T(8,128)(2,1)S(1)}, bf16[3,64,384]{2,1,0:T(8,128)(2,1)S(1)}, u32[]{:S(2)}, u32[]{:S(2)}) collective-permute-start(bf16[3,64,384]{2,1,0:T(8,128)(2,1)S(1)} %get-tuple-element.80), channel_id=1, source_target_pairs={{0,4},{4,0},{1,5},{5,1},{2,6},{6,2},{3,7},{7,3},{8,12},{12,8},{9,1... | collective-permute-start | bytes 442376 | tf_op jit(solution)/shard_map/ppermute | solution.py:36
  29.4 1.7 %collective-permute-start.15 = (bf16[64,384]{1,0:T(8,128)(2,1)S(1)}, bf16[64,384]{1,0:T(8,128)(2,1)S(1)}, u32[]{:S(2)}, u32[]{:S(2)}) collective-permute-start(bf16[64,384]{1,0:T(8,128)(2,1)S(1)} %get-tuple-element.81), channel_id=1, source_target_pairs={{0,3},{1,2},{2,1},{3,0},{4,7},{5,6},{6,5},{7,4},{8,11},{9,10},{10,... | collective-permute-start | bytes 147464 | tf_op jit(solution)/shard_map/ppermute | solution.py:36
  31.1 0.7 %collective-permute-start.16 = (bf16[64,384]{1,0:T(8,128)(2,1)S(1)}, bf16[64,384]{1,0:T(8,128)(2,1)S(1)}, u32[]{:S(2)}, u32[]{:S(2)}) collective-permute-start(bf16[64,384]{1,0:T(8,128)(2,1)S(1)} %get-tuple-element.82), channel_id=1, source_target_pairs={{0,7},{1,6},{2,5},{3,4},{4,3},{5,2},{6,1},{7,0},{8,15},{9,14},{10,... | collective-permute-start | bytes 147464 | tf_op jit(solution)/shard_map/ppermute | solution.py:58
  31.8 1.9 %collective-permute-done.15.edge_ref = bf16[64,384]{1,0:T(8,128)(2,1)S(1)} collective-permute-done((bf16[64,384]{1,0:T(8,128)(2,1)S(1)}, bf16[64,384]{1,0:T(8,128)(2,1)S(1)}, u32[]{:S(2)}, u32[]{:S(2)}) %collective-permute-start.15) | collective-permute-done | bytes 49184 | tf_op jit(solution)/shard_map/ppermute | solution.py:36
  33.7 2.8 %collective-permute-done.16.corner_ref = bf16[64,384]{1,0:T(8,128)(2,1)S(1)} collective-permute-done((bf16[64,384]{1,0:T(8,128)(2,1)S(1)}, bf16[64,384]{1,0:T(8,128)(2,1)S(1)}, u32[]{:S(2)}, u32[]{:S(2)}) %collective-permute-start.16) | collective-permute-done | bytes 49184 | tf_op jit(solution)/shard_map/ppermute | solution.py:58
  36.4 0.0 collective-permute-done.14.other_ref
  36.4 2.1 %finish.1 = bf16[4,4,8,768]{3,2,1,0:T(8,128)(2,1)} custom-call(f32[2,64,384]{2,1,0:T(8,128)S(1)} %get-tuple-element.78.inner_ref, f32[64,384]{1,0:T(8,128)S(1)} %get-tuple-element.79.dq_ref, bf16[3,64,384]{2,1,0:T(8,128)(2,1)S(1)} %collective-permute-done.14.other_ref, bf16[64,384]{1,0:T(8,128)(2,1)S(1)} %collective-permute-done.15.edge_ref, ...), custom_call_target="tpu_custom_call" | custom-call | flops 2000000000 | tf_op jit(solution)/shard_map/finish/pallas_call | solution.py:598
  (12 shorter events, 0.2 us)
Async XLA Ops:
  0.0 1.6 %copy-start = (bf16[3,768,384]{2,1,0:T(8,128)(2,1)S(1)}, bf16[3,768,384]{2,1,0:T(8,128)(2,1)}, u32[]{:S(2)}) copy-start(bf16[3,768,384]{2,1,0:T(8,128)(2,1)} %qkv_ref.5) | copy-start | bytes 5308420
  0.0 1.1 %copy-start.2 = (bf16[4,4,8,768]{3,2,1,0:T(8,128)(2,1)S(1)}, bf16[4,4,8,768]{3,2,1,0:T(8,128)(2,1)}, u32[]{:S(2)}) copy-start(bf16[4,4,8,768]{3,2,1,0:T(8,128)(2,1)} %tokens_ref.1) | copy-start | bytes 589828
  1.1 0.8 %copy-start.4 = (f32[768]{0:T(1024)S(1)}, f32[768]{0:T(1024)}, u32[]{:S(2)}) copy-start(f32[768]{0:T(1024)} %gain_ref.3) | copy-start | bytes 9220
  1.1 0.8 %copy-start.5 = (s32[1,1,2]{2,1,0:T(1,128)S(1)}, s32[1,1,2]{2,1,0:T(1,128)}, u32[]{:S(2)}) copy-start(s32[1,1,2]{2,1,0:T(1,128)} %count_ref.1) | copy-start | bytes 28
  1.9 4.6 %copy-start.1 = (bf16[384,768]{1,0:T(8,128)(2,1)S(1)}, bf16[384,768]{1,0:T(8,128)(2,1)}, u32[]{:S(2)}) copy-start(bf16[384,768]{1,0:T(8,128)(2,1)} %out_weight_ref.1) | copy-start | bytes 1769476
  1.9 4.6 %copy-start.3 = (bf16[4,4,8,768]{3,2,1,0:T(8,128)(2,1)S(1)}, bf16[4,4,8,768]{3,2,1,0:T(8,128)(2,1)}, u32[]{:S(2)}) copy-start(bf16[4,4,8,768]{3,2,1,0:T(8,128)(2,1)} %grad_ref.1) | copy-start | bytes 589828
  1.9 4.6 %copy-start.6 = (f32[6]{0:T(128)S(1)}, f32[6]{0:T(128)}, u32[]{:S(2)}) copy-start(f32[6]{0:T(128)} %scale_in.1) | copy-start | bytes 76
  2.5 6.1 %collective-permute-start.1 = (bf16[64,384]{1,0:T(8,128)(2,1)S(1)}, bf16[64,384]{1,0:T(8,128)(2,1)S(1)}, u32[]{:S(2)}, u32[]{:S(2)}) collective-permute-start(bf16[64,384]{1,0:T(8,128)(2,1)S(1)} %get-tuple-element.52), channel_id=1, source_target_pairs={{0,3},{1,2},{2,1},{3,0},{4,7},{5,6},{6,5},{7,4},{8,11},{9,10},{10,... | collective-permute-start | bytes 147464 | tf_op jit(solution)/shard_map/ppermute | solution.py:36
  5.2 6.1 %collective-permute-start.2 = (bf16[64,384]{1,0:T(8,128)(2,1)S(1)}, bf16[64,384]{1,0:T(8,128)(2,1)S(1)}, u32[]{:S(2)}, u32[]{:S(2)}) collective-permute-start(bf16[64,384]{1,0:T(8,128)(2,1)S(1)} %get-tuple-element.54), channel_id=1, source_target_pairs={{0,7},{1,6},{2,5},{3,4},{4,3},{5,2},{6,1},{7,0},{8,15},{9,14},{10,... | collective-permute-start | bytes 147464 | tf_op jit(solution)/shard_map/ppermute | solution.py:58
  6.2 5.1 %collective-permute-start.3 = (bf16[2,64,384]{2,1,0:T(8,128)(2,1)S(1)}, bf16[2,64,384]{2,1,0:T(8,128)(2,1)S(1)}, u32[]{:S(2)}, u32[]{:S(2)}) collective-permute-start(bf16[2,64,384]{2,1,0:T(8,128)(2,1)S(1)} %get-tuple-element.55), channel_id=1, source_target_pairs={{0,4},{4,0},{1,5},{5,1},{2,6},{6,2},{3,7},{7,3},{8,12},{12,8},{9,1... | collective-permute-start | bytes 294920 | tf_op jit(solution)/shard_map/ppermute | solution.py:36
  7.3 6.5 %collective-permute-start = (bf16[2,64,384]{2,1,0:T(8,128)(2,1)S(1)}, bf16[2,64,384]{2,1,0:T(8,128)(2,1)S(1)}, u32[]{:S(2)}, u32[]{:S(2)}) collective-permute-start(bf16[2,64,384]{2,1,0:T(8,128)(2,1)S(1)} %get-tuple-element.51), channel_id=1, source_target_pairs={{0,4},{4,0},{1,5},{5,1},{2,6},{6,2},{3,7},{7,3},{8,12},{12,8},{9,1... | collective-permute-start | bytes 294920 | tf_op jit(solution)/shard_map/ppermute | solution.py:36
  8.7 9.3 %collective-permute-start.6 = (bf16[3,64,384]{2,1,0:T(8,128)(2,1)S(1)}, bf16[3,64,384]{2,1,0:T(8,128)(2,1)S(1)}, u32[]{:S(2)}, u32[]{:S(2)}) collective-permute-start(bf16[3,64,384]{2,1,0:T(8,128)(2,1)S(1)} %pad_maximum_fusion.refs_0_.refs_2_), channel_id=1, source_target_pairs={{0,1},{1,0},{2,3},{3,2},{8,16},{9,17},{10,18},{11,19},{16,8},{17,9... | collective-permute-start | bytes 442376 | tf_op jit(solution)/shard_map/ppermute | solution.py:48
  9.8 6.5 %collective-permute-start.4 = (bf16[3,64,384]{2,1,0:T(8,128)(2,1)S(1)}, bf16[3,64,384]{2,1,0:T(8,128)(2,1)S(1)}, u32[]{:S(2)}, u32[]{:S(2)}) collective-permute-start(bf16[3,64,384]{2,1,0:T(8,128)(2,1)S(1)} %pad_maximum_fusion.refs_0_.refs_2_), channel_id=1, source_target_pairs={{0,8},{1,9},{2,10},{3,11},{8,0},{9,1},{10,2},{11,3},{16,24},{17,25... | collective-permute-start | bytes 442376 | tf_op jit(solution)/shard_map/ppermute | solution.py:48
  11.4 6.6 %collective-permute-start.7 = (bf16[3,64,384]{2,1,0:T(8,128)(2,1)S(1)}, bf16[3,64,384]{2,1,0:T(8,128)(2,1)S(1)}, u32[]{:S(2)}, u32[]{:S(2)}) collective-permute-start(bf16[3,64,384]{2,1,0:T(8,128)(2,1)S(1)} %pad_maximum_fusion.1.refs_1_.refs_3_), channel_id=1, source_target_pairs={{0,1},{1,0},{2,3},{3,2},{8,16},{9,17},{10,18},{11,19},{16,8},{17,9... | collective-permute-start | bytes 442376 | tf_op jit(solution)/shard_map/ppermute | solution.py:48
  13.1 4.9 %collective-permute-start.5 = (bf16[3,64,384]{2,1,0:T(8,128)(2,1)S(1)}, bf16[3,64,384]{2,1,0:T(8,128)(2,1)S(1)}, u32[]{:S(2)}, u32[]{:S(2)}) collective-permute-start(bf16[3,64,384]{2,1,0:T(8,128)(2,1)S(1)} %pad_maximum_fusion.1.refs_1_.refs_3_), channel_id=1, source_target_pairs={{0,8},{1,9},{2,10},{3,11},{8,0},{9,1},{10,2},{11,3},{16,24},{17,25... | collective-permute-start | bytes 442376 | tf_op jit(solution)/shard_map/ppermute | solution.py:48
  13.9 10.5 %collective-permute-start.12 = (bf16[4,64,384]{2,1,0:T(8,128)(2,1)S(1)}, bf16[4,64,384]{2,1,0:T(8,128)(2,1)S(1)}, u32[]{:S(2)}, u32[]{:S(2)}) collective-permute-start(bf16[4,64,384]{2,1,0:T(8,128)(2,1)S(1)} %constant_dynamic-update-slice_fusion.qg_ref), channel_id=1, source_target_pairs={{0,1},{1,0},{2,3},{3,2},{8,16},{9,17},{10,18},{11,19},{16,8},{17,9... | collective-permute-start | bytes 589832 | tf_op jit(solution)/shard_map/ppermute | solution.py:48
  16.3 8.1 %collective-permute-start.11 = (bf16[4,64,384]{2,1,0:T(8,128)(2,1)S(1)}, bf16[4,64,384]{2,1,0:T(8,128)(2,1)S(1)}, u32[]{:S(2)}, u32[]{:S(2)}) collective-permute-start(bf16[4,64,384]{2,1,0:T(8,128)(2,1)S(1)} %constant_dynamic-update-slice_fusion.qg_ref), channel_id=1, source_target_pairs={{0,8},{1,9},{2,10},{3,11},{8,0},{9,1},{10,2},{11,3},{16,24},{17,25... | collective-permute-start | bytes 589832 | tf_op jit(solution)/shard_map/ppermute | solution.py:48
  18.0 2.8 %collective-permute-start.8 = (bf16[6,64,384]{2,1,0:T(8,128)(2,1)S(1)}, bf16[6,64,384]{2,1,0:T(8,128)(2,1)S(1)}, u32[]{:S(2)}, u32[]{:S(2)}) collective-permute-start(bf16[6,64,384]{2,1,0:T(8,128)(2,1)S(1)} %slice_dynamic-update-slice_fusion), channel_id=1, source_target_pairs={{0,1},{1,0},{2,3},{3,2},{4,5},{5,4},{6,7},{7,6},{8,9},{9,8},{10,11... | collective-permute-start | bytes 884744 | tf_op jit(solution)/shard_map/ppermute | solution.py:36
  21.5 4.9 %collective-permute-start.10 = (f32[6,256]{1,0:T(8,128)S(1)}, f32[6,256]{1,0:T(8,128)S(1)}, u32[]{:S(2)}, u32[]{:S(2)}) collective-permute-start(f32[6,256]{1,0:T(8,128)S(1)} %get-tuple-element.60.stats_ref), channel_id=1, source_target_pairs={{0,1},{1,0},{2,3},{3,2},{8,16},{9,17},{10,18},{11,19},{16,8},{17,9... | collective-permute-start | bytes 18440 | tf_op jit(solution)/shard_map/ppermute | solution.py:48
  22.0 4.5 %collective-permute-start.9 = (f32[6,256]{1,0:T(8,128)S(1)}, f32[6,256]{1,0:T(8,128)S(1)}, u32[]{:S(2)}, u32[]{:S(2)}) collective-permute-start(f32[6,256]{1,0:T(8,128)S(1)} %get-tuple-element.60.stats_ref), channel_id=1, source_target_pairs={{0,8},{1,9},{2,10},{3,11},{8,0},{9,1},{10,2},{11,3},{16,24},{17,25... | collective-permute-start | bytes 18440 | tf_op jit(solution)/shard_map/ppermute | solution.py:48
  26.8 1.9 %collective-permute-start.13 = (bf16[2,64,384]{2,1,0:T(8,128)(2,1)S(1)}, bf16[2,64,384]{2,1,0:T(8,128)(2,1)S(1)}, u32[]{:S(2)}, u32[]{:S(2)}) collective-permute-start(bf16[2,64,384]{2,1,0:T(8,128)(2,1)S(1)} %cross_sibling.1), channel_id=1, source_target_pairs={{0,1},{1,0},{2,3},{3,2},{4,5},{5,4},{6,7},{7,6},{8,9},{9,8},{10,11... | collective-permute-start | bytes 294920 | tf_op jit(solution)/shard_map/ppermute | solution.py:36
  28.8 7.7 %collective-permute-start.14 = (bf16[3,64,384]{2,1,0:T(8,128)(2,1)S(1)}, bf16[3,64,384]{2,1,0:T(8,128)(2,1)S(1)}, u32[]{:S(2)}, u32[]{:S(2)}) collective-permute-start(bf16[3,64,384]{2,1,0:T(8,128)(2,1)S(1)} %get-tuple-element.80), channel_id=1, source_target_pairs={{0,4},{4,0},{1,5},{5,1},{2,6},{6,2},{3,7},{7,3},{8,12},{12,8},{9,1... | collective-permute-start | bytes 442376 | tf_op jit(solution)/shard_map/ppermute | solution.py:36
  29.4 4.3 %collective-permute-start.15 = (bf16[64,384]{1,0:T(8,128)(2,1)S(1)}, bf16[64,384]{1,0:T(8,128)(2,1)S(1)}, u32[]{:S(2)}, u32[]{:S(2)}) collective-permute-start(bf16[64,384]{1,0:T(8,128)(2,1)S(1)} %get-tuple-element.81), channel_id=1, source_target_pairs={{0,3},{1,2},{2,1},{3,0},{4,7},{5,6},{6,5},{7,4},{8,11},{9,10},{10,... | collective-permute-start | bytes 147464 | tf_op jit(solution)/shard_map/ppermute | solution.py:36
  31.1 5.4 %collective-permute-start.16 = (bf16[64,384]{1,0:T(8,128)(2,1)S(1)}, bf16[64,384]{1,0:T(8,128)(2,1)S(1)}, u32[]{:S(2)}, u32[]{:S(2)}) collective-permute-start(bf16[64,384]{1,0:T(8,128)(2,1)S(1)} %get-tuple-element.82), channel_id=1, source_target_pairs={{0,7},{1,6},{2,5},{3,4},{4,3},{5,2},{6,1},{7,0},{8,15},{9,14},{10,... | collective-permute-start | bytes 147464 | tf_op jit(solution)/shard_map/ppermute | solution.py:58

commit v4 on v3

--- a/solution.py
+++ b/solution.py
@@ -125,7 +125,7 @@
 
 def key_value_kernel(
     count_ref, x_ref, gain_ref, qkv_ref,
-    kv_own_ref, kv_other_ref, edge_ref, corner_ref, normed_ref, raw_ref, inverse_ref,
+    kv_own_ref, kv_other_ref, edge_ref, normed_ref, raw_ref, inverse_ref,
 ):
     cells = x_ref.shape[0]
     blocks = cells // CELLS
@@ -152,13 +152,13 @@
     kv_own_ref[...] = jnp.where(upper, high, low).astype(BF16).reshape(shape)
     kv_other_ref[...] = jnp.where(upper, low, high).astype(BF16).reshape(shape)
     edge_ref[...] = kv_own_ref[0]
+
+
+def query_grad_kernel(
+    scale_in, order_ref, normed_ref, grad_ref, qkv_ref, out_weight_ref, kv_other_ref,
+    qg_own_ref, qg_other_ref, corner_ref, raw_ref, inverse_ref, scale_ref,
+):
     corner_ref[...] = kv_other_ref[0]
-
-
-def query_grad_kernel(
-    scale_in, order_ref, normed_ref, grad_ref, qkv_ref, out_weight_ref,
-    qg_own_ref, qg_other_ref, raw_ref, inverse_ref, scale_ref,
-):
     cells, width = normed_ref.shape
     upper = lax.rem(lax.axis_index("lat"), 2) == 1
     all_scales = scale_in[...].reshape(1, HEADS) * (1.0 / math.sqrt(HEAD_DIM))
@@ -285,9 +285,11 @@
         weights[j] = jnp.where(row_half == j % 2, cols[lane_tile(j)], 0.0).astype(BF16)
 
 
-def own_score_kernel(rows, scale_ref, qg_ref, *refs):
+def own_score_kernel(rows, scale_ref, qkv_ref, qg_ref, *refs):
     kv_refs, refs = refs[:rows], refs[rows:]
-    weights, backward, sums_ref, e_mid, p_mid, e_left, p_left = refs
+    turned_ref, weights, backward, sums_ref, e_mid, p_mid, e_left, p_left = refs
+    for c in range(3):
+        turned_ref[c] = qkv_ref[c].T
     queries = 4 * CELLS
     query_tables(qg_ref, weights, backward)
     sums = [jnp.zeros((8, queries), F32) for _ in range(2 * HALF)]
@@ -548,7 +550,7 @@
 
 def finish_kernel(
     inner_ref, dq_ref, other_ref, edge_ref, corner_ref,
-    query_raw, query_inverse, key_raw, key_inverse, x_ref, order_ref, gain_ref, qkv_ref, out_ref,
+    query_raw, query_inverse, key_raw, key_inverse, x_ref, order_ref, gain_ref, turned_ref, out_ref,
 ):
     frames, lat_rows, lon_cols, width = out_ref.shape
     cells = frames * lat_rows * lon_cols
@@ -573,12 +575,12 @@
         joined(dkv_mine[:, :HALF_WIDTH], dkv_theirs[:, :HALF_WIDTH]),
         joined(dkv_mine[:, HALF_WIDTH:], dkv_theirs[:, HALF_WIDTH:]),
     ]
-    grad_normed = dot_last(grads[2].astype(BF16), qkv_ref[2])
+    grad_normed = dot(grads[2].astype(BF16), turned_ref[2])
     for c, (raw, inverse) in enumerate(((query_raw, query_inverse), (key_raw, key_inverse))):
         raw, inverse = raw[...], inverse[...]
         inner = head_means(raw * grads[c])
         grad_raw = inverse * grads[c] - inverse * inverse * inverse * raw * inner
-        grad_normed = grad_normed + dot_last(grad_raw.astype(BF16), qkv_ref[c])
+        grad_normed = grad_normed + dot(grad_raw.astype(BF16), turned_ref[c])
     order = order_ref[...]
     x = x_ref[...].astype(F32)
     inverse = lax.rsqrt(jnp.mean(x * x, -1, keepdims=True) + EPS)
@@ -624,19 +626,19 @@
         micros=10.0,
     )
     projected = ((cells, head_width), F32)
-    kv_own, kv_other, edge, corner, normed, key_raw, key_inverse = kernel_call(
+    kv_own, kv_other, edge, normed, key_raw, key_inverse = kernel_call(
         key_value_kernel, "key_value",
-        [qg_shape, qg_shape, edge_shape, edge_shape, ((cells, width), BF16), projected, projected],
+        [qg_shape, qg_shape, edge_shape, ((cells, width), BF16), projected, projected],
         [key_count, x, norm_gain, qkv_weight], micros=2.0,
     )
     edge = pair_swap(edge, "lon", 1)
+    kv_made, kv_other = kv_other, pair_swap(kv_other, "lat", 0)
+    qg_own, qg_other, corner, query_raw, query_inverse, scales = kernel_call(
+        query_grad_kernel, "query_grad",
+        [qg_shape, qg_shape, edge_shape, projected, projected, ((HALF, 4 * CELLS), F32)],
+        [logit_scale, order, normed, grad_out, qkv_weight, out_weight, kv_made], micros=5.0,
+    )
     corner = corner_swap(corner)
-    kv_other = pair_swap(kv_other, "lat", 0)
-    qg_own, qg_other, query_raw, query_inverse, scales = kernel_call(
-        query_grad_kernel, "query_grad",
-        [qg_shape, qg_shape, projected, projected, ((HALF, 4 * CELLS), F32)],
-        [logit_scale, order, normed, grad_out, qkv_weight, out_weight], micros=5.0,
-    )
     qg_other = pair_swap(qg_other, "lat", 0)
     (kv_other,) = kernel_call(join_kernel, "join", [qg_shape], [kv_other], micros=3.0)
     kv_rows = [
@@ -663,10 +665,10 @@
         left = ((HALF, groups * CELLS, 2 * CELLS), F32)
         return [mid, mid, left, left]
 
-    weights, backward, sums, *own_kept = kernel_call(
+    turned, weights, backward, sums, *own_kept = kernel_call(
         functools.partial(own_score_kernel, rows), "own_score",
-        tables + [sums_shape] + kept(rows),
-        [scales, qg_both, *kv_rows], micros=1.5,
+        [((3, head_width, width), BF16)] + tables + [sums_shape] + kept(rows),
+        [scales, qkv_weight, qg_both, *kv_rows], micros=1.5,
     )
     siblings = jnp.stack([kv[2] for kv in kv_rows + kv_away], 0)
     siblings = pair_swap(siblings, "lon", 0)
@@ -734,7 +736,7 @@
     (grad_tokens,) = kernel_call(
         finish_kernel, "finish", [(tokens.shape, BF16)],
         [inner, dq_own, other, edge, corner, query_raw, query_inverse, key_raw, key_inverse,
-         x, order, norm_gain, qkv_weight],
+         x, order, norm_gain, turned],
         micros=2.0,
     )
     return grad_tokens

time: 38.7 us -> 38.4 us (level)
  starting transfers between devices: 21.6 us -> 19.5 us
  waiting for transfers between devices: 6.12 us -> 7.73 us
    ppermute x8, starting transfers between devices: 10.7 us -> 8.72 us  [frame_swap(): return lax.ppermute(array, ('tm', 'lon'), pairs)]
    ppermute x2, waiting for transfers between devices: 2.78 us -> 4.29 us  [corner_swap(): return lax.ppermute(array, ('lat', 'lon'), pairs)]
    ppermute x8, waiting for transfers between devices: 0.83 us -> 1.81 us  [frame_swap(): return lax.ppermute(array, ('tm', 'lon'), pairs)]
    ppermute x7, waiting for transfers between devices: 2.51 us -> 1.64 us  [pair_swap(): return lax.ppermute(array, axis, pairs)]
  transfers between devices with their start and end apart: 17 -> 17, of which waited for: 5 -> 6; matrix products, arithmetic and copies ran while one was open for 0% -> 0% of each run, Pallas kernels for 15% -> 16%
where the time goes in v4:
time: 38.4 us; the launch traced here: 38.2 us
  starting transfers between devices  19.5 us (51%)
  Pallas kernels  9.01 us (23%)
  waiting for transfers between devices  7.73 us (20%)
  local copies, waits for them, and re-layouts  1.76 us (5%)
    ppermute x7, starting transfers between devices, pair_swap(): return lax.ppermute(array, axis, pairs)  9.14 us
    pallas_call x13, Pallas kernels, kernel_call(): pl.pallas_call(body, name=name, out_shape=[jax.ShapeDtypeStruct(shape, dt...  9.01 us
    ppermute x8, starting transfers between devices, frame_swap(): return lax.ppermute(array, ('tm', 'lon'), pairs)  8.72 us
    ppermute x2, waiting for transfers between devices, corner_swap(): return lax.ppermute(array, ('lat', 'lon'), pairs)  4.29 us
    ppermute x8, waiting for transfers between devices, frame_swap(): return lax.ppermute(array, ('tm', 'lon'), pairs)  1.81 us
    unnamed x20, local copies, waits for them, and re-layouts  1.73 us
    ppermute x2, starting transfers between devices, corner_swap(): return lax.ppermute(array, ('lat', 'lon'), pairs)  1.65 us
    ppermute x7, waiting for transfers between devices, pair_swap(): return lax.ppermute(array, axis, pairs)  1.64 us
  transfers between devices with their start and end apart: 17, of which 6 were waited for; matrix products, arithmetic and copies ran while one was open for 0% of the time, Pallas kernels for 16%

profile of v4, /device:TPU:1, one launch (start us, length us, event | category | flops | bytes accessed | tf_op | source)
XLA Modules:
  0.0 38.2 jit_solution(10011532832123045566)
XLA Ops:
  0.0 0.0 copy-start
  0.0 0.0 copy-start.2
  0.0 1.1 %copy-done.2 = bf16[4,4,8,768]{3,2,1,0:T(8,128)(2,1)S(1)} copy-done((bf16[4,4,8,768]{3,2,1,0:T(8,128)(2,1)S(1)}, bf16[4,4,8,768]{3,2,1,0:T(8,128)(2,1)}, u32[]{:S(2)}) %copy-start.2) | copy-done | bytes 196632
  1.1 0.0 copy-start.4
  1.1 0.0 copy-start.5
  1.1 0.2 order.1
  1.3 0.3 copy-done
  1.6 0.3 copy-done.4
  1.9 0.0 copy-done.5
  1.9 0.0 copy-start.1
  1.9 0.0 copy-start.3
  1.9 0.0 copy-start.6
  1.9 0.6 %key_value.1 = (bf16[2,64,384]{2,1,0:T(8,128)(2,1)S(1)}, bf16[2,64,384]{2,1,0:T(8,128)(2,1)S(1)}, bf16[64,384]{1,0:T(8,128)(2,1)S(1)}, bf16[128,768]{1,0:T(8,128...) custom-call(s32[1,1,2]{2,1,0:T(1,128)S(1)} %copy-done.5, bf16[128,768]{1,0:T(8,128)(2,1)S(1)} %get-tuple-element.48.x_ref, ...), custom_call_target="tpu_custom_call" | custom-call | flops 2000000000 | tf_op jit(solution)/shard_map/key_value/pallas_call | solution.py:600
  2.5 2.7 %collective-permute-start.1 = (bf16[64,384]{1,0:T(8,128)(2,1)S(1)}, bf16[64,384]{1,0:T(8,128)(2,1)S(1)}, u32[]{:S(2)}, u32[]{:S(2)}) collective-permute-start(bf16[64,384]{1,0:T(8,128)(2,1)S(1)} %get-tuple-element.54), channel_id=1, source_target_pairs={{0,3},{1,2},{2,1},{3,0},{4,7},{5,6},{6,5},{7,4},{8,11},{9,10},{10,... | collective-permute-start | bytes 147464 | tf_op jit(solution)/shard_map/ppermute | solution.py:36
  5.2 1.2 %collective-permute-start.3 = (bf16[2,64,384]{2,1,0:T(8,128)(2,1)S(1)}, bf16[2,64,384]{2,1,0:T(8,128)(2,1)S(1)}, u32[]{:S(2)}, u32[]{:S(2)}) collective-permute-start(bf16[2,64,384]{2,1,0:T(8,128)(2,1)S(1)} %get-tuple-element.50.kv_other_ref), channel_id=1, source_target_pairs={{0,4},{4,0},{1,5},{5,1},{2,6},{6,2},{3,7},{7,3},{8,12},{12,8},{9,1... | collective-permute-start | bytes 294920 | tf_op jit(solution)/shard_map/ppermute | solution.py:36
  6.4 0.0 copy-done.1
  6.4 0.0 copy-done.3
  6.4 0.0 copy-done.6
  6.4 0.8 %query_grad.1 = (bf16[2,64,384]{2,1,0:T(8,128)(2,1)S(1)}, bf16[2,64,384]{2,1,0:T(8,128)(2,1)S(1)}, bf16[64,384]{1,0:T(8,128)(2,1)S(1)}, f32[128,384]{1,0:T(8,128...) custom-call(f32[6]{0:T(128)S(1)} %copy-done.6, bf16[128,128]{1,0:T(8,128)(2,1)S(1)} %get-tuple-element.47.order_ref, ...), custom_call_target="tpu_custom_call" | custom-call | flops 5000000000 | tf_op jit(solution)/shard_map/query_grad/pallas_call | solution.py:600
  7.3 0.4 %collective-permute-start.2 = (bf16[64,384]{1,0:T(8,128)(2,1)S(1)}, bf16[64,384]{1,0:T(8,128)(2,1)S(1)}, u32[]{:S(2)}, u32[]{:S(2)}) collective-permute-start(bf16[64,384]{1,0:T(8,128)(2,1)S(1)} %get-tuple-element.56), channel_id=1, source_target_pairs={{0,7},{1,6},{2,5},{3,4},{4,3},{5,2},{6,1},{7,0},{8,15},{9,14},{10,... | collective-permute-start | bytes 147464 | tf_op jit(solution)/shard_map/ppermute | solution.py:58
  7.7 1.2 %collective-permute-start = (bf16[2,64,384]{2,1,0:T(8,128)(2,1)S(1)}, bf16[2,64,384]{2,1,0:T(8,128)(2,1)S(1)}, u32[]{:S(2)}, u32[]{:S(2)}) collective-permute-start(bf16[2,64,384]{2,1,0:T(8,128)(2,1)S(1)} %get-tuple-element.53), channel_id=1, source_target_pairs={{0,4},{4,0},{1,5},{5,1},{2,6},{6,2},{3,7},{7,3},{8,12},{12,8},{9,1... | collective-permute-start | bytes 294920 | tf_op jit(solution)/shard_map/ppermute | solution.py:36
  8.9 0.0 collective-permute-done.1
  8.9 0.6 %collective-permute-start.6 = (bf16[3,64,384]{2,1,0:T(8,128)(2,1)S(1)}, bf16[3,64,384]{2,1,0:T(8,128)(2,1)S(1)}, u32[]{:S(2)}, u32[]{:S(2)}) collective-permute-start(bf16[3,64,384]{2,1,0:T(8,128)(2,1)S(1)} %pad_maximum_fusion.refs_0_.refs_2_), channel_id=1, source_target_pairs={{0,1},{1,0},{2,3},{3,2},{8,16},{9,17},{10,18},{11,19},{16,8},{17,9... | collective-permute-start | bytes 442376 | tf_op jit(solution)/shard_map/ppermute | solution.py:48
  9.5 2.0 %collective-permute-start.4 = (bf16[3,64,384]{2,1,0:T(8,128)(2,1)S(1)}, bf16[3,64,384]{2,1,0:T(8,128)(2,1)S(1)}, u32[]{:S(2)}, u32[]{:S(2)}) collective-permute-start(bf16[3,64,384]{2,1,0:T(8,128)(2,1)S(1)} %pad_maximum_fusion.refs_0_.refs_2_), channel_id=1, source_target_pairs={{0,8},{1,9},{2,10},{3,11},{8,0},{9,1},{10,2},{11,3},{16,24},{17,25... | collective-permute-start | bytes 442376 | tf_op jit(solution)/shard_map/ppermute | solution.py:48
  11.6 0.0 collective-permute-done.3.kv_in
  11.6 0.6 %collective-permute-done.2 = bf16[64,384]{1,0:T(8,128)(2,1)S(1)} collective-permute-done((bf16[64,384]{1,0:T(8,128)(2,1)S(1)}, bf16[64,384]{1,0:T(8,128)(2,1)S(1)}, u32[]{:S(2)}, u32[]{:S(2)}) %collective-permute-start.2) | collective-permute-done | bytes 49184 | tf_op jit(solution)/shard_map/ppermute | solution.py:58
  12.3 0.5 %collective-permute-start.7 = (bf16[3,64,384]{2,1,0:T(8,128)(2,1)S(1)}, bf16[3,64,384]{2,1,0:T(8,128)(2,1)S(1)}, u32[]{:S(2)}, u32[]{:S(2)}) collective-permute-start(bf16[3,64,384]{2,1,0:T(8,128)(2,1)S(1)} %pad_maximum_fusion.1.refs_1_.refs_3_), channel_id=1, source_target_pairs={{0,1},{1,0},{2,3},{3,2},{8,16},{9,17},{10,18},{11,19},{16,8},{17,9... | collective-permute-start | bytes 442376 | tf_op jit(solution)/shard_map/ppermute | solution.py:48
  12.8 2.1 %collective-permute-start.5 = (bf16[3,64,384]{2,1,0:T(8,128)(2,1)S(1)}, bf16[3,64,384]{2,1,0:T(8,128)(2,1)S(1)}, u32[]{:S(2)}, u32[]{:S(2)}) collective-permute-start(bf16[3,64,384]{2,1,0:T(8,128)(2,1)S(1)} %pad_maximum_fusion.1.refs_1_.refs_3_), channel_id=1, source_target_pairs={{0,8},{1,9},{2,10},{3,11},{8,0},{9,1},{10,2},{11,3},{16,24},{17,25... | collective-permute-start | bytes 442376 | tf_op jit(solution)/shard_map/ppermute | solution.py:48
  14.9 0.0 collective-permute-done
  14.9 0.3 collective-permute-start.12
  15.3 0.9 %own_score.1 = (bf16[3,384,768]{2,1,0:T(8,128)(2,1)S(1)}, bf16[6,128,256]{2,1,0:T(8,128)(2,1)S(1)}, bf16[6,256,128]{2,1,0:T(8,128)(2,1)S(1)}, f32[6,8,256]{2,1,0...) custom-call(f32[3,256]{1,0:T(4,128)S(1)} %get-tuple-element.51.scale, ...), custom_call_target="tpu_custom_call" | custom-call | flops 1500000000 | tf_op jit(solution)/shard_map/own_score/pallas_call | solution.py:600
  16.1 0.0 collective-permute-done.4.refs_0_.refs_2_
  16.2 1.2 %collective-permute-start.11 = (bf16[4,64,384]{2,1,0:T(8,128)(2,1)S(1)}, bf16[4,64,384]{2,1,0:T(8,128)(2,1)S(1)}, u32[]{:S(2)}, u32[]{:S(2)}) collective-permute-start(bf16[4,64,384]{2,1,0:T(8,128)(2,1)S(1)} %constant_dynamic-update-slice_fusion.qg_ref), channel_id=1, source_target_pairs={{0,8},{1,9},{2,10},{3,11},{8,0},{9,1},{10,2},{11,3},{16,24},{17,25... | collective-permute-start | bytes 589832 | tf_op jit(solution)/shard_map/ppermute | solution.py:48
  17.4 1.8 %collective-permute-done.5.refs_1_.refs_3_ = bf16[3,64,384]{2,1,0:T(8,128)(2,1)S(1)} collective-permute-done((bf16[3,64,384]{2,1,0:T(8,128)(2,1)S(1)}, bf16[3,64,384]{2,1,0:T(8,128)(2,1)S(1)}, u32[]{:S(2)}, u32[]{:S(2)}) %collective-permute-start.5) | collective-permute-done | bytes 147488 | tf_op jit(solution)/shard_map/ppermute | solution.py:48
  19.2 0.0 collective-permute-done.6.refs_2_.refs_4_
  19.2 0.0 collective-permute-done.7.refs_3_.refs_5_
  19.2 0.8 %collective-permute-start.8 = (bf16[6,64,384]{2,1,0:T(8,128)(2,1)S(1)}, bf16[6,64,384]{2,1,0:T(8,128)(2,1)S(1)}, u32[]{:S(2)}, u32[]{:S(2)}) collective-permute-start(bf16[6,64,384]{2,1,0:T(8,128)(2,1)S(1)} %slice_dynamic-update-slice_fusion), channel_id=1, source_target_pairs={{0,1},{1,0},{2,3},{3,2},{4,5},{5,4},{6,7},{7,6},{8,9},{9,8},{10,11... | collective-permute-start | bytes 884744 | tf_op jit(solution)/shard_map/ppermute | solution.py:36
  20.0 0.7 %away_score.1 = (f32[6,8,256]{2,1,0:T(8,128)S(1)}, f32[3,512,256]{2,1,0:T(8,128)S(1)}, f32[3,512,256]{2,1,0:T(8,128)S(1)}, f32[3,256,128]{2,1,0:T(8,128)S(1)}, f32[3,256,128]{2,1,0:T(8,128)S(1)}) custom-call(f32[3,256]{1,0:T(4,128)S(1)} %get-tuple-element.51.scale_ref, bf16[6,128,256]{2,1,0:T(8,128)(2,1)S(1)} %get-tuple-element.57.weights, ...), custom_call_target="tpu_custom_call" | custom-call | flops 20000000000 | tf_op jit(solution)/shard_map/away_score/pallas_call | solution.py:600
  20.7 0.5 %collective-permute-done.8.keys_ref.refs_4_ = bf16[6,64,384]{2,1,0:T(8,128)(2,1)S(1)} collective-permute-done((bf16[6,64,384]{2,1,0:T(8,128)(2,1)S(1)}, bf16[6,64,384]{2,1,0:T(8,128)(2,1)S(1)}, u32[]{:S(2)}, u32[]{:S(2)}) %collective-permute-start.8) | collective-permute-done | bytes 294944 | tf_op jit(solution)/shard_map/ppermute | solution.py:36
  21.2 0.7 %sibling.1 = (f32[2,64,384]{2,1,0:T(8,128)S(1)}, f32[6,256]{1,0:T(8,128)S(1)}, f32[192,128]{1,0:T(8,128)S(1)}) custom-call(f32[3,256]{1,0:T(4,128)S(1)} %get-tuple-element.51.scale_ref, bf16[6,128,256]{2,1,0:T(8,128)(2,1)S(1)} %get-tuple-element.57.weights, bf16[6,256,128]{2,1,0:T(8,128)(2,1)S(1)} %get-tuple-element.58.backward, ...), custom_call_target="tpu_custom_call" | custom-call | flops 1500000000 | tf_op jit(solution)/shard_map/sibling/pallas_call | solution.py:600
  21.9 0.4 %collective-permute-start.10 = (f32[6,256]{1,0:T(8,128)S(1)}, f32[6,256]{1,0:T(8,128)S(1)}, u32[]{:S(2)}, u32[]{:S(2)}) collective-permute-start(f32[6,256]{1,0:T(8,128)S(1)} %get-tuple-element.61.stats_ref), channel_id=1, source_target_pairs={{0,1},{1,0},{2,3},{3,2},{8,16},{9,17},{10,18},{11,19},{16,8},{17,9... | collective-permute-start | bytes 18440 | tf_op jit(solution)/shard_map/ppermute | solution.py:48
  22.3 1.5 %collective-permute-start.9 = (f32[6,256]{1,0:T(8,128)S(1)}, f32[6,256]{1,0:T(8,128)S(1)}, u32[]{:S(2)}, u32[]{:S(2)}) collective-permute-start(f32[6,256]{1,0:T(8,128)S(1)} %get-tuple-element.61.stats_ref), channel_id=1, source_target_pairs={{0,8},{1,9},{2,10},{3,11},{8,0},{9,1},{10,2},{11,3},{16,24},{17,25... | collective-permute-start | bytes 18440 | tf_op jit(solution)/shard_map/ppermute | solution.py:48
  23.8 0.0 collective-permute-done.12.refs_1_
  23.8 0.0 collective-permute-done.11.refs_0_
  23.8 0.9 %cross_score.1 = (bf16[2,6,256,128]{3,2,1,0:T(8,128)(2,1)S(1)}, f32[2,3,256,256]{3,2,1,0:T(8,128)S(1)}, f32[2,3,256,256]{3,2,1,0:T(8,128)S(1)}, f32[2,2,3,128,12...) custom-call(f32[3,256]{1,0:T(4,128)S(1)} %get-tuple-element.51.scale_ref, ...), custom_call_target="tpu_custom_call" | custom-call | flops 2000000000 | tf_op jit(solution)/shard_map/cross_score/pallas_call | solution.py:600
  24.7 1.2 %own_back.1 = (f32[2,3,64,384]{3,2,1,0:T(8,128)S(1)}, f32[64,384]{1,0:T(8,128)S(1)}, bf16[64,384]{1,0:T(8,128)(2,1)S(1)}) custom-call(f32[3,256]{1,0:T(4,128)S(1)} %get-tuple-element.51.scale_ref, f32[6,256]{1,0:T(8,128)S(1)} %get-tuple-element.61.stats_ref, bf16[6,256,128]{2,1,0:T(8,128)(2,1)S(1)} %get-tuple-element.58.backward, ...), custom_call_target="tpu_custom_call" | custom-call | flops 2000000000 | tf_op jit(solution)/shard_map/own_back/pallas_call | solution.py:600
  25.9 0.0 collective-permute-done.10.far_stats
  25.9 0.0 collective-permute-done.9.near_stats
  25.9 0.3 cross_sibling.1
  26.2 1.0 %collective-permute-start.13 = (bf16[2,64,384]{2,1,0:T(8,128)(2,1)S(1)}, bf16[2,64,384]{2,1,0:T(8,128)(2,1)S(1)}, u32[]{:S(2)}, u32[]{:S(2)}) collective-permute-start(bf16[2,64,384]{2,1,0:T(8,128)(2,1)S(1)} %cross_sibling.1), channel_id=1, source_target_pairs={{0,1},{1,0},{2,3},{3,2},{4,5},{5,4},{6,7},{7,6},{8,9},{9,8},{10,11... | collective-permute-start | bytes 294920 | tf_op jit(solution)/shard_map/ppermute | solution.py:36
  27.2 0.8 %cross_back.1.total_ref = f32[2,3,64,384]{3,2,1,0:T(8,128)S(1)} custom-call(f32[3,256]{1,0:T(4,128)S(1)} %get-tuple-element.51.scale_ref, f32[6,256]{1,0:T(8,128)S(1)} %collective-permute-done.9.near_stats, f32[6,256]{1,0:T(8,128)S(1)} %collective-permute-done.10.far_stats, bf16[2,6,256,128]{3,2,1,0:T(8,128)(2,1)S(1)} %get-tuple-element.62.backward, ...), custom_call_target="tpu_custom_call" | custom-call | flops 1500000000 | tf_op jit(solution)/shard_map/cross_back/pallas_call | solution.py:600
  28.0 0.1 collective-permute-done.13.sibling_ref
  28.2 0.2 collective-permute-start.14
  28.4 2.0 %collective-permute-start.15 = (bf16[64,384]{1,0:T(8,128)(2,1)S(1)}, bf16[64,384]{1,0:T(8,128)(2,1)S(1)}, u32[]{:S(2)}, u32[]{:S(2)}) collective-permute-start(bf16[64,384]{1,0:T(8,128)(2,1)S(1)} %get-tuple-element.82), channel_id=1, source_target_pairs={{0,3},{1,2},{2,1},{3,0},{4,7},{5,6},{6,5},{7,4},{8,11},{9,10},{10,... | collective-permute-start | bytes 147464 | tf_op jit(solution)/shard_map/ppermute | solution.py:36
  30.4 1.3 %collective-permute-start.16 = (bf16[64,384]{1,0:T(8,128)(2,1)S(1)}, bf16[64,384]{1,0:T(8,128)(2,1)S(1)}, u32[]{:S(2)}, u32[]{:S(2)}) collective-permute-start(bf16[64,384]{1,0:T(8,128)(2,1)S(1)} %get-tuple-element.83), channel_id=1, source_target_pairs={{0,7},{1,6},{2,5},{3,4},{4,3},{5,2},{6,1},{7,0},{8,15},{9,14},{10,... | collective-permute-start | bytes 147464 | tf_op jit(solution)/shard_map/ppermute | solution.py:58
  31.7 1.0 %collective-permute-done.15.edge_ref = bf16[64,384]{1,0:T(8,128)(2,1)S(1)} collective-permute-done((bf16[64,384]{1,0:T(8,128)(2,1)S(1)}, bf16[64,384]{1,0:T(8,128)(2,1)S(1)}, u32[]{:S(2)}, u32[]{:S(2)}) %collective-permute-start.15) | collective-permute-done | bytes 49184 | tf_op jit(solution)/shard_map/ppermute | solution.py:36
  32.7 3.7 %collective-permute-done.16.corner_ref = bf16[64,384]{1,0:T(8,128)(2,1)S(1)} collective-permute-done((bf16[64,384]{1,0:T(8,128)(2,1)S(1)}, bf16[64,384]{1,0:T(8,128)(2,1)S(1)}, u32[]{:S(2)}, u32[]{:S(2)}) %collective-permute-start.16) | collective-permute-done | bytes 49184 | tf_op jit(solution)/shard_map/ppermute | solution.py:58
  36.3 0.0 collective-permute-done.14.other_ref
  36.3 1.9 %finish.1 = bf16[4,4,8,768]{3,2,1,0:T(8,128)(2,1)} custom-call(f32[2,64,384]{2,1,0:T(8,128)S(1)} %get-tuple-element.79.inner_ref, f32[64,384]{1,0:T(8,128)S(1)} %get-tuple-element.80.dq_ref, bf16[3,64,384]{2,1,0:T(8,128)(2,1)S(1)} %collective-permute-done.14.other_ref, bf16[64,384]{1,0:T(8,128)(2,1)S(1)} %collective-permute-done.15.edge_ref, ...), custom_call_target="tpu_custom_call" | custom-call | flops 2000000000 | tf_op jit(solution)/shard_map/finish/pallas_call | solution.py:600
  (12 shorter events, 0.2 us)
Async XLA Ops:
  0.0 1.6 %copy-start = (bf16[3,768,384]{2,1,0:T(8,128)(2,1)S(1)}, bf16[3,768,384]{2,1,0:T(8,128)(2,1)}, u32[]{:S(2)}) copy-start(bf16[3,768,384]{2,1,0:T(8,128)(2,1)} %qkv_ref.5) | copy-start | bytes 5308420
  0.0 1.1 %copy-start.2 = (bf16[4,4,8,768]{3,2,1,0:T(8,128)(2,1)S(1)}, bf16[4,4,8,768]{3,2,1,0:T(8,128)(2,1)}, u32[]{:S(2)}) copy-start(bf16[4,4,8,768]{3,2,1,0:T(8,128)(2,1)} %tokens_ref.1) | copy-start | bytes 589828
  1.1 0.8 %copy-start.4 = (f32[768]{0:T(1024)S(1)}, f32[768]{0:T(1024)}, u32[]{:S(2)}) copy-start(f32[768]{0:T(1024)} %gain_ref.3) | copy-start | bytes 9220
  1.1 0.8 %copy-start.5 = (s32[1,1,2]{2,1,0:T(1,128)S(1)}, s32[1,1,2]{2,1,0:T(1,128)}, u32[]{:S(2)}) copy-start(s32[1,1,2]{2,1,0:T(1,128)} %count_ref.1) | copy-start | bytes 28
  1.9 4.5 %copy-start.1 = (bf16[384,768]{1,0:T(8,128)(2,1)S(1)}, bf16[384,768]{1,0:T(8,128)(2,1)}, u32[]{:S(2)}) copy-start(bf16[384,768]{1,0:T(8,128)(2,1)} %out_weight_ref.1) | copy-start | bytes 1769476
  1.9 4.5 %copy-start.3 = (bf16[4,4,8,768]{3,2,1,0:T(8,128)(2,1)S(1)}, bf16[4,4,8,768]{3,2,1,0:T(8,128)(2,1)}, u32[]{:S(2)}) copy-start(bf16[4,4,8,768]{3,2,1,0:T(8,128)(2,1)} %grad_ref.1) | copy-start | bytes 589828
  1.9 4.5 %copy-start.6 = (f32[6]{0:T(128)S(1)}, f32[6]{0:T(128)}, u32[]{:S(2)}) copy-start(f32[6]{0:T(128)} %scale_in.1) | copy-start | bytes 76
  2.5 6.4 %collective-permute-start.1 = (bf16[64,384]{1,0:T(8,128)(2,1)S(1)}, bf16[64,384]{1,0:T(8,128)(2,1)S(1)}, u32[]{:S(2)}, u32[]{:S(2)}) collective-permute-start(bf16[64,384]{1,0:T(8,128)(2,1)S(1)} %get-tuple-element.54), channel_id=1, source_target_pairs={{0,3},{1,2},{2,1},{3,0},{4,7},{5,6},{6,5},{7,4},{8,11},{9,10},{10,... | collective-permute-start | bytes 147464 | tf_op jit(solution)/shard_map/ppermute | solution.py:36
  5.2 6.4 %collective-permute-start.3 = (bf16[2,64,384]{2,1,0:T(8,128)(2,1)S(1)}, bf16[2,64,384]{2,1,0:T(8,128)(2,1)S(1)}, u32[]{:S(2)}, u32[]{:S(2)}) collective-permute-start(bf16[2,64,384]{2,1,0:T(8,128)(2,1)S(1)} %get-tuple-element.50.kv_other_ref), channel_id=1, source_target_pairs={{0,4},{4,0},{1,5},{5,1},{2,6},{6,2},{3,7},{7,3},{8,12},{12,8},{9,1... | collective-permute-start | bytes 294920 | tf_op jit(solution)/shard_map/ppermute | solution.py:36
  7.3 5.0 %collective-permute-start.2 = (bf16[64,384]{1,0:T(8,128)(2,1)S(1)}, bf16[64,384]{1,0:T(8,128)(2,1)S(1)}, u32[]{:S(2)}, u32[]{:S(2)}) collective-permute-start(bf16[64,384]{1,0:T(8,128)(2,1)S(1)} %get-tuple-element.56), channel_id=1, source_target_pairs={{0,7},{1,6},{2,5},{3,4},{4,3},{5,2},{6,1},{7,0},{8,15},{9,14},{10,... | collective-permute-start | bytes 147464 | tf_op jit(solution)/shard_map/ppermute | solution.py:58
  7.7 7.2 %collective-permute-start = (bf16[2,64,384]{2,1,0:T(8,128)(2,1)S(1)}, bf16[2,64,384]{2,1,0:T(8,128)(2,1)S(1)}, u32[]{:S(2)}, u32[]{:S(2)}) collective-permute-start(bf16[2,64,384]{2,1,0:T(8,128)(2,1)S(1)} %get-tuple-element.53), channel_id=1, source_target_pairs={{0,4},{4,0},{1,5},{5,1},{2,6},{6,2},{3,7},{7,3},{8,12},{12,8},{9,1... | collective-permute-start | bytes 294920 | tf_op jit(solution)/shard_map/ppermute | solution.py:36
  8.9 10.2 %collective-permute-start.6 = (bf16[3,64,384]{2,1,0:T(8,128)(2,1)S(1)}, bf16[3,64,384]{2,1,0:T(8,128)(2,1)S(1)}, u32[]{:S(2)}, u32[]{:S(2)}) collective-permute-start(bf16[3,64,384]{2,1,0:T(8,128)(2,1)S(1)} %pad_maximum_fusion.refs_0_.refs_2_), channel_id=1, source_target_pairs={{0,1},{1,0},{2,3},{3,2},{8,16},{9,17},{10,18},{11,19},{16,8},{17,9... | collective-permute-start | bytes 442376 | tf_op jit(solution)/shard_map/ppermute | solution.py:48
  9.5 6.6 %collective-permute-start.4 = (bf16[3,64,384]{2,1,0:T(8,128)(2,1)S(1)}, bf16[3,64,384]{2,1,0:T(8,128)(2,1)S(1)}, u32[]{:S(2)}, u32[]{:S(2)}) collective-permute-start(bf16[3,64,384]{2,1,0:T(8,128)(2,1)S(1)} %pad_maximum_fusion.refs_0_.refs_2_), channel_id=1, source_target_pairs={{0,8},{1,9},{2,10},{3,11},{8,0},{9,1},{10,2},{11,3},{16,24},{17,25... | collective-permute-start | bytes 442376 | tf_op jit(solution)/shard_map/ppermute | solution.py:48
  12.3 6.9 %collective-permute-start.7 = (bf16[3,64,384]{2,1,0:T(8,128)(2,1)S(1)}, bf16[3,64,384]{2,1,0:T(8,128)(2,1)S(1)}, u32[]{:S(2)}, u32[]{:S(2)}) collective-permute-start(bf16[3,64,384]{2,1,0:T(8,128)(2,1)S(1)} %pad_maximum_fusion.1.refs_1_.refs_3_), channel_id=1, source_target_pairs={{0,1},{1,0},{2,3},{3,2},{8,16},{9,17},{10,18},{11,19},{16,8},{17,9... | collective-permute-start | bytes 442376 | tf_op jit(solution)/shard_map/ppermute | solution.py:48
  12.8 6.3 %collective-permute-start.5 = (bf16[3,64,384]{2,1,0:T(8,128)(2,1)S(1)}, bf16[3,64,384]{2,1,0:T(8,128)(2,1)S(1)}, u32[]{:S(2)}, u32[]{:S(2)}) collective-permute-start(bf16[3,64,384]{2,1,0:T(8,128)(2,1)S(1)} %pad_maximum_fusion.1.refs_1_.refs_3_), channel_id=1, source_target_pairs={{0,8},{1,9},{2,10},{3,11},{8,0},{9,1},{10,2},{11,3},{16,24},{17,25... | collective-permute-start | bytes 442376 | tf_op jit(solution)/shard_map/ppermute | solution.py:48
  14.9 8.9 %collective-permute-start.12 = (bf16[4,64,384]{2,1,0:T(8,128)(2,1)S(1)}, bf16[4,64,384]{2,1,0:T(8,128)(2,1)S(1)}, u32[]{:S(2)}, u32[]{:S(2)}) collective-permute-start(bf16[4,64,384]{2,1,0:T(8,128)(2,1)S(1)} %constant_dynamic-update-slice_fusion.qg_ref), channel_id=1, source_target_pairs={{0,1},{1,0},{2,3},{3,2},{8,16},{9,17},{10,18},{11,19},{16,8},{17,9... | collective-permute-start | bytes 589832 | tf_op jit(solution)/shard_map/ppermute | solution.py:48
  16.2 7.7 %collective-permute-start.11 = (bf16[4,64,384]{2,1,0:T(8,128)(2,1)S(1)}, bf16[4,64,384]{2,1,0:T(8,128)(2,1)S(1)}, u32[]{:S(2)}, u32[]{:S(2)}) collective-permute-start(bf16[4,64,384]{2,1,0:T(8,128)(2,1)S(1)} %constant_dynamic-update-slice_fusion.qg_ref), channel_id=1, source_target_pairs={{0,8},{1,9},{2,10},{3,11},{8,0},{9,1},{10,2},{11,3},{16,24},{17,25... | collective-permute-start | bytes 589832 | tf_op jit(solution)/shard_map/ppermute | solution.py:48
  19.2 2.0 %collective-permute-start.8 = (bf16[6,64,384]{2,1,0:T(8,128)(2,1)S(1)}, bf16[6,64,384]{2,1,0:T(8,128)(2,1)S(1)}, u32[]{:S(2)}, u32[]{:S(2)}) collective-permute-start(bf16[6,64,384]{2,1,0:T(8,128)(2,1)S(1)} %slice_dynamic-update-slice_fusion), channel_id=1, source_target_pairs={{0,1},{1,0},{2,3},{3,2},{4,5},{5,4},{6,7},{7,6},{8,9},{9,8},{10,11... | collective-permute-start | bytes 884744 | tf_op jit(solution)/shard_map/ppermute | solution.py:36
  21.9 4.0 %collective-permute-start.10 = (f32[6,256]{1,0:T(8,128)S(1)}, f32[6,256]{1,0:T(8,128)S(1)}, u32[]{:S(2)}, u32[]{:S(2)}) collective-permute-start(f32[6,256]{1,0:T(8,128)S(1)} %get-tuple-element.61.stats_ref), channel_id=1, source_target_pairs={{0,1},{1,0},{2,3},{3,2},{8,16},{9,17},{10,18},{11,19},{16,8},{17,9... | collective-permute-start | bytes 18440 | tf_op jit(solution)/shard_map/ppermute | solution.py:48
  22.3 3.6 %collective-permute-start.9 = (f32[6,256]{1,0:T(8,128)S(1)}, f32[6,256]{1,0:T(8,128)S(1)}, u32[]{:S(2)}, u32[]{:S(2)}) collective-permute-start(f32[6,256]{1,0:T(8,128)S(1)} %get-tuple-element.61.stats_ref), channel_id=1, source_target_pairs={{0,8},{1,9},{2,10},{3,11},{8,0},{9,1},{10,2},{11,3},{16,24},{17,25... | collective-permute-start | bytes 18440 | tf_op jit(solution)/shard_map/ppermute | solution.py:48
  26.2 1.9 %collective-permute-start.13 = (bf16[2,64,384]{2,1,0:T(8,128)(2,1)S(1)}, bf16[2,64,384]{2,1,0:T(8,128)(2,1)S(1)}, u32[]{:S(2)}, u32[]{:S(2)}) collective-permute-start(bf16[2,64,384]{2,1,0:T(8,128)(2,1)S(1)} %cross_sibling.1), channel_id=1, source_target_pairs={{0,1},{1,0},{2,3},{3,2},{4,5},{5,4},{6,7},{7,6},{8,9},{9,8},{10,11... | collective-permute-start | bytes 294920 | tf_op jit(solution)/shard_map/ppermute | solution.py:36
  28.2 8.2 %collective-permute-start.14 = (bf16[3,64,384]{2,1,0:T(8,128)(2,1)S(1)}, bf16[3,64,384]{2,1,0:T(8,128)(2,1)S(1)}, u32[]{:S(2)}, u32[]{:S(2)}) collective-permute-start(bf16[3,64,384]{2,1,0:T(8,128)(2,1)S(1)} %get-tuple-element.81), channel_id=1, source_target_pairs={{0,4},{4,0},{1,5},{5,1},{2,6},{6,2},{3,7},{7,3},{8,12},{12,8},{9,1... | collective-permute-start | bytes 442376 | tf_op jit(solution)/shard_map/ppermute | solution.py:36
  28.4 4.3 %collective-permute-start.15 = (bf16[64,384]{1,0:T(8,128)(2,1)S(1)}, bf16[64,384]{1,0:T(8,128)(2,1)S(1)}, u32[]{:S(2)}, u32[]{:S(2)}) collective-permute-start(bf16[64,384]{1,0:T(8,128)(2,1)S(1)} %get-tuple-element.82), channel_id=1, source_target_pairs={{0,3},{1,2},{2,1},{3,0},{4,7},{5,6},{6,5},{7,4},{8,11},{9,10},{10,... | collective-permute-start | bytes 147464 | tf_op jit(solution)/shard_map/ppermute | solution.py:36
  30.4 5.9 %collective-permute-start.16 = (bf16[64,384]{1,0:T(8,128)(2,1)S(1)}, bf16[64,384]{1,0:T(8,128)(2,1)S(1)}, u32[]{:S(2)}, u32[]{:S(2)}) collective-permute-start(bf16[64,384]{1,0:T(8,128)(2,1)S(1)} %get-tuple-element.83), channel_id=1, source_target_pairs={{0,7},{1,6},{2,5},{3,4},{4,3},{5,2},{6,1},{7,0},{8,15},{9,14},{10,... | collective-permute-start | bytes 147464 | tf_op jit(solution)/shard_map/ppermute | solution.py:58

commit v5 on v4

--- a/solution.py
+++ b/solution.py
@@ -84,8 +84,9 @@
     low = (values - high.astype(F32)).astype(BF16)
     pieces = []
     for start in range(0, values.shape[1], TILE):
-        cut = slice(start, start + TILE)
-        pieces.append(dot(high[:, cut], ones) + dot(low[:, cut], ones))
+        cut = slice(start, min(start + TILE, values.shape[1]))
+        square = ones[: cut.stop - start, : cut.stop - start]
+        pieces.append(dot(high[:, cut], square) + dot(low[:, cut], square))
     return jnp.concatenate(pieces, 1) * (1.0 / HEAD_DIM)
 
 
@@ -243,35 +244,40 @@
 LAST = slice(2 * CELLS, 4 * CELLS)
 
 
-def score_groups(place, frames, kv_refs, weights_ref, scale_ref, sums, e_mid, p_mid, e_left, p_left):
-    rows = place.rows
+def score_groups(place, groups, kv_refs, weights_ref, scale_ref, sums, e_mid, p_mid, e_left, p_left):
     side = [jnp.zeros((8, 2 * CELLS), F32) for _ in range(2 * HALF)]
-    for index, ref in enumerate(kv_refs):
-        frame, row = frames[index // rows], index % rows
+    for index, (group, ref) in enumerate(zip(groups, kv_refs)):
         keys = ref[1:3].reshape(2 * CELLS, PAIR_WIDTH)
-        bias = key_bias(keys) + place.bias(frame, row, 4 * CELLS)
+        bias = key_bias(keys) + place.bias(*group, 4 * CELLS)
         exps, probs = score(keys, bias, weights_ref, ALL, scale_ref, sums)
         for h in range(HALF):
             e_mid[h, index * 2 * CELLS : (index + 1) * 2 * CELLS] = exps[h]
             p_mid[h, index * 2 * CELLS : (index + 1) * 2 * CELLS] = probs[h]
     for index in range(0, len(kv_refs), 2):
-        frame, row = frames[index // rows], index % rows
         pair = [kv_refs[index][0], kv_refs[index + 1][0]]
-        bias = jnp.concatenate(
-            [
-                jnp.broadcast_to(
-                    key_bias(keys) + place.bias(frame, row + i, 2 * CELLS), (CELLS, 2 * CELLS)
-                )
-                for i, keys in enumerate(pair)
-            ],
-            0,
-        )
+        bias = side_bias(place, groups[index : index + 2], pair)
         keys = jnp.concatenate(pair, 0)
         exps, probs = score(keys, bias, weights_ref, FIRST, scale_ref, side)
         for h in range(HALF):
             e_left[h, index * CELLS : (index + 2) * CELLS] = exps[h]
             p_left[h, index * CELLS : (index + 2) * CELLS] = probs[h]
     return [jnp.concatenate([a[:, FIRST] + b, a[:, LAST]], 1) for a, b in zip(sums, side)]
+
+
+def side_bias(place, groups, keys):
+    return jnp.concatenate(
+        [
+            jnp.broadcast_to(
+                key_bias(keys[i]) + place.bias(*groups[i], 2 * CELLS), (CELLS, 2 * CELLS)
+            )
+            for i in range(2)
+        ],
+        0,
+    )
+
+
+def away_groups(rows):
+    return [(1, 0), (2, 0)], [(frame, row) for frame in (1, 2) for row in range(1, rows)]
 
 
 def query_tables(qg_ref, weights, backward):
@@ -294,20 +300,20 @@
     query_tables(qg_ref, weights, backward)
     sums = [jnp.zeros((8, queries), F32) for _ in range(2 * HALF)]
     sums = score_groups(
-        Place(rows), (0,), kv_refs, weights, scale_ref, sums,
+        Place(rows), [(0, row) for row in range(rows)], kv_refs, weights, scale_ref, sums,
         e_mid, p_mid, e_left, p_left,
     )
     for j in range(2 * HALF):
         sums_ref[j] = sums[j]
 
 
-def away_score_kernel(rows, scale_ref, weights, sums_in, *refs):
-    kv_refs, refs = refs[: 2 * rows], refs[2 * rows :]
+def away_score_kernel(rows, part, scale_ref, weights, sums_in, *refs):
+    groups = away_groups(rows)[part]
+    kv_refs, refs = refs[: len(groups)], refs[len(groups) :]
     sums_ref, e_mid, p_mid, e_left, p_left = refs
     sums = [sums_in[j] for j in range(2 * HALF)]
     sums = score_groups(
-        Place(rows), (1, 2), kv_refs, weights, scale_ref, sums,
-        e_mid, p_mid, e_left, p_left,
+        Place(rows), groups, kv_refs, weights, scale_ref, sums, e_mid, p_mid, e_left, p_left
     )
     for j in range(2 * HALF):
         sums_ref[j] = sums[j]
@@ -338,29 +344,19 @@
     return dot_first(keys[:, lane_tile(h)], grads)[own]
 
 
-def side_bias(place, frame, row, keys):
-    return jnp.concatenate(
-        [
-            jnp.broadcast_to(
-                key_bias(keys[i]) + place.bias(frame, row + i, 2 * CELLS), (CELLS, 2 * CELLS)
-            )
-            for i in range(2)
-        ],
-        0,
-    )
-
-
 def sibling_kernel(
-    rows, scale_ref, weights, backward, sums_in, keys_ref, part_ref, stats_ref, dq_ref
+    rows, scale_ref, weights, backward, sums_in, early_ref, late_ref, part_ref, stats_ref, dq_ref
 ):
     place = Place(rows)
     side = [jnp.zeros((8, 2 * CELLS), F32) for _ in range(2 * HALF)]
+    first, second = away_groups(rows)
+    groups = [(0, row) for row in range(rows)] + first + second
+    pairs = [early_ref[i : i + 2] for i in range(0, rows + 2, 2)]
+    pairs += [late_ref[i : i + 2] for i in range(0, len(second), 2)]
     made = []
-    for index in range(0, 3 * rows, 2):
-        bias = side_bias(
-            place, index // rows, index % rows, [keys_ref[index], keys_ref[index + 1]]
-        )
-        keys = keys_ref[index : index + 2].reshape(2 * CELLS, PAIR_WIDTH)
+    for index, pair in enumerate(pairs):
+        bias = side_bias(place, groups[2 * index : 2 * index + 2], pair)
+        keys = pair.reshape(2 * CELLS, PAIR_WIDTH)
         made.append(score(keys, bias, weights, LAST, scale_ref, side))
     inverse, delta = [], []
     for h in range(HALF):
@@ -382,7 +378,7 @@
         if index < rows:
             part = key_grads(pieces, backward, LAST)
             part_ref[index : index + 2] = part.reshape(2, CELLS, PAIR_WIDTH)
-    keys = keys_ref[...].reshape(3 * rows * CELLS, PAIR_WIDTH)
+    keys = jnp.concatenate(pairs, 0).reshape(3 * rows * CELLS, PAIR_WIDTH)
     for h in range(HALF):
         dq_ref[h * HEAD_DIM : (h + 1) * HEAD_DIM] = query_grads(
             keys, jnp.concatenate([g[h] for g in grads], 0), h
@@ -412,7 +408,7 @@
                 pair = [kv_refs[row][0], kv_refs[row + 1][0]]
             else:
                 pair = [sibling_ref[row], sibling_ref[row + 1]]
-            bias = side_bias(place, 0, row, pair)
+            bias = side_bias(place, [(0, row), (0, row + 1)], pair)
             keys = jnp.concatenate(pair, 0)
             for side in range(2):
                 exps, probs = score(keys, bias, weights.at[side], lanes, scale_ref, None)
@@ -483,7 +479,8 @@
 
 def own_back_kernel(
     rows, scale_ref, stats_ref, backward, e_mid, p_mid, e_left, p_left,
-    away_e_mid, away_p_mid, away_e_left, away_p_left, dq_sibling, *refs,
+    first_e_mid, first_p_mid, first_e_left, first_p_left,
+    second_e_mid, second_p_mid, second_e_left, second_p_left, dq_sibling, *refs,
 ):
     kv_refs, refs = refs[: 3 * rows], refs[3 * rows :]
     own_ref, dq_own_ref, dq_other_ref, d_mid, d_left = refs
@@ -494,8 +491,10 @@
         at = slice(index * 2 * CELLS, (index + 1) * 2 * CELLS)
         if index < rows:
             exps, probs, start = e_mid, p_mid, index * 2 * CELLS
+        elif index < rows + 2:
+            exps, probs, start = first_e_mid, first_p_mid, (index - rows) * 2 * CELLS
         else:
-            exps, probs, start = away_e_mid, away_p_mid, (index - rows) * 2 * CELLS
+            exps, probs, start = second_e_mid, second_p_mid, (index - rows - 2) * 2 * CELLS
         cut = slice(start, start + 2 * CELLS)
         pieces = grad_parts(
             [exps[h, cut] for h in range(HALF)], [probs[h, cut] for h in range(HALF)],
@@ -513,8 +512,10 @@
         at = slice(index * CELLS, (index + 2) * CELLS)
         if index < rows:
             exps, probs, start = e_left, p_left, index * CELLS
+        elif index < rows + 2:
+            exps, probs, start = first_e_left, first_p_left, (index - rows) * CELLS
         else:
-            exps, probs, start = away_e_left, away_p_left, (index - rows) * CELLS
+            exps, probs, start = second_e_left, second_p_left, (index - rows - 2) * CELLS
         cut = slice(start, start + 2 * CELLS)
         pieces = grad_parts(
             [exps[h, cut] for h in range(HALF)], [probs[h, cut] for h in range(HALF)],
@@ -548,47 +549,59 @@
     corner_ref[...] = total_ref[1, 0].astype(BF16)
 
 
+def heads_back(query, inner, edge, raws, inverses, weights):
+    pair = jnp.concatenate([inner[0] + edge, inner[1]], 0)
+    query = jnp.concatenate([query[:, :HALF_WIDTH], query[:, HALF_WIDTH:]], 0)
+    grads = (query, pair[:, :HALF_WIDTH], pair[:, HALF_WIDTH:])
+    total = dot(grads[2].astype(BF16), weights[2])
+    for c in range(2):
+        mean = head_means(raws[c] * grads[c])
+        cubed = inverses[c] * inverses[c] * inverses[c]
+        grad_raw = inverses[c] * grads[c] - cubed * raws[c] * mean
+        total = total + dot(grad_raw.astype(BF16), weights[c])
+    return total
+
+
+def own_finish_kernel(
+    inner_ref, dq_ref, edge_ref, query_raw, query_inverse, key_raw, key_inverse, turned_ref,
+    total_ref, raws_ref, inverses_ref, weights_ref,
+):
+    upper = lax.rem(lax.axis_index("lat"), 2) == 1
+
+    def split(array):
+        low, high = array[:, :HALF_WIDTH], array[:, HALF_WIDTH:]
+        return jnp.where(upper, high, low), jnp.where(upper, low, high)
+
+    raws, other_raws = zip(split(query_raw[...]), split(key_raw[...]))
+    inverses, other_inverses = zip(split(query_inverse[...]), split(key_inverse[...]))
+    weights = []
+    for c in range(3):
+        low, high = turned_ref[c, :HALF_WIDTH], turned_ref[c, HALF_WIDTH:]
+        weights.append(jnp.where(upper, high, low))
+        weights_ref[c] = jnp.where(upper, low, high)
+    for c in range(2):
+        raws_ref[c] = other_raws[c]
+        inverses_ref[c] = other_inverses[c]
+    total_ref[...] = heads_back(
+        dq_ref[...], inner_ref[...], edge_ref[...].astype(F32), raws, inverses, weights
+    )
+
+
 def finish_kernel(
-    inner_ref, dq_ref, other_ref, edge_ref, corner_ref,
-    query_raw, query_inverse, key_raw, key_inverse, x_ref, order_ref, gain_ref, turned_ref, out_ref,
-):
-    frames, lat_rows, lon_cols, width = out_ref.shape
-    cells = frames * lat_rows * lon_cols
-    parity = lax.rem(lax.axis_index("lon"), 2)
-    upper = lax.rem(lax.axis_index("lat"), 2) == 1
-
-    def joined(mine, theirs):
-        return jnp.where(
-            upper, jnp.concatenate([theirs, mine], 1), jnp.concatenate([mine, theirs], 1)
-        )
-
-    def by_slot(packed):
-        return jnp.concatenate([packed[:, :HALF_WIDTH], packed[:, HALF_WIDTH:]], 0)
-
-    def with_edge(inner, edge):
-        return jnp.concatenate([inner[0] + edge.astype(F32), inner[1]], 0)
-
-    dkv_mine = with_edge(inner_ref[...], edge_ref[...])
-    dkv_theirs = with_edge(other_ref[:2].astype(F32), corner_ref[...])
-    grads = [
-        joined(by_slot(dq_ref[...]), by_slot(other_ref[2].astype(F32))),
-        joined(dkv_mine[:, :HALF_WIDTH], dkv_theirs[:, :HALF_WIDTH]),
-        joined(dkv_mine[:, HALF_WIDTH:], dkv_theirs[:, HALF_WIDTH:]),
-    ]
-    grad_normed = dot(grads[2].astype(BF16), turned_ref[2])
-    for c, (raw, inverse) in enumerate(((query_raw, query_inverse), (key_raw, key_inverse))):
-        raw, inverse = raw[...], inverse[...]
-        inner = head_means(raw * grads[c])
-        grad_raw = inverse * grads[c] - inverse * inverse * inverse * raw * inner
-        grad_normed = grad_normed + dot(grad_raw.astype(BF16), turned_ref[c])
+    total_ref, other_ref, corner_ref, raws_ref, inverses_ref, weights_ref,
+    x_ref, order_ref, gain_ref, out_ref,
+):
+    grad_normed = total_ref[...] + heads_back(
+        other_ref[2].astype(F32), other_ref[:2].astype(F32), corner_ref[...].astype(F32),
+        (raws_ref[0], raws_ref[1]), (inverses_ref[0], inverses_ref[1]), weights_ref,
+    )
     order = order_ref[...]
     x = x_ref[...].astype(F32)
     inverse = lax.rsqrt(jnp.mean(x * x, -1, keepdims=True) + EPS)
-    grad = gain_ref[...].reshape(1, width) * grad_normed
-    inner = jnp.mean(x * grad, -1, keepdims=True)
-    grad = (inverse * grad - inverse * inverse * inverse * x * inner).astype(BF16)
-    grad = dot_first(order, grad)
-    out_ref[...] = grad.reshape(out_ref.shape).astype(BF16)
+    grad = gain_ref[...].reshape(1, x.shape[1]) * grad_normed
+    mean = jnp.mean(x * grad, -1, keepdims=True)
+    grad = (inverse * grad - inverse * inverse * inverse * x * mean).astype(BF16)
+    out_ref[...] = dot_first(order, grad).reshape(out_ref.shape).astype(BF16)
 
 
 VMEM = pl.BlockSpec(memory_space=pltpu.VMEM)
@@ -670,18 +683,23 @@
         [((3, head_width, width), BF16)] + tables + [sums_shape] + kept(rows),
         [scales, qkv_weight, qg_both, *kv_rows], micros=1.5,
     )
-    siblings = jnp.stack([kv[2] for kv in kv_rows + kv_away], 0)
-    siblings = pair_swap(siblings, "lon", 0)
-    sums, *away_kept = kernel_call(
-        functools.partial(away_score_kernel, rows), "away_score",
-        [sums_shape] + kept(2 * rows), [scales, weights, sums, *kv_away],
-        micros=20.0,
-    )
+    kv_parts = [[kv_away[(frame - 1) * rows + row] for frame, row in part]
+                for part in away_groups(rows)]
+    early = pair_swap(jnp.stack([kv[2] for kv in kv_rows + kv_parts[0]], 0), "lon", 0)
+    late = pair_swap(jnp.stack([kv[2] for kv in kv_parts[1]], 0), "lon", 0)
+    away_kept = []
+    for which, kvs in enumerate(kv_parts):
+        sums, *made = kernel_call(
+            functools.partial(away_score_kernel, rows, which), "away_score",
+            [sums_shape] + kept(len(kvs)), [scales, weights, sums, *kvs],
+            micros=(1.5, 20.0)[which],
+        )
+        away_kept += made
     half_part = (rows, CELLS, PAIR_WIDTH)
     sibling_part, stats, dq_sibling = kernel_call(
         functools.partial(sibling_kernel, rows), "sibling",
         [(half_part, F32), ((2 * HALF, queries), F32), ((HALF_WIDTH, 2 * CELLS), F32)],
-        [scales, weights, backward, sums, siblings], micros=1.5,
+        [scales, weights, backward, sums, early, late], micros=1.5,
     )
     near_stats, far_stats = frame_swap(stats, 0), frame_swap(stats, 1)
     cross_mid = ((2, HALF, rows * 2 * CELLS, queries), F32)
@@ -689,7 +707,7 @@
     cross_backward, e_mid, p_mid, e_side, p_side = kernel_call(
         functools.partial(cross_score_kernel, rows), "cross_score",
         [((2,) + tables[1][0], BF16), cross_mid, cross_mid, cross_side, cross_side],
-        [scales, *qg_away, *kv_rows, siblings], micros=2.0,
+        [scales, *qg_away, *kv_rows, early], micros=2.0,
         scratch=[pltpu.VMEM((2,) + tables[0][0], BF16)],
     )
     part = (rows, blocks + 1, CELLS, PAIR_WIDTH)
@@ -697,7 +715,8 @@
     own_part, dq_own, dq_other = kernel_call(
         functools.partial(own_back_kernel, rows), "own_back",
         [(part, F32), (packed, F32), (packed, BF16)],
-        [scales, stats, backward, *own_kept, *away_kept, dq_sibling, *kv_rows, *kv_away],
+        [scales, stats, backward, *own_kept, *away_kept, dq_sibling, *kv_rows,
+         *kv_parts[0], *kv_parts[1]],
         micros=2.0,
         scratch=[
             pltpu.VMEM((HALF, 3 * rows * 2 * CELLS, queries), BF16),
@@ -733,11 +752,16 @@
     edge = pair_swap(edge, "lon", 1)
     corner = corner_swap(corner)
     other = pair_swap(to_lat, "lat", 0)
+    halved = ((2, cells, HALF_WIDTH), F32)
+    summed, raws, inverses, weights = kernel_call(
+        own_finish_kernel, "own_finish",
+        [((cells, width), F32), halved, halved, ((3, HALF_WIDTH, width), BF16)],
+        [inner, dq_own, edge, query_raw, query_inverse, key_raw, key_inverse, turned],
+        micros=1.0,
+    )
     (grad_tokens,) = kernel_call(
         finish_kernel, "finish", [(tokens.shape, BF16)],
-        [inner, dq_own, other, edge, corner, query_raw, query_inverse, key_raw, key_inverse,
-         x, order, norm_gain, turned],
-        micros=2.0,
+        [summed, other, corner, raws, inverses, weights, x, order, norm_gain], micros=2.0,
     )
     return grad_tokens
 

time: 38.4 us -> 38.1 us (level)
  waiting for transfers between devices: 7.73 us -> 4.75 us
  starting transfers between devices: 19.5 us -> 21.1 us
  Pallas kernels: 9.01 us -> 10.1 us
    ppermute x8, waiting for transfers between devices: 1.81 us -> 0.02 us  [frame_swap(): return lax.ppermute(array, ('tm', 'lon'), pairs)]
    ppermute x7 -> x8, starting transfers between devices: 9.14 us -> 10.6 us  [pair_swap(): return lax.ppermute(array, axis, pairs)]
    pallas_call x13 -> x15, Pallas kernels: 9.01 us -> 10.1 us  [kernel_call(): pl.pallas_call(body, name=name, out_shape=[jax.ShapeDtypeStruct(shape, dt...]
    ppermute x2, waiting for transfers between devices: 4.29 us -> 3.36 us  [corner_swap(): return lax.ppermute(array, ('lat', 'lon'), pairs)]
    ppermute x7 -> x8, waiting for transfers between devices: 1.64 us -> 1.37 us  [pair_swap(): return lax.ppermute(array, axis, pairs)]
    unnamed x20 -> x15, local copies, waits for them, and re-layouts: 1.73 us -> 1.68 us
  transfers between devices with their start and end apart: 17 -> 18, of which waited for: 6 -> 5; matrix products, arithmetic and copies ran while one was open for 0% -> 0% of each run, Pallas kernels for 16% -> 19%
where the time goes in v5:
time: 38.1 us; the launch traced here: 38 us
  starting transfers between devices  21.1 us (55%)
  Pallas kernels  10.1 us (27%)
  waiting for transfers between devices  4.75 us (12%)
  local copies, waits for them, and re-layouts  1.74 us (5%)
    ppermute x8, starting transfers between devices, pair_swap(): return lax.ppermute(array, axis, pairs)  10.6 us
    pallas_call x15, Pallas kernels, kernel_call(): pl.pallas_call(body, name=name, out_shape=[jax.ShapeDtypeStruct(shape, dt...  10.1 us
    ppermute x8, starting transfers between devices, frame_swap(): return lax.ppermute(array, ('tm', 'lon'), pairs)  8.72 us
    ppermute x2, waiting for transfers between devices, corner_swap(): return lax.ppermute(array, ('lat', 'lon'), pairs)  3.36 us
    ppermute x2, starting transfers between devices, corner_swap(): return lax.ppermute(array, ('lat', 'lon'), pairs)  1.78 us
    unnamed x15, local copies, waits for them, and re-layouts  1.68 us
    ppermute x8, waiting for transfers between devices, pair_swap(): return lax.ppermute(array, axis, pairs)  1.37 us
  transfers between devices with their start and end apart: 18, of which 5 were waited for; matrix products, arithmetic and copies ran while one was open for 0% of the time, Pallas kernels for 19%

profile of v5, /device:TPU:1, one launch (start us, length us, event | category | flops | bytes accessed | tf_op | source)
XLA Modules:
  0.0 38.0 jit_solution(16000973018020483209)
XLA Ops:
  0.0 0.0 copy-start
  0.0 0.0 copy-start.2
  0.0 1.1 %copy-done.2 = bf16[4,4,8,768]{3,2,1,0:T(8,128)(2,1)S(1)} copy-done((bf16[4,4,8,768]{3,2,1,0:T(8,128)(2,1)S(1)}, bf16[4,4,8,768]{3,2,1,0:T(8,128)(2,1)}, u32[]{:S(2)}) %copy-start.2) | copy-done | bytes 196632
  1.1 0.0 copy-start.4
  1.1 0.0 copy-start.5
  1.1 0.2 order.1
  1.3 0.3 copy-done
  1.6 0.3 copy-done.4
  1.9 0.0 copy-done.5
  1.9 0.0 copy-start.1
  1.9 0.0 copy-start.3
  1.9 0.0 copy-start.6
  1.9 0.6 %key_value.1 = (bf16[2,64,384]{2,1,0:T(8,128)(2,1)S(1)}, bf16[2,64,384]{2,1,0:T(8,128)(2,1)S(1)}, bf16[64,384]{1,0:T(8,128)(2,1)S(1)}, bf16[128,768]{1,0:T(8,128...) custom-call(s32[1,1,2]{2,1,0:T(1,128)S(1)} %copy-done.5, bf16[128,768]{1,0:T(8,128)(2,1)S(1)} %get-tuple-element.57.x_ref, ...), custom_call_target="tpu_custom_call" | custom-call | flops 2000000000 | tf_op jit(solution)/shard_map/key_value/pallas_call | solution.py:613
  2.5 2.7 %collective-permute-start.1 = (bf16[64,384]{1,0:T(8,128)(2,1)S(1)}, bf16[64,384]{1,0:T(8,128)(2,1)S(1)}, u32[]{:S(2)}, u32[]{:S(2)}) collective-permute-start(bf16[64,384]{1,0:T(8,128)(2,1)S(1)} %get-tuple-element.63), channel_id=1, source_target_pairs={{0,3},{1,2},{2,1},{3,0},{4,7},{5,6},{6,5},{7,4},{8,11},{9,10},{10,... | collective-permute-start | bytes 147464 | tf_op jit(solution)/shard_map/ppermute | solution.py:36
  5.2 1.2 %collective-permute-start.3 = (bf16[2,64,384]{2,1,0:T(8,128)(2,1)S(1)}, bf16[2,64,384]{2,1,0:T(8,128)(2,1)S(1)}, u32[]{:S(2)}, u32[]{:S(2)}) collective-permute-start(bf16[2,64,384]{2,1,0:T(8,128)(2,1)S(1)} %get-tuple-element.59.kv_other_ref), channel_id=1, source_target_pairs={{0,4},{4,0},{1,5},{5,1},{2,6},{6,2},{3,7},{7,3},{8,12},{12,8},{9,1... | collective-permute-start | bytes 294920 | tf_op jit(solution)/shard_map/ppermute | solution.py:36
  6.4 0.0 copy-done.1
  6.4 0.0 copy-done.3
  6.4 0.0 copy-done.6
  6.4 0.9 %query_grad.1 = (bf16[2,64,384]{2,1,0:T(8,128)(2,1)S(1)}, bf16[2,64,384]{2,1,0:T(8,128)(2,1)S(1)}, bf16[64,384]{1,0:T(8,128)(2,1)S(1)}, f32[128,384]{1,0:T(8,128...) custom-call(f32[6]{0:T(128)S(1)} %copy-done.6, bf16[128,128]{1,0:T(8,128)(2,1)S(1)} %get-tuple-element.56.order_ref, ...), custom_call_target="tpu_custom_call" | custom-call | flops 5000000000 | tf_op jit(solution)/shard_map/query_grad/pallas_call | solution.py:613
  7.3 0.4 %collective-permute-start.2 = (bf16[64,384]{1,0:T(8,128)(2,1)S(1)}, bf16[64,384]{1,0:T(8,128)(2,1)S(1)}, u32[]{:S(2)}, u32[]{:S(2)}) collective-permute-start(bf16[64,384]{1,0:T(8,128)(2,1)S(1)} %get-tuple-element.65), channel_id=1, source_target_pairs={{0,7},{1,6},{2,5},{3,4},{4,3},{5,2},{6,1},{7,0},{8,15},{9,14},{10,... | collective-permute-start | bytes 147464 | tf_op jit(solution)/shard_map/ppermute | solution.py:58
  7.7 1.2 %collective-permute-start = (bf16[2,64,384]{2,1,0:T(8,128)(2,1)S(1)}, bf16[2,64,384]{2,1,0:T(8,128)(2,1)S(1)}, u32[]{:S(2)}, u32[]{:S(2)}) collective-permute-start(bf16[2,64,384]{2,1,0:T(8,128)(2,1)S(1)} %get-tuple-element.62), channel_id=1, source_target_pairs={{0,4},{4,0},{1,5},{5,1},{2,6},{6,2},{3,7},{7,3},{8,12},{12,8},{9,1... | collective-permute-start | bytes 294920 | tf_op jit(solution)/shard_map/ppermute | solution.py:36
  8.9 0.0 collective-permute-done.1
  8.9 0.6 %collective-permute-start.5 = (bf16[3,64,384]{2,1,0:T(8,128)(2,1)S(1)}, bf16[3,64,384]{2,1,0:T(8,128)(2,1)S(1)}, u32[]{:S(2)}, u32[]{:S(2)}) collective-permute-start(bf16[3,64,384]{2,1,0:T(8,128)(2,1)S(1)} %pad_maximum_fusion.1.refs_0_.refs_2_), channel_id=1, source_target_pairs={{0,1},{1,0},{2,3},{3,2},{8,16},{9,17},{10,18},{11,19},{16,8},{17,9... | collective-permute-start | bytes 442376 | tf_op jit(solution)/shard_map/ppermute | solution.py:48
  9.6 2.0 %collective-permute-start.4 = (bf16[3,64,384]{2,1,0:T(8,128)(2,1)S(1)}, bf16[3,64,384]{2,1,0:T(8,128)(2,1)S(1)}, u32[]{:S(2)}, u32[]{:S(2)}) collective-permute-start(bf16[3,64,384]{2,1,0:T(8,128)(2,1)S(1)} %pad_maximum_fusion.1.refs_0_.refs_2_), channel_id=1, source_target_pairs={{0,8},{1,9},{2,10},{3,11},{8,0},{9,1},{10,2},{11,3},{16,24},{17,25... | collective-permute-start | bytes 442376 | tf_op jit(solution)/shard_map/ppermute | solution.py:48
  11.6 0.0 collective-permute-done.3.kv_in
  11.6 0.6 %collective-permute-done.2 = bf16[64,384]{1,0:T(8,128)(2,1)S(1)} collective-permute-done((bf16[64,384]{1,0:T(8,128)(2,1)S(1)}, bf16[64,384]{1,0:T(8,128)(2,1)S(1)}, u32[]{:S(2)}, u32[]{:S(2)}) %collective-permute-start.2) | collective-permute-done | bytes 49184 | tf_op jit(solution)/shard_map/ppermute | solution.py:58
  12.3 0.6 %collective-permute-start.7 = (bf16[3,64,384]{2,1,0:T(8,128)(2,1)S(1)}, bf16[3,64,384]{2,1,0:T(8,128)(2,1)S(1)}, u32[]{:S(2)}, u32[]{:S(2)}) collective-permute-start(bf16[3,64,384]{2,1,0:T(8,128)(2,1)S(1)} %pad_maximum_fusion.2.refs_1_.refs_3_), channel_id=1, source_target_pairs={{0,1},{1,0},{2,3},{3,2},{8,16},{9,17},{10,18},{11,19},{16,8},{17,9... | collective-permute-start | bytes 442376 | tf_op jit(solution)/shard_map/ppermute | solution.py:48
  12.8 2.0 %collective-permute-start.6 = (bf16[3,64,384]{2,1,0:T(8,128)(2,1)S(1)}, bf16[3,64,384]{2,1,0:T(8,128)(2,1)S(1)}, u32[]{:S(2)}, u32[]{:S(2)}) collective-permute-start(bf16[3,64,384]{2,1,0:T(8,128)(2,1)S(1)} %pad_maximum_fusion.2.refs_1_.refs_3_), channel_id=1, source_target_pairs={{0,8},{1,9},{2,10},{3,11},{8,0},{9,1},{10,2},{11,3},{16,24},{17,25... | collective-permute-start | bytes 442376 | tf_op jit(solution)/shard_map/ppermute | solution.py:48
  14.9 0.0 collective-permute-done
  14.9 0.3 collective-permute-start.13
  15.2 0.9 %own_score.1 = (bf16[3,384,768]{2,1,0:T(8,128)(2,1)S(1)}, bf16[6,128,256]{2,1,0:T(8,128)(2,1)S(1)}, bf16[6,256,128]{2,1,0:T(8,128)(2,1)S(1)}, f32[6,8,256]{2,1,0...) custom-call(f32[3,256]{1,0:T(4,128)S(1)} %get-tuple-element.60.scale, ...), custom_call_target="tpu_custom_call" | custom-call | flops 1500000000 | tf_op jit(solution)/shard_map/own_score/pallas_call | solution.py:613
  16.1 0.0 collective-permute-done.5.refs_1_.refs_3_
  16.1 1.2 %collective-permute-start.12 = (bf16[4,64,384]{2,1,0:T(8,128)(2,1)S(1)}, bf16[4,64,384]{2,1,0:T(8,128)(2,1)S(1)}, u32[]{:S(2)}, u32[]{:S(2)}) collective-permute-start(bf16[4,64,384]{2,1,0:T(8,128)(2,1)S(1)} %constant_dynamic-update-slice_fusion.qg_ref), channel_id=1, source_target_pairs={{0,8},{1,9},{2,10},{3,11},{8,0},{9,1},{10,2},{11,3},{16,24},{17,25... | collective-permute-start | bytes 589832 | tf_op jit(solution)/shard_map/ppermute | solution.py:48
  17.3 0.0 collective-permute-done.4.refs_0_.refs_2_
  17.4 1.3 %collective-permute-start.8 = (bf16[4,64,384]{2,1,0:T(8,128)(2,1)S(1)}, bf16[4,64,384]{2,1,0:T(8,128)(2,1)S(1)}, u32[]{:S(2)}, u32[]{:S(2)}) collective-permute-start(bf16[4,64,384]{2,1,0:T(8,128)(2,1)S(1)} %pad_maximum_fusion), channel_id=1, source_target_pairs={{0,1},{1,0},{2,3},{3,2},{4,5},{5,4},{6,7},{7,6},{8,9},{9,8},{10,11... | collective-permute-start | bytes 589832 | tf_op jit(solution)/shard_map/ppermute | solution.py:36
  18.7 0.4 %away_score.2 = (f32[6,8,256]{2,1,0:T(8,128)S(1)}, f32[3,256,256]{2,1,0:T(8,128)S(1)}, f32[3,256,256]{2,1,0:T(8,128)S(1)}, f32[3,128,128]{2,1,0:T(8,128)S(1)}, f32[3,128,128]{2,1,0:T(8,128)S(1)}) custom-call(f32[3,256]{1,0:T(4,128)S(1)} %get-tuple-element.60.scale_ref, bf16[6,128,256]{2,1,0:T(8,128)(2,1)S(1)} %get-tuple-element.66.weights, ...), custom_call_target="tpu_custom_call" | custom-call | flops 1500000000 | tf_op jit(solution)/shard_map/away_score/pallas_call | solution.py:613
  19.1 0.0 collective-permute-done.7.refs_1_.refs_5_
  19.2 0.0 collective-permute-done.6.refs_0_.refs_4_
  19.2 0.7 %collective-permute-start.9 = (bf16[2,64,384]{2,1,0:T(8,128)(2,1)S(1)}, bf16[2,64,384]{2,1,0:T(8,128)(2,1)S(1)}, u32[]{:S(2)}, u32[]{:S(2)}) collective-permute-start(bf16[2,64,384]{2,1,0:T(8,128)(2,1)S(1)} %pad_maximum_fusion.3), channel_id=1, source_target_pairs={{0,1},{1,0},{2,3},{3,2},{4,5},{5,4},{6,7},{7,6},{8,9},{9,8},{10,11... | collective-permute-start | bytes 294920 | tf_op jit(solution)/shard_map/ppermute | solution.py:36
  19.9 0.4 %away_score.3 = (f32[6,8,256]{2,1,0:T(8,128)S(1)}, f32[3,256,256]{2,1,0:T(8,128)S(1)}, f32[3,256,256]{2,1,0:T(8,128)S(1)}, f32[3,128,128]{2,1,0:T(8,128)S(1)}, f32[3,128,128]{2,1,0:T(8,128)S(1)}) custom-call(f32[3,256]{1,0:T(4,128)S(1)} %get-tuple-element.60.scale_ref, bf16[6,128,256]{2,1,0:T(8,128)(2,1)S(1)} %get-tuple-element.66.weights, ...), custom_call_target="tpu_custom_call" | custom-call | flops 20000000000 | tf_op jit(solution)/shard_map/away_score/pallas_call | solution.py:613
  20.4 0.5 %collective-permute-done.9.late_ref = bf16[2,64,384]{2,1,0:T(8,128)(2,1)S(1)} collective-permute-done((bf16[2,64,384]{2,1,0:T(8,128)(2,1)S(1)}, bf16[2,64,384]{2,1,0:T(8,128)(2,1)S(1)}, u32[]{:S(2)}, u32[]{:S(2)}) %collective-permute-start.9) | collective-permute-done | bytes 98336 | tf_op jit(solution)/shard_map/ppermute | solution.py:36
  20.9 0.0 collective-permute-done.8.early_ref.refs_4_
  20.9 0.7 %sibling.1 = (f32[2,64,384]{2,1,0:T(8,128)S(1)}, f32[6,256]{1,0:T(8,128)S(1)}, f32[192,128]{1,0:T(8,128)S(1)}) custom-call(f32[3,256]{1,0:T(4,128)S(1)} %get-tuple-element.60.scale_ref, bf16[6,128,256]{2,1,0:T(8,128)(2,1)S(1)} %get-tuple-element.66.weights, bf16[6,256,128]{2,1,0:T(8,128)(2,1)S(1)} %get-tuple-element.67.backward, ...), custom_call_target="tpu_custom_call" | custom-call | flops 1500000000 | tf_op jit(solution)/shard_map/sibling/pallas_call | solution.py:613
  21.6 0.4 %collective-permute-start.11 = (f32[6,256]{1,0:T(8,128)S(1)}, f32[6,256]{1,0:T(8,128)S(1)}, u32[]{:S(2)}, u32[]{:S(2)}) collective-permute-start(f32[6,256]{1,0:T(8,128)S(1)} %get-tuple-element.71.stats_ref), channel_id=1, source_target_pairs={{0,1},{1,0},{2,3},{3,2},{8,16},{9,17},{10,18},{11,19},{16,8},{17,9... | collective-permute-start | bytes 18440 | tf_op jit(solution)/shard_map/ppermute | solution.py:48
  22.0 1.5 %collective-permute-start.10 = (f32[6,256]{1,0:T(8,128)S(1)}, f32[6,256]{1,0:T(8,128)S(1)}, u32[]{:S(2)}, u32[]{:S(2)}) collective-permute-start(f32[6,256]{1,0:T(8,128)S(1)} %get-tuple-element.71.stats_ref), channel_id=1, source_target_pairs={{0,8},{1,9},{2,10},{3,11},{8,0},{9,1},{10,2},{11,3},{16,24},{17,25... | collective-permute-start | bytes 18440 | tf_op jit(solution)/shard_map/ppermute | solution.py:48
  23.5 0.0 collective-permute-done.13.refs_1_
  23.5 0.0 collective-permute-done.12.refs_0_
  23.5 0.9 %cross_score.1 = (bf16[2,6,256,128]{3,2,1,0:T(8,128)(2,1)S(1)}, f32[2,3,256,256]{3,2,1,0:T(8,128)S(1)}, f32[2,3,256,256]{3,2,1,0:T(8,128)S(1)}, f32[2,2,3,128,12...) custom-call(f32[3,256]{1,0:T(4,128)S(1)} %get-tuple-element.60.scale_ref, ...), custom_call_target="tpu_custom_call" | custom-call | flops 2000000000 | tf_op jit(solution)/shard_map/cross_score/pallas_call | solution.py:613
  24.4 1.2 %own_back.1 = (f32[2,3,64,384]{3,2,1,0:T(8,128)S(1)}, f32[64,384]{1,0:T(8,128)S(1)}, bf16[64,384]{1,0:T(8,128)(2,1)S(1)}) custom-call(f32[3,256]{1,0:T(4,128)S(1)} %get-tuple-element.60.scale_ref, f32[6,256]{1,0:T(8,128)S(1)} %get-tuple-element.71.stats_ref, bf16[6,256,128]{2,1,0:T(8,128)(2,1)S(1)} %get-tuple-element.67.backward, ...), custom_call_target="tpu_custom_call" | custom-call | flops 2000000000 | tf_op jit(solution)/shard_map/own_back/pallas_call | solution.py:613
  25.6 0.0 collective-permute-done.11.far_stats
  25.6 0.0 collective-permute-done.10.near_stats
  25.6 0.3 cross_sibling.1
  25.9 1.0 %collective-permute-start.14 = (bf16[2,64,384]{2,1,0:T(8,128)(2,1)S(1)}, bf16[2,64,384]{2,1,0:T(8,128)(2,1)S(1)}, u32[]{:S(2)}, u32[]{:S(2)}) collective-permute-start(bf16[2,64,384]{2,1,0:T(8,128)(2,1)S(1)} %cross_sibling.1), channel_id=1, source_target_pairs={{0,1},{1,0},{2,3},{3,2},{4,5},{5,4},{6,7},{7,6},{8,9},{9,8},{10,11... | collective-permute-start | bytes 294920 | tf_op jit(solution)/shard_map/ppermute | solution.py:36
  26.9 0.8 %cross_back.1.total_ref = f32[2,3,64,384]{3,2,1,0:T(8,128)S(1)} custom-call(f32[3,256]{1,0:T(4,128)S(1)} %get-tuple-element.60.scale_ref, f32[6,256]{1,0:T(8,128)S(1)} %collective-permute-done.10.near_stats, f32[6,256]{1,0:T(8,128)S(1)} %collective-permute-done.11.far_stats, bf16[2,6,256,128]{3,2,1,0:T(8,128)(2,1)S(1)} %get-tuple-element.72.backward, ...), custom_call_target="tpu_custom_call" | custom-call | flops 1500000000 | tf_op jit(solution)/shard_map/cross_back/pallas_call | solution.py:613
  27.7 0.1 collective-permute-done.14.sibling_ref
  27.9 0.2 collective-permute-start.16
  28.1 2.2 %collective-permute-start.15 = (bf16[64,384]{1,0:T(8,128)(2,1)S(1)}, bf16[64,384]{1,0:T(8,128)(2,1)S(1)}, u32[]{:S(2)}, u32[]{:S(2)}) collective-permute-start(bf16[64,384]{1,0:T(8,128)(2,1)S(1)} %get-tuple-element.95), channel_id=1, source_target_pairs={{0,3},{1,2},{2,1},{3,0},{4,7},{5,6},{6,5},{7,4},{8,11},{9,10},{10,... | collective-permute-start | bytes 147464 | tf_op jit(solution)/shard_map/ppermute | solution.py:36
  30.3 1.4 %collective-permute-start.17 = (bf16[64,384]{1,0:T(8,128)(2,1)S(1)}, bf16[64,384]{1,0:T(8,128)(2,1)S(1)}, u32[]{:S(2)}, u32[]{:S(2)}) collective-permute-start(bf16[64,384]{1,0:T(8,128)(2,1)S(1)} %get-tuple-element.103), channel_id=1, source_target_pairs={{0,7},{1,6},{2,5},{3,4},{4,3},{5,2},{6,1},{7,0},{8,15},{9,14},{10,... | collective-permute-start | bytes 147464 | tf_op jit(solution)/shard_map/ppermute | solution.py:58
  31.7 0.7 %collective-permute-done.15.edge_ref = bf16[64,384]{1,0:T(8,128)(2,1)S(1)} collective-permute-done((bf16[64,384]{1,0:T(8,128)(2,1)S(1)}, bf16[64,384]{1,0:T(8,128)(2,1)S(1)}, u32[]{:S(2)}, u32[]{:S(2)}) %collective-permute-start.15) | collective-permute-done | bytes 49184 | tf_op jit(solution)/shard_map/ppermute | solution.py:36
  32.4 1.2 %own_finish.1 = (f32[128,768]{1,0:T(8,128)S(1)}, f32[2,128,192]{2,1,0:T(8,128)S(1)}, f32[2,128,192]{2,1,0:T(8,128)S(1)}, bf16[3,192,768]{2,1,0:T(8,128)(2,1)S(1)}) custom-call(f32[2,64,384]{2,1,0:T(8,128)S(1)} %get-tuple-element.93.inner_ref, f32[64,384]{1,0:T(8,128)S(1)} %get-tuple-element.94.dq_ref, bf16[64,384]{1,0:T(8,128)(2,1)S(1)} %collective-permute-done.15.edge_ref, ...), custom_call_target="tpu_custom_call" | custom-call | flops 1000000000 | tf_op jit(solution)/shard_map/own_finish/pallas_call | solution.py:613
  33.6 2.7 %collective-permute-done.17.corner_ref = bf16[64,384]{1,0:T(8,128)(2,1)S(1)} collective-permute-done((bf16[64,384]{1,0:T(8,128)(2,1)S(1)}, bf16[64,384]{1,0:T(8,128)(2,1)S(1)}, u32[]{:S(2)}, u32[]{:S(2)}) %collective-permute-start.17) | collective-permute-done | bytes 49184 | tf_op jit(solution)/shard_map/ppermute | solution.py:58
  36.3 0.0 collective-permute-done.16.other_ref
  36.3 1.6 %finish.1 = bf16[4,4,8,768]{3,2,1,0:T(8,128)(2,1)} custom-call(f32[128,768]{1,0:T(8,128)S(1)} %get-tuple-element.101.total_ref, bf16[3,64,384]{2,1,0:T(8,128)(2,1)S(1)} %collective-permute-done.16.other_ref, bf16[64,384]{1,0:T(8,128)(2,1)S(1)} %collective-permute-done.17.corner_ref, f32[2,128,192]{2,1,0:T(8,128)S(1)} %get-tuple-element.104.raws_ref, ...), custom_call_target="tpu_custom_call" | custom-call | flops 2000000000 | tf_op jit(solution)/shard_map/finish/pallas_call | solution.py:613
  (14 shorter events, 0.2 us)
Async XLA Ops:
  0.0 1.6 %copy-start = (bf16[3,768,384]{2,1,0:T(8,128)(2,1)S(1)}, bf16[3,768,384]{2,1,0:T(8,128)(2,1)}, u32[]{:S(2)}) copy-start(bf16[3,768,384]{2,1,0:T(8,128)(2,1)} %qkv_ref.5) | copy-start | bytes 5308420
  0.0 1.1 %copy-start.2 = (bf16[4,4,8,768]{3,2,1,0:T(8,128)(2,1)S(1)}, bf16[4,4,8,768]{3,2,1,0:T(8,128)(2,1)}, u32[]{:S(2)}) copy-start(bf16[4,4,8,768]{3,2,1,0:T(8,128)(2,1)} %tokens_ref.1) | copy-start | bytes 589828
  1.1 0.8 %copy-start.4 = (f32[768]{0:T(1024)S(1)}, f32[768]{0:T(1024)}, u32[]{:S(2)}) copy-start(f32[768]{0:T(1024)} %gain_ref.3) | copy-start | bytes 9220
  1.1 0.8 %copy-start.5 = (s32[1,1,2]{2,1,0:T(1,128)S(1)}, s32[1,1,2]{2,1,0:T(1,128)}, u32[]{:S(2)}) copy-start(s32[1,1,2]{2,1,0:T(1,128)} %count_ref.1) | copy-start | bytes 28
  1.9 4.5 %copy-start.1 = (bf16[384,768]{1,0:T(8,128)(2,1)S(1)}, bf16[384,768]{1,0:T(8,128)(2,1)}, u32[]{:S(2)}) copy-start(bf16[384,768]{1,0:T(8,128)(2,1)} %out_weight_ref.1) | copy-start | bytes 1769476
  1.9 4.5 %copy-start.3 = (bf16[4,4,8,768]{3,2,1,0:T(8,128)(2,1)S(1)}, bf16[4,4,8,768]{3,2,1,0:T(8,128)(2,1)}, u32[]{:S(2)}) copy-start(bf16[4,4,8,768]{3,2,1,0:T(8,128)(2,1)} %grad_ref.1) | copy-start | bytes 589828
  1.9 4.5 %copy-start.6 = (f32[6]{0:T(128)S(1)}, f32[6]{0:T(128)}, u32[]{:S(2)}) copy-start(f32[6]{0:T(128)} %scale_in.1) | copy-start | bytes 76
  2.5 6.4 %collective-permute-start.1 = (bf16[64,384]{1,0:T(8,128)(2,1)S(1)}, bf16[64,384]{1,0:T(8,128)(2,1)S(1)}, u32[]{:S(2)}, u32[]{:S(2)}) collective-permute-start(bf16[64,384]{1,0:T(8,128)(2,1)S(1)} %get-tuple-element.63), channel_id=1, source_target_pairs={{0,3},{1,2},{2,1},{3,0},{4,7},{5,6},{6,5},{7,4},{8,11},{9,10},{10,... | collective-permute-start | bytes 147464 | tf_op jit(solution)/shard_map/ppermute | solution.py:36
  5.2 6.4 %collective-permute-start.3 = (bf16[2,64,384]{2,1,0:T(8,128)(2,1)S(1)}, bf16[2,64,384]{2,1,0:T(8,128)(2,1)S(1)}, u32[]{:S(2)}, u32[]{:S(2)}) collective-permute-start(bf16[2,64,384]{2,1,0:T(8,128)(2,1)S(1)} %get-tuple-element.59.kv_other_ref), channel_id=1, source_target_pairs={{0,4},{4,0},{1,5},{5,1},{2,6},{6,2},{3,7},{7,3},{8,12},{12,8},{9,1... | collective-permute-start | bytes 294920 | tf_op jit(solution)/shard_map/ppermute | solution.py:36
  7.3 5.0 %collective-permute-start.2 = (bf16[64,384]{1,0:T(8,128)(2,1)S(1)}, bf16[64,384]{1,0:T(8,128)(2,1)S(1)}, u32[]{:S(2)}, u32[]{:S(2)}) collective-permute-start(bf16[64,384]{1,0:T(8,128)(2,1)S(1)} %get-tuple-element.65), channel_id=1, source_target_pairs={{0,7},{1,6},{2,5},{3,4},{4,3},{5,2},{6,1},{7,0},{8,15},{9,14},{10,... | collective-permute-start | bytes 147464 | tf_op jit(solution)/shard_map/ppermute | solution.py:58
  7.7 7.2 %collective-permute-start = (bf16[2,64,384]{2,1,0:T(8,128)(2,1)S(1)}, bf16[2,64,384]{2,1,0:T(8,128)(2,1)S(1)}, u32[]{:S(2)}, u32[]{:S(2)}) collective-permute-start(bf16[2,64,384]{2,1,0:T(8,128)(2,1)S(1)} %get-tuple-element.62), channel_id=1, source_target_pairs={{0,4},{4,0},{1,5},{5,1},{2,6},{6,2},{3,7},{7,3},{8,12},{12,8},{9,1... | collective-permute-start | bytes 294920 | tf_op jit(solution)/shard_map/ppermute | solution.py:36
  8.9 7.2 %collective-permute-start.5 = (bf16[3,64,384]{2,1,0:T(8,128)(2,1)S(1)}, bf16[3,64,384]{2,1,0:T(8,128)(2,1)S(1)}, u32[]{:S(2)}, u32[]{:S(2)}) collective-permute-start(bf16[3,64,384]{2,1,0:T(8,128)(2,1)S(1)} %pad_maximum_fusion.1.refs_0_.refs_2_), channel_id=1, source_target_pairs={{0,1},{1,0},{2,3},{3,2},{8,16},{9,17},{10,18},{11,19},{16,8},{17,9... | collective-permute-start | bytes 442376 | tf_op jit(solution)/shard_map/ppermute | solution.py:48
  9.6 7.8 %collective-permute-start.4 = (bf16[3,64,384]{2,1,0:T(8,128)(2,1)S(1)}, bf16[3,64,384]{2,1,0:T(8,128)(2,1)S(1)}, u32[]{:S(2)}, u32[]{:S(2)}) collective-permute-start(bf16[3,64,384]{2,1,0:T(8,128)(2,1)S(1)} %pad_maximum_fusion.1.refs_0_.refs_2_), channel_id=1, source_target_pairs={{0,8},{1,9},{2,10},{3,11},{8,0},{9,1},{10,2},{11,3},{16,24},{17,25... | collective-permute-start | bytes 442376 | tf_op jit(solution)/shard_map/ppermute | solution.py:48
  12.3 6.9 %collective-permute-start.7 = (bf16[3,64,384]{2,1,0:T(8,128)(2,1)S(1)}, bf16[3,64,384]{2,1,0:T(8,128)(2,1)S(1)}, u32[]{:S(2)}, u32[]{:S(2)}) collective-permute-start(bf16[3,64,384]{2,1,0:T(8,128)(2,1)S(1)} %pad_maximum_fusion.2.refs_1_.refs_3_), channel_id=1, source_target_pairs={{0,1},{1,0},{2,3},{3,2},{8,16},{9,17},{10,18},{11,19},{16,8},{17,9... | collective-permute-start | bytes 442376 | tf_op jit(solution)/shard_map/ppermute | solution.py:48
  12.8 6.3 %collective-permute-start.6 = (bf16[3,64,384]{2,1,0:T(8,128)(2,1)S(1)}, bf16[3,64,384]{2,1,0:T(8,128)(2,1)S(1)}, u32[]{:S(2)}, u32[]{:S(2)}) collective-permute-start(bf16[3,64,384]{2,1,0:T(8,128)(2,1)S(1)} %pad_maximum_fusion.2.refs_1_.refs_3_), channel_id=1, source_target_pairs={{0,8},{1,9},{2,10},{3,11},{8,0},{9,1},{10,2},{11,3},{16,24},{17,25... | collective-permute-start | bytes 442376 | tf_op jit(solution)/shard_map/ppermute | solution.py:48
  14.9 8.6 %collective-permute-start.13 = (bf16[4,64,384]{2,1,0:T(8,128)(2,1)S(1)}, bf16[4,64,384]{2,1,0:T(8,128)(2,1)S(1)}, u32[]{:S(2)}, u32[]{:S(2)}) collective-permute-start(bf16[4,64,384]{2,1,0:T(8,128)(2,1)S(1)} %constant_dynamic-update-slice_fusion.qg_ref), channel_id=1, source_target_pairs={{0,1},{1,0},{2,3},{3,2},{8,16},{9,17},{10,18},{11,19},{16,8},{17,9... | collective-permute-start | bytes 589832 | tf_op jit(solution)/shard_map/ppermute | solution.py:48
  16.1 7.4 %collective-permute-start.12 = (bf16[4,64,384]{2,1,0:T(8,128)(2,1)S(1)}, bf16[4,64,384]{2,1,0:T(8,128)(2,1)S(1)}, u32[]{:S(2)}, u32[]{:S(2)}) collective-permute-start(bf16[4,64,384]{2,1,0:T(8,128)(2,1)S(1)} %constant_dynamic-update-slice_fusion.qg_ref), channel_id=1, source_target_pairs={{0,8},{1,9},{2,10},{3,11},{8,0},{9,1},{10,2},{11,3},{16,24},{17,25... | collective-permute-start | bytes 589832 | tf_op jit(solution)/shard_map/ppermute | solution.py:48
  17.4 3.5 %collective-permute-start.8 = (bf16[4,64,384]{2,1,0:T(8,128)(2,1)S(1)}, bf16[4,64,384]{2,1,0:T(8,128)(2,1)S(1)}, u32[]{:S(2)}, u32[]{:S(2)}) collective-permute-start(bf16[4,64,384]{2,1,0:T(8,128)(2,1)S(1)} %pad_maximum_fusion), channel_id=1, source_target_pairs={{0,1},{1,0},{2,3},{3,2},{4,5},{5,4},{6,7},{7,6},{8,9},{9,8},{10,11... | collective-permute-start | bytes 589832 | tf_op jit(solution)/shard_map/ppermute | solution.py:36
  19.2 1.7 %collective-permute-start.9 = (bf16[2,64,384]{2,1,0:T(8,128)(2,1)S(1)}, bf16[2,64,384]{2,1,0:T(8,128)(2,1)S(1)}, u32[]{:S(2)}, u32[]{:S(2)}) collective-permute-start(bf16[2,64,384]{2,1,0:T(8,128)(2,1)S(1)} %pad_maximum_fusion.3), channel_id=1, source_target_pairs={{0,1},{1,0},{2,3},{3,2},{4,5},{5,4},{6,7},{7,6},{8,9},{9,8},{10,11... | collective-permute-start | bytes 294920 | tf_op jit(solution)/shard_map/ppermute | solution.py:36
  21.6 4.0 %collective-permute-start.11 = (f32[6,256]{1,0:T(8,128)S(1)}, f32[6,256]{1,0:T(8,128)S(1)}, u32[]{:S(2)}, u32[]{:S(2)}) collective-permute-start(f32[6,256]{1,0:T(8,128)S(1)} %get-tuple-element.71.stats_ref), channel_id=1, source_target_pairs={{0,1},{1,0},{2,3},{3,2},{8,16},{9,17},{10,18},{11,19},{16,8},{17,9... | collective-permute-start | bytes 18440 | tf_op jit(solution)/shard_map/ppermute | solution.py:48
  22.0 3.6 %collective-permute-start.10 = (f32[6,256]{1,0:T(8,128)S(1)}, f32[6,256]{1,0:T(8,128)S(1)}, u32[]{:S(2)}, u32[]{:S(2)}) collective-permute-start(f32[6,256]{1,0:T(8,128)S(1)} %get-tuple-element.71.stats_ref), channel_id=1, source_target_pairs={{0,8},{1,9},{2,10},{3,11},{8,0},{9,1},{10,2},{11,3},{16,24},{17,25... | collective-permute-start | bytes 18440 | tf_op jit(solution)/shard_map/ppermute | solution.py:48
  25.9 1.9 %collective-permute-start.14 = (bf16[2,64,384]{2,1,0:T(8,128)(2,1)S(1)}, bf16[2,64,384]{2,1,0:T(8,128)(2,1)S(1)}, u32[]{:S(2)}, u32[]{:S(2)}) collective-permute-start(bf16[2,64,384]{2,1,0:T(8,128)(2,1)S(1)} %cross_sibling.1), channel_id=1, source_target_pairs={{0,1},{1,0},{2,3},{3,2},{4,5},{5,4},{6,7},{7,6},{8,9},{9,8},{10,11... | collective-permute-start | bytes 294920 | tf_op jit(solution)/shard_map/ppermute | solution.py:36
  27.9 8.4 %collective-permute-start.16 = (bf16[3,64,384]{2,1,0:T(8,128)(2,1)S(1)}, bf16[3,64,384]{2,1,0:T(8,128)(2,1)S(1)}, u32[]{:S(2)}, u32[]{:S(2)}) collective-permute-start(bf16[3,64,384]{2,1,0:T(8,128)(2,1)S(1)} %get-tuple-element.102), channel_id=1, source_target_pairs={{0,4},{4,0},{1,5},{5,1},{2,6},{6,2},{3,7},{7,3},{8,12},{12,8},{9,1... | collective-permute-start | bytes 442376 | tf_op jit(solution)/shard_map/ppermute | solution.py:36
  28.1 4.3 %collective-permute-start.15 = (bf16[64,384]{1,0:T(8,128)(2,1)S(1)}, bf16[64,384]{1,0:T(8,128)(2,1)S(1)}, u32[]{:S(2)}, u32[]{:S(2)}) collective-permute-start(bf16[64,384]{1,0:T(8,128)(2,1)S(1)} %get-tuple-element.95), channel_id=1, source_target_pairs={{0,3},{1,2},{2,1},{3,0},{4,7},{5,6},{6,5},{7,4},{8,11},{9,10},{10,... | collective-permute-start | bytes 147464 | tf_op jit(solution)/shard_map/ppermute | solution.py:36
  30.3 6.0 %collective-permute-start.17 = (bf16[64,384]{1,0:T(8,128)(2,1)S(1)}, bf16[64,384]{1,0:T(8,128)(2,1)S(1)}, u32[]{:S(2)}, u32[]{:S(2)}) collective-permute-start(bf16[64,384]{1,0:T(8,128)(2,1)S(1)} %get-tuple-element.103), channel_id=1, source_target_pairs={{0,7},{1,6},{2,5},{3,4},{4,3},{5,2},{6,1},{7,0},{8,15},{9,14},{10,... | collective-permute-start | bytes 147464 | tf_op jit(solution)/shard_map/ppermute | solution.py:58

commit v6 on v5

--- a/solution.py
+++ b/solution.py
@@ -652,8 +652,9 @@
         [logit_scale, order, normed, grad_out, qkv_weight, out_weight, kv_made], micros=5.0,
     )
     corner = corner_swap(corner)
+    (kv_other,) = kernel_call(join_kernel, "join", [qg_shape], [kv_other], micros=3.0)
+    qg_other, kv_other = lax.optimization_barrier((qg_other, kv_other))
     qg_other = pair_swap(qg_other, "lat", 0)
-    (kv_other,) = kernel_call(join_kernel, "join", [qg_shape], [kv_other], micros=3.0)
     kv_rows = [
         jnp.concatenate([edge[None], kv_own], 0),
         jnp.concatenate([corner[None], kv_other], 0),

time: 38.1 us -> 36.8 us (0.966)
  waiting for transfers between devices: 4.75 us -> 3.8 us
  starting transfers between devices: 21.1 us -> 20.5 us
    ppermute x2, waiting for transfers between devices: 3.36 us -> 0.39 us  [corner_swap(): return lax.ppermute(array, ('lat', 'lon'), pairs)]
    ppermute x8, waiting for transfers between devices: 1.37 us -> 3.39 us  [pair_swap(): return lax.ppermute(array, axis, pairs)]
    ppermute x2, starting transfers between devices: 1.78 us -> 1.14 us  [corner_swap(): return lax.ppermute(array, ('lat', 'lon'), pairs)]
    ppermute x8, starting transfers between devices: 8.72 us -> 9.12 us  [frame_swap(): return lax.ppermute(array, ('tm', 'lon'), pairs)]
  transfers between devices with their start and end apart: 18 -> 18, of which waited for: 5 -> 5; matrix products, arithmetic and copies ran while one was open for 0% -> 0% of each run, Pallas kernels for 19% -> 20%
where the time goes in v6:
time: 36.8 us; the launch traced here: 36.4 us
  starting transfers between devices  20.5 us (56%)
  Pallas kernels  10.1 us (27%)
  waiting for transfers between devices  3.8 us (10%)
  local copies, waits for them, and re-layouts  1.74 us (5%)
    ppermute x8, starting transfers between devices, pair_swap(): return lax.ppermute(array, axis, pairs)  10.2 us
    pallas_call x15, Pallas kernels, kernel_call(): pl.pallas_call(body, name=name, out_shape=[jax.ShapeDtypeStruct(shape, dt...  10.1 us
    ppermute x8, starting transfers between devices, frame_swap(): return lax.ppermute(array, ('tm', 'lon'), pairs)  9.12 us
    ppermute x8, waiting for transfers between devices, pair_swap(): return lax.ppermute(array, axis, pairs)  3.39 us
    unnamed x15, local copies, waits for them, and re-layouts  1.68 us
    ppermute x2, starting transfers between devices, corner_swap(): return lax.ppermute(array, ('lat', 'lon'), pairs)  1.14 us
  transfers between devices with their start and end apart: 18, of which 5 were waited for; matrix products, arithmetic and copies ran while one was open for 0% of the time, Pallas kernels for 20%

profile of v6, /device:TPU:1, one launch (start us, length us, event | category | flops | bytes accessed | tf_op | source)
XLA Modules:
  0.0 36.4 jit_solution(652579338718782074)
XLA Ops:
  0.0 0.0 copy-start
  0.0 0.0 copy-start.2
  0.0 1.1 %copy-done.2 = bf16[4,4,8,768]{3,2,1,0:T(8,128)(2,1)S(1)} copy-done((bf16[4,4,8,768]{3,2,1,0:T(8,128)(2,1)S(1)}, bf16[4,4,8,768]{3,2,1,0:T(8,128)(2,1)}, u32[]{:S(2)}) %copy-start.2) | copy-done | bytes 196632
  1.1 0.0 copy-start.4
  1.1 0.0 copy-start.5
  1.1 0.2 order.1
  1.3 0.3 copy-done
  1.6 0.3 copy-done.4
  1.9 0.0 copy-done.5
  1.9 0.0 copy-start.1
  1.9 0.0 copy-start.3
  1.9 0.0 copy-start.6
  1.9 0.6 %key_value.1 = (bf16[2,64,384]{2,1,0:T(8,128)(2,1)S(1)}, bf16[2,64,384]{2,1,0:T(8,128)(2,1)S(1)}, bf16[64,384]{1,0:T(8,128)(2,1)S(1)}, bf16[128,768]{1,0:T(8,128...) custom-call(s32[1,1,2]{2,1,0:T(1,128)S(1)} %copy-done.5, bf16[128,768]{1,0:T(8,128)(2,1)S(1)} %get-tuple-element.59.x_ref, ...), custom_call_target="tpu_custom_call" | custom-call | flops 2000000000 | tf_op jit(solution)/shard_map/key_value/pallas_call | solution.py:613
  2.5 2.7 %collective-permute-start.2 = (bf16[64,384]{1,0:T(8,128)(2,1)S(1)}, bf16[64,384]{1,0:T(8,128)(2,1)S(1)}, u32[]{:S(2)}, u32[]{:S(2)}) collective-permute-start(bf16[64,384]{1,0:T(8,128)(2,1)S(1)} %get-tuple-element.66), channel_id=1, source_target_pairs={{0,3},{1,2},{2,1},{3,0},{4,7},{5,6},{6,5},{7,4},{8,11},{9,10},{10,... | collective-permute-start | bytes 147464 | tf_op jit(solution)/shard_map/ppermute | solution.py:36
  5.2 1.2 %collective-permute-start = (bf16[2,64,384]{2,1,0:T(8,128)(2,1)S(1)}, bf16[2,64,384]{2,1,0:T(8,128)(2,1)S(1)}, u32[]{:S(2)}, u32[]{:S(2)}) collective-permute-start(bf16[2,64,384]{2,1,0:T(8,128)(2,1)S(1)} %get-tuple-element.61.kv_other_ref), channel_id=1, source_target_pairs={{0,4},{4,0},{1,5},{5,1},{2,6},{6,2},{3,7},{7,3},{8,12},{12,8},{9,1... | collective-permute-start | bytes 294920 | tf_op jit(solution)/shard_map/ppermute | solution.py:36
  6.4 0.0 copy-done.1
  6.4 0.0 copy-done.3
  6.4 0.0 copy-done.6
  6.4 0.9 %query_grad.1 = (bf16[2,64,384]{2,1,0:T(8,128)(2,1)S(1)}, bf16[2,64,384]{2,1,0:T(8,128)(2,1)S(1)}, bf16[64,384]{1,0:T(8,128)(2,1)S(1)}, f32[128,384]{1,0:T(8,128...) custom-call(f32[6]{0:T(128)S(1)} %copy-done.6, bf16[128,128]{1,0:T(8,128)(2,1)S(1)} %get-tuple-element.58.order_ref, ...), custom_call_target="tpu_custom_call" | custom-call | flops 5000000000 | tf_op jit(solution)/shard_map/query_grad/pallas_call | solution.py:613
  7.3 0.4 %collective-permute-start.3 = (bf16[64,384]{1,0:T(8,128)(2,1)S(1)}, bf16[64,384]{1,0:T(8,128)(2,1)S(1)}, u32[]{:S(2)}, u32[]{:S(2)}) collective-permute-start(bf16[64,384]{1,0:T(8,128)(2,1)S(1)} %get-tuple-element.68), channel_id=1, source_target_pairs={{0,7},{1,6},{2,5},{3,4},{4,3},{5,2},{6,1},{7,0},{8,15},{9,14},{10,... | collective-permute-start | bytes 147464 | tf_op jit(solution)/shard_map/ppermute | solution.py:58
  7.7 0.0 collective-permute-done.2
  7.7 0.1 collective-permute-start.5
  7.8 2.6 %collective-permute-start.4 = (bf16[3,64,384]{2,1,0:T(8,128)(2,1)S(1)}, bf16[3,64,384]{2,1,0:T(8,128)(2,1)S(1)}, u32[]{:S(2)}, u32[]{:S(2)}) collective-permute-start(bf16[3,64,384]{2,1,0:T(8,128)(2,1)S(1)} %pad_maximum_fusion.1.refs_0_.refs_2_), channel_id=1, source_target_pairs={{0,8},{1,9},{2,10},{3,11},{8,0},{9,1},{10,2},{11,3},{16,24},{17,25... | collective-permute-start | bytes 442376 | tf_op jit(solution)/shard_map/ppermute | solution.py:48
  10.4 0.0 collective-permute-done.kv_in
  10.4 1.3 %collective-permute-start.1 = (bf16[2,64,384]{2,1,0:T(8,128)(2,1)S(1)}, bf16[2,64,384]{2,1,0:T(8,128)(2,1)S(1)}, u32[]{:S(2)}, u32[]{:S(2)}) collective-permute-start(bf16[2,64,384]{2,1,0:T(8,128)(2,1)S(1)} %get-tuple-element.65), channel_id=1, source_target_pairs={{0,4},{4,0},{1,5},{5,1},{2,6},{6,2},{3,7},{7,3},{8,12},{12,8},{9,1... | collective-permute-start | bytes 294920 | tf_op jit(solution)/shard_map/ppermute | solution.py:36
  11.7 0.1 collective-permute-done.3
  11.8 1.1 %collective-permute-start.7 = (bf16[3,64,384]{2,1,0:T(8,128)(2,1)S(1)}, bf16[3,64,384]{2,1,0:T(8,128)(2,1)S(1)}, u32[]{:S(2)}, u32[]{:S(2)}) collective-permute-start(bf16[3,64,384]{2,1,0:T(8,128)(2,1)S(1)} %pad_maximum_fusion.2.refs_1_.refs_3_), channel_id=1, source_target_pairs={{0,1},{1,0},{2,3},{3,2},{8,16},{9,17},{10,18},{11,19},{16,8},{17,9... | collective-permute-start | bytes 442376 | tf_op jit(solution)/shard_map/ppermute | solution.py:48
  13.0 1.5 %collective-permute-start.6 = (bf16[3,64,384]{2,1,0:T(8,128)(2,1)S(1)}, bf16[3,64,384]{2,1,0:T(8,128)(2,1)S(1)}, u32[]{:S(2)}, u32[]{:S(2)}) collective-permute-start(bf16[3,64,384]{2,1,0:T(8,128)(2,1)S(1)} %pad_maximum_fusion.2.refs_1_.refs_3_), channel_id=1, source_target_pairs={{0,8},{1,9},{2,10},{3,11},{8,0},{9,1},{10,2},{11,3},{16,24},{17,25... | collective-permute-start | bytes 442376 | tf_op jit(solution)/shard_map/ppermute | solution.py:48
  14.4 0.0 collective-permute-done.1
  14.5 1.6 %collective-permute-start.13 = (bf16[4,64,384]{2,1,0:T(8,128)(2,1)S(1)}, bf16[4,64,384]{2,1,0:T(8,128)(2,1)S(1)}, u32[]{:S(2)}, u32[]{:S(2)}) collective-permute-start(bf16[4,64,384]{2,1,0:T(8,128)(2,1)S(1)} %constant_dynamic-update-slice_fusion.qg_ref), channel_id=1, source_target_pairs={{0,1},{1,0},{2,3},{3,2},{8,16},{9,17},{10,18},{11,19},{16,8},{17,9... | collective-permute-start | bytes 589832 | tf_op jit(solution)/shard_map/ppermute | solution.py:48
  16.1 0.0 collective-permute-done.5.refs_1_.refs_3_
  16.1 0.3 collective-permute-start.12
  16.4 0.0 collective-permute-done.4.refs_0_.refs_2_
  16.4 2.0 %collective-permute-start.8 = (bf16[4,64,384]{2,1,0:T(8,128)(2,1)S(1)}, bf16[4,64,384]{2,1,0:T(8,128)(2,1)S(1)}, u32[]{:S(2)}, u32[]{:S(2)}) collective-permute-start(bf16[4,64,384]{2,1,0:T(8,128)(2,1)S(1)} %pad_maximum_fusion), channel_id=1, source_target_pairs={{0,1},{1,0},{2,3},{3,2},{4,5},{5,4},{6,7},{7,6},{8,9},{9,8},{10,11... | collective-permute-start | bytes 589832 | tf_op jit(solution)/shard_map/ppermute | solution.py:36
  18.5 0.9 %own_score.1 = (bf16[3,384,768]{2,1,0:T(8,128)(2,1)S(1)}, bf16[6,128,256]{2,1,0:T(8,128)(2,1)S(1)}, bf16[6,256,128]{2,1,0:T(8,128)(2,1)S(1)}, f32[6,8,256]{2,1,0...) custom-call(f32[3,256]{1,0:T(4,128)S(1)} %get-tuple-element.62.scale, ...), custom_call_target="tpu_custom_call" | custom-call | flops 1500000000 | tf_op jit(solution)/shard_map/own_score/pallas_call | solution.py:613
  19.4 0.4 %away_score.2 = (f32[6,8,256]{2,1,0:T(8,128)S(1)}, f32[3,256,256]{2,1,0:T(8,128)S(1)}, f32[3,256,256]{2,1,0:T(8,128)S(1)}, f32[3,128,128]{2,1,0:T(8,128)S(1)}, f32[3,128,128]{2,1,0:T(8,128)S(1)}) custom-call(f32[3,256]{1,0:T(4,128)S(1)} %get-tuple-element.62.scale_ref, bf16[6,128,256]{2,1,0:T(8,128)(2,1)S(1)} %get-tuple-element.70.weights, ...), custom_call_target="tpu_custom_call" | custom-call | flops 1500000000 | tf_op jit(solution)/shard_map/away_score/pallas_call | solution.py:613
  19.8 0.0 collective-permute-done.7.refs_1_.refs_5_
  19.8 0.0 collective-permute-done.6.refs_0_.refs_4_
  19.9 0.1 collective-permute-start.9
  19.9 0.4 %away_score.3 = (f32[6,8,256]{2,1,0:T(8,128)S(1)}, f32[3,256,256]{2,1,0:T(8,128)S(1)}, f32[3,256,256]{2,1,0:T(8,128)S(1)}, f32[3,128,128]{2,1,0:T(8,128)S(1)}, f32[3,128,128]{2,1,0:T(8,128)S(1)}) custom-call(f32[3,256]{1,0:T(4,128)S(1)} %get-tuple-element.62.scale_ref, bf16[6,128,256]{2,1,0:T(8,128)(2,1)S(1)} %get-tuple-element.70.weights, ...), custom_call_target="tpu_custom_call" | custom-call | flops 20000000000 | tf_op jit(solution)/shard_map/away_score/pallas_call | solution.py:613
  20.4 0.9 %collective-permute-done.9.late_ref = bf16[2,64,384]{2,1,0:T(8,128)(2,1)S(1)} collective-permute-done((bf16[2,64,384]{2,1,0:T(8,128)(2,1)S(1)}, bf16[2,64,384]{2,1,0:T(8,128)(2,1)S(1)}, u32[]{:S(2)}, u32[]{:S(2)}) %collective-permute-start.9) | collective-permute-done | bytes 98336 | tf_op jit(solution)/shard_map/ppermute | solution.py:36
  21.2 0.0 collective-permute-done.8.early_ref.refs_4_
  21.2 0.7 %sibling.1 = (f32[2,64,384]{2,1,0:T(8,128)S(1)}, f32[6,256]{1,0:T(8,128)S(1)}, f32[192,128]{1,0:T(8,128)S(1)}) custom-call(f32[3,256]{1,0:T(4,128)S(1)} %get-tuple-element.62.scale_ref, bf16[6,128,256]{2,1,0:T(8,128)(2,1)S(1)} %get-tuple-element.70.weights, bf16[6,256,128]{2,1,0:T(8,128)(2,1)S(1)} %get-tuple-element.71.backward, ...), custom_call_target="tpu_custom_call" | custom-call | flops 1500000000 | tf_op jit(solution)/shard_map/sibling/pallas_call | solution.py:613
  21.9 0.2 collective-permute-start.11
  22.1 1.7 %collective-permute-start.10 = (f32[6,256]{1,0:T(8,128)S(1)}, f32[6,256]{1,0:T(8,128)S(1)}, u32[]{:S(2)}, u32[]{:S(2)}) collective-permute-start(f32[6,256]{1,0:T(8,128)S(1)} %get-tuple-element.75.stats_ref), channel_id=1, source_target_pairs={{0,8},{1,9},{2,10},{3,11},{8,0},{9,1},{10,2},{11,3},{16,24},{17,25... | collective-permute-start | bytes 18440 | tf_op jit(solution)/shard_map/ppermute | solution.py:48
  23.9 0.0 collective-permute-done.13.refs_1_
  23.9 0.0 collective-permute-done.12.refs_0_
  23.9 0.9 %cross_score.1 = (bf16[2,6,256,128]{3,2,1,0:T(8,128)(2,1)S(1)}, f32[2,3,256,256]{3,2,1,0:T(8,128)S(1)}, f32[2,3,256,256]{3,2,1,0:T(8,128)S(1)}, f32[2,2,3,128,12...) custom-call(f32[3,256]{1,0:T(4,128)S(1)} %get-tuple-element.62.scale_ref, ...), custom_call_target="tpu_custom_call" | custom-call | flops 2000000000 | tf_op jit(solution)/shard_map/cross_score/pallas_call | solution.py:613
  24.8 1.2 %own_back.1 = (f32[2,3,64,384]{3,2,1,0:T(8,128)S(1)}, f32[64,384]{1,0:T(8,128)S(1)}, bf16[64,384]{1,0:T(8,128)(2,1)S(1)}) custom-call(f32[3,256]{1,0:T(4,128)S(1)} %get-tuple-element.62.scale_ref, f32[6,256]{1,0:T(8,128)S(1)} %get-tuple-element.75.stats_ref, bf16[6,256,128]{2,1,0:T(8,128)(2,1)S(1)} %get-tuple-element.71.backward, ...), custom_call_target="tpu_custom_call" | custom-call | flops 2000000000 | tf_op jit(solution)/shard_map/own_back/pallas_call | solution.py:613
  26.0 0.0 collective-permute-done.11.far_stats
  26.0 0.0 collective-permute-done.10.near_stats
  26.0 0.3 cross_sibling.1
  26.2 0.7 %collective-permute-start.14 = (bf16[2,64,384]{2,1,0:T(8,128)(2,1)S(1)}, bf16[2,64,384]{2,1,0:T(8,128)(2,1)S(1)}, u32[]{:S(2)}, u32[]{:S(2)}) collective-permute-start(bf16[2,64,384]{2,1,0:T(8,128)(2,1)S(1)} %cross_sibling.1), channel_id=1, source_target_pairs={{0,1},{1,0},{2,3},{3,2},{4,5},{5,4},{6,7},{7,6},{8,9},{9,8},{10,11... | collective-permute-start | bytes 294920 | tf_op jit(solution)/shard_map/ppermute | solution.py:36
  27.0 0.8 %cross_back.1.total_ref = f32[2,3,64,384]{3,2,1,0:T(8,128)S(1)} custom-call(f32[3,256]{1,0:T(4,128)S(1)} %get-tuple-element.62.scale_ref, f32[6,256]{1,0:T(8,128)S(1)} %collective-permute-done.10.near_stats, f32[6,256]{1,0:T(8,128)S(1)} %collective-permute-done.11.far_stats, bf16[2,6,256,128]{3,2,1,0:T(8,128)(2,1)S(1)} %get-tuple-element.76.backward, ...), custom_call_target="tpu_custom_call" | custom-call | flops 1500000000 | tf_op jit(solution)/shard_map/cross_back/pallas_call | solution.py:613
  27.8 0.1 collective-permute-done.14.sibling_ref
  27.9 1.1 %collective-permute-start.16 = (bf16[3,64,384]{2,1,0:T(8,128)(2,1)S(1)}, bf16[3,64,384]{2,1,0:T(8,128)(2,1)S(1)}, u32[]{:S(2)}, u32[]{:S(2)}) collective-permute-start(bf16[3,64,384]{2,1,0:T(8,128)(2,1)S(1)} %get-tuple-element.106), channel_id=1, source_target_pairs={{0,4},{4,0},{1,5},{5,1},{2,6},{6,2},{3,7},{7,3},{8,12},{12,8},{9,1... | collective-permute-start | bytes 442376 | tf_op jit(solution)/shard_map/ppermute | solution.py:36
  29.1 1.1 %collective-permute-start.15 = (bf16[64,384]{1,0:T(8,128)(2,1)S(1)}, bf16[64,384]{1,0:T(8,128)(2,1)S(1)}, u32[]{:S(2)}, u32[]{:S(2)}) collective-permute-start(bf16[64,384]{1,0:T(8,128)(2,1)S(1)} %get-tuple-element.99), channel_id=1, source_target_pairs={{0,3},{1,2},{2,1},{3,0},{4,7},{5,6},{6,5},{7,4},{8,11},{9,10},{10,... | collective-permute-start | bytes 147464 | tf_op jit(solution)/shard_map/ppermute | solution.py:36
  30.2 0.8 %collective-permute-start.17 = (bf16[64,384]{1,0:T(8,128)(2,1)S(1)}, bf16[64,384]{1,0:T(8,128)(2,1)S(1)}, u32[]{:S(2)}, u32[]{:S(2)}) collective-permute-start(bf16[64,384]{1,0:T(8,128)(2,1)S(1)} %get-tuple-element.107), channel_id=1, source_target_pairs={{0,7},{1,6},{2,5},{3,4},{4,3},{5,2},{6,1},{7,0},{8,15},{9,14},{10,... | collective-permute-start | bytes 147464 | tf_op jit(solution)/shard_map/ppermute | solution.py:58
  30.9 2.4 %collective-permute-done.15.edge_ref = bf16[64,384]{1,0:T(8,128)(2,1)S(1)} collective-permute-done((bf16[64,384]{1,0:T(8,128)(2,1)S(1)}, bf16[64,384]{1,0:T(8,128)(2,1)S(1)}, u32[]{:S(2)}, u32[]{:S(2)}) %collective-permute-start.15) | collective-permute-done | bytes 49184 | tf_op jit(solution)/shard_map/ppermute | solution.py:36
  33.3 1.2 %own_finish.1 = (f32[128,768]{1,0:T(8,128)S(1)}, f32[2,128,192]{2,1,0:T(8,128)S(1)}, f32[2,128,192]{2,1,0:T(8,128)S(1)}, bf16[3,192,768]{2,1,0:T(8,128)(2,1)S(1)}) custom-call(f32[2,64,384]{2,1,0:T(8,128)S(1)} %get-tuple-element.97.inner_ref, f32[64,384]{1,0:T(8,128)S(1)} %get-tuple-element.98.dq_ref, bf16[64,384]{1,0:T(8,128)(2,1)S(1)} %collective-permute-done.15.edge_ref, ...), custom_call_target="tpu_custom_call" | custom-call | flops 1000000000 | tf_op jit(solution)/shard_map/own_finish/pallas_call | solution.py:613
  34.5 0.3 collective-permute-done.17.corner_ref
  34.8 0.0 collective-permute-done.16.other_ref
  34.8 1.6 %finish.1 = bf16[4,4,8,768]{3,2,1,0:T(8,128)(2,1)} custom-call(f32[128,768]{1,0:T(8,128)S(1)} %get-tuple-element.105.total_ref, bf16[3,64,384]{2,1,0:T(8,128)(2,1)S(1)} %collective-permute-done.16.other_ref, bf16[64,384]{1,0:T(8,128)(2,1)S(1)} %collective-permute-done.17.corner_ref, f32[2,128,192]{2,1,0:T(8,128)S(1)} %get-tuple-element.108.raws_ref, ...), custom_call_target="tpu_custom_call" | custom-call | flops 2000000000 | tf_op jit(solution)/shard_map/finish/pallas_call | solution.py:613
  (14 shorter events, 0.2 us)
Async XLA Ops:
  0.0 1.6 %copy-start = (bf16[3,768,384]{2,1,0:T(8,128)(2,1)S(1)}, bf16[3,768,384]{2,1,0:T(8,128)(2,1)}, u32[]{:S(2)}) copy-start(bf16[3,768,384]{2,1,0:T(8,128)(2,1)} %qkv_ref.5) | copy-start | bytes 5308420
  0.0 1.1 %copy-start.2 = (bf16[4,4,8,768]{3,2,1,0:T(8,128)(2,1)S(1)}, bf16[4,4,8,768]{3,2,1,0:T(8,128)(2,1)}, u32[]{:S(2)}) copy-start(bf16[4,4,8,768]{3,2,1,0:T(8,128)(2,1)} %tokens_ref.1) | copy-start | bytes 589828
  1.1 0.8 %copy-start.4 = (f32[768]{0:T(1024)S(1)}, f32[768]{0:T(1024)}, u32[]{:S(2)}) copy-start(f32[768]{0:T(1024)} %gain_ref.3) | copy-start | bytes 9220
  1.1 0.8 %copy-start.5 = (s32[1,1,2]{2,1,0:T(1,128)S(1)}, s32[1,1,2]{2,1,0:T(1,128)}, u32[]{:S(2)}) copy-start(s32[1,1,2]{2,1,0:T(1,128)} %count_ref.1) | copy-start | bytes 28
  1.9 4.5 %copy-start.1 = (bf16[384,768]{1,0:T(8,128)(2,1)S(1)}, bf16[384,768]{1,0:T(8,128)(2,1)}, u32[]{:S(2)}) copy-start(bf16[384,768]{1,0:T(8,128)(2,1)} %out_weight_ref.1) | copy-start | bytes 1769476
  1.9 4.5 %copy-start.3 = (bf16[4,4,8,768]{3,2,1,0:T(8,128)(2,1)S(1)}, bf16[4,4,8,768]{3,2,1,0:T(8,128)(2,1)}, u32[]{:S(2)}) copy-start(bf16[4,4,8,768]{3,2,1,0:T(8,128)(2,1)} %grad_ref.1) | copy-start | bytes 589828
  1.9 4.5 %copy-start.6 = (f32[6]{0:T(128)S(1)}, f32[6]{0:T(128)}, u32[]{:S(2)}) copy-start(f32[6]{0:T(128)} %scale_in.1) | copy-start | bytes 76
  2.5 5.2 %collective-permute-start.2 = (bf16[64,384]{1,0:T(8,128)(2,1)S(1)}, bf16[64,384]{1,0:T(8,128)(2,1)S(1)}, u32[]{:S(2)}, u32[]{:S(2)}) collective-permute-start(bf16[64,384]{1,0:T(8,128)(2,1)S(1)} %get-tuple-element.66), channel_id=1, source_target_pairs={{0,3},{1,2},{2,1},{3,0},{4,7},{5,6},{6,5},{7,4},{8,11},{9,10},{10,... | collective-permute-start | bytes 147464 | tf_op jit(solution)/shard_map/ppermute | solution.py:36
  5.2 5.2 %collective-permute-start = (bf16[2,64,384]{2,1,0:T(8,128)(2,1)S(1)}, bf16[2,64,384]{2,1,0:T(8,128)(2,1)S(1)}, u32[]{:S(2)}, u32[]{:S(2)}) collective-permute-start(bf16[2,64,384]{2,1,0:T(8,128)(2,1)S(1)} %get-tuple-element.61.kv_other_ref), channel_id=1, source_target_pairs={{0,4},{4,0},{1,5},{5,1},{2,6},{6,2},{3,7},{7,3},{8,12},{12,8},{9,1... | collective-permute-start | bytes 294920 | tf_op jit(solution)/shard_map/ppermute | solution.py:36
  7.3 4.5 %collective-permute-start.3 = (bf16[64,384]{1,0:T(8,128)(2,1)S(1)}, bf16[64,384]{1,0:T(8,128)(2,1)S(1)}, u32[]{:S(2)}, u32[]{:S(2)}) collective-permute-start(bf16[64,384]{1,0:T(8,128)(2,1)S(1)} %get-tuple-element.68), channel_id=1, source_target_pairs={{0,7},{1,6},{2,5},{3,4},{4,3},{5,2},{6,1},{7,0},{8,15},{9,14},{10,... | collective-permute-start | bytes 147464 | tf_op jit(solution)/shard_map/ppermute | solution.py:58
  7.7 8.3 %collective-permute-start.5 = (bf16[3,64,384]{2,1,0:T(8,128)(2,1)S(1)}, bf16[3,64,384]{2,1,0:T(8,128)(2,1)S(1)}, u32[]{:S(2)}, u32[]{:S(2)}) collective-permute-start(bf16[3,64,384]{2,1,0:T(8,128)(2,1)S(1)} %pad_maximum_fusion.1.refs_0_.refs_2_), channel_id=1, source_target_pairs={{0,1},{1,0},{2,3},{3,2},{8,16},{9,17},{10,18},{11,19},{16,8},{17,9... | collective-permute-start | bytes 442376 | tf_op jit(solution)/shard_map/ppermute | solution.py:48
  7.8 8.6 %collective-permute-start.4 = (bf16[3,64,384]{2,1,0:T(8,128)(2,1)S(1)}, bf16[3,64,384]{2,1,0:T(8,128)(2,1)S(1)}, u32[]{:S(2)}, u32[]{:S(2)}) collective-permute-start(bf16[3,64,384]{2,1,0:T(8,128)(2,1)S(1)} %pad_maximum_fusion.1.refs_0_.refs_2_), channel_id=1, source_target_pairs={{0,8},{1,9},{2,10},{3,11},{8,0},{9,1},{10,2},{11,3},{16,24},{17,25... | collective-permute-start | bytes 442376 | tf_op jit(solution)/shard_map/ppermute | solution.py:48
  10.4 4.0 %collective-permute-start.1 = (bf16[2,64,384]{2,1,0:T(8,128)(2,1)S(1)}, bf16[2,64,384]{2,1,0:T(8,128)(2,1)S(1)}, u32[]{:S(2)}, u32[]{:S(2)}) collective-permute-start(bf16[2,64,384]{2,1,0:T(8,128)(2,1)S(1)} %get-tuple-element.65), channel_id=1, source_target_pairs={{0,4},{4,0},{1,5},{5,1},{2,6},{6,2},{3,7},{7,3},{8,12},{12,8},{9,1... | collective-permute-start | bytes 294920 | tf_op jit(solution)/shard_map/ppermute | solution.py:36
  11.8 8.0 %collective-permute-start.7 = (bf16[3,64,384]{2,1,0:T(8,128)(2,1)S(1)}, bf16[3,64,384]{2,1,0:T(8,128)(2,1)S(1)}, u32[]{:S(2)}, u32[]{:S(2)}) collective-permute-start(bf16[3,64,384]{2,1,0:T(8,128)(2,1)S(1)} %pad_maximum_fusion.2.refs_1_.refs_3_), channel_id=1, source_target_pairs={{0,1},{1,0},{2,3},{3,2},{8,16},{9,17},{10,18},{11,19},{16,8},{17,9... | collective-permute-start | bytes 442376 | tf_op jit(solution)/shard_map/ppermute | solution.py:48
  13.0 6.9 %collective-permute-start.6 = (bf16[3,64,384]{2,1,0:T(8,128)(2,1)S(1)}, bf16[3,64,384]{2,1,0:T(8,128)(2,1)S(1)}, u32[]{:S(2)}, u32[]{:S(2)}) collective-permute-start(bf16[3,64,384]{2,1,0:T(8,128)(2,1)S(1)} %pad_maximum_fusion.2.refs_1_.refs_3_), channel_id=1, source_target_pairs={{0,8},{1,9},{2,10},{3,11},{8,0},{9,1},{10,2},{11,3},{16,24},{17,25... | collective-permute-start | bytes 442376 | tf_op jit(solution)/shard_map/ppermute | solution.py:48
  14.5 9.4 %collective-permute-start.13 = (bf16[4,64,384]{2,1,0:T(8,128)(2,1)S(1)}, bf16[4,64,384]{2,1,0:T(8,128)(2,1)S(1)}, u32[]{:S(2)}, u32[]{:S(2)}) collective-permute-start(bf16[4,64,384]{2,1,0:T(8,128)(2,1)S(1)} %constant_dynamic-update-slice_fusion.qg_ref), channel_id=1, source_target_pairs={{0,1},{1,0},{2,3},{3,2},{8,16},{9,17},{10,18},{11,19},{16,8},{17,9... | collective-permute-start | bytes 589832 | tf_op jit(solution)/shard_map/ppermute | solution.py:48
  16.1 7.8 %collective-permute-start.12 = (bf16[4,64,384]{2,1,0:T(8,128)(2,1)S(1)}, bf16[4,64,384]{2,1,0:T(8,128)(2,1)S(1)}, u32[]{:S(2)}, u32[]{:S(2)}) collective-permute-start(bf16[4,64,384]{2,1,0:T(8,128)(2,1)S(1)} %constant_dynamic-update-slice_fusion.qg_ref), channel_id=1, source_target_pairs={{0,8},{1,9},{2,10},{3,11},{8,0},{9,1},{10,2},{11,3},{16,24},{17,25... | collective-permute-start | bytes 589832 | tf_op jit(solution)/shard_map/ppermute | solution.py:48
  16.4 4.8 %collective-permute-start.8 = (bf16[4,64,384]{2,1,0:T(8,128)(2,1)S(1)}, bf16[4,64,384]{2,1,0:T(8,128)(2,1)S(1)}, u32[]{:S(2)}, u32[]{:S(2)}) collective-permute-start(bf16[4,64,384]{2,1,0:T(8,128)(2,1)S(1)} %pad_maximum_fusion), channel_id=1, source_target_pairs={{0,1},{1,0},{2,3},{3,2},{4,5},{5,4},{6,7},{7,6},{8,9},{9,8},{10,11... | collective-permute-start | bytes 589832 | tf_op jit(solution)/shard_map/ppermute | solution.py:36
  19.9 1.4 %collective-permute-start.9 = (bf16[2,64,384]{2,1,0:T(8,128)(2,1)S(1)}, bf16[2,64,384]{2,1,0:T(8,128)(2,1)S(1)}, u32[]{:S(2)}, u32[]{:S(2)}) collective-permute-start(bf16[2,64,384]{2,1,0:T(8,128)(2,1)S(1)} %pad_maximum_fusion.3), channel_id=1, source_target_pairs={{0,1},{1,0},{2,3},{3,2},{4,5},{5,4},{6,7},{7,6},{8,9},{9,8},{10,11... | collective-permute-start | bytes 294920 | tf_op jit(solution)/shard_map/ppermute | solution.py:36
  21.9 4.0 %collective-permute-start.11 = (f32[6,256]{1,0:T(8,128)S(1)}, f32[6,256]{1,0:T(8,128)S(1)}, u32[]{:S(2)}, u32[]{:S(2)}) collective-permute-start(f32[6,256]{1,0:T(8,128)S(1)} %get-tuple-element.75.stats_ref), channel_id=1, source_target_pairs={{0,1},{1,0},{2,3},{3,2},{8,16},{9,17},{10,18},{11,19},{16,8},{17,9... | collective-permute-start | bytes 18440 | tf_op jit(solution)/shard_map/ppermute | solution.py:48
  22.1 3.8 %collective-permute-start.10 = (f32[6,256]{1,0:T(8,128)S(1)}, f32[6,256]{1,0:T(8,128)S(1)}, u32[]{:S(2)}, u32[]{:S(2)}) collective-permute-start(f32[6,256]{1,0:T(8,128)S(1)} %get-tuple-element.75.stats_ref), channel_id=1, source_target_pairs={{0,8},{1,9},{2,10},{3,11},{8,0},{9,1},{10,2},{11,3},{16,24},{17,25... | collective-permute-start | bytes 18440 | tf_op jit(solution)/shard_map/ppermute | solution.py:48
  26.2 1.7 %collective-permute-start.14 = (bf16[2,64,384]{2,1,0:T(8,128)(2,1)S(1)}, bf16[2,64,384]{2,1,0:T(8,128)(2,1)S(1)}, u32[]{:S(2)}, u32[]{:S(2)}) collective-permute-start(bf16[2,64,384]{2,1,0:T(8,128)(2,1)S(1)} %cross_sibling.1), channel_id=1, source_target_pairs={{0,1},{1,0},{2,3},{3,2},{4,5},{5,4},{6,7},{7,6},{8,9},{9,8},{10,11... | collective-permute-start | bytes 294920 | tf_op jit(solution)/shard_map/ppermute | solution.py:36
  27.9 6.9 %collective-permute-start.16 = (bf16[3,64,384]{2,1,0:T(8,128)(2,1)S(1)}, bf16[3,64,384]{2,1,0:T(8,128)(2,1)S(1)}, u32[]{:S(2)}, u32[]{:S(2)}) collective-permute-start(bf16[3,64,384]{2,1,0:T(8,128)(2,1)S(1)} %get-tuple-element.106), channel_id=1, source_target_pairs={{0,4},{4,0},{1,5},{5,1},{2,6},{6,2},{3,7},{7,3},{8,12},{12,8},{9,1... | collective-permute-start | bytes 442376 | tf_op jit(solution)/shard_map/ppermute | solution.py:36
  29.1 4.3 %collective-permute-start.15 = (bf16[64,384]{1,0:T(8,128)(2,1)S(1)}, bf16[64,384]{1,0:T(8,128)(2,1)S(1)}, u32[]{:S(2)}, u32[]{:S(2)}) collective-permute-start(bf16[64,384]{1,0:T(8,128)(2,1)S(1)} %get-tuple-element.99), channel_id=1, source_target_pairs={{0,3},{1,2},{2,1},{3,0},{4,7},{5,6},{6,5},{7,4},{8,11},{9,10},{10,... | collective-permute-start | bytes 147464 | tf_op jit(solution)/shard_map/ppermute | solution.py:36
  30.2 4.6 %collective-permute-start.17 = (bf16[64,384]{1,0:T(8,128)(2,1)S(1)}, bf16[64,384]{1,0:T(8,128)(2,1)S(1)}, u32[]{:S(2)}, u32[]{:S(2)}) collective-permute-start(bf16[64,384]{1,0:T(8,128)(2,1)S(1)} %get-tuple-element.107), channel_id=1, source_target_pairs={{0,7},{1,6},{2,5},{3,4},{4,3},{5,2},{6,1},{7,0},{8,15},{9,14},{10,... | collective-permute-start | bytes 147464 | tf_op jit(solution)/shard_map/ppermute | solution.py:58

commit v7 on v6

--- a/solution.py
+++ b/solution.py
@@ -344,18 +344,39 @@
     return dot_first(keys[:, lane_tile(h)], grads)[own]
 
 
+def sibling_score_kernel(rows, scale_ref, weights, early_ref, sums_ref, e_out, p_out):
+    side = [jnp.zeros((8, 2 * CELLS), F32) for _ in range(2 * HALF)]
+    groups = [(0, row) for row in range(rows)] + away_groups(rows)[0]
+    for i in range(0, rows + 2, 2):
+        pair = early_ref[i : i + 2]
+        bias = side_bias(Place(rows), groups[i : i + 2], pair)
+        keys = pair.reshape(2 * CELLS, PAIR_WIDTH)
+        exps, probs = score(keys, bias, weights, LAST, scale_ref, side)
+        for h in range(HALF):
+            e_out[h, i * CELLS : (i + 2) * CELLS] = exps[h]
+            p_out[h, i * CELLS : (i + 2) * CELLS] = probs[h]
+    for j in range(2 * HALF):
+        sums_ref[j] = side[j]
+
+
 def sibling_kernel(
-    rows, scale_ref, weights, backward, sums_in, early_ref, late_ref, part_ref, stats_ref, dq_ref
+    rows, scale_ref, weights, backward, sums_in, side_in, e_early, p_early, early_ref, late_ref,
+    part_ref, stats_ref, dq_ref,
 ):
     place = Place(rows)
-    side = [jnp.zeros((8, 2 * CELLS), F32) for _ in range(2 * HALF)]
-    first, second = away_groups(rows)
-    groups = [(0, row) for row in range(rows)] + first + second
+    side = [side_in[j] for j in range(2 * HALF)]
+    second = away_groups(rows)[1]
     pairs = [early_ref[i : i + 2] for i in range(0, rows + 2, 2)]
     pairs += [late_ref[i : i + 2] for i in range(0, len(second), 2)]
     made = []
-    for index, pair in enumerate(pairs):
-        bias = side_bias(place, groups[2 * index : 2 * index + 2], pair)
+    for i in range(0, rows + 2, 2):
+        at = slice(i * CELLS, (i + 2) * CELLS)
+        made.append(
+            ([e_early[h, at] for h in range(HALF)], [p_early[h, at] for h in range(HALF)])
+        )
+    for i in range(0, len(second), 2):
+        pair = late_ref[i : i + 2]
+        bias = side_bias(place, second[i : i + 2], pair)
         keys = pair.reshape(2 * CELLS, PAIR_WIDTH)
         made.append(score(keys, bias, weights, LAST, scale_ref, side))
     inverse, delta = [], []
@@ -697,10 +718,15 @@
         )
         away_kept += made
     half_part = (rows, CELLS, PAIR_WIDTH)
+    side_sums, *early_kept = kernel_call(
+        functools.partial(sibling_score_kernel, rows), "sibling_score",
+        [((2 * HALF, 8, 2 * CELLS), F32)] + [((HALF, (rows + 2) * CELLS, 2 * CELLS), F32)] * 2,
+        [scales, weights, early], micros=0.5,
+    )
     sibling_part, stats, dq_sibling = kernel_call(
         functools.partial(sibling_kernel, rows), "sibling",
         [(half_part, F32), ((2 * HALF, queries), F32), ((HALF_WIDTH, 2 * CELLS), F32)],
-        [scales, weights, backward, sums, early, late], micros=1.5,
+        [scales, weights, backward, sums, side_sums, *early_kept, early, late], micros=1.5,
     )
     near_stats, far_stats = frame_swap(stats, 0), frame_swap(stats, 1)
     cross_mid = ((2, HALF, rows * 2 * CELLS, queries), F32)

time: 36.8 us -> 36.7 us (level)
    pallas_call x15 -> x16, Pallas kernels: 10.1 us -> 10.1 us  [kernel_call(): pl.pallas_call(body, name=name, out_shape=[jax.ShapeDtypeStruct(shape, dt...]
where the time goes in v7:
time: 36.7 us; the launch traced here: 36.3 us
  starting transfers between devices  20.5 us (56%)
  Pallas kernels  10.1 us (28%)
  waiting for transfers between devices  3.55 us (10%)
  local copies, waits for them, and re-layouts  1.74 us (5%)
    ppermute x8, starting transfers between devices, pair_swap(): return lax.ppermute(array, axis, pairs)  10.3 us
    pallas_call x16, Pallas kernels, kernel_call(): pl.pallas_call(body, name=name, out_shape=[jax.ShapeDtypeStruct(shape, dt...  10.1 us
    ppermute x8, starting transfers between devices, frame_swap(): return lax.ppermute(array, ('tm', 'lon'), pairs)  9.11 us
    ppermute x8, waiting for transfers between devices, pair_swap(): return lax.ppermute(array, axis, pairs)  3.13 us
    unnamed x15, local copies, waits for them, and re-layouts  1.68 us
    ppermute x2, starting transfers between devices, corner_swap(): return lax.ppermute(array, ('lat', 'lon'), pairs)  1.11 us
  transfers between devices with their start and end apart: 18, of which 5 were waited for; matrix products, arithmetic and copies ran while one was open for 0% of the time, Pallas kernels for 20%

profile of v7, /device:TPU:1, one launch (start us, length us, event | category | flops | bytes accessed | tf_op | source)
XLA Modules:
  0.0 36.3 jit_solution(18300577668733866911)
XLA Ops:
  0.0 0.0 copy-start
  0.0 0.0 copy-start.2
  0.0 1.1 %copy-done.2 = bf16[4,4,8,768]{3,2,1,0:T(8,128)(2,1)S(1)} copy-done((bf16[4,4,8,768]{3,2,1,0:T(8,128)(2,1)S(1)}, bf16[4,4,8,768]{3,2,1,0:T(8,128)(2,1)}, u32[]{:S(2)}) %copy-start.2) | copy-done | bytes 196632
  1.1 0.0 copy-start.4
  1.1 0.0 copy-start.5
  1.1 0.2 order.1
  1.3 0.3 copy-done
  1.6 0.3 copy-done.4
  1.9 0.0 copy-done.5
  1.9 0.0 copy-start.1
  1.9 0.0 copy-start.3
  1.9 0.0 copy-start.6
  1.9 0.6 %key_value.1 = (bf16[2,64,384]{2,1,0:T(8,128)(2,1)S(1)}, bf16[2,64,384]{2,1,0:T(8,128)(2,1)S(1)}, bf16[64,384]{1,0:T(8,128)(2,1)S(1)}, bf16[128,768]{1,0:T(8,128...) custom-call(s32[1,1,2]{2,1,0:T(1,128)S(1)} %copy-done.5, bf16[128,768]{1,0:T(8,128)(2,1)S(1)} %get-tuple-element.62.x_ref, ...), custom_call_target="tpu_custom_call" | custom-call | flops 2000000000 | tf_op jit(solution)/shard_map/key_value/pallas_call | solution.py:634
  2.5 2.7 %collective-permute-start.2 = (bf16[64,384]{1,0:T(8,128)(2,1)S(1)}, bf16[64,384]{1,0:T(8,128)(2,1)S(1)}, u32[]{:S(2)}, u32[]{:S(2)}) collective-permute-start(bf16[64,384]{1,0:T(8,128)(2,1)S(1)} %get-tuple-element.69), channel_id=1, source_target_pairs={{0,3},{1,2},{2,1},{3,0},{4,7},{5,6},{6,5},{7,4},{8,11},{9,10},{10,... | collective-permute-start | bytes 147464 | tf_op jit(solution)/shard_map/ppermute | solution.py:36
  5.2 1.2 %collective-permute-start = (bf16[2,64,384]{2,1,0:T(8,128)(2,1)S(1)}, bf16[2,64,384]{2,1,0:T(8,128)(2,1)S(1)}, u32[]{:S(2)}, u32[]{:S(2)}) collective-permute-start(bf16[2,64,384]{2,1,0:T(8,128)(2,1)S(1)} %get-tuple-element.64.kv_other_ref), channel_id=1, source_target_pairs={{0,4},{4,0},{1,5},{5,1},{2,6},{6,2},{3,7},{7,3},{8,12},{12,8},{9,1... | collective-permute-start | bytes 294920 | tf_op jit(solution)/shard_map/ppermute | solution.py:36
  6.4 0.0 copy-done.1
  6.4 0.0 copy-done.3
  6.4 0.0 copy-done.6
  6.4 0.9 %query_grad.1 = (bf16[2,64,384]{2,1,0:T(8,128)(2,1)S(1)}, bf16[2,64,384]{2,1,0:T(8,128)(2,1)S(1)}, bf16[64,384]{1,0:T(8,128)(2,1)S(1)}, f32[128,384]{1,0:T(8,128...) custom-call(f32[6]{0:T(128)S(1)} %copy-done.6, bf16[128,128]{1,0:T(8,128)(2,1)S(1)} %get-tuple-element.61.order_ref, ...), custom_call_target="tpu_custom_call" | custom-call | flops 5000000000 | tf_op jit(solution)/shard_map/query_grad/pallas_call | solution.py:634
  7.3 0.4 %collective-permute-start.3 = (bf16[64,384]{1,0:T(8,128)(2,1)S(1)}, bf16[64,384]{1,0:T(8,128)(2,1)S(1)}, u32[]{:S(2)}, u32[]{:S(2)}) collective-permute-start(bf16[64,384]{1,0:T(8,128)(2,1)S(1)} %get-tuple-element.71), channel_id=1, source_target_pairs={{0,7},{1,6},{2,5},{3,4},{4,3},{5,2},{6,1},{7,0},{8,15},{9,14},{10,... | collective-permute-start | bytes 147464 | tf_op jit(solution)/shard_map/ppermute | solution.py:58
  7.7 0.0 collective-permute-done.2
  7.7 0.1 collective-permute-start.5
  7.8 2.6 %collective-permute-start.4 = (bf16[3,64,384]{2,1,0:T(8,128)(2,1)S(1)}, bf16[3,64,384]{2,1,0:T(8,128)(2,1)S(1)}, u32[]{:S(2)}, u32[]{:S(2)}) collective-permute-start(bf16[3,64,384]{2,1,0:T(8,128)(2,1)S(1)} %pad_maximum_fusion.1.refs_0_.refs_2_), channel_id=1, source_target_pairs={{0,8},{1,9},{2,10},{3,11},{8,0},{9,1},{10,2},{11,3},{16,24},{17,25... | collective-permute-start | bytes 442376 | tf_op jit(solution)/shard_map/ppermute | solution.py:48
  10.4 0.0 collective-permute-done.kv_in
  10.4 1.3 %collective-permute-start.1 = (bf16[2,64,384]{2,1,0:T(8,128)(2,1)S(1)}, bf16[2,64,384]{2,1,0:T(8,128)(2,1)S(1)}, u32[]{:S(2)}, u32[]{:S(2)}) collective-permute-start(bf16[2,64,384]{2,1,0:T(8,128)(2,1)S(1)} %get-tuple-element.68), channel_id=1, source_target_pairs={{0,4},{4,0},{1,5},{5,1},{2,6},{6,2},{3,7},{7,3},{8,12},{12,8},{9,1... | collective-permute-start | bytes 294920 | tf_op jit(solution)/shard_map/ppermute | solution.py:36
  11.7 0.1 collective-permute-done.3
  11.8 1.1 %collective-permute-start.7 = (bf16[3,64,384]{2,1,0:T(8,128)(2,1)S(1)}, bf16[3,64,384]{2,1,0:T(8,128)(2,1)S(1)}, u32[]{:S(2)}, u32[]{:S(2)}) collective-permute-start(bf16[3,64,384]{2,1,0:T(8,128)(2,1)S(1)} %pad_maximum_fusion.2.refs_1_.refs_3_), channel_id=1, source_target_pairs={{0,1},{1,0},{2,3},{3,2},{8,16},{9,17},{10,18},{11,19},{16,8},{17,9... | collective-permute-start | bytes 442376 | tf_op jit(solution)/shard_map/ppermute | solution.py:48
  13.0 1.5 %collective-permute-start.6 = (bf16[3,64,384]{2,1,0:T(8,128)(2,1)S(1)}, bf16[3,64,384]{2,1,0:T(8,128)(2,1)S(1)}, u32[]{:S(2)}, u32[]{:S(2)}) collective-permute-start(bf16[3,64,384]{2,1,0:T(8,128)(2,1)S(1)} %pad_maximum_fusion.2.refs_1_.refs_3_), channel_id=1, source_target_pairs={{0,8},{1,9},{2,10},{3,11},{8,0},{9,1},{10,2},{11,3},{16,24},{17,25... | collective-permute-start | bytes 442376 | tf_op jit(solution)/shard_map/ppermute | solution.py:48
  14.4 0.0 collective-permute-done.1
  14.5 1.6 %collective-permute-start.13 = (bf16[4,64,384]{2,1,0:T(8,128)(2,1)S(1)}, bf16[4,64,384]{2,1,0:T(8,128)(2,1)S(1)}, u32[]{:S(2)}, u32[]{:S(2)}) collective-permute-start(bf16[4,64,384]{2,1,0:T(8,128)(2,1)S(1)} %constant_dynamic-update-slice_fusion.qg_ref), channel_id=1, source_target_pairs={{0,1},{1,0},{2,3},{3,2},{8,16},{9,17},{10,18},{11,19},{16,8},{17,9... | collective-permute-start | bytes 589832 | tf_op jit(solution)/shard_map/ppermute | solution.py:48
  16.1 0.0 collective-permute-done.5.refs_1_.refs_3_
  16.1 0.3 collective-permute-start.12
  16.4 0.0 collective-permute-done.4.refs_0_.refs_2_
  16.4 2.0 %collective-permute-start.8 = (bf16[4,64,384]{2,1,0:T(8,128)(2,1)S(1)}, bf16[4,64,384]{2,1,0:T(8,128)(2,1)S(1)}, u32[]{:S(2)}, u32[]{:S(2)}) collective-permute-start(bf16[4,64,384]{2,1,0:T(8,128)(2,1)S(1)} %pad_maximum_fusion), channel_id=1, source_target_pairs={{0,1},{1,0},{2,3},{3,2},{4,5},{5,4},{6,7},{7,6},{8,9},{9,8},{10,11... | collective-permute-start | bytes 589832 | tf_op jit(solution)/shard_map/ppermute | solution.py:36
  18.5 0.9 %own_score.1 = (bf16[3,384,768]{2,1,0:T(8,128)(2,1)S(1)}, bf16[6,128,256]{2,1,0:T(8,128)(2,1)S(1)}, bf16[6,256,128]{2,1,0:T(8,128)(2,1)S(1)}, f32[6,8,256]{2,1,0...) custom-call(f32[3,256]{1,0:T(4,128)S(1)} %get-tuple-element.65.scale, ...), custom_call_target="tpu_custom_call" | custom-call | flops 1500000000 | tf_op jit(solution)/shard_map/own_score/pallas_call | solution.py:634
  19.4 0.4 %away_score.2 = (f32[6,8,256]{2,1,0:T(8,128)S(1)}, f32[3,256,256]{2,1,0:T(8,128)S(1)}, f32[3,256,256]{2,1,0:T(8,128)S(1)}, f32[3,128,128]{2,1,0:T(8,128)S(1)}, f32[3,128,128]{2,1,0:T(8,128)S(1)}) custom-call(f32[3,256]{1,0:T(4,128)S(1)} %get-tuple-element.65.scale_ref, bf16[6,128,256]{2,1,0:T(8,128)(2,1)S(1)} %get-tuple-element.73.weights, ...), custom_call_target="tpu_custom_call" | custom-call | flops 1500000000 | tf_op jit(solution)/shard_map/away_score/pallas_call | solution.py:634
  19.8 0.0 collective-permute-done.7.refs_1_.refs_5_
  19.8 0.0 collective-permute-done.6.refs_0_.refs_4_
  19.9 0.1 collective-permute-start.9
  19.9 0.4 %away_score.3 = (f32[6,8,256]{2,1,0:T(8,128)S(1)}, f32[3,256,256]{2,1,0:T(8,128)S(1)}, f32[3,256,256]{2,1,0:T(8,128)S(1)}, f32[3,128,128]{2,1,0:T(8,128)S(1)}, f32[3,128,128]{2,1,0:T(8,128)S(1)}) custom-call(f32[3,256]{1,0:T(4,128)S(1)} %get-tuple-element.65.scale_ref, bf16[6,128,256]{2,1,0:T(8,128)(2,1)S(1)} %get-tuple-element.73.weights, ...), custom_call_target="tpu_custom_call" | custom-call | flops 20000000000 | tf_op jit(solution)/shard_map/away_score/pallas_call | solution.py:634
  20.4 0.0 collective-permute-done.8.early_ref.refs_4_
  20.4 0.3 sibling_score.1
  20.7 0.6 %collective-permute-done.9.late_ref = bf16[2,64,384]{2,1,0:T(8,128)(2,1)S(1)} collective-permute-done((bf16[2,64,384]{2,1,0:T(8,128)(2,1)S(1)}, bf16[2,64,384]{2,1,0:T(8,128)(2,1)S(1)}, u32[]{:S(2)}, u32[]{:S(2)}) %collective-permute-start.9) | collective-permute-done | bytes 98336 | tf_op jit(solution)/shard_map/ppermute | solution.py:36
  21.2 0.5 %sibling.1 = (f32[2,64,384]{2,1,0:T(8,128)S(1)}, f32[6,256]{1,0:T(8,128)S(1)}, f32[192,128]{1,0:T(8,128)S(1)}) custom-call(f32[3,256]{1,0:T(4,128)S(1)} %get-tuple-element.65.scale_ref, bf16[6,128,256]{2,1,0:T(8,128)(2,1)S(1)} %get-tuple-element.73.weights, bf16[6,256,128]{2,1,0:T(8,128)(2,1)S(1)} %get-tuple-element.74.backward, ...), custom_call_target="tpu_custom_call" | custom-call | flops 1500000000 | tf_op jit(solution)/shard_map/sibling/pallas_call | solution.py:634
  21.7 0.2 collective-permute-start.11
  22.0 1.7 %collective-permute-start.10 = (f32[6,256]{1,0:T(8,128)S(1)}, f32[6,256]{1,0:T(8,128)S(1)}, u32[]{:S(2)}, u32[]{:S(2)}) collective-permute-start(f32[6,256]{1,0:T(8,128)S(1)} %get-tuple-element.81.stats_ref), channel_id=1, source_target_pairs={{0,8},{1,9},{2,10},{3,11},{8,0},{9,1},{10,2},{11,3},{16,24},{17,25... | collective-permute-start | bytes 18440 | tf_op jit(solution)/shard_map/ppermute | solution.py:48
  23.7 0.0 collective-permute-done.13.refs_1_
  23.7 0.0 collective-permute-done.12.refs_0_
  23.7 0.9 %cross_score.1 = (bf16[2,6,256,128]{3,2,1,0:T(8,128)(2,1)S(1)}, f32[2,3,256,256]{3,2,1,0:T(8,128)S(1)}, f32[2,3,256,256]{3,2,1,0:T(8,128)S(1)}, f32[2,2,3,128,12...) custom-call(f32[3,256]{1,0:T(4,128)S(1)} %get-tuple-element.65.scale_ref, ...), custom_call_target="tpu_custom_call" | custom-call | flops 2000000000 | tf_op jit(solution)/shard_map/cross_score/pallas_call | solution.py:634
  24.6 1.1 %own_back.1 = (f32[2,3,64,384]{3,2,1,0:T(8,128)S(1)}, f32[64,384]{1,0:T(8,128)S(1)}, bf16[64,384]{1,0:T(8,128)(2,1)S(1)}) custom-call(f32[3,256]{1,0:T(4,128)S(1)} %get-tuple-element.65.scale_ref, f32[6,256]{1,0:T(8,128)S(1)} %get-tuple-element.81.stats_ref, bf16[6,256,128]{2,1,0:T(8,128)(2,1)S(1)} %get-tuple-element.74.backward, ...), custom_call_target="tpu_custom_call" | custom-call | flops 2000000000 | tf_op jit(solution)/shard_map/own_back/pallas_call | solution.py:634
  25.7 0.0 collective-permute-done.11.far_stats
  25.7 0.0 collective-permute-done.10.near_stats
  25.8 0.3 cross_sibling.1
  26.0 0.7 %collective-permute-start.14 = (bf16[2,64,384]{2,1,0:T(8,128)(2,1)S(1)}, bf16[2,64,384]{2,1,0:T(8,128)(2,1)S(1)}, u32[]{:S(2)}, u32[]{:S(2)}) collective-permute-start(bf16[2,64,384]{2,1,0:T(8,128)(2,1)S(1)} %cross_sibling.1), channel_id=1, source_target_pairs={{0,1},{1,0},{2,3},{3,2},{4,5},{5,4},{6,7},{7,6},{8,9},{9,8},{10,11... | collective-permute-start | bytes 294920 | tf_op jit(solution)/shard_map/ppermute | solution.py:36
  26.7 0.8 %cross_back.1.total_ref = f32[2,3,64,384]{3,2,1,0:T(8,128)S(1)} custom-call(f32[3,256]{1,0:T(4,128)S(1)} %get-tuple-element.65.scale_ref, f32[6,256]{1,0:T(8,128)S(1)} %collective-permute-done.10.near_stats, f32[6,256]{1,0:T(8,128)S(1)} %collective-permute-done.11.far_stats, bf16[2,6,256,128]{3,2,1,0:T(8,128)(2,1)S(1)} %get-tuple-element.82.backward, ...), custom_call_target="tpu_custom_call" | custom-call | flops 1500000000 | tf_op jit(solution)/shard_map/cross_back/pallas_call | solution.py:634
  27.6 0.1 collective-permute-done.14.sibling_ref
  27.7 1.1 %collective-permute-start.16 = (bf16[3,64,384]{2,1,0:T(8,128)(2,1)S(1)}, bf16[3,64,384]{2,1,0:T(8,128)(2,1)S(1)}, u32[]{:S(2)}, u32[]{:S(2)}) collective-permute-start(bf16[3,64,384]{2,1,0:T(8,128)(2,1)S(1)} %get-tuple-element.112), channel_id=1, source_target_pairs={{0,4},{4,0},{1,5},{5,1},{2,6},{6,2},{3,7},{7,3},{8,12},{12,8},{9,1... | collective-permute-start | bytes 442376 | tf_op jit(solution)/shard_map/ppermute | solution.py:36
  28.9 1.1 %collective-permute-start.15 = (bf16[64,384]{1,0:T(8,128)(2,1)S(1)}, bf16[64,384]{1,0:T(8,128)(2,1)S(1)}, u32[]{:S(2)}, u32[]{:S(2)}) collective-permute-start(bf16[64,384]{1,0:T(8,128)(2,1)S(1)} %get-tuple-element.105), channel_id=1, source_target_pairs={{0,3},{1,2},{2,1},{3,0},{4,7},{5,6},{6,5},{7,4},{8,11},{9,10},{10,... | collective-permute-start | bytes 147464 | tf_op jit(solution)/shard_map/ppermute | solution.py:36
  30.0 0.7 %collective-permute-start.17 = (bf16[64,384]{1,0:T(8,128)(2,1)S(1)}, bf16[64,384]{1,0:T(8,128)(2,1)S(1)}, u32[]{:S(2)}, u32[]{:S(2)}) collective-permute-start(bf16[64,384]{1,0:T(8,128)(2,1)S(1)} %get-tuple-element.113), channel_id=1, source_target_pairs={{0,7},{1,6},{2,5},{3,4},{4,3},{5,2},{6,1},{7,0},{8,15},{9,14},{10,... | collective-permute-start | bytes 147464 | tf_op jit(solution)/shard_map/ppermute | solution.py:58
  30.7 2.4 %collective-permute-done.15.edge_ref = bf16[64,384]{1,0:T(8,128)(2,1)S(1)} collective-permute-done((bf16[64,384]{1,0:T(8,128)(2,1)S(1)}, bf16[64,384]{1,0:T(8,128)(2,1)S(1)}, u32[]{:S(2)}, u32[]{:S(2)}) %collective-permute-start.15) | collective-permute-done | bytes 49184 | tf_op jit(solution)/shard_map/ppermute | solution.py:36
  33.1 1.2 %own_finish.1 = (f32[128,768]{1,0:T(8,128)S(1)}, f32[2,128,192]{2,1,0:T(8,128)S(1)}, f32[2,128,192]{2,1,0:T(8,128)S(1)}, bf16[3,192,768]{2,1,0:T(8,128)(2,1)S(1)}) custom-call(f32[2,64,384]{2,1,0:T(8,128)S(1)} %get-tuple-element.103.inner_ref, f32[64,384]{1,0:T(8,128)S(1)} %get-tuple-element.104.dq_ref, ...), custom_call_target="tpu_custom_call" | custom-call | flops 1000000000 | tf_op jit(solution)/shard_map/own_finish/pallas_call | solution.py:634
  34.3 0.3 collective-permute-done.17.corner_ref
  34.6 0.0 collective-permute-done.16.other_ref
  34.6 1.6 %finish.1 = bf16[4,4,8,768]{3,2,1,0:T(8,128)(2,1)} custom-call(f32[128,768]{1,0:T(8,128)S(1)} %get-tuple-element.111.total_ref, bf16[3,64,384]{2,1,0:T(8,128)(2,1)S(1)} %collective-permute-done.16.other_ref, bf16[64,384]{1,0:T(8,128)(2,1)S(1)} %collective-permute-done.17.corner_ref, f32[2,128,192]{2,1,0:T(8,128)S(1)} %get-tuple-element.114.raws_ref, ...), custom_call_target="tpu_custom_call" | custom-call | flops 2000000000 | tf_op jit(solution)/shard_map/finish/pallas_call | solution.py:634
  (14 shorter events, 0.2 us)
Async XLA Ops:
  0.0 1.6 %copy-start = (bf16[3,768,384]{2,1,0:T(8,128)(2,1)S(1)}, bf16[3,768,384]{2,1,0:T(8,128)(2,1)}, u32[]{:S(2)}) copy-start(bf16[3,768,384]{2,1,0:T(8,128)(2,1)} %qkv_ref.5) | copy-start | bytes 5308420
  0.0 1.1 %copy-start.2 = (bf16[4,4,8,768]{3,2,1,0:T(8,128)(2,1)S(1)}, bf16[4,4,8,768]{3,2,1,0:T(8,128)(2,1)}, u32[]{:S(2)}) copy-start(bf16[4,4,8,768]{3,2,1,0:T(8,128)(2,1)} %tokens_ref.1) | copy-start | bytes 589828
  1.1 0.8 %copy-start.4 = (f32[768]{0:T(1024)S(1)}, f32[768]{0:T(1024)}, u32[]{:S(2)}) copy-start(f32[768]{0:T(1024)} %gain_ref.3) | copy-start | bytes 9220
  1.1 0.8 %copy-start.5 = (s32[1,1,2]{2,1,0:T(1,128)S(1)}, s32[1,1,2]{2,1,0:T(1,128)}, u32[]{:S(2)}) copy-start(s32[1,1,2]{2,1,0:T(1,128)} %count_ref.1) | copy-start | bytes 28
  1.9 4.5 %copy-start.1 = (bf16[384,768]{1,0:T(8,128)(2,1)S(1)}, bf16[384,768]{1,0:T(8,128)(2,1)}, u32[]{:S(2)}) copy-start(bf16[384,768]{1,0:T(8,128)(2,1)} %out_weight_ref.1) | copy-start | bytes 1769476
  1.9 4.5 %copy-start.3 = (bf16[4,4,8,768]{3,2,1,0:T(8,128)(2,1)S(1)}, bf16[4,4,8,768]{3,2,1,0:T(8,128)(2,1)}, u32[]{:S(2)}) copy-start(bf16[4,4,8,768]{3,2,1,0:T(8,128)(2,1)} %grad_ref.1) | copy-start | bytes 589828
  1.9 4.5 %copy-start.6 = (f32[6]{0:T(128)S(1)}, f32[6]{0:T(128)}, u32[]{:S(2)}) copy-start(f32[6]{0:T(128)} %scale_in.1) | copy-start | bytes 76
  2.5 5.2 %collective-permute-start.2 = (bf16[64,384]{1,0:T(8,128)(2,1)S(1)}, bf16[64,384]{1,0:T(8,128)(2,1)S(1)}, u32[]{:S(2)}, u32[]{:S(2)}) collective-permute-start(bf16[64,384]{1,0:T(8,128)(2,1)S(1)} %get-tuple-element.69), channel_id=1, source_target_pairs={{0,3},{1,2},{2,1},{3,0},{4,7},{5,6},{6,5},{7,4},{8,11},{9,10},{10,... | collective-permute-start | bytes 147464 | tf_op jit(solution)/shard_map/ppermute | solution.py:36
  5.2 5.2 %collective-permute-start = (bf16[2,64,384]{2,1,0:T(8,128)(2,1)S(1)}, bf16[2,64,384]{2,1,0:T(8,128)(2,1)S(1)}, u32[]{:S(2)}, u32[]{:S(2)}) collective-permute-start(bf16[2,64,384]{2,1,0:T(8,128)(2,1)S(1)} %get-tuple-element.64.kv_other_ref), channel_id=1, source_target_pairs={{0,4},{4,0},{1,5},{5,1},{2,6},{6,2},{3,7},{7,3},{8,12},{12,8},{9,1... | collective-permute-start | bytes 294920 | tf_op jit(solution)/shard_map/ppermute | solution.py:36
  7.3 4.5 %collective-permute-start.3 = (bf16[64,384]{1,0:T(8,128)(2,1)S(1)}, bf16[64,384]{1,0:T(8,128)(2,1)S(1)}, u32[]{:S(2)}, u32[]{:S(2)}) collective-permute-start(bf16[64,384]{1,0:T(8,128)(2,1)S(1)} %get-tuple-element.71), channel_id=1, source_target_pairs={{0,7},{1,6},{2,5},{3,4},{4,3},{5,2},{6,1},{7,0},{8,15},{9,14},{10,... | collective-permute-start | bytes 147464 | tf_op jit(solution)/shard_map/ppermute | solution.py:58
  7.7 8.3 %collective-permute-start.5 = (bf16[3,64,384]{2,1,0:T(8,128)(2,1)S(1)}, bf16[3,64,384]{2,1,0:T(8,128)(2,1)S(1)}, u32[]{:S(2)}, u32[]{:S(2)}) collective-permute-start(bf16[3,64,384]{2,1,0:T(8,128)(2,1)S(1)} %pad_maximum_fusion.1.refs_0_.refs_2_), channel_id=1, source_target_pairs={{0,1},{1,0},{2,3},{3,2},{8,16},{9,17},{10,18},{11,19},{16,8},{17,9... | collective-permute-start | bytes 442376 | tf_op jit(solution)/shard_map/ppermute | solution.py:48
  7.8 8.6 %collective-permute-start.4 = (bf16[3,64,384]{2,1,0:T(8,128)(2,1)S(1)}, bf16[3,64,384]{2,1,0:T(8,128)(2,1)S(1)}, u32[]{:S(2)}, u32[]{:S(2)}) collective-permute-start(bf16[3,64,384]{2,1,0:T(8,128)(2,1)S(1)} %pad_maximum_fusion.1.refs_0_.refs_2_), channel_id=1, source_target_pairs={{0,8},{1,9},{2,10},{3,11},{8,0},{9,1},{10,2},{11,3},{16,24},{17,25... | collective-permute-start | bytes 442376 | tf_op jit(solution)/shard_map/ppermute | solution.py:48
  10.4 4.0 %collective-permute-start.1 = (bf16[2,64,384]{2,1,0:T(8,128)(2,1)S(1)}, bf16[2,64,384]{2,1,0:T(8,128)(2,1)S(1)}, u32[]{:S(2)}, u32[]{:S(2)}) collective-permute-start(bf16[2,64,384]{2,1,0:T(8,128)(2,1)S(1)} %get-tuple-element.68), channel_id=1, source_target_pairs={{0,4},{4,0},{1,5},{5,1},{2,6},{6,2},{3,7},{7,3},{8,12},{12,8},{9,1... | collective-permute-start | bytes 294920 | tf_op jit(solution)/shard_map/ppermute | solution.py:36
  11.8 8.0 %collective-permute-start.7 = (bf16[3,64,384]{2,1,0:T(8,128)(2,1)S(1)}, bf16[3,64,384]{2,1,0:T(8,128)(2,1)S(1)}, u32[]{:S(2)}, u32[]{:S(2)}) collective-permute-start(bf16[3,64,384]{2,1,0:T(8,128)(2,1)S(1)} %pad_maximum_fusion.2.refs_1_.refs_3_), channel_id=1, source_target_pairs={{0,1},{1,0},{2,3},{3,2},{8,16},{9,17},{10,18},{11,19},{16,8},{17,9... | collective-permute-start | bytes 442376 | tf_op jit(solution)/shard_map/ppermute | solution.py:48
  13.0 6.8 %collective-permute-start.6 = (bf16[3,64,384]{2,1,0:T(8,128)(2,1)S(1)}, bf16[3,64,384]{2,1,0:T(8,128)(2,1)S(1)}, u32[]{:S(2)}, u32[]{:S(2)}) collective-permute-start(bf16[3,64,384]{2,1,0:T(8,128)(2,1)S(1)} %pad_maximum_fusion.2.refs_1_.refs_3_), channel_id=1, source_target_pairs={{0,8},{1,9},{2,10},{3,11},{8,0},{9,1},{10,2},{11,3},{16,24},{17,25... | collective-permute-start | bytes 442376 | tf_op jit(solution)/shard_map/ppermute | solution.py:48
  14.5 9.2 %collective-permute-start.13 = (bf16[4,64,384]{2,1,0:T(8,128)(2,1)S(1)}, bf16[4,64,384]{2,1,0:T(8,128)(2,1)S(1)}, u32[]{:S(2)}, u32[]{:S(2)}) collective-permute-start(bf16[4,64,384]{2,1,0:T(8,128)(2,1)S(1)} %constant_dynamic-update-slice_fusion.qg_ref), channel_id=1, source_target_pairs={{0,1},{1,0},{2,3},{3,2},{8,16},{9,17},{10,18},{11,19},{16,8},{17,9... | collective-permute-start | bytes 589832 | tf_op jit(solution)/shard_map/ppermute | solution.py:48
  16.1 7.6 %collective-permute-start.12 = (bf16[4,64,384]{2,1,0:T(8,128)(2,1)S(1)}, bf16[4,64,384]{2,1,0:T(8,128)(2,1)S(1)}, u32[]{:S(2)}, u32[]{:S(2)}) collective-permute-start(bf16[4,64,384]{2,1,0:T(8,128)(2,1)S(1)} %constant_dynamic-update-slice_fusion.qg_ref), channel_id=1, source_target_pairs={{0,8},{1,9},{2,10},{3,11},{8,0},{9,1},{10,2},{11,3},{16,24},{17,25... | collective-permute-start | bytes 589832 | tf_op jit(solution)/shard_map/ppermute | solution.py:48
  16.4 3.9 %collective-permute-start.8 = (bf16[4,64,384]{2,1,0:T(8,128)(2,1)S(1)}, bf16[4,64,384]{2,1,0:T(8,128)(2,1)S(1)}, u32[]{:S(2)}, u32[]{:S(2)}) collective-permute-start(bf16[4,64,384]{2,1,0:T(8,128)(2,1)S(1)} %pad_maximum_fusion), channel_id=1, source_target_pairs={{0,1},{1,0},{2,3},{3,2},{4,5},{5,4},{6,7},{7,6},{8,9},{9,8},{10,11... | collective-permute-start | bytes 589832 | tf_op jit(solution)/shard_map/ppermute | solution.py:36
  19.9 1.4 %collective-permute-start.9 = (bf16[2,64,384]{2,1,0:T(8,128)(2,1)S(1)}, bf16[2,64,384]{2,1,0:T(8,128)(2,1)S(1)}, u32[]{:S(2)}, u32[]{:S(2)}) collective-permute-start(bf16[2,64,384]{2,1,0:T(8,128)(2,1)S(1)} %pad_maximum_fusion.3), channel_id=1, source_target_pairs={{0,1},{1,0},{2,3},{3,2},{4,5},{5,4},{6,7},{7,6},{8,9},{9,8},{10,11... | collective-permute-start | bytes 294920 | tf_op jit(solution)/shard_map/ppermute | solution.py:36
  21.7 4.0 %collective-permute-start.11 = (f32[6,256]{1,0:T(8,128)S(1)}, f32[6,256]{1,0:T(8,128)S(1)}, u32[]{:S(2)}, u32[]{:S(2)}) collective-permute-start(f32[6,256]{1,0:T(8,128)S(1)} %get-tuple-element.81.stats_ref), channel_id=1, source_target_pairs={{0,1},{1,0},{2,3},{3,2},{8,16},{9,17},{10,18},{11,19},{16,8},{17,9... | collective-permute-start | bytes 18440 | tf_op jit(solution)/shard_map/ppermute | solution.py:48
  22.0 3.8 %collective-permute-start.10 = (f32[6,256]{1,0:T(8,128)S(1)}, f32[6,256]{1,0:T(8,128)S(1)}, u32[]{:S(2)}, u32[]{:S(2)}) collective-permute-start(f32[6,256]{1,0:T(8,128)S(1)} %get-tuple-element.81.stats_ref), channel_id=1, source_target_pairs={{0,8},{1,9},{2,10},{3,11},{8,0},{9,1},{10,2},{11,3},{16,24},{17,25... | collective-permute-start | bytes 18440 | tf_op jit(solution)/shard_map/ppermute | solution.py:48
  26.0 1.7 %collective-permute-start.14 = (bf16[2,64,384]{2,1,0:T(8,128)(2,1)S(1)}, bf16[2,64,384]{2,1,0:T(8,128)(2,1)S(1)}, u32[]{:S(2)}, u32[]{:S(2)}) collective-permute-start(bf16[2,64,384]{2,1,0:T(8,128)(2,1)S(1)} %cross_sibling.1), channel_id=1, source_target_pairs={{0,1},{1,0},{2,3},{3,2},{4,5},{5,4},{6,7},{7,6},{8,9},{9,8},{10,11... | collective-permute-start | bytes 294920 | tf_op jit(solution)/shard_map/ppermute | solution.py:36
  27.7 6.9 %collective-permute-start.16 = (bf16[3,64,384]{2,1,0:T(8,128)(2,1)S(1)}, bf16[3,64,384]{2,1,0:T(8,128)(2,1)S(1)}, u32[]{:S(2)}, u32[]{:S(2)}) collective-permute-start(bf16[3,64,384]{2,1,0:T(8,128)(2,1)S(1)} %get-tuple-element.112), channel_id=1, source_target_pairs={{0,4},{4,0},{1,5},{5,1},{2,6},{6,2},{3,7},{7,3},{8,12},{12,8},{9,1... | collective-permute-start | bytes 442376 | tf_op jit(solution)/shard_map/ppermute | solution.py:36
  28.9 4.3 %collective-permute-start.15 = (bf16[64,384]{1,0:T(8,128)(2,1)S(1)}, bf16[64,384]{1,0:T(8,128)(2,1)S(1)}, u32[]{:S(2)}, u32[]{:S(2)}) collective-permute-start(bf16[64,384]{1,0:T(8,128)(2,1)S(1)} %get-tuple-element.105), channel_id=1, source_target_pairs={{0,3},{1,2},{2,1},{3,0},{4,7},{5,6},{6,5},{7,4},{8,11},{9,10},{10,... | collective-permute-start | bytes 147464 | tf_op jit(solution)/shard_map/ppermute | solution.py:36
  30.0 4.6 %collective-permute-start.17 = (bf16[64,384]{1,0:T(8,128)(2,1)S(1)}, bf16[64,384]{1,0:T(8,128)(2,1)S(1)}, u32[]{:S(2)}, u32[]{:S(2)}) collective-permute-start(bf16[64,384]{1,0:T(8,128)(2,1)S(1)} %get-tuple-element.113), channel_id=1, source_target_pairs={{0,7},{1,6},{2,5},{3,4},{4,3},{5,2},{6,1},{7,0},{8,15},{9,14},{10,... | collective-permute-start | bytes 147464 | tf_op jit(solution)/shard_map/ppermute | solution.py:58

commit v8 on v6

--- a/solution.py
+++ b/solution.py
@@ -179,10 +179,6 @@
     shape = (cells // CELLS, CELLS, PAIR_WIDTH)
     qg_own_ref[...] = jnp.where(upper, high, low).astype(BF16).reshape(shape)
     qg_other_ref[...] = jnp.where(upper, low, high).astype(BF16).reshape(shape)
-
-
-def join_kernel(kv_in, kv_ref):
-    kv_ref[...] = kv_in[...]
 
 
 def lane_tile(j):
@@ -652,7 +648,6 @@
         [logit_scale, order, normed, grad_out, qkv_weight, out_weight, kv_made], micros=5.0,
     )
     corner = corner_swap(corner)
-    (kv_other,) = kernel_call(join_kernel, "join", [qg_shape], [kv_other], micros=3.0)
     qg_other, kv_other = lax.optimization_barrier((qg_other, kv_other))
     qg_other = pair_swap(qg_other, "lat", 0)
     kv_rows = [

time: 36.8 us -> 36.8 us (level)
    pallas_call x15 -> x14, Pallas kernels: 10.1 us -> 10 us  [kernel_call(): pl.pallas_call(body, name=name, out_shape=[jax.ShapeDtypeStruct(shape, dt...]
where the time goes in v8:
time: 36.8 us; the launch traced here: 36.4 us
  starting transfers between devices  20.4 us (55%)
  Pallas kernels  10 us (27%)
  waiting for transfers between devices  3.86 us (10%)
  local copies, waits for them, and re-layouts  1.74 us (5%)
    ppermute x8, starting transfers between devices, pair_swap(): return lax.ppermute(array, axis, pairs)  10.2 us
    pallas_call x14, Pallas kernels, kernel_call(): pl.pallas_call(body, name=name, out_shape=[jax.ShapeDtypeStruct(shape, dt...  10 us
    ppermute x8, starting transfers between devices, frame_swap(): return lax.ppermute(array, ('tm', 'lon'), pairs)  9.09 us
    ppermute x8, waiting for transfers between devices, pair_swap(): return lax.ppermute(array, axis, pairs)  3.39 us
    unnamed x15, local copies, waits for them, and re-layouts  1.68 us
    ppermute x2, starting transfers between devices, corner_swap(): return lax.ppermute(array, ('lat', 'lon'), pairs)  1.14 us
  transfers between devices with their start and end apart: 18, of which 5 were waited for; matrix products, arithmetic and copies ran while one was open for 0% of the time, Pallas kernels for 20%

profile of v8, /device:TPU:1, one launch (start us, length us, event | category | flops | bytes accessed | tf_op | source)
XLA Modules:
  0.0 36.4 jit_solution(13286737776480516505)
XLA Ops:
  0.0 0.0 copy-start
  0.0 0.0 copy-start.2
  0.0 1.1 %copy-done.2 = bf16[4,4,8,768]{3,2,1,0:T(8,128)(2,1)S(1)} copy-done((bf16[4,4,8,768]{3,2,1,0:T(8,128)(2,1)S(1)}, bf16[4,4,8,768]{3,2,1,0:T(8,128)(2,1)}, u32[]{:S(2)}) %copy-start.2) | copy-done | bytes 196632
  1.1 0.0 copy-start.4
  1.1 0.0 copy-start.5
  1.1 0.2 order.1
  1.3 0.3 copy-done
  1.6 0.3 copy-done.4
  1.9 0.0 copy-done.5
  1.9 0.0 copy-start.1
  1.9 0.0 copy-start.3
  1.9 0.0 copy-start.6
  1.9 0.6 %key_value.1 = (bf16[2,64,384]{2,1,0:T(8,128)(2,1)S(1)}, bf16[2,64,384]{2,1,0:T(8,128)(2,1)S(1)}, bf16[64,384]{1,0:T(8,128)(2,1)S(1)}, bf16[128,768]{1,0:T(8,128...) custom-call(s32[1,1,2]{2,1,0:T(1,128)S(1)} %copy-done.5, bf16[128,768]{1,0:T(8,128)(2,1)S(1)} %get-tuple-element.59.x_ref, ...), custom_call_target="tpu_custom_call" | custom-call | flops 2000000000 | tf_op jit(solution)/shard_map/key_value/pallas_call | solution.py:609
  2.5 2.7 %collective-permute-start.2 = (bf16[64,384]{1,0:T(8,128)(2,1)S(1)}, bf16[64,384]{1,0:T(8,128)(2,1)S(1)}, u32[]{:S(2)}, u32[]{:S(2)}) collective-permute-start(bf16[64,384]{1,0:T(8,128)(2,1)S(1)} %get-tuple-element.66), channel_id=1, source_target_pairs={{0,3},{1,2},{2,1},{3,0},{4,7},{5,6},{6,5},{7,4},{8,11},{9,10},{10,... | collective-permute-start | bytes 147464 | tf_op jit(solution)/shard_map/ppermute | solution.py:36
  5.2 1.2 %collective-permute-start = (bf16[2,64,384]{2,1,0:T(8,128)(2,1)S(1)}, bf16[2,64,384]{2,1,0:T(8,128)(2,1)S(1)}, u32[]{:S(2)}, u32[]{:S(2)}) collective-permute-start(bf16[2,64,384]{2,1,0:T(8,128)(2,1)S(1)} %get-tuple-element.61.kv_other_ref), channel_id=1, source_target_pairs={{0,4},{4,0},{1,5},{5,1},{2,6},{6,2},{3,7},{7,3},{8,12},{12,8},{9,1... | collective-permute-start | bytes 294920 | tf_op jit(solution)/shard_map/ppermute | solution.py:36
  6.4 0.0 copy-done.1
  6.4 0.0 copy-done.3
  6.4 0.0 copy-done.6
  6.4 0.8 %query_grad.1 = (bf16[2,64,384]{2,1,0:T(8,128)(2,1)S(1)}, bf16[2,64,384]{2,1,0:T(8,128)(2,1)S(1)}, bf16[64,384]{1,0:T(8,128)(2,1)S(1)}, f32[128,384]{1,0:T(8,128...) custom-call(f32[6]{0:T(128)S(1)} %copy-done.6, bf16[128,128]{1,0:T(8,128)(2,1)S(1)} %get-tuple-element.58.order_ref, ...), custom_call_target="tpu_custom_call" | custom-call | flops 5000000000 | tf_op jit(solution)/shard_map/query_grad/pallas_call | solution.py:609
  7.3 0.4 %collective-permute-start.3 = (bf16[64,384]{1,0:T(8,128)(2,1)S(1)}, bf16[64,384]{1,0:T(8,128)(2,1)S(1)}, u32[]{:S(2)}, u32[]{:S(2)}) collective-permute-start(bf16[64,384]{1,0:T(8,128)(2,1)S(1)} %get-tuple-element.68), channel_id=1, source_target_pairs={{0,7},{1,6},{2,5},{3,4},{4,3},{5,2},{6,1},{7,0},{8,15},{9,14},{10,... | collective-permute-start | bytes 147464 | tf_op jit(solution)/shard_map/ppermute | solution.py:58
  7.7 0.0 collective-permute-done.2
  7.7 0.1 collective-permute-start.5
  7.8 2.6 %collective-permute-start.4 = (bf16[3,64,384]{2,1,0:T(8,128)(2,1)S(1)}, bf16[3,64,384]{2,1,0:T(8,128)(2,1)S(1)}, u32[]{:S(2)}, u32[]{:S(2)}) collective-permute-start(bf16[3,64,384]{2,1,0:T(8,128)(2,1)S(1)} %pad_maximum_fusion.1.refs_0_.refs_2_), channel_id=1, source_target_pairs={{0,8},{1,9},{2,10},{3,11},{8,0},{9,1},{10,2},{11,3},{16,24},{17,25... | collective-permute-start | bytes 442376 | tf_op jit(solution)/shard_map/ppermute | solution.py:48
  10.4 0.0 collective-permute-done
  10.4 1.2 %collective-permute-start.1 = (bf16[2,64,384]{2,1,0:T(8,128)(2,1)S(1)}, bf16[2,64,384]{2,1,0:T(8,128)(2,1)S(1)}, u32[]{:S(2)}, u32[]{:S(2)}) collective-permute-start(bf16[2,64,384]{2,1,0:T(8,128)(2,1)S(1)} %get-tuple-element.65), channel_id=1, source_target_pairs={{0,4},{4,0},{1,5},{5,1},{2,6},{6,2},{3,7},{7,3},{8,12},{12,8},{9,1... | collective-permute-start | bytes 294920 | tf_op jit(solution)/shard_map/ppermute | solution.py:36
  11.6 0.1 collective-permute-done.3
  11.8 1.1 %collective-permute-start.7 = (bf16[3,64,384]{2,1,0:T(8,128)(2,1)S(1)}, bf16[3,64,384]{2,1,0:T(8,128)(2,1)S(1)}, u32[]{:S(2)}, u32[]{:S(2)}) collective-permute-start(bf16[3,64,384]{2,1,0:T(8,128)(2,1)S(1)} %pad_maximum_fusion.2.refs_1_.refs_3_), channel_id=1, source_target_pairs={{0,1},{1,0},{2,3},{3,2},{8,16},{9,17},{10,18},{11,19},{16,8},{17,9... | collective-permute-start | bytes 442376 | tf_op jit(solution)/shard_map/ppermute | solution.py:48
  12.9 1.6 %collective-permute-start.6 = (bf16[3,64,384]{2,1,0:T(8,128)(2,1)S(1)}, bf16[3,64,384]{2,1,0:T(8,128)(2,1)S(1)}, u32[]{:S(2)}, u32[]{:S(2)}) collective-permute-start(bf16[3,64,384]{2,1,0:T(8,128)(2,1)S(1)} %pad_maximum_fusion.2.refs_1_.refs_3_), channel_id=1, source_target_pairs={{0,8},{1,9},{2,10},{3,11},{8,0},{9,1},{10,2},{11,3},{16,24},{17,25... | collective-permute-start | bytes 442376 | tf_op jit(solution)/shard_map/ppermute | solution.py:48
  14.4 0.0 collective-permute-done.1
  14.5 1.5 %collective-permute-start.13 = (bf16[4,64,384]{2,1,0:T(8,128)(2,1)S(1)}, bf16[4,64,384]{2,1,0:T(8,128)(2,1)S(1)}, u32[]{:S(2)}, u32[]{:S(2)}) collective-permute-start(bf16[4,64,384]{2,1,0:T(8,128)(2,1)S(1)} %constant_dynamic-update-slice_fusion.qg_ref), channel_id=1, source_target_pairs={{0,1},{1,0},{2,3},{3,2},{8,16},{9,17},{10,18},{11,19},{16,8},{17,9... | collective-permute-start | bytes 589832 | tf_op jit(solution)/shard_map/ppermute | solution.py:48
  16.0 0.0 collective-permute-done.5.refs_1_.refs_3_
  16.0 0.3 collective-permute-start.12
  16.3 0.0 collective-permute-done.4.refs_0_.refs_2_
  16.4 2.0 %collective-permute-start.8 = (bf16[4,64,384]{2,1,0:T(8,128)(2,1)S(1)}, bf16[4,64,384]{2,1,0:T(8,128)(2,1)S(1)}, u32[]{:S(2)}, u32[]{:S(2)}) collective-permute-start(bf16[4,64,384]{2,1,0:T(8,128)(2,1)S(1)} %pad_maximum_fusion), channel_id=1, source_target_pairs={{0,1},{1,0},{2,3},{3,2},{4,5},{5,4},{6,7},{7,6},{8,9},{9,8},{10,11... | collective-permute-start | bytes 589832 | tf_op jit(solution)/shard_map/ppermute | solution.py:36
  18.4 0.9 %own_score.1 = (bf16[3,384,768]{2,1,0:T(8,128)(2,1)S(1)}, bf16[6,128,256]{2,1,0:T(8,128)(2,1)S(1)}, bf16[6,256,128]{2,1,0:T(8,128)(2,1)S(1)}, f32[6,8,256]{2,1,0...) custom-call(f32[3,256]{1,0:T(4,128)S(1)} %get-tuple-element.62.scale, ...), custom_call_target="tpu_custom_call" | custom-call | flops 1500000000 | tf_op jit(solution)/shard_map/own_score/pallas_call | solution.py:609
  19.3 0.4 %away_score.2 = (f32[6,8,256]{2,1,0:T(8,128)S(1)}, f32[3,256,256]{2,1,0:T(8,128)S(1)}, f32[3,256,256]{2,1,0:T(8,128)S(1)}, f32[3,128,128]{2,1,0:T(8,128)S(1)}, f32[3,128,128]{2,1,0:T(8,128)S(1)}) custom-call(f32[3,256]{1,0:T(4,128)S(1)} %get-tuple-element.62.scale_ref, bf16[6,128,256]{2,1,0:T(8,128)(2,1)S(1)} %get-tuple-element.70.weights, ...), custom_call_target="tpu_custom_call" | custom-call | flops 1500000000 | tf_op jit(solution)/shard_map/away_score/pallas_call | solution.py:609
  19.7 0.0 collective-permute-done.7.refs_1_.refs_5_
  19.7 0.0 collective-permute-done.6.refs_0_.refs_4_
  19.8 0.1 collective-permute-start.9
  19.9 0.4 %away_score.3 = (f32[6,8,256]{2,1,0:T(8,128)S(1)}, f32[3,256,256]{2,1,0:T(8,128)S(1)}, f32[3,256,256]{2,1,0:T(8,128)S(1)}, f32[3,128,128]{2,1,0:T(8,128)S(1)}, f32[3,128,128]{2,1,0:T(8,128)S(1)}) custom-call(f32[3,256]{1,0:T(4,128)S(1)} %get-tuple-element.62.scale_ref, bf16[6,128,256]{2,1,0:T(8,128)(2,1)S(1)} %get-tuple-element.70.weights, ...), custom_call_target="tpu_custom_call" | custom-call | flops 20000000000 | tf_op jit(solution)/shard_map/away_score/pallas_call | solution.py:609
  20.3 0.9 %collective-permute-done.9.late_ref = bf16[2,64,384]{2,1,0:T(8,128)(2,1)S(1)} collective-permute-done((bf16[2,64,384]{2,1,0:T(8,128)(2,1)S(1)}, bf16[2,64,384]{2,1,0:T(8,128)(2,1)S(1)}, u32[]{:S(2)}, u32[]{:S(2)}) %collective-permute-start.9) | collective-permute-done | bytes 98336 | tf_op jit(solution)/shard_map/ppermute | solution.py:36
  21.1 0.0 collective-permute-done.8.early_ref.refs_4_
  21.1 0.7 %sibling.1 = (f32[2,64,384]{2,1,0:T(8,128)S(1)}, f32[6,256]{1,0:T(8,128)S(1)}, f32[192,128]{1,0:T(8,128)S(1)}) custom-call(f32[3,256]{1,0:T(4,128)S(1)} %get-tuple-element.62.scale_ref, bf16[6,128,256]{2,1,0:T(8,128)(2,1)S(1)} %get-tuple-element.70.weights, bf16[6,256,128]{2,1,0:T(8,128)(2,1)S(1)} %get-tuple-element.71.backward, ...), custom_call_target="tpu_custom_call" | custom-call | flops 1500000000 | tf_op jit(solution)/shard_map/sibling/pallas_call | solution.py:609
  21.8 0.2 collective-permute-start.11
  22.1 1.7 %collective-permute-start.10 = (f32[6,256]{1,0:T(8,128)S(1)}, f32[6,256]{1,0:T(8,128)S(1)}, u32[]{:S(2)}, u32[]{:S(2)}) collective-permute-start(f32[6,256]{1,0:T(8,128)S(1)} %get-tuple-element.75.stats_ref), channel_id=1, source_target_pairs={{0,8},{1,9},{2,10},{3,11},{8,0},{9,1},{10,2},{11,3},{16,24},{17,25... | collective-permute-start | bytes 18440 | tf_op jit(solution)/shard_map/ppermute | solution.py:48
  23.8 0.0 collective-permute-done.13.refs_1_
  23.8 0.0 collective-permute-done.12.refs_0_
  23.8 0.9 %cross_score.1 = (bf16[2,6,256,128]{3,2,1,0:T(8,128)(2,1)S(1)}, f32[2,3,256,256]{3,2,1,0:T(8,128)S(1)}, f32[2,3,256,256]{3,2,1,0:T(8,128)S(1)}, f32[2,2,3,128,12...) custom-call(f32[3,256]{1,0:T(4,128)S(1)} %get-tuple-element.62.scale_ref, ...), custom_call_target="tpu_custom_call" | custom-call | flops 2000000000 | tf_op jit(solution)/shard_map/cross_score/pallas_call | solution.py:609
  24.7 1.2 %own_back.1 = (f32[2,3,64,384]{3,2,1,0:T(8,128)S(1)}, f32[64,384]{1,0:T(8,128)S(1)}, bf16[64,384]{1,0:T(8,128)(2,1)S(1)}) custom-call(f32[3,256]{1,0:T(4,128)S(1)} %get-tuple-element.62.scale_ref, f32[6,256]{1,0:T(8,128)S(1)} %get-tuple-element.75.stats_ref, bf16[6,256,128]{2,1,0:T(8,128)(2,1)S(1)} %get-tuple-element.71.backward, ...), custom_call_target="tpu_custom_call" | custom-call | flops 2000000000 | tf_op jit(solution)/shard_map/own_back/pallas_call | solution.py:609
  25.9 0.0 collective-permute-done.11.far_stats
  25.9 0.0 collective-permute-done.10.near_stats
  25.9 0.3 cross_sibling.1
  26.2 0.7 %collective-permute-start.14 = (bf16[2,64,384]{2,1,0:T(8,128)(2,1)S(1)}, bf16[2,64,384]{2,1,0:T(8,128)(2,1)S(1)}, u32[]{:S(2)}, u32[]{:S(2)}) collective-permute-start(bf16[2,64,384]{2,1,0:T(8,128)(2,1)S(1)} %cross_sibling.1), channel_id=1, source_target_pairs={{0,1},{1,0},{2,3},{3,2},{4,5},{5,4},{6,7},{7,6},{8,9},{9,8},{10,11... | collective-permute-start | bytes 294920 | tf_op jit(solution)/shard_map/ppermute | solution.py:36
  26.9 0.8 %cross_back.1.total_ref = f32[2,3,64,384]{3,2,1,0:T(8,128)S(1)} custom-call(f32[3,256]{1,0:T(4,128)S(1)} %get-tuple-element.62.scale_ref, f32[6,256]{1,0:T(8,128)S(1)} %collective-permute-done.10.near_stats, f32[6,256]{1,0:T(8,128)S(1)} %collective-permute-done.11.far_stats, bf16[2,6,256,128]{3,2,1,0:T(8,128)(2,1)S(1)} %get-tuple-element.76.backward, ...), custom_call_target="tpu_custom_call" | custom-call | flops 1500000000 | tf_op jit(solution)/shard_map/cross_back/pallas_call | solution.py:609
  27.7 0.1 collective-permute-done.14.sibling_ref
  27.9 1.1 %collective-permute-start.16 = (bf16[3,64,384]{2,1,0:T(8,128)(2,1)S(1)}, bf16[3,64,384]{2,1,0:T(8,128)(2,1)S(1)}, u32[]{:S(2)}, u32[]{:S(2)}) collective-permute-start(bf16[3,64,384]{2,1,0:T(8,128)(2,1)S(1)} %get-tuple-element.106), channel_id=1, source_target_pairs={{0,4},{4,0},{1,5},{5,1},{2,6},{6,2},{3,7},{7,3},{8,12},{12,8},{9,1... | collective-permute-start | bytes 442376 | tf_op jit(solution)/shard_map/ppermute | solution.py:36
  29.0 1.1 %collective-permute-start.15 = (bf16[64,384]{1,0:T(8,128)(2,1)S(1)}, bf16[64,384]{1,0:T(8,128)(2,1)S(1)}, u32[]{:S(2)}, u32[]{:S(2)}) collective-permute-start(bf16[64,384]{1,0:T(8,128)(2,1)S(1)} %get-tuple-element.99), channel_id=1, source_target_pairs={{0,3},{1,2},{2,1},{3,0},{4,7},{5,6},{6,5},{7,4},{8,11},{9,10},{10,... | collective-permute-start | bytes 147464 | tf_op jit(solution)/shard_map/ppermute | solution.py:36
  30.1 0.7 %collective-permute-start.17 = (bf16[64,384]{1,0:T(8,128)(2,1)S(1)}, bf16[64,384]{1,0:T(8,128)(2,1)S(1)}, u32[]{:S(2)}, u32[]{:S(2)}) collective-permute-start(bf16[64,384]{1,0:T(8,128)(2,1)S(1)} %get-tuple-element.107), channel_id=1, source_target_pairs={{0,7},{1,6},{2,5},{3,4},{4,3},{5,2},{6,1},{7,0},{8,15},{9,14},{10,... | collective-permute-start | bytes 147464 | tf_op jit(solution)/shard_map/ppermute | solution.py:58
  30.9 2.4 %collective-permute-done.15.edge_ref = bf16[64,384]{1,0:T(8,128)(2,1)S(1)} collective-permute-done((bf16[64,384]{1,0:T(8,128)(2,1)S(1)}, bf16[64,384]{1,0:T(8,128)(2,1)S(1)}, u32[]{:S(2)}, u32[]{:S(2)}) %collective-permute-start.15) | collective-permute-done | bytes 49184 | tf_op jit(solution)/shard_map/ppermute | solution.py:36
  33.2 1.2 %own_finish.1 = (f32[128,768]{1,0:T(8,128)S(1)}, f32[2,128,192]{2,1,0:T(8,128)S(1)}, f32[2,128,192]{2,1,0:T(8,128)S(1)}, bf16[3,192,768]{2,1,0:T(8,128)(2,1)S(1)}) custom-call(f32[2,64,384]{2,1,0:T(8,128)S(1)} %get-tuple-element.97.inner_ref, f32[64,384]{1,0:T(8,128)S(1)} %get-tuple-element.98.dq_ref, bf16[64,384]{1,0:T(8,128)(2,1)S(1)} %collective-permute-done.15.edge_ref, ...), custom_call_target="tpu_custom_call" | custom-call | flops 1000000000 | tf_op jit(solution)/shard_map/own_finish/pallas_call | solution.py:609
  34.4 0.3 collective-permute-done.17.corner_ref
  34.7 0.0 collective-permute-done.16.other_ref
  34.7 1.6 %finish.1 = bf16[4,4,8,768]{3,2,1,0:T(8,128)(2,1)} custom-call(f32[128,768]{1,0:T(8,128)S(1)} %get-tuple-element.105.total_ref, bf16[3,64,384]{2,1,0:T(8,128)(2,1)S(1)} %collective-permute-done.16.other_ref, bf16[64,384]{1,0:T(8,128)(2,1)S(1)} %collective-permute-done.17.corner_ref, f32[2,128,192]{2,1,0:T(8,128)S(1)} %get-tuple-element.108.raws_ref, ...), custom_call_target="tpu_custom_call" | custom-call | flops 2000000000 | tf_op jit(solution)/shard_map/finish/pallas_call | solution.py:609
  (13 shorter events, 0.2 us)
Async XLA Ops:
  0.0 1.6 %copy-start = (bf16[3,768,384]{2,1,0:T(8,128)(2,1)S(1)}, bf16[3,768,384]{2,1,0:T(8,128)(2,1)}, u32[]{:S(2)}) copy-start(bf16[3,768,384]{2,1,0:T(8,128)(2,1)} %qkv_ref.5) | copy-start | bytes 5308420
  0.0 1.1 %copy-start.2 = (bf16[4,4,8,768]{3,2,1,0:T(8,128)(2,1)S(1)}, bf16[4,4,8,768]{3,2,1,0:T(8,128)(2,1)}, u32[]{:S(2)}) copy-start(bf16[4,4,8,768]{3,2,1,0:T(8,128)(2,1)} %tokens_ref.1) | copy-start | bytes 589828
  1.1 0.8 %copy-start.4 = (f32[768]{0:T(1024)S(1)}, f32[768]{0:T(1024)}, u32[]{:S(2)}) copy-start(f32[768]{0:T(1024)} %gain_ref.3) | copy-start | bytes 9220
  1.1 0.8 %copy-start.5 = (s32[1,1,2]{2,1,0:T(1,128)S(1)}, s32[1,1,2]{2,1,0:T(1,128)}, u32[]{:S(2)}) copy-start(s32[1,1,2]{2,1,0:T(1,128)} %count_ref.1) | copy-start | bytes 28
  1.9 4.5 %copy-start.1 = (bf16[384,768]{1,0:T(8,128)(2,1)S(1)}, bf16[384,768]{1,0:T(8,128)(2,1)}, u32[]{:S(2)}) copy-start(bf16[384,768]{1,0:T(8,128)(2,1)} %out_weight_ref.1) | copy-start | bytes 1769476
  1.9 4.5 %copy-start.3 = (bf16[4,4,8,768]{3,2,1,0:T(8,128)(2,1)S(1)}, bf16[4,4,8,768]{3,2,1,0:T(8,128)(2,1)}, u32[]{:S(2)}) copy-start(bf16[4,4,8,768]{3,2,1,0:T(8,128)(2,1)} %grad_ref.1) | copy-start | bytes 589828
  1.9 4.5 %copy-start.6 = (f32[6]{0:T(128)S(1)}, f32[6]{0:T(128)}, u32[]{:S(2)}) copy-start(f32[6]{0:T(128)} %scale_in.1) | copy-start | bytes 76
  2.5 5.2 %collective-permute-start.2 = (bf16[64,384]{1,0:T(8,128)(2,1)S(1)}, bf16[64,384]{1,0:T(8,128)(2,1)S(1)}, u32[]{:S(2)}, u32[]{:S(2)}) collective-permute-start(bf16[64,384]{1,0:T(8,128)(2,1)S(1)} %get-tuple-element.66), channel_id=1, source_target_pairs={{0,3},{1,2},{2,1},{3,0},{4,7},{5,6},{6,5},{7,4},{8,11},{9,10},{10,... | collective-permute-start | bytes 147464 | tf_op jit(solution)/shard_map/ppermute | solution.py:36
  5.2 5.2 %collective-permute-start = (bf16[2,64,384]{2,1,0:T(8,128)(2,1)S(1)}, bf16[2,64,384]{2,1,0:T(8,128)(2,1)S(1)}, u32[]{:S(2)}, u32[]{:S(2)}) collective-permute-start(bf16[2,64,384]{2,1,0:T(8,128)(2,1)S(1)} %get-tuple-element.61.kv_other_ref), channel_id=1, source_target_pairs={{0,4},{4,0},{1,5},{5,1},{2,6},{6,2},{3,7},{7,3},{8,12},{12,8},{9,1... | collective-permute-start | bytes 294920 | tf_op jit(solution)/shard_map/ppermute | solution.py:36
  7.3 4.5 %collective-permute-start.3 = (bf16[64,384]{1,0:T(8,128)(2,1)S(1)}, bf16[64,384]{1,0:T(8,128)(2,1)S(1)}, u32[]{:S(2)}, u32[]{:S(2)}) collective-permute-start(bf16[64,384]{1,0:T(8,128)(2,1)S(1)} %get-tuple-element.68), channel_id=1, source_target_pairs={{0,7},{1,6},{2,5},{3,4},{4,3},{5,2},{6,1},{7,0},{8,15},{9,14},{10,... | collective-permute-start | bytes 147464 | tf_op jit(solution)/shard_map/ppermute | solution.py:58
  7.7 8.3 %collective-permute-start.5 = (bf16[3,64,384]{2,1,0:T(8,128)(2,1)S(1)}, bf16[3,64,384]{2,1,0:T(8,128)(2,1)S(1)}, u32[]{:S(2)}, u32[]{:S(2)}) collective-permute-start(bf16[3,64,384]{2,1,0:T(8,128)(2,1)S(1)} %pad_maximum_fusion.1.refs_0_.refs_2_), channel_id=1, source_target_pairs={{0,1},{1,0},{2,3},{3,2},{8,16},{9,17},{10,18},{11,19},{16,8},{17,9... | collective-permute-start | bytes 442376 | tf_op jit(solution)/shard_map/ppermute | solution.py:48
  7.8 8.5 %collective-permute-start.4 = (bf16[3,64,384]{2,1,0:T(8,128)(2,1)S(1)}, bf16[3,64,384]{2,1,0:T(8,128)(2,1)S(1)}, u32[]{:S(2)}, u32[]{:S(2)}) collective-permute-start(bf16[3,64,384]{2,1,0:T(8,128)(2,1)S(1)} %pad_maximum_fusion.1.refs_0_.refs_2_), channel_id=1, source_target_pairs={{0,8},{1,9},{2,10},{3,11},{8,0},{9,1},{10,2},{11,3},{16,24},{17,25... | collective-permute-start | bytes 442376 | tf_op jit(solution)/shard_map/ppermute | solution.py:48
  10.4 4.1 %collective-permute-start.1 = (bf16[2,64,384]{2,1,0:T(8,128)(2,1)S(1)}, bf16[2,64,384]{2,1,0:T(8,128)(2,1)S(1)}, u32[]{:S(2)}, u32[]{:S(2)}) collective-permute-start(bf16[2,64,384]{2,1,0:T(8,128)(2,1)S(1)} %get-tuple-element.65), channel_id=1, source_target_pairs={{0,4},{4,0},{1,5},{5,1},{2,6},{6,2},{3,7},{7,3},{8,12},{12,8},{9,1... | collective-permute-start | bytes 294920 | tf_op jit(solution)/shard_map/ppermute | solution.py:36
  11.8 7.9 %collective-permute-start.7 = (bf16[3,64,384]{2,1,0:T(8,128)(2,1)S(1)}, bf16[3,64,384]{2,1,0:T(8,128)(2,1)S(1)}, u32[]{:S(2)}, u32[]{:S(2)}) collective-permute-start(bf16[3,64,384]{2,1,0:T(8,128)(2,1)S(1)} %pad_maximum_fusion.2.refs_1_.refs_3_), channel_id=1, source_target_pairs={{0,1},{1,0},{2,3},{3,2},{8,16},{9,17},{10,18},{11,19},{16,8},{17,9... | collective-permute-start | bytes 442376 | tf_op jit(solution)/shard_map/ppermute | solution.py:48
  12.9 6.8 %collective-permute-start.6 = (bf16[3,64,384]{2,1,0:T(8,128)(2,1)S(1)}, bf16[3,64,384]{2,1,0:T(8,128)(2,1)S(1)}, u32[]{:S(2)}, u32[]{:S(2)}) collective-permute-start(bf16[3,64,384]{2,1,0:T(8,128)(2,1)S(1)} %pad_maximum_fusion.2.refs_1_.refs_3_), channel_id=1, source_target_pairs={{0,8},{1,9},{2,10},{3,11},{8,0},{9,1},{10,2},{11,3},{16,24},{17,25... | collective-permute-start | bytes 442376 | tf_op jit(solution)/shard_map/ppermute | solution.py:48
  14.5 9.3 %collective-permute-start.13 = (bf16[4,64,384]{2,1,0:T(8,128)(2,1)S(1)}, bf16[4,64,384]{2,1,0:T(8,128)(2,1)S(1)}, u32[]{:S(2)}, u32[]{:S(2)}) collective-permute-start(bf16[4,64,384]{2,1,0:T(8,128)(2,1)S(1)} %constant_dynamic-update-slice_fusion.qg_ref), channel_id=1, source_target_pairs={{0,1},{1,0},{2,3},{3,2},{8,16},{9,17},{10,18},{11,19},{16,8},{17,9... | collective-permute-start | bytes 589832 | tf_op jit(solution)/shard_map/ppermute | solution.py:48
  16.0 7.8 %collective-permute-start.12 = (bf16[4,64,384]{2,1,0:T(8,128)(2,1)S(1)}, bf16[4,64,384]{2,1,0:T(8,128)(2,1)S(1)}, u32[]{:S(2)}, u32[]{:S(2)}) collective-permute-start(bf16[4,64,384]{2,1,0:T(8,128)(2,1)S(1)} %constant_dynamic-update-slice_fusion.qg_ref), channel_id=1, source_target_pairs={{0,8},{1,9},{2,10},{3,11},{8,0},{9,1},{10,2},{11,3},{16,24},{17,25... | collective-permute-start | bytes 589832 | tf_op jit(solution)/shard_map/ppermute | solution.py:48
  16.4 4.8 %collective-permute-start.8 = (bf16[4,64,384]{2,1,0:T(8,128)(2,1)S(1)}, bf16[4,64,384]{2,1,0:T(8,128)(2,1)S(1)}, u32[]{:S(2)}, u32[]{:S(2)}) collective-permute-start(bf16[4,64,384]{2,1,0:T(8,128)(2,1)S(1)} %pad_maximum_fusion), channel_id=1, source_target_pairs={{0,1},{1,0},{2,3},{3,2},{4,5},{5,4},{6,7},{7,6},{8,9},{9,8},{10,11... | collective-permute-start | bytes 589832 | tf_op jit(solution)/shard_map/ppermute | solution.py:36
  19.8 1.4 %collective-permute-start.9 = (bf16[2,64,384]{2,1,0:T(8,128)(2,1)S(1)}, bf16[2,64,384]{2,1,0:T(8,128)(2,1)S(1)}, u32[]{:S(2)}, u32[]{:S(2)}) collective-permute-start(bf16[2,64,384]{2,1,0:T(8,128)(2,1)S(1)} %pad_maximum_fusion.3), channel_id=1, source_target_pairs={{0,1},{1,0},{2,3},{3,2},{4,5},{5,4},{6,7},{7,6},{8,9},{9,8},{10,11... | collective-permute-start | bytes 294920 | tf_op jit(solution)/shard_map/ppermute | solution.py:36
  21.8 4.0 %collective-permute-start.11 = (f32[6,256]{1,0:T(8,128)S(1)}, f32[6,256]{1,0:T(8,128)S(1)}, u32[]{:S(2)}, u32[]{:S(2)}) collective-permute-start(f32[6,256]{1,0:T(8,128)S(1)} %get-tuple-element.75.stats_ref), channel_id=1, source_target_pairs={{0,1},{1,0},{2,3},{3,2},{8,16},{9,17},{10,18},{11,19},{16,8},{17,9... | collective-permute-start | bytes 18440 | tf_op jit(solution)/shard_map/ppermute | solution.py:48
  22.1 3.8 %collective-permute-start.10 = (f32[6,256]{1,0:T(8,128)S(1)}, f32[6,256]{1,0:T(8,128)S(1)}, u32[]{:S(2)}, u32[]{:S(2)}) collective-permute-start(f32[6,256]{1,0:T(8,128)S(1)} %get-tuple-element.75.stats_ref), channel_id=1, source_target_pairs={{0,8},{1,9},{2,10},{3,11},{8,0},{9,1},{10,2},{11,3},{16,24},{17,25... | collective-permute-start | bytes 18440 | tf_op jit(solution)/shard_map/ppermute | solution.py:48
  26.2 1.6 %collective-permute-start.14 = (bf16[2,64,384]{2,1,0:T(8,128)(2,1)S(1)}, bf16[2,64,384]{2,1,0:T(8,128)(2,1)S(1)}, u32[]{:S(2)}, u32[]{:S(2)}) collective-permute-start(bf16[2,64,384]{2,1,0:T(8,128)(2,1)S(1)} %cross_sibling.1), channel_id=1, source_target_pairs={{0,1},{1,0},{2,3},{3,2},{4,5},{5,4},{6,7},{7,6},{8,9},{9,8},{10,11... | collective-permute-start | bytes 294920 | tf_op jit(solution)/shard_map/ppermute | solution.py:36
  27.9 6.9 %collective-permute-start.16 = (bf16[3,64,384]{2,1,0:T(8,128)(2,1)S(1)}, bf16[3,64,384]{2,1,0:T(8,128)(2,1)S(1)}, u32[]{:S(2)}, u32[]{:S(2)}) collective-permute-start(bf16[3,64,384]{2,1,0:T(8,128)(2,1)S(1)} %get-tuple-element.106), channel_id=1, source_target_pairs={{0,4},{4,0},{1,5},{5,1},{2,6},{6,2},{3,7},{7,3},{8,12},{12,8},{9,1... | collective-permute-start | bytes 442376 | tf_op jit(solution)/shard_map/ppermute | solution.py:36
  29.0 4.3 %collective-permute-start.15 = (bf16[64,384]{1,0:T(8,128)(2,1)S(1)}, bf16[64,384]{1,0:T(8,128)(2,1)S(1)}, u32[]{:S(2)}, u32[]{:S(2)}) collective-permute-start(bf16[64,384]{1,0:T(8,128)(2,1)S(1)} %get-tuple-element.99), channel_id=1, source_target_pairs={{0,3},{1,2},{2,1},{3,0},{4,7},{5,6},{6,5},{7,4},{8,11},{9,10},{10,... | collective-permute-start | bytes 147464 | tf_op jit(solution)/shard_map/ppermute | solution.py:36
  30.1 4.6 %collective-permute-start.17 = (bf16[64,384]{1,0:T(8,128)(2,1)S(1)}, bf16[64,384]{1,0:T(8,128)(2,1)S(1)}, u32[]{:S(2)}, u32[]{:S(2)}) collective-permute-start(bf16[64,384]{1,0:T(8,128)(2,1)S(1)} %get-tuple-element.107), channel_id=1, source_target_pairs={{0,7},{1,6},{2,5},{3,4},{4,3},{5,2},{6,1},{7,0},{8,15},{9,14},{10,... | collective-permute-start | bytes 147464 | tf_op jit(solution)/shard_map/ppermute | solution.py:58
